TPU v7x, 32 devices: a whole 2x2x4 slice. The times are simulated.
32 devices in a mesh: rep: 2 (over x), exp: 16 (over z, y, core).
Axes of the slice: x: 2, y: 2, z: 4, core: 2. Of those that a mesh axis runs over, the one named last changes fastest.
Arguments:
- tokens: bfloat16 [128, 256, 1280], P(('rep', 'exp')), may hold values from -19 to 19
- slot_params: bfloat16 [1280, 16], replicated, may hold values from -1 to 1
- expert_in: bfloat16 [16, 1280, 2560], P('exp'), may hold values from -0.15625 to 0.15625
- expert_out: bfloat16 [16, 2560, 1280], P('exp'), may hold values from -0.125 to 0.125
- grad_out: bfloat16 [128, 256, 1280], P(('rep', 'exp')), may hold values from -6 to 6
Outputs:
- grad_tokens: bfloat16 [128, 256, 1280], P(('rep', 'exp'))
- grad_params: float32 [1280, 16], replicated
- grad_expert_in: bfloat16 [16, 1280, 2560], P('exp', 'rep')
- grad_expert_out: bfloat16 [16, 2560, 1280], P('exp', 'rep')
All inputs are finite; a program needn't handle non-finite values.
Results may differ from a plain program's by a relative error of at most 0.0093.
Values may be sent and summed in bfloat16 or wider, within the bound.
No kernel may reach another device: no remote copies, remote signals or barrier semaphores. Data moves between devices by JAX's collectives and lax.ppermute only.
A program may use at most 128 MiB of HBM per device.

v0:
```python
import math

import jax
import jax.numpy as jnp
from jax import lax
from jax.sharding import PartitionSpec as P

GELU_C = math.sqrt(2.0 / math.pi)
CUBIC = 0.044715


def gelu_tanh(values):
    inner = GELU_C * (values + CUBIC * values * values * values)
    return 0.5 * values * (1.0 + jnp.tanh(inner))


def gelu_slope(values):
    tangent = jnp.tanh(GELU_C * (values + CUBIC * values * values * values))
    return 0.5 * (1.0 + tangent) + 0.5 * values * (1.0 - tangent * tangent) * GELU_C * (
        1.0 + 3.0 * CUBIC * values * values
    )


def replica_terms(left, right, replicas):
    left_split = left.reshape(replicas, -1, left.shape[1])
    right_split = right.reshape(replicas, -1, right.shape[1])
    terms = jnp.einsum(
        "rka,rkb->rab", left_split, right_split, preferred_element_type=jnp.float32
    ).astype(jnp.bfloat16)
    terms = lax.optimization_barrier(terms)
    return jnp.sum(terms.astype(jnp.float32), axis=0)


def backward_rows(rows_grad, weight_in, weight_out, preact):
    d_acts = lax.dot_general(
        rows_grad, weight_out, (((1,), (1,)), ((), ())), preferred_element_type=jnp.float32
    )
    d_hidden = (d_acts * gelu_slope(preact)).astype(jnp.bfloat16)
    d_rows = lax.dot_general(
        d_hidden, weight_in, (((1,), (1,)), ((), ())), preferred_element_type=jnp.float32
    ).astype(jnp.bfloat16)
    return (d_hidden, d_rows)


def body(tokens, slot_params, expert_in, expert_out, grad_out):
    width = tokens.shape[2]
    logits = jnp.einsum("bmd,ds->bsm", tokens, slot_params, preferred_element_type=jnp.float32)
    dispatch = jax.nn.softmax(logits, axis=2)
    combine = jax.nn.softmax(logits, axis=1)
    dispatch_low = dispatch.astype(jnp.bfloat16)
    combine_low = combine.astype(jnp.bfloat16)
    slot_in = jnp.einsum(
        "bsm,bmd->bsd", dispatch_low, tokens, preferred_element_type=jnp.float32
    ).astype(jnp.bfloat16)
    rows_in = lax.all_to_all(slot_in, "exp", split_axis=1, concat_axis=0, tiled=True)
    slot_grad = jnp.einsum(
        "bsm,bmd->bsd", combine_low, grad_out, preferred_element_type=jnp.float32
    ).astype(jnp.bfloat16)
    rows_grad = lax.all_to_all(slot_grad, "exp", split_axis=1, concat_axis=0, tiled=True)
    rows_in = rows_in.reshape(-1, width)
    rows_grad = rows_grad.reshape(-1, width)
    weight_in = expert_in[0]
    weight_out = expert_out[0]
    preact = jnp.dot(rows_in, weight_in, preferred_element_type=jnp.float32)
    activations = gelu_tanh(preact).astype(jnp.bfloat16)
    rows_out = jnp.dot(activations, weight_out, preferred_element_type=jnp.float32).astype(
        jnp.bfloat16
    )
    slot_out = lax.all_to_all(
        rows_out.reshape(-1, 1, width), "exp", split_axis=0, concat_axis=1, tiled=True
    )
    d_hidden, d_rows = backward_rows(rows_grad, weight_in, weight_out, preact)
    d_slot_in = lax.all_to_all(
        d_rows.reshape(-1, 1, width), "exp", split_axis=0, concat_axis=1, tiled=True
    )
    replicas = lax.axis_size("rep")
    input_columns, act_columns = (
        lax.all_to_all(rows_in, "rep", split_axis=1, concat_axis=0, tiled=True),
        lax.all_to_all(activations, "rep", split_axis=1, concat_axis=0, tiled=True),
    )
    all_hidden, all_grad = (
        lax.all_gather(d_hidden, "rep", axis=0, tiled=True),
        lax.all_gather(rows_grad, "rep", axis=0, tiled=True),
    )
    grad_in = replica_terms(input_columns, all_hidden, replicas)
    grad_outer = replica_terms(act_columns, all_grad, replicas)
    grad_expert_in = grad_in.astype(jnp.bfloat16)[None]
    grad_expert_out = grad_outer.astype(jnp.bfloat16)[None]
    d_combine = jnp.einsum("bmd,bsd->bsm", grad_out, slot_out, preferred_element_type=jnp.float32)
    d_dispatch = jnp.einsum("bmd,bsd->bsm", tokens, d_slot_in, preferred_element_type=jnp.float32)
    d_logits = combine * (d_combine - jnp.sum(combine * d_combine, axis=1, keepdims=True))
    d_logits = d_logits + dispatch * (
        d_dispatch - jnp.sum(dispatch * d_dispatch, axis=2, keepdims=True)
    )
    d_logits_low = d_logits.astype(jnp.bfloat16)
    grad_tokens = jnp.einsum(
        "bsm,bsd->bmd", dispatch_low, d_slot_in, preferred_element_type=jnp.float32
    )
    grad_tokens = grad_tokens + jnp.einsum(
        "bsm,ds->bmd", d_logits_low, slot_params, preferred_element_type=jnp.float32
    )
    local_params = jnp.einsum(
        "bmd,bsm->ds", tokens, d_logits_low, preferred_element_type=jnp.float32
    )
    grad_params = lax.psum(local_params, ("rep", "exp"))
    return (grad_tokens.astype(jnp.bfloat16), grad_params, grad_expert_in, grad_expert_out)


def solution(mesh):
    in_specs = (
        P(("rep", "exp"), None, None),
        P(),
        P("exp", None, None),
        P("exp", None, None),
        P(("rep", "exp"), None, None),
    )
    out_specs = (P(("rep", "exp"), None, None), P(), P("exp", "rep", None), P("exp", "rep", None))
    return jax.shard_map(body, mesh=mesh, in_specs=in_specs, out_specs=out_specs, check_vma=False)
```

profile of v0, /device:TPU:0, one launch (start us, length us, event | category | flops | bytes accessed | tf_op | source)
XLA Modules:
  0.0 258.4 jit_solution(736469782453837742)
XLA Ops:
  7.2 1.7 copy-done
  8.9 1.5 convolution_bitcast_fusion.1
  10.5 0.7 fusion.69
  11.2 0.5 convolution_convert_fusion.2
  11.7 0.8 copy.26
  12.5 7.4 %all-to-all-start.1 = ((bf16[4,16,1280]{2,0,1:T(4,128)(2,1)}), bf16[4,16,1280]{2,0,1:T(4,128)(2,1)S(1)}, u32[]{:S(2)}, u32[]{:S(2)}) async-start(bf16[4,16,1280]{2,0,1:T(4,128)(2,1)} %copy.26), calls=%async_computation.1 | async-start | bytes 327680 | tf_op jit(solution)/shard_map/all_to_all | solution.py:55
  19.9 0.7 fusion.68
  20.5 2.2 convolution_convert_fusion.3
  22.7 0.8 copy.25
  23.5 4.9 %all-to-all-done.1 = bf16[4,16,1280]{2,0,1:T(4,128)(2,1)S(1)} async-done(((bf16[4,16,1280]{2,0,1:T(4,128)(2,1)}), bf16[4,16,1280]{2,0,1:T(4,128)(2,1)S(1)}, u32[]{:S(2)}, u32[]{:S(2)}) %all-to-all-start.1) | async-done | bytes 163872 | tf_op jit(solution)/shard_map/all_to_all | solution.py:55
  28.3 3.5 %all-to-all-start = ((bf16[4,16,1280]{2,0,1:T(4,128)(2,1)}), bf16[4,16,1280]{2,0,1:T(4,128)(2,1)S(1)}, u32[]{:S(2)}, u32[]{:S(2)}) async-start(bf16[4,16,1280]{2,0,1:T(4,128)(2,1)} %copy.25), calls=%async_computation | async-start | bytes 327680 | tf_op jit(solution)/shard_map/all_to_all | solution.py:59
  31.8 0.1 all_to_all.86
  32.0 8.3 %all-to-all-done = bf16[4,16,1280]{2,0,1:T(4,128)(2,1)S(1)} async-done(((bf16[4,16,1280]{2,0,1:T(4,128)(2,1)}), bf16[4,16,1280]{2,0,1:T(4,128)(2,1)S(1)}, u32[]{:S(2)}, u32[]{:S(2)}) %all-to-all-start) | async-done | bytes 163872 | tf_op jit(solution)/shard_map/all_to_all | solution.py:59
  40.3 4.4 %multiply_convert_fusion = (bf16[64,2560]{1,0:T(8,128)(2,1)S(1)}, f32[64,2560]{1,0:T(8,128)S(1)}) fusion(bf16[64,1280]{1,0:T(8,128)(2,1)S(1)} %reshape.46, bf16[1,1280,2560]{2,1,0:T(8,128)(2,1)} %param.7), kind=kOutput, calls=%fused_computation.42 | convolution fusion | flops 420904960 | bytes 7700480 | tf_op jit(solution)/shard_map/dot_general | solution.py:64
  44.7 5.1 %fusion.15 = bf16[64,2560]{1,0:T(8,128)(2,1)S(1)} fusion(bf16[64,1280]{1,0:T(8,128)(2,1)S(1)} %reshape.45, bf16[1,2560,1280]{2,1,0:T(8,128)(2,1)} %param.8, f32[64,2560]{1,0:T(8,128)S(1)} %get-tuple-element.9), kind=kOutput, calls=%fused_computation.16 | convolution fusion | flops 422543360 | bytes 7700480 | tf_op jit(solution)/shard_map/dot_general | solution.py:35
  49.8 2.1 fusion.24
  51.9 9.7 %all_gather.6 = bf16[128,2560]{1,0:T(8,128)(2,1)} all-gather(bf16[64,2560]{1,0:T(8,128)(2,1)S(1)} %fusion.15), channel_id=1, replica_groups=mesh['rep'=2,'exp'=16] {'rep'}, dimensions={0}, use_global_device_ids=true | all-gather | bytes 983040 | tf_op jit(solution)/shard_map/all_gather | solution.py:82
  61.7 0.7 copy.31
  62.3 4.1 %all-to-all-start.4 = ((bf16[64,2,640]{2,0,1:T(8,128)(2,1)}), bf16[64,2,640]{2,0,1:T(8,128)(2,1)}, u32[]{:S(2)}, u32[]{:S(2)}) async-start(bf16[64,2,640]{2,0,1:T(8,128)(2,1)} %copy.31), calls=%async_computation.4 | async-start | bytes 327680 | tf_op jit(solution)/shard_map/all_to_all | solution.py:78
  66.4 0.5 broadcast.32
  66.9 0.7 reduce.4
  67.6 0.8 reshape.55
  68.4 4.1 %fusion.27 = bf16[64,1,1280]{2,0,1:T(8,128)(2,1)S(1)} fusion(bf16[64,2560]{1,0:T(8,128)(2,1)S(1)} %get-tuple-element.8, bf16[1,2560,1280]{2,1,0:T(8,128)(2,1)} %param.8), kind=kOutput, calls=%fused_computation.22 | convolution fusion | flops 419512320 | bytes 7045120 | tf_op jit(solution)/shard_map/dot_general | solution.py:66
  72.5 0.7 reduce.5
  73.2 0.8 reshape.57
  74.0 0.7 copy.49
  74.7 6.0 %all_gather.7 = bf16[128,1280]{1,0:T(8,128)(2,1)S(1)} all-gather(bf16[64,1280]{1,0:T(8,128)(2,1)S(1)} %reshape.45), channel_id=1, replica_groups=mesh['rep'=2,'exp'=16] {'rep'}, dimensions={0}, use_global_device_ids=true | all-gather | bytes 491520 | tf_op jit(solution)/shard_map/all_gather | solution.py:83
  80.7 3.5 %all-to-all-start.5 = ((bf16[64,2,1280]{2,0,1:T(8,128)(2,1)}), bf16[64,2,1280]{2,0,1:T(8,128)(2,1)S(1)}, u32[]{:S(2)}, u32[]{:S(2)}) async-start(bf16[64,2,1280]{2,0,1:T(8,128)(2,1)} %bitcast.103), calls=%async_computation.5 | async-start | bytes 655360 | tf_op jit(solution)/shard_map/all_to_all | solution.py:79
  84.2 5.8 %convolution_convert_fusion.1 = bf16[2,640,2560]{2,1,0:T(8,128)(2,1)} fusion(bf16[2,64,2560]{2,1,0:T(8,128)(2,1)} %bitcast.99, bf16[64,2,640]{2,0,1:T(8,128)(2,1)} %all-to-all-done.4), kind=kOutput, calls=%fused_computation.13 | convolution fusion | flops 422707200 | bytes 7372800 | tf_op jit(solution)/shard_map/rka,rkb->rab/dot_general | solution.py:27
  90.0 6.7 %reduce_sum.64 = bf16[640,2560]{1,0:T(8,128)(2,1)} reduce(bf16[2,640,2560]{2,1,0:T(8,128)(2,1)} %convolution_convert_fusion.1, bf16[]{:T(256)} %constant.18.clone.1), dimensions={0}, to_apply=%region_7.0 | reduce | flops 1638400 | bytes 9830402 | tf_op jit(solution)/shard_map/reduce_sum | solution.py:31
  96.7 3.7 %all-to-all-start.2 = ((bf16[16,2,2560]{2,1,0:T(2,128)(2,1)}), bf16[16,2,2560]{2,1,0:T(2,128)(2,1)S(1)}, u32[]{:S(2)}, u32[]{:S(2)}) async-start(bf16[16,2,2560]{2,1,0:T(2,128)(2,1)} %reshape.55), calls=%async_computation.2 | async-start | bytes 327680 | tf_op jit(solution)/shard_map/all_to_all | solution.py:73
  100.4 4.6 %convolution_convert_fusion = bf16[2,1280,1280]{2,1,0:T(8,128)(2,1)} fusion(bf16[2,64,1280]{2,1,0:T(8,128)(2,1)S(1)} %bitcast.102, bf16[64,2,1280]{2,0,1:T(8,128)(2,1)S(1)} %all-to-all-done.5), kind=kOutput, calls=%fused_computation.4 | convolution fusion | flops 422707200 | bytes 7208960 | tf_op jit(solution)/shard_map/rka,rkb->rab/dot_general | solution.py:27
  105.1 6.6 %reduce_sum.65 = bf16[1280,1280]{1,0:T(8,128)(2,1)} reduce(bf16[2,1280,1280]{2,1,0:T(8,128)(2,1)} %convolution_convert_fusion, bf16[]{:T(256)} %constant.18.clone.1), dimensions={0}, to_apply=%region_8.0 | reduce | flops 1638400 | bytes 9830402 | tf_op jit(solution)/shard_map/reduce_sum | solution.py:31
  111.6 5.8 %all-to-all-start.3 = ((bf16[16,2,2560]{2,1,0:T(2,128)(2,1)}), bf16[16,2,2560]{2,1,0:T(2,128)(2,1)S(1)}, u32[]{:S(2)}, u32[]{:S(2)}) async-start(bf16[16,2,2560]{2,1,0:T(2,128)(2,1)} %reshape.57), calls=%async_computation.3 | async-start | bytes 327680 | tf_op jit(solution)/shard_map/all_to_all | solution.py:69
  117.4 0.0 all-reduce.2.cloned.1.call-start
  117.5 0.1 reshape.56
  117.6 0.9 reduce.2
  118.6 3.3 %fusion.51 = f32[4,256,1280]{2,1,0:T(8,128)} fusion(bf16[16,4,1,1280]{3,1,0,2:T(4,128)(2,1)S(1)} %all_to_all.79, f32[4,16]{1,0:T(4,128)S(1)} %get-tuple-element.6, f32[4,16,256]{2,1,0:T(8,128)S(1)} %convolution_bitcast_fusion.1), kind=kOutput, calls=%fused_computation.50 | convolution fusion | flops 41992512 | bytes 5472512 | tf_op jit(solution)/shard_map/bsm,bsd->bmd/dot_general | solution.py:96
  121.9 0.8 fusion.49
  122.7 3.2 %all-to-all-done.3 = bf16[16,2,2560]{2,1,0:T(2,128)(2,1)S(1)} async-done(((bf16[16,2,2560]{2,1,0:T(2,128)(2,1)}), bf16[16,2,2560]{2,1,0:T(2,128)(2,1)S(1)}, u32[]{:S(2)}, u32[]{:S(2)}) %all-to-all-start.3) | async-done | bytes 163872 | tf_op jit(solution)/shard_map/all_to_all | solution.py:69
  125.9 0.1 reshape.58
  126.0 0.9 reduce.3
  127.0 2.5 fusion.46
  129.5 1.1 fusion.38
  130.6 1.1 convolution_bitcast_fusion
  131.8 4.9 %add_convert_fusion = bf16[4,256,1280]{2,1,0:T(8,128)(2,1)} fusion(f32[4,256,1280]{2,1,0:T(8,128)} %fusion.51, f32[4,16,256]{2,1,0:T(8,128)S(1)} %fusion.38, f32[4,16,256]{2,1,0:T(8,128)S(1)} %fusion.46, bf16[1280,16]{0,1:T(8,128)(2,1)S(1)} %copy-done.2, f32[4,16,256]{2,1,0:T(8,128)S(1)} %copy-done.1, f32[4,256]{1,0:T(4,128)S(1)} %get-tuple-element.4), kind=kOutput, calls=%fused_computation.14 | convolution fusion | flops 44680208 | bytes 8105984 | tf_op jit(solution)/shard_map/bsm,ds->bmd/dot_general | solution.py:99
  136.7 113.3 %all-reduce.2.cloned.1.call-done = f32[1280,16]{0,1:T(8,128)} async-done(((f32[1280,16]{0,1:T(8,128)}), f32[1280,16]{0,1:T(8,128)}) %all-reduce.2.cloned.1.call-update) | async-done | bytes 81936 | tf_op jit(solution)/shard_map/psum | solution.py:105
  250.0 1.5 copy.53
  (18 shorter events, 0.2 us)
Async XLA Ops:
  7.2 1.7 copy-start
  12.5 15.9 %all-to-all-start.1 = ((bf16[4,16,1280]{2,0,1:T(4,128)(2,1)}), bf16[4,16,1280]{2,0,1:T(4,128)(2,1)S(1)}, u32[]{:S(2)}, u32[]{:S(2)}) async-start(bf16[4,16,1280]{2,0,1:T(4,128)(2,1)} %copy.26), calls=%async_computation.1 | async-start | bytes 327680 | tf_op jit(solution)/shard_map/all_to_all | solution.py:55
  28.3 12.0 %all-to-all-start = ((bf16[4,16,1280]{2,0,1:T(4,128)(2,1)}), bf16[4,16,1280]{2,0,1:T(4,128)(2,1)S(1)}, u32[]{:S(2)}, u32[]{:S(2)}) async-start(bf16[4,16,1280]{2,0,1:T(4,128)(2,1)} %copy.25), calls=%async_computation | async-start | bytes 327680 | tf_op jit(solution)/shard_map/all_to_all | solution.py:59
  40.3 9.5 %slice-start = ((s8[6553600]{0:T(1024)(128)(4,1)}), s8[4194304]{0:T(1024)(128)(4,1)S(1)}, s32[]{:S(2)}) async-start(s8[6553600]{0:T(1024)(128)(4,1)} %bitcast.94), calls=%async_computation.7 | async-start | bytes 8388608
  44.7 5.1 %slice-start.1 = ((s8[6553600]{0:T(1024)(128)(4,1)}), s8[2359296]{0:T(1024)(128)(4,1)S(1)}, s32[]{:S(2)}) async-start(s8[6553600]{0:T(1024)(128)(4,1)} %bitcast.94), calls=%async_computation.8 | async-start | bytes 4718592
  62.3 18.4 %all-to-all-start.4 = ((bf16[64,2,640]{2,0,1:T(8,128)(2,1)}), bf16[64,2,640]{2,0,1:T(8,128)(2,1)}, u32[]{:S(2)}, u32[]{:S(2)}) async-start(bf16[64,2,640]{2,0,1:T(8,128)(2,1)} %copy.31), calls=%async_computation.4 | async-start | bytes 327680 | tf_op jit(solution)/shard_map/all_to_all | solution.py:78
  80.7 16.0 %all-to-all-start.5 = ((bf16[64,2,1280]{2,0,1:T(8,128)(2,1)}), bf16[64,2,1280]{2,0,1:T(8,128)(2,1)S(1)}, u32[]{:S(2)}, u32[]{:S(2)}) async-start(bf16[64,2,1280]{2,0,1:T(8,128)(2,1)} %bitcast.103), calls=%async_computation.5 | async-start | bytes 655360 | tf_op jit(solution)/shard_map/all_to_all | solution.py:79
  96.7 14.9 %all-to-all-start.2 = ((bf16[16,2,2560]{2,1,0:T(2,128)(2,1)}), bf16[16,2,2560]{2,1,0:T(2,128)(2,1)S(1)}, u32[]{:S(2)}, u32[]{:S(2)}) async-start(bf16[16,2,2560]{2,1,0:T(2,128)(2,1)} %reshape.55), calls=%async_computation.2 | async-start | bytes 327680 | tf_op jit(solution)/shard_map/all_to_all | solution.py:73
  111.6 14.3 %all-to-all-start.3 = ((bf16[16,2,2560]{2,1,0:T(2,128)(2,1)}), bf16[16,2,2560]{2,1,0:T(2,128)(2,1)S(1)}, u32[]{:S(2)}, u32[]{:S(2)}) async-start(bf16[16,2,2560]{2,1,0:T(2,128)(2,1)} %reshape.57), calls=%async_computation.3 | async-start | bytes 327680 | tf_op jit(solution)/shard_map/all_to_all | solution.py:69
  117.4 132.6 %all-reduce.2.cloned.1.call-start = ((), (), s32[]{:S(2)}) async-start(), calls=%async_computation.6 | async-start | bytes 163840 | tf_op jit(solution)/shard_map/psum | solution.py:105
  118.6 12.0 %copy-start.1 = (f32[4,16,256]{2,1,0:T(8,128)S(1)}, f32[4,16,256]{2,1,0:T(8,128)}, u32[]{:S(2)}) copy-start(f32[4,16,256]{2,1,0:T(8,128)} %get-tuple-element.5) | copy-start | bytes 196612
  121.9 9.9 %copy-start.2 = (bf16[1280,16]{0,1:T(8,128)(2,1)S(1)}, bf16[1280,16]{0,1:T(8,128)(2,1)}, u32[]{:S(2)}) copy-start(bf16[1280,16]{0,1:T(8,128)(2,1)} %param.6) | copy-start | bytes 122884
Sparse Core Ops, SparseCore 0:
  131.9 118.0 all-reduce.1
where the time goes:
time: 261 us; the launch traced here: 258 us
  waiting for transfers between devices  130 us (50%)
  matrix products  42.9 us (16%)
  starting transfers between devices  27.9 us (11%)
  other arithmetic  19 us (7%)
  blocking collectives  15.7 us (6%)
  between operations  14.2 us (5%)
  local copies, waits for them, and re-layouts  8.81 us (3%)
    psum x1, waiting for transfers between devices, body(): grad_params = lax.psum(local_params, ('rep', 'exp'))  113 us
    reduce_sum x2, other arithmetic, replica_terms(): return jnp.sum(terms.astype(jnp.float32), axis=0)  13.3 us
    dot_general x2, matrix products, replica_terms(): jnp.einsum('rka,rkb->rab', left_split, right_split, preferred_element_typ...  10.5 us
    all_gather x1, blocking collectives, body(): lax.all_gather(d_hidden, 'rep', axis=0, tiled=True)  9.74 us
    all_to_all x1, waiting for transfers between devices, body(): lax.all_to_all(slot_grad, 'exp', split_axis=1, concat_axis=0, tiled=True)  8.3 us
    all_to_all x1, starting transfers between devices, body(): lax.all_to_all(slot_in, 'exp', split_axis=1, concat_axis=0, tiled=True)  7.39 us
    all_gather x1, blocking collectives, body(): lax.all_gather(rows_grad, 'rep', axis=0, tiled=True)  5.98 us
    all_to_all x1, starting transfers between devices, body(): lax.all_to_all(rows_out.reshape(-1, 1, width), 'exp', split_axis=0, conca...  5.79 us
  transfers between devices with their start and end apart: 7, of which 4 were waited for; matrix products, arithmetic and copies ran while one was open for 18% of the time, Pallas kernels for 0%

commit v1 on v0

v1 whole, which is shorter than its diff:
```python
import math

import jax
import jax.numpy as jnp
from jax import lax
from jax.sharding import PartitionSpec as P

GELU_C = math.sqrt(2.0 / math.pi)
CUBIC = 0.044715


def gelu_parts(values):
    tangent = jnp.tanh(GELU_C * (values + CUBIC * values * values * values))
    acts = 0.5 * values * (1.0 + tangent)
    slope = 0.5 * (1.0 + tangent) + 0.5 * values * (1.0 - tangent * tangent) * GELU_C * (
        1.0 + 3.0 * CUBIC * values * values
    )
    return acts, slope


def dot(left, right, contract):
    return lax.dot_general(
        left, right, (contract, ((), ())), preferred_element_type=jnp.float32
    )


def expert_hidden(rows_in, rows_grad, weight_in, weight_out):
    preact = dot(rows_in, weight_in, ((1,), (0,)))
    acts, slope = gelu_parts(preact)
    d_acts = dot(rows_grad, weight_out, ((1,), (1,)))
    return acts.astype(jnp.bfloat16), (d_acts * slope).astype(jnp.bfloat16)


def sum_everywhere(part, axes):
    count = lax.axis_size(axes)
    pieces = part.reshape(count, -1)
    pieces = lax.all_to_all(pieces, axes, split_axis=0, concat_axis=0, tiled=True)
    mine = jnp.sum(pieces, axis=0, keepdims=True)
    mine = jnp.broadcast_to(mine, pieces.shape)
    whole = lax.all_to_all(mine, axes, split_axis=0, concat_axis=0, tiled=True)
    return whole.reshape(part.shape)


def body(tokens, slot_params, expert_in, expert_out, grad_out):
    images, _, width = tokens.shape
    weight_in = expert_in[0]
    weight_out = expert_out[0]
    hidden = weight_in.shape[1]
    replicas = lax.axis_size("rep")
    logits = jnp.einsum("bmd,ds->bsm", tokens, slot_params, preferred_element_type=jnp.float32)
    dispatch = jax.nn.softmax(logits, axis=2)
    combine = jax.nn.softmax(logits, axis=1)
    dispatch_low = dispatch.astype(jnp.bfloat16)
    combine_low = combine.astype(jnp.bfloat16)
    slot_in = jnp.einsum(
        "bsm,bmd->bsd", dispatch_low, tokens, preferred_element_type=jnp.float32
    ).astype(jnp.bfloat16)
    slot_grad = jnp.einsum(
        "bsm,bmd->bsd", combine_low, grad_out, preferred_element_type=jnp.float32
    ).astype(jnp.bfloat16)
    slots = slot_in.shape[1]
    sent = jnp.swapaxes(jnp.concatenate([slot_in, slot_grad], axis=0), 0, 1)
    rows = lax.all_to_all(sent, "exp", split_axis=0, concat_axis=0, tiled=True)
    others = lax.ppermute(rows, "rep", [(i, (i + 1) % replicas) for i in range(replicas)])

    rows_in = rows[:, :images].reshape(-1, width)
    rows_grad = rows[:, images:].reshape(-1, width)
    acts, d_hidden = expert_hidden(rows_in, rows_grad, weight_in, weight_out)
    rows_out = dot(acts, weight_out, ((1,), (0,))).astype(jnp.bfloat16)
    d_rows = dot(d_hidden, weight_in, ((1,), (1,))).astype(jnp.bfloat16)
    back = jnp.concatenate(
        [rows_out.reshape(slots, images, width), d_rows.reshape(slots, images, width)], axis=1
    )
    back = lax.all_to_all(back, "exp", split_axis=0, concat_axis=0, tiled=True)

    others_in = others[:, :images].reshape(-1, width)
    others_grad = others[:, images:].reshape(-1, width)
    others_acts, others_hidden = expert_hidden(others_in, others_grad, weight_in, weight_out)
    mine = lax.axis_index("rep")

    def share(array, full):
        size = full // replicas
        return lax.dynamic_slice_in_dim(array, mine * size, size, axis=1)

    left_in = share(jnp.concatenate([rows_in, others_in], axis=0), width)
    left_acts = share(jnp.concatenate([acts, others_acts], axis=0), hidden)
    all_hidden = jnp.concatenate([d_hidden, others_hidden], axis=0)
    all_grad = jnp.concatenate([rows_grad, others_grad], axis=0)
    grad_expert_in = dot(left_in, all_hidden, ((0,), (0,))).astype(jnp.bfloat16)[None]
    grad_expert_out = dot(left_acts, all_grad, ((0,), (0,))).astype(jnp.bfloat16)[None]

    slot_out = back[:, :images]
    d_slot_in = back[:, images:]
    d_combine = jnp.einsum("bmd,sbd->bsm", grad_out, slot_out, preferred_element_type=jnp.float32)
    d_dispatch = jnp.einsum("bmd,sbd->bsm", tokens, d_slot_in, preferred_element_type=jnp.float32)
    d_logits = combine * (d_combine - jnp.sum(combine * d_combine, axis=1, keepdims=True))
    d_logits = d_logits + dispatch * (
        d_dispatch - jnp.sum(dispatch * d_dispatch, axis=2, keepdims=True)
    )
    d_logits_low = d_logits.astype(jnp.bfloat16)
    local_params = jnp.einsum(
        "bsm,bmd->sd", d_logits_low, tokens, preferred_element_type=jnp.float32
    )
    grad_params = sum_everywhere(local_params, ("rep", "exp")).T
    grad_tokens = jnp.einsum(
        "bsm,sbd->bmd", dispatch_low, d_slot_in, preferred_element_type=jnp.float32
    )
    grad_tokens = grad_tokens + jnp.einsum(
        "bsm,ds->bmd", d_logits_low, slot_params, preferred_element_type=jnp.float32
    )
    return (grad_tokens.astype(jnp.bfloat16), grad_params, grad_expert_in, grad_expert_out)


def solution(mesh):
    in_specs = (
        P(("rep", "exp"), None, None),
        P(),
        P("exp", None, None),
        P("exp", None, None),
        P(("rep", "exp"), None, None),
    )
    out_specs = (P(("rep", "exp"), None, None), P(), P("exp", "rep", None), P("exp", "rep", None))
    return jax.shard_map(body, mesh=mesh, in_specs=in_specs, out_specs=out_specs, check_vma=False)
```

time: 261 us -> 105 us (0.40)
  waiting for transfers between devices: 130 us -> 18.2 us
  blocking collectives: 15.7 us -> 0 us
  other arithmetic: 19 us -> 4.18 us
  between operations: 14.2 us -> 0.85 us
  starting transfers between devices: 27.9 us -> 20.6 us
  local copies, waits for them, and re-layouts: 8.81 us -> 15.7 us
    psum x1 -> x0, waiting for transfers between devices: 113 us -> none  [body(): grad_params = lax.psum(local_params, ('rep', 'exp'))]
    all_gather x2 -> x0, blocking collectives: 15.7 us -> none  [the longest x1 9.74 us: body(): lax.all_gather(d_hidden, 'rep', axis=0, tiled=True)]
    reduce_sum x2 -> x1, other arithmetic: 13.3 us -> 0.07 us  [sum_everywhere(): mine = jnp.sum(pieces, axis=0, keepdims=True)]
    all_to_all x6 -> x4, starting transfers between devices: 27.9 us -> 19.1 us  [the longest x1 7.43 us: body(): rows = lax.all_to_all(sent, 'exp', split_axis=0, concat_axis=0, tiled=True)]
    reshape x3 -> x7, local copies, waits for them, and re-layouts: 0.6 us -> 7.23 us  [the longest x1 1.62 us: body(): d_rows.reshape(slots, images, width)]
    slice x0 -> x3, local copies, waits for them, and re-layouts: none -> 4.48 us  [the longest x1 1.92 us: body(): others_in = others[:, :images].reshape(-1, width)]
    unnamed x15 -> x28, local copies, waits for them, and re-layouts: 5.1 us -> 1.81 us
    all_to_all x6 -> x4, waiting for transfers between devices: 16.4 us -> 18.2 us  [the longest x1 11.2 us: body(): rows = lax.all_to_all(sent, 'exp', split_axis=0, concat_axis=0, tiled=True)]
  transfers between devices with their start and end apart: 7 -> 5, of which waited for: 4 -> 3; matrix products, arithmetic and copies ran while one was open for 18% -> 35% of each run, Pallas kernels for 0% -> 0%
where the time goes in v1:
time: 105 us; the launch traced here: 104 us
  matrix products  44.5 us (42%)
  starting transfers between devices  20.6 us (20%)
  waiting for transfers between devices  18.2 us (17%)
  local copies, waits for them, and re-layouts  15.7 us (15%)
  other arithmetic  4.18 us (4%)
    dot_general x8, matrix products, dot(): lax.dot_general(left, right, (contract, ((), ())), preferred_element_type...  30 us
    all_to_all x1, waiting for transfers between devices, body(): rows = lax.all_to_all(sent, 'exp', split_axis=0, concat_axis=0, tiled=True)  11.2 us
    all_to_all x1, starting transfers between devices, body(): rows = lax.all_to_all(sent, 'exp', split_axis=0, concat_axis=0, tiled=True)  7.43 us
    all_to_all x1, starting transfers between devices, sum_everywhere(): lax.all_to_all(pieces, axes, split_axis=0, concat_axis=0, tiled=True)  4.9 us
    dot_general x1, matrix products, body(): jnp.einsum('bsm,ds->bmd', d_logits_low, slot_params, preferred_element_ty...  4.88 us
    all_to_all x1, waiting for transfers between devices, sum_everywhere(): lax.all_to_all(pieces, axes, split_axis=0, concat_axis=0, tiled=True)  4.32 us
    all_to_all x1, starting transfers between devices, body(): back = lax.all_to_all(back, 'exp', split_axis=0, concat_axis=0, tiled=True)  4.19 us
    dot_general x1, matrix products, body(): jnp.einsum('bsm,sbd->bmd', dispatch_low, d_slot_in, preferred_element_typ...  3.28 us
  transfers between devices with their start and end apart: 5, of which 3 were waited for; matrix products, arithmetic and copies ran while one was open for 35% of the time, Pallas kernels for 0%

profile of v1, /device:TPU:0, one launch (start us, length us, event | category | flops | bytes accessed | tf_op | source)
XLA Modules:
  0.0 104.0 jit_solution(17819552216857674113)
XLA Ops:
  0.6 0.0 copy-start
  0.6 1.7 %copy-done = bf16[4,256,1280]{2,1,0:T(8,128)(2,1)S(1)} copy-done((bf16[4,256,1280]{2,1,0:T(8,128)(2,1)S(1)}, bf16[4,256,1280]{2,1,0:T(8,128)(2,1)}, u32[]{:S(2)}) %copy-start) | copy-done | bytes 2621464
  2.4 1.5 %convolution_bitcast_fusion.1 = f32[4,16,256]{2,1,0:T(8,128)S(1)} fusion(bf16[4,256,1280]{2,1,0:T(8,128)(2,1)S(1)} %copy-done, bf16[1280,16]{0,1:T(8,128)(2,1)} %param.6), kind=kOutput, calls=%fused_computation.39 | convolution fusion | flops 41943040 | bytes 2727936 | tf_op jit(solution)/shard_map/bmd,ds->bsm/dot_general | solution.py:50
  3.9 0.7 fusion.91
  4.6 0.7 fusion.92
  5.3 0.5 convolution_convert_fusion.3
  5.8 2.2 %convolution_convert_fusion.2 = bf16[4,16,1280]{2,1,0:T(8,128)(2,1)S(1)} fusion(bf16[4,256,1280]{2,1,0:T(8,128)(2,1)} %param.9, f32[4,256]{1,0:T(4,128)S(1)} %get-tuple-element.10, f32[4,16,256]{2,1,0:T(8,128)S(1)} %convolution_bitcast_fusion.1), kind=kOutput, calls=%fused_computation.27 | convolution fusion | flops 42075152 | bytes 2854912 | tf_op jit(solution)/shard_map/bsm,bmd->bsd/dot_general | solution.py:58
  8.1 0.8 copy.17
  8.9 7.4 %all-to-all-start = ((bf16[16,8,1280]{2,1,0:T(8,128)(2,1)}), bf16[16,8,1280]{2,1,0:T(8,128)(2,1)}, u32[]{:S(2)}, u32[]{:S(2)}) async-start(bf16[16,8,1280]{2,1,0:T(8,128)(2,1)} %copy.17), calls=%async_computation | async-start | bytes 655360 | tf_op jit(solution)/shard_map/all_to_all | solution.py:63
  16.3 11.2 %all-to-all-done = bf16[16,8,1280]{2,1,0:T(8,128)(2,1)} async-done(((bf16[16,8,1280]{2,1,0:T(8,128)(2,1)}), bf16[16,8,1280]{2,1,0:T(8,128)(2,1)}, u32[]{:S(2)}, u32[]{:S(2)}) %all-to-all-start) | async-done | bytes 327712 | tf_op jit(solution)/shard_map/all_to_all | solution.py:63
  27.5 1.2 %fusion.90 = (bf16[16,4,1280]{2,1,0:T(4,128)(2,1)S(1)}, bf16[16,4,1280]{2,1,0:T(4,128)(2,1)S(1)}) fusion(bf16[16,8,1280]{2,1,0:T(8,128)(2,1)} %all-to-all-done), kind=kLoop, calls=%fused_computation.97 | loop fusion | bytes 655360 | tf_op jit(solution)/shard_map/slice | solution.py:66
  28.8 0.0 slice-start
  28.8 0.0 slice-start.2
  28.8 4.4 %multiply_convert_fusion.1 = (bf16[64,2560]{1,0:T(8,128)(2,1)S(1)}, f32[64,2560]{1,0:T(8,128)S(1)}) fusion(bf16[64,1280]{1,0:T(8,128)(2,1)S(1)} %reshape.46, bf16[1,1280,2560]{2,1,0:T(8,128)(2,1)} %param.7), kind=kOutput, calls=%fused_computation.61 | convolution fusion | flops 420904960 | bytes 7700480 | tf_op jit(solution)/shard_map/dot_general | solution.py:22
  33.2 0.0 slice-start.1
  33.2 0.0 slice-start.3
  33.2 5.1 %fusion.27 = bf16[64,2560]{1,0:T(8,128)(2,1)S(1)} fusion(bf16[64,1280]{1,0:T(8,128)(2,1)S(1)} %reshape.48, bf16[1,2560,1280]{2,1,0:T(8,128)(2,1)} %param.8, f32[64,2560]{1,0:T(8,128)S(1)} %get-tuple-element.15), kind=kOutput, calls=%fused_computation.24 | convolution fusion | flops 422543360 | bytes 7700480 | tf_op jit(solution)/shard_map/dot_general | solution.py:22
  38.4 2.8 %fusion.30 = bf16[64,1280]{1,0:T(8,128)(2,1)} fusion(bf16[64,2560]{1,0:T(8,128)(2,1)S(1)} %fusion.27, bf16[1,1280,2560]{2,1,0:T(8,128)(2,1)S(1)} %bitcast.64), kind=kOutput, calls=%fused_computation.25 | convolution fusion | flops 419512320 | bytes 7045120 | tf_op jit(solution)/shard_map/dot_general | solution.py:22
  41.1 1.5 %collective-permute-start = (bf16[16,8,1280]{2,1,0:T(8,128)(2,1)}, bf16[16,8,1280]{2,1,0:T(8,128)(2,1)}, u32[]{:S(2)}, u32[]{:S(2)}) collective-permute-start(bf16[16,8,1280]{2,1,0:T(8,128)(2,1)} %all-to-all-done), channel_id=1, source_target_pairs={{0,16},{16,0},{1,17},{17,1},{2,18},{18,2},{3,19},{19,3},{4,20},{20... | collective-permute-start | bytes 983048 | tf_op jit(solution)/shard_map/ppermute | solution.py:64
  42.6 1.9 %fusion.33 = bf16[64,1280]{1,0:T(8,128)(2,1)} fusion(bf16[64,2560]{1,0:T(8,128)(2,1)S(1)} %get-tuple-element.14, bf16[1,2560,1280]{2,1,0:T(8,128)(2,1)S(1)} %bitcast.66), kind=kOutput, calls=%fused_computation.26 | convolution fusion | flops 419512320 | bytes 7045120 | tf_op jit(solution)/shard_map/dot_general | solution.py:22
  44.5 1.6 %reshape.49 = bf16[16,4,1280]{2,1,0:T(4,128)(2,1)} reshape(bf16[64,1280]{1,0:T(8,128)(2,1)} %fusion.30) | data formatting | bytes 327680 | tf_op jit(solution)/shard_map/reshape | solution.py:72
  46.2 1.6 %reshape.47 = bf16[16,4,1280]{2,1,0:T(4,128)(2,1)} reshape(bf16[64,1280]{1,0:T(8,128)(2,1)} %fusion.33) | data formatting | bytes 327680 | tf_op jit(solution)/shard_map/reshape | solution.py:72
  47.8 1.9 %pad_maximum_fusion = bf16[16,8,1280]{2,1,0:T(8,128)(2,1)} fusion(bf16[16,4,1280]{2,1,0:T(4,128)(2,1)} %reshape.49, bf16[16,4,1280]{2,1,0:T(4,128)(2,1)} %reshape.47), kind=kLoop, calls=%fused_computation.64 | loop fusion | flops 655360 | bytes 655360 | tf_op jit(solution)/shard_map/concatenate | solution.py:71
  49.7 4.2 %all-to-all-start.1 = ((bf16[16,8,1280]{2,1,0:T(8,128)(2,1)}), bf16[16,8,1280]{2,1,0:T(8,128)(2,1)}, u32[]{:S(2)}, u32[]{:S(2)}) async-start(bf16[16,8,1280]{2,1,0:T(8,128)(2,1)} %pad_maximum_fusion), calls=%async_computation.1 | async-start | bytes 655360 | tf_op jit(solution)/shard_map/all_to_all | solution.py:74
  53.9 1.9 %fusion.88 = (bf16[16,4,1280]{2,1,0:T(4,128)(2,1)}, bf16[16,4,1280]{2,1,0:T(4,128)(2,1)}) fusion(bf16[16,8,1280]{2,1,0:T(8,128)(2,1)} %collective-permute-done), kind=kLoop, calls=%fused_computation.95 | loop fusion | bytes 655360 | tf_op jit(solution)/shard_map/slice | solution.py:76
  55.8 1.6 %reshape.51 = bf16[64,1280]{1,0:T(8,128)(2,1)} reshape(bf16[16,4,1280]{2,1,0:T(4,128)(2,1)} %get-tuple-element.4) | data formatting | bytes 327680 | tf_op jit(solution)/shard_map/reshape | solution.py:76
  57.4 5.2 %multiply_convert_fusion = (bf16[64,2560]{1,0:T(8,128)(2,1)}, f32[64,2560]{1,0:T(8,128)}) fusion(bf16[64,1280]{1,0:T(8,128)(2,1)} %reshape.51, bf16[1,1280,2560]{2,1,0:T(8,128)(2,1)} %param.7), kind=kOutput, calls=%fused_computation.60 | convolution fusion | flops 420904960 | bytes 7700480 | tf_op jit(solution)/shard_map/dot_general | solution.py:22
  62.6 1.6 %reshape.52 = bf16[64,1280]{1,0:T(8,128)(2,1)} reshape(bf16[16,4,1280]{2,1,0:T(4,128)(2,1)} %get-tuple-element.5) | data formatting | bytes 327680 | tf_op jit(solution)/shard_map/reshape | solution.py:77
  64.2 5.2 %fusion.24 = bf16[64,2560]{1,0:T(8,128)(2,1)S(1)} fusion(bf16[64,1280]{1,0:T(8,128)(2,1)} %reshape.52, bf16[1,2560,1280]{2,1,0:T(8,128)(2,1)} %param.8, f32[64,2560]{1,0:T(8,128)} %get-tuple-element.17), kind=kOutput, calls=%fused_computation.23 | convolution fusion | flops 422543360 | bytes 7700480 | tf_op jit(solution)/shard_map/dot_general | solution.py:22
  69.4 0.0 copy-start.6
  69.4 2.8 %fusion.17 = bf16[1,640,2560]{2,1,0:T(8,128)(2,1)} fusion(bf16[64,2560]{1,0:T(8,128)(2,1)S(1)} %fusion.24, bf16[64,2560]{1,0:T(8,128)(2,1)S(1)} %fusion.27, s32[]{:T(128)S(6)} %select_n.6, bf16[64,1280]{1,0:T(8,128)(2,1)S(1)} %copy-done.3, bf16[64,1280]{1,0:T(8,128)(2,1)S(1)} %copy-done.5), kind=kOutput, calls=%fused_computation.20 | convolution fusion | flops 422707200 | bytes 4259844 | tf_op jit(solution)/shard_map/dot_general | solution.py:22
  72.2 2.8 %fusion.16 = bf16[1,1280,1280]{2,1,0:T(8,128)(2,1)} fusion(s32[]{:T(128)S(6)} %select_n.7, bf16[64,2560]{1,0:T(8,128)(2,1)S(1)} %get-tuple-element.14, bf16[64,2560]{1,0:T(8,128)(2,1)S(1)} %copy-done.6, bf16[64,1280]{1,0:T(8,128)(2,1)S(1)} %copy-done.4, bf16[64,1280]{1,0:T(8,128)(2,1)S(1)} %reshape.48), kind=kOutput, calls=%fused_computation.17 | convolution fusion | flops 422379520 | bytes 4259844 | tf_op jit(solution)/shard_map/dot_general | solution.py:22
  75.0 1.4 %fusion.89 = (bf16[16,4,1280]{2,1,0:T(4,128)(2,1)S(1)}, bf16[16,4,1280]{2,1,0:T(4,128)(2,1)S(1)}) fusion(bf16[16,8,1280]{2,1,0:T(8,128)(2,1)} %all-to-all-done.1), kind=kLoop, calls=%fused_computation.96 | loop fusion | bytes 655360 | tf_op jit(solution)/shard_map/slice | solution.py:92
  76.3 0.8 fusion.68
  77.1 0.8 fusion.66
  77.9 0.6 fusion.44
  78.5 0.5 convolution_bitcast_fusion
  79.0 0.7 all_to_all.21
  79.7 4.9 %all-to-all-start.2 = ((f32[32,1,640]{2,1,0:T(1,128)}), f32[32,1,640]{2,1,0:T(1,128)S(1)}, u32[]{:S(2)}, u32[]{:S(2)}) async-start(f32[32,1,640]{2,1,0:T(1,128)} %all_to_all.21), calls=%async_computation.2 | async-start | bytes 163840 | tf_op jit(solution)/shard_map/all_to_all | solution.py:37
  84.6 3.3 %fusion.70 = f32[4,256,1280]{2,1,0:T(8,128)} fusion(bf16[16,4,1280]{2,1,0:T(4,128)(2,1)S(1)} %get-tuple-element.7, f32[4,16]{1,0:T(4,128)S(1)} %get-tuple-element.12, f32[4,16,256]{2,1,0:T(8,128)S(1)} %convolution_bitcast_fusion.1), kind=kOutput, calls=%fused_computation.75 | convolution fusion | flops 41992512 | bytes 5472512 | tf_op jit(solution)/shard_map/bsm,sbd->bmd/dot_general | solution.py:105
  87.9 4.3 %all-to-all-done.2 = f32[32,1,640]{2,1,0:T(1,128)S(1)} async-done(((f32[32,1,640]{2,1,0:T(1,128)}), f32[32,1,640]{2,1,0:T(1,128)S(1)}, u32[]{:S(2)}, u32[]{:S(2)}) %all-to-all-start.2) | async-done | bytes 81952 | tf_op jit(solution)/shard_map/all_to_all | solution.py:37
  92.2 0.1 reduce_sum.49
  92.3 0.7 broadcast_in_dim.6
  93.0 2.6 %all-to-all-start.3 = ((f32[32,1,640]{2,1,0:T(1,128)}), f32[32,1,640]{2,1,0:T(1,128)S(1)}, u32[]{:S(2)}, u32[]{:S(2)}) async-start(f32[32,1,640]{2,1,0:T(1,128)} %broadcast_in_dim.6), calls=%async_computation.3 | async-start | bytes 163840 | tf_op jit(solution)/shard_map/all_to_all | solution.py:40
  95.6 4.9 %add_convert_fusion = bf16[4,256,1280]{2,1,0:T(8,128)(2,1)} fusion(f32[4,256,1280]{2,1,0:T(8,128)} %fusion.70, f32[4,16,256]{2,1,0:T(8,128)S(1)} %fusion.44, f32[4,16,256]{2,1,0:T(8,128)S(1)} %fusion.66, bf16[1280,16]{0,1:T(8,128)(2,1)S(1)} %copy-done.8, f32[4,16,256]{2,1,0:T(8,128)S(1)} %copy-done.7, f32[4,256]{1,0:T(4,128)S(1)} %get-tuple-element.10), kind=kOutput, calls=%fused_computation.18 | convolution fusion | flops 44680208 | bytes 8105984 | tf_op jit(solution)/shard_map/bsm,ds->bmd/dot_general | solution.py:108
  100.5 2.7 %all-to-all-done.3 = f32[32,1,640]{2,1,0:T(1,128)S(1)} async-done(((f32[32,1,640]{2,1,0:T(1,128)}), f32[32,1,640]{2,1,0:T(1,128)S(1)}, u32[]{:S(2)}, u32[]{:S(2)}) %all-to-all-start.3) | async-done | bytes 81952 | tf_op jit(solution)/shard_map/all_to_all | solution.py:40
  103.2 0.2 reduce.1
  103.4 0.7 reshape.50
  (28 shorter events, 0.2 us)
Async XLA Ops:
  0.6 1.7 %copy-start = (bf16[4,256,1280]{2,1,0:T(8,128)(2,1)S(1)}, bf16[4,256,1280]{2,1,0:T(8,128)(2,1)}, u32[]{:S(2)}) copy-start(bf16[4,256,1280]{2,1,0:T(8,128)(2,1)} %param.5) | copy-start | bytes 7864324
  8.9 18.6 %all-to-all-start = ((bf16[16,8,1280]{2,1,0:T(8,128)(2,1)}), bf16[16,8,1280]{2,1,0:T(8,128)(2,1)}, u32[]{:S(2)}, u32[]{:S(2)}) async-start(bf16[16,8,1280]{2,1,0:T(8,128)(2,1)} %copy.17), calls=%async_computation | async-start | bytes 655360 | tf_op jit(solution)/shard_map/all_to_all | solution.py:63
  28.8 4.4 %copy-start.2 = (bf16[64,1280]{1,0:T(8,128)(2,1)}, bf16[64,1280]{1,0:T(8,128)(2,1)S(1)}, u32[]{:S(2)}) copy-start(bf16[64,1280]{1,0:T(8,128)(2,1)S(1)} %reshape.46) | copy-start | bytes 491524
  28.8 9.5 %slice-start = ((s8[6553600]{0:T(1024)(128)(4,1)}), s8[4194304]{0:T(1024)(128)(4,1)S(1)}, s32[]{:S(2)}) async-start(s8[6553600]{0:T(1024)(128)(4,1)} %bitcast.63), calls=%async_computation.4 | async-start | bytes 8388608
  28.8 13.8 %slice-start.2 = ((s8[6553600]{0:T(1024)(128)(4,1)}), s8[4194304]{0:T(1024)(128)(4,1)S(1)}, s32[]{:S(2)}) async-start(s8[6553600]{0:T(1024)(128)(4,1)} %bitcast.65), calls=%async_computation.6 | async-start | bytes 8388608
  33.2 5.1 %slice-start.1 = ((s8[6553600]{0:T(1024)(128)(4,1)}), s8[2359296]{0:T(1024)(128)(4,1)S(1)}, s32[]{:S(2)}) async-start(s8[6553600]{0:T(1024)(128)(4,1)} %bitcast.63), calls=%async_computation.5 | async-start | bytes 4718592
  33.2 9.4 %slice-start.3 = ((s8[6553600]{0:T(1024)(128)(4,1)}), s8[2359296]{0:T(1024)(128)(4,1)S(1)}, s32[]{:S(2)}) async-start(s8[6553600]{0:T(1024)(128)(4,1)} %bitcast.65), calls=%async_computation.7 | async-start | bytes 4718592
  41.1 12.8 %collective-permute-start = (bf16[16,8,1280]{2,1,0:T(8,128)(2,1)}, bf16[16,8,1280]{2,1,0:T(8,128)(2,1)}, u32[]{:S(2)}, u32[]{:S(2)}) collective-permute-start(bf16[16,8,1280]{2,1,0:T(8,128)(2,1)} %all-to-all-done), channel_id=1, source_target_pairs={{0,16},{16,0},{1,17},{17,1},{2,18},{18,2},{3,19},{19,3},{4,20},{20... | collective-permute-start | bytes 983048 | tf_op jit(solution)/shard_map/ppermute | solution.py:64
  49.7 25.3 %all-to-all-start.1 = ((bf16[16,8,1280]{2,1,0:T(8,128)(2,1)}), bf16[16,8,1280]{2,1,0:T(8,128)(2,1)}, u32[]{:S(2)}, u32[]{:S(2)}) async-start(bf16[16,8,1280]{2,1,0:T(8,128)(2,1)} %pad_maximum_fusion), calls=%async_computation.1 | async-start | bytes 655360 | tf_op jit(solution)/shard_map/all_to_all | solution.py:74
  64.2 5.2 %copy-start.3 = (bf16[64,1280]{1,0:T(8,128)(2,1)S(1)}, bf16[64,1280]{1,0:T(8,128)(2,1)}, u32[]{:S(2)}) copy-start(bf16[64,1280]{1,0:T(8,128)(2,1)} %copy-done.2) | copy-start | bytes 491524
  64.2 5.2 %copy-start.5 = (bf16[64,1280]{1,0:T(8,128)(2,1)S(1)}, bf16[64,1280]{1,0:T(8,128)(2,1)}, u32[]{:S(2)}) copy-start(bf16[64,1280]{1,0:T(8,128)(2,1)} %reshape.51) | copy-start | bytes 491524
  69.4 2.8 %copy-start.4 = (bf16[64,1280]{1,0:T(8,128)(2,1)S(1)}, bf16[64,1280]{1,0:T(8,128)(2,1)}, u32[]{:S(2)}) copy-start(bf16[64,1280]{1,0:T(8,128)(2,1)} %reshape.52) | copy-start | bytes 491524
  69.4 2.8 %copy-start.6 = (bf16[64,2560]{1,0:T(8,128)(2,1)S(1)}, bf16[64,2560]{1,0:T(8,128)(2,1)}, u32[]{:S(2)}) copy-start(bf16[64,2560]{1,0:T(8,128)(2,1)} %get-tuple-element.16) | copy-start | bytes 983044
  75.0 2.9 %copy-start.9 = (f32[4,16,256]{2,1,0:T(8,128)S(1)}, f32[4,16,256]{2,1,0:T(8,128)}, u32[]{:S(2)}) copy-start(f32[4,16,256]{2,1,0:T(8,128)} %get-tuple-element.13) | copy-start | bytes 196612
  75.0 3.6 %copy-start.7 = (f32[4,16,256]{2,1,0:T(8,128)S(1)}, f32[4,16,256]{2,1,0:T(8,128)}, u32[]{:S(2)}) copy-start(f32[4,16,256]{2,1,0:T(8,128)} %get-tuple-element.11) | copy-start | bytes 196612
  75.0 2.1 %copy-start.1 = (bf16[4,256,1280]{2,1,0:T(8,128)(2,1)S(1)}, bf16[4,256,1280]{2,1,0:T(8,128)(2,1)}, u32[]{:S(2)}) copy-start(bf16[4,256,1280]{2,1,0:T(8,128)(2,1)} %param.9) | copy-start | bytes 7864324
  79.0 16.6 %copy-start.8 = (bf16[1280,16]{0,1:T(8,128)(2,1)S(1)}, bf16[1280,16]{0,1:T(8,128)(2,1)}, u32[]{:S(2)}) copy-start(bf16[1280,16]{0,1:T(8,128)(2,1)} %param.6) | copy-start | bytes 122884
  79.7 12.5 %all-to-all-start.2 = ((f32[32,1,640]{2,1,0:T(1,128)}), f32[32,1,640]{2,1,0:T(1,128)S(1)}, u32[]{:S(2)}, u32[]{:S(2)}) async-start(f32[32,1,640]{2,1,0:T(1,128)} %all_to_all.21), calls=%async_computation.2 | async-start | bytes 163840 | tf_op jit(solution)/shard_map/all_to_all | solution.py:37
  93.0 10.2 %all-to-all-start.3 = ((f32[32,1,640]{2,1,0:T(1,128)}), f32[32,1,640]{2,1,0:T(1,128)S(1)}, u32[]{:S(2)}, u32[]{:S(2)}) async-start(f32[32,1,640]{2,1,0:T(1,128)} %broadcast_in_dim.6), calls=%async_computation.3 | async-start | bytes 163840 | tf_op jit(solution)/shard_map/all_to_all | solution.py:40

commit v2 on v1

v2 whole, which is shorter than its diff:
```python
import math

import jax
import jax.numpy as jnp
from jax import lax
from jax.experimental import pallas as pl
from jax.experimental.pallas import tpu as pltpu
from jax.sharding import PartitionSpec as P

GELU_C = math.sqrt(2.0 / math.pi)
CUBIC = 0.044715
LOW = jnp.bfloat16
WIDE = jnp.float32
LANES = 128
VMEM_BYTES = 24 * 1024 * 1024
WHOLE = pl.BlockSpec(memory_space=pltpu.VMEM)


def params_of(limit=VMEM_BYTES):
    return pltpu.CompilerParams(vmem_limit_bytes=limit)


def gelu_parts(values):
    square = values * values
    tangent = jnp.tanh(GELU_C * (values + CUBIC * square * values))
    half = 0.5 * (1.0 + tangent)
    slope = half + 0.5 * values * (1.0 - tangent * tangent) * GELU_C * (1.0 + 3.0 * CUBIC * square)
    return values * half, slope


def dot(left, right, over_left, over_right):
    return lax.dot_general(
        left, right, (((over_left,), (over_right,)), ((), ())), preferred_element_type=WIDE
    )


def softmax(values, axis):
    raised = jnp.exp(values - jnp.max(values, axis=axis, keepdims=True))
    return raised / jnp.sum(raised, axis=axis, keepdims=True)


def fill(ref, array):
    for tile in range(ref.shape[0]):
        ref[tile] = array[:, tile * LANES : (tile + 1) * LANES].astype(WIDE)


def whole(ref):
    return jnp.concatenate([ref[tile] for tile in range(ref.shape[0])], axis=1)


def take(ref, start, count, stride, first=0, tiles=None):
    tiles = ref.shape[0] if tiles is None else tiles
    picked = [ref[first + tile, pl.ds(start, count, stride=stride), :] for tile in range(tiles)]
    return jnp.concatenate(picked, axis=1)


def put(ref, start, count, stride, array):
    for tile in range(ref.shape[0]):
        ref[tile, pl.ds(start, count, stride=stride), :] = array[
            :, tile * LANES : (tile + 1) * LANES
        ]


def tiles_of(total, width):
    return pltpu.VMEM((width // LANES, total, LANES), WIDE)


def gather_kernel(tokens, params, grads, sent, dispatch, combine, tokens_v, grads_v, rows, sems):
    images = tokens.shape[0]
    slots = params.shape[0]
    copies = []
    for kind, (source, target) in enumerate(((tokens, tokens_v), (grads, grads_v))):
        for image in range(images):
            copy = pltpu.make_async_copy(
                source.at[image], target.at[image], sems.at[kind, image]
            )
            copy.start()
            copies.append(copy)
    low = []
    for image in range(images):
        copies[image].wait()
        logits = dot(params[...], tokens_v[image], 1, 1)
        over_tokens = softmax(logits, 1)
        over_slots = softmax(logits, 0)
        dispatch[image] = over_tokens
        combine[image] = over_slots
        low.append((over_tokens.astype(LOW), over_slots.astype(LOW)))
    stride = 2 * images
    for image in range(images):
        put(rows, 2 * image, slots, stride, dot(low[image][0], tokens_v[image], 1, 0))
    for image in range(images):
        copies[images + image].wait()
        put(rows, 2 * image + 1, slots, stride, dot(low[image][1], grads_v[image], 1, 0))
    sent[...] = whole(rows).astype(LOW)


def gather(tokens, params, grads):
    images, length, width = tokens.shape
    slots = params.shape[0]
    weights = jax.ShapeDtypeStruct((images, slots, length), WIDE)
    place = pl.BlockSpec(memory_space=pl.ANY)
    return pl.pallas_call(
        gather_kernel,
        out_shape=(
            jax.ShapeDtypeStruct((slots * images * 2, width), LOW),
            weights,
            weights,
        ),
        in_specs=[place, WHOLE, place],
        out_specs=(WHOLE, WHOLE, WHOLE),
        scratch_shapes=[
            pltpu.VMEM(tokens.shape, LOW),
            pltpu.VMEM(grads.shape, LOW),
            tiles_of(slots * images * 2, width),
            pltpu.SemaphoreType.DMA((2, images)),
        ],
        compiler_params=params_of(),
        cost_estimate=pl.CostEstimate(
            flops=6 * images * slots * length * width,
            bytes_accessed=4 * images * length * width,
            transcendentals=2 * images * slots * length,
        ),
        name="gather_slots",
    )(tokens, params, grads)


def expert_kernel(rows, w_in, w_out, back, acts, hidden, wide, low, sums):
    step = pl.program_id(0)
    count = rows.shape[0] // 2

    @pl.when(step == 0)
    def _():
        fill(wide, rows[...])
        low[0] = take(wide, 0, count, 2).astype(LOW)
        low[1] = take(wide, 1, count, 2).astype(LOW)
        sums[...] = jnp.zeros_like(sums)

    preact = dot(low[0], w_in[...], 1, 0)
    d_acts = dot(low[1], w_out[...], 1, 1)
    values, slope = gelu_parts(preact)
    values = values.astype(LOW)
    d_hidden = (d_acts * slope).astype(LOW)
    acts[...] = values
    hidden[...] = d_hidden
    sums[0] += dot(values, w_out[...], 1, 0)
    sums[1] += dot(d_hidden, w_in[...], 1, 1)

    @pl.when(step == pl.num_programs(0) - 1)
    def _():
        put(wide, 0, count, 2, sums[0])
        put(wide, 1, count, 2, sums[1])
        back[...] = whole(wide).astype(LOW)


def expert(rows, w_in, w_out, tile):
    total, width = rows.shape
    hidden = w_in.shape[1]
    count = total // 2
    kept = jax.ShapeDtypeStruct((count, hidden), LOW)
    return pl.pallas_call(
        expert_kernel,
        grid=(hidden // tile,),
        out_shape=(jax.ShapeDtypeStruct(rows.shape, LOW), kept, kept),
        in_specs=[
            pl.BlockSpec((total, width), lambda i: (0, 0)),
            pl.BlockSpec((width, tile), lambda i: (0, i)),
            pl.BlockSpec((tile, width), lambda i: (i, 0)),
        ],
        out_specs=(
            pl.BlockSpec((total, width), lambda i: (0, 0)),
            pl.BlockSpec((count, tile), lambda i: (0, i)),
            pl.BlockSpec((count, tile), lambda i: (0, i)),
        ),
        scratch_shapes=[
            tiles_of(total, width),
            pltpu.VMEM((2, count, width), LOW),
            pltpu.VMEM((2, count, width), WIDE),
        ],
        compiler_params=params_of(),
        cost_estimate=pl.CostEstimate(
            flops=8 * count * hidden * width,
            bytes_accessed=4 * hidden * width,
            transcendentals=count * hidden,
        ),
        name="expert_rows",
    )(rows, w_in, w_out)


def weights_kernel(
    mine, rows, others, w_in, w_out, acts, hidden, grad_in, grad_out, wide, low, grads, turned
):
    step = pl.program_id(0)
    count = rows.shape[0] // 2
    share = turned.shape[0]
    replicas = low.shape[1] // share

    @pl.when(step == 0)
    def _():
        left, right = [], []
        for source in (rows, others):
            fill(wide, source[...])
            tiles = share // LANES
            left.append(take(wide, 0, count, 2, mine[0] * tiles, tiles))
            right.append(take(wide, 1, count, 2))
        low[...] = take(wide, 0, count, 2).astype(LOW)
        turned[...] = jnp.concatenate(left, axis=0).T.astype(LOW)
        grads[...] = jnp.concatenate(right, axis=0).astype(LOW)

    preact = dot(low[...], w_in[...], 1, 0)
    d_acts = dot(grads[count:, :], w_out[...], 1, 1)
    values, slope = gelu_parts(preact)
    all_hidden = jnp.concatenate([hidden[...], (d_acts * slope).astype(LOW)], axis=0)
    grad_in[...] = dot(turned[...], all_hidden, 1, 0).astype(LOW)

    @pl.when(step < pl.num_programs(0) // replicas)
    def _():
        all_acts = jnp.concatenate([acts[...], values.astype(LOW)], axis=0)
        grad_out[...] = dot(all_acts, grads[...], 0, 0).astype(LOW)


def weight_grads(mine, rows, others, w_in, w_out, acts, hidden_low, replicas, tile):
    total, width = rows.shape
    hidden = w_in.shape[1]
    count = total // 2
    steps = hidden // tile
    own = steps // replicas

    def column(i, mine):
        return (0, lax.rem(i + mine[0] * own, steps))

    def row(i, mine):
        return (lax.rem(i + mine[0] * own, steps), 0)

    def fixed(i, mine):
        return (0, 0)

    return pl.pallas_call(
        weights_kernel,
        grid_spec=pltpu.PrefetchScalarGridSpec(
            num_scalar_prefetch=1,
            grid=(steps,),
            in_specs=[
                pl.BlockSpec((total, width), fixed),
                pl.BlockSpec((total, width), fixed),
                pl.BlockSpec((width, tile), column),
                pl.BlockSpec((tile, width), row),
                pl.BlockSpec((count, tile), column),
                pl.BlockSpec((count, tile), column),
            ],
            out_specs=(
                pl.BlockSpec((width // replicas, tile), column),
                pl.BlockSpec((tile, width), lambda i, mine: (jnp.minimum(i, own - 1), 0)),
            ),
            scratch_shapes=[
                tiles_of(total, width),
                pltpu.VMEM((count, width), LOW),
                pltpu.VMEM((2 * count, width), LOW),
                pltpu.VMEM((width // replicas, 2 * count), LOW),
            ],
        ),
        out_shape=(
            jax.ShapeDtypeStruct((width // replicas, hidden), LOW),
            jax.ShapeDtypeStruct((hidden // replicas, width), LOW),
        ),
        compiler_params=params_of(),
        cost_estimate=pl.CostEstimate(
            flops=(4 + 8 // replicas) * count * hidden * width,
            bytes_accessed=(4 + 4 // replicas) * hidden * width,
            transcendentals=count * hidden,
        ),
        name="weight_grads",
    )(mine, rows, others, w_in, w_out, acts, hidden_low)


def logits_kernel(back, tokens, params, grads, dispatch, combine, left, right, local, wide):
    images = tokens.shape[0]
    slots = params.shape[0]
    stride = 2 * images
    fill(wide, back[...])
    total = jnp.zeros(local.shape, WIDE)
    for image in range(images):
        slot_out = take(wide, 2 * image, slots, stride).astype(LOW)
        d_slot_in = take(wide, 2 * image + 1, slots, stride).astype(LOW)
        over_tokens = dispatch[image]
        over_slots = combine[image]
        d_combine = dot(slot_out, grads[image], 1, 1)
        d_dispatch = dot(d_slot_in, tokens[image], 1, 1)
        d_logits = over_slots * (
            d_combine - jnp.sum(over_slots * d_combine, axis=0, keepdims=True)
        )
        d_logits += over_tokens * (
            d_dispatch - jnp.sum(over_tokens * d_dispatch, axis=1, keepdims=True)
        )
        low = d_logits.astype(LOW)
        left[image, :slots, :] = over_tokens.astype(LOW)
        left[image, slots:, :] = low
        right[image, :slots, :] = d_slot_in
        right[image, slots:, :] = params[...]
        total += dot(low, tokens[image], 1, 0)
    local[...] = total


def logits_grads(back, tokens, params, grads, dispatch, combine):
    images, length, width = tokens.shape
    slots = params.shape[0]
    return pl.pallas_call(
        logits_kernel,
        out_shape=(
            jax.ShapeDtypeStruct((images, 2 * slots, length), LOW),
            jax.ShapeDtypeStruct((images, 2 * slots, width), LOW),
            jax.ShapeDtypeStruct((slots, width), WIDE),
        ),
        in_specs=[WHOLE] * 6,
        out_specs=(WHOLE,) * 3,
        scratch_shapes=[tiles_of(*back.shape)],
        compiler_params=params_of(),
        cost_estimate=pl.CostEstimate(
            flops=6 * images * slots * length * width,
            bytes_accessed=4 * images * length * width,
            transcendentals=0,
        ),
        name="logits_grads",
    )(back, tokens, params, grads, dispatch, combine)


def tokens_kernel(left, right, out):
    out[0] = dot(left[0], right[0], 0, 0).astype(LOW)


def tokens_grads(left, right):
    images, deep, length = left.shape
    width = right.shape[2]
    return pl.pallas_call(
        tokens_kernel,
        grid=(images,),
        out_shape=jax.ShapeDtypeStruct((images, length, width), LOW),
        in_specs=[
            pl.BlockSpec((1, deep, length), lambda i: (i, 0, 0)),
            pl.BlockSpec((1, deep, width), lambda i: (i, 0, 0)),
        ],
        out_specs=pl.BlockSpec((1, length, width), lambda i: (i, 0, 0)),
        compiler_params=params_of(),
        cost_estimate=pl.CostEstimate(
            flops=2 * images * deep * length * width,
            bytes_accessed=2 * images * length * width,
            transcendentals=0,
        ),
        name="tokens_grads",
    )(left, right)


def sum_everywhere(part, axes):
    count = lax.axis_size(axes)
    pieces = part.reshape(count, -1)
    pieces = lax.all_to_all(pieces, axes, split_axis=0, concat_axis=0, tiled=True)
    mine = jnp.sum(pieces, axis=0, keepdims=True)
    mine = jnp.broadcast_to(mine, pieces.shape)
    whole = lax.all_to_all(mine, axes, split_axis=0, concat_axis=0, tiled=True)
    return whole.reshape(part.shape)


def body(tokens, slot_params, expert_in, expert_out, grad_out):
    weight_in = expert_in[0]
    weight_out = expert_out[0]
    params = slot_params.T
    replicas = lax.axis_size("rep")
    mine = lax.axis_index("rep").astype(jnp.int32).reshape(1)

    sent, dispatch, combine = gather(tokens, params, grad_out)
    rows = lax.all_to_all(sent, "exp", split_axis=0, concat_axis=0, tiled=True)
    others = lax.ppermute(rows, "rep", [(i, (i + 1) % replicas) for i in range(replicas)])
    back, acts, hidden = expert(rows, weight_in, weight_out, 512)
    back = lax.all_to_all(back, "exp", split_axis=0, concat_axis=0, tiled=True)
    grad_expert_in, grad_expert_out = weight_grads(
        mine, rows, others, weight_in, weight_out, acts, hidden, replicas, 256
    )
    left, right, local = logits_grads(back, tokens, params, grad_out, dispatch, combine)
    grad_params = sum_everywhere(local, ("rep", "exp")).T
    grad_tokens = tokens_grads(left, right)
    return (grad_tokens, grad_params, grad_expert_in[None], grad_expert_out[None])


def solution(mesh):
    in_specs = (
        P(("rep", "exp"), None, None),
        P(),
        P("exp", None, None),
        P("exp", None, None),
        P(("rep", "exp"), None, None),
    )
    out_specs = (P(("rep", "exp"), None, None), P(), P("exp", "rep", None), P("exp", "rep", None))
    return jax.shard_map(body, mesh=mesh, in_specs=in_specs, out_specs=out_specs, check_vma=False)
```

time: 105 us -> 104 us (level)
  matrix products: 44.5 us -> 0 us
  Pallas kernels: 0 us -> 31.3 us
  blocking collectives: 0 us -> 18.3 us
  starting transfers between devices: 20.6 us -> 10.8 us
  local copies, waits for them, and re-layouts: 15.7 us -> 25 us
  other arithmetic: 4.18 us -> 0.26 us
  waiting for transfers between devices: 18.2 us -> 17.1 us
    dot_general x16 -> x0, matrix products: 44.5 us -> none  [the longest x8 30 us: dot(): lax.dot_general(left, right, (contract, ((), ())), preferred_element_type...]
    pallas_call x0 -> x5, Pallas kernels: none -> 31.3 us  [the longest x1 13.2 us: weight_grads(): pl.pallas_call(weights_kernel, grid_spec=pltpu.PrefetchScalarGridSpec(num...]
    unnamed x28 -> x38, local copies, waits for them, and re-layouts: 1.81 us -> 22.9 us
    all_to_all x0 -> x1, blocking collectives: none -> 18.3 us  [body(): rows = lax.all_to_all(sent, 'exp', split_axis=0, concat_axis=0, tiled=True)]
    all_to_all x1 -> x0, waiting for transfers between devices: 11.2 us -> none  [body(): rows = lax.all_to_all(sent, 'exp', split_axis=0, concat_axis=0, tiled=True)]
    all_to_all x1, waiting for transfers between devices: 0.01 us -> 9.5 us  [body(): back = lax.all_to_all(back, 'exp', split_axis=0, concat_axis=0, tiled=True)]
    all_to_all x1 -> x0, starting transfers between devices: 7.43 us -> none  [body(): rows = lax.all_to_all(sent, 'exp', split_axis=0, concat_axis=0, tiled=True)]
    reshape x6 -> x0, local copies, waits for them, and re-layouts: 6.57 us -> none  [the longest x1 1.62 us: body(): d_rows.reshape(slots, images, width)]
  transfers between devices with their start and end apart: 5 -> 4, of which waited for: 3 -> 2; matrix products, arithmetic and copies ran while one was open for 35% -> 1% of each run, Pallas kernels for 0% -> 18%
where the time goes in v2:
time: 104 us; the launch traced here: 103 us
  Pallas kernels  31.3 us (30%)
  local copies, waits for them, and re-layouts  25 us (24%)
  blocking collectives  18.3 us (18%)
  waiting for transfers between devices  17.1 us (16%)
  starting transfers between devices  10.8 us (10%)
    unnamed x38, local copies, waits for them, and re-layouts  22.9 us
    all_to_all x1, blocking collectives, body(): rows = lax.all_to_all(sent, 'exp', split_axis=0, concat_axis=0, tiled=True)  18.3 us
    pallas_call x1, Pallas kernels, weight_grads(): pl.pallas_call(weights_kernel, grid_spec=pltpu.PrefetchScalarGridSpec(num...  13.2 us
    all_to_all x1, waiting for transfers between devices, body(): back = lax.all_to_all(back, 'exp', split_axis=0, concat_axis=0, tiled=True)  9.5 us
    pallas_call x1, Pallas kernels, expert(): pl.pallas_call(expert_kernel, grid=(hidden // tile,), out_shape=(jax.Shap...  7.63 us
    all_to_all x1, waiting for transfers between devices, sum_everywhere(): lax.all_to_all(pieces, axes, split_axis=0, concat_axis=0, tiled=True)  7.6 us
    pallas_call x1, Pallas kernels, gather(): pl.pallas_call(gather_kernel, out_shape=(jax.ShapeDtypeStruct((slots * im...  5.25 us
    all_to_all x1, starting transfers between devices, body(): back = lax.all_to_all(back, 'exp', split_axis=0, concat_axis=0, tiled=True)  3.54 us
  transfers between devices with their start and end apart: 4, of which 2 were waited for; matrix products, arithmetic and copies ran while one was open for 1% of the time, Pallas kernels for 18%

profile of v2, /device:TPU:0, one launch (start us, length us, event | category | flops | bytes accessed | tf_op | source)
XLA Modules:
  0.0 103.4 jit_solution(3484713549379311290)
XLA Ops:
  0.6 0.0 copy-start.4
  0.6 1.7 %copy-done.4 = bf16[4,256,1280]{2,1,0:T(8,128)(2,1)S(1)} copy-done((bf16[4,256,1280]{2,1,0:T(8,128)(2,1)S(1)}, bf16[4,256,1280]{2,1,0:T(8,128)(2,1)}, u32[]{:S(2)}) %copy-start.4) | copy-done | bytes 2621464
  2.4 0.0 copy-start.6
  2.4 1.7 %copy-done.6 = bf16[4,256,1280]{2,1,0:T(8,128)(2,1)S(1)} copy-done((bf16[4,256,1280]{2,1,0:T(8,128)(2,1)S(1)}, bf16[4,256,1280]{2,1,0:T(8,128)(2,1)}, u32[]{:S(2)}) %copy-start.6) | copy-done | bytes 2621464
  4.1 0.8 copy-done.15
  4.9 5.3 %gather_slots.1 = (bf16[128,1280]{1,0:T(8,128)(2,1)S(1)}, f32[4,16,256]{2,1,0:T(8,128)S(1)}, f32[4,16,256]{2,1,0:T(8,128)S(1)}) custom-call(bf16[4,256,1280]{2,1,0:T(8,128)(2,1)S(1)} %copy-done.4, bf16[16,1280]{1,0:T(8,128)(2,1)S(1)} %bitcast.21, bf16[4,256,1280]{2,1,0:T(8,128)(2,1)S(1)} %copy-done.6), custom_call_target="tpu_custom_call" | custom-call | flops 125829120 | bytes 5242880 | tf_op jit(solution)/shard_map/gather_slots/pallas_call | solution.py:102
  10.2 18.3 %all_to_all.38 = bf16[16,8,1280]{2,1,0:T(8,128)(2,1)S(1)} all-to-all(bf16[16,8,1280]{2,1,0:T(8,128)(2,1)S(1)} %bitcast.20), channel_id=1, replica_groups=mesh['rep'=2,'exp'=16] {'exp'}, dimensions={0} | all-to-all | bytes 655360 | tf_op jit(solution)/shard_map/all_to_all | solution.py:370
  28.4 0.0 copy-start
  28.4 2.9 %copy-done = bf16[1,1280,2560]{2,1,0:T(8,128)(2,1)S(1)} copy-done((bf16[1,1280,2560]{2,1,0:T(8,128)(2,1)S(1)}, bf16[1,1280,2560]{2,1,0:T(8,128)(2,1)}, u32[]{:S(2)}) %copy-start) | copy-done | bytes 6553624
  31.3 0.0 copy-start.2
  31.3 2.9 %copy-done.2 = bf16[1,2560,1280]{2,1,0:T(8,128)(2,1)S(1)} copy-done((bf16[1,2560,1280]{2,1,0:T(8,128)(2,1)S(1)}, bf16[1,2560,1280]{2,1,0:T(8,128)(2,1)}, u32[]{:S(2)}) %copy-start.2) | copy-done | bytes 6553624
  34.2 0.0 copy-start.5
  34.2 0.0 copy-start.16
  34.2 7.6 %expert_rows.1 = (bf16[128,1280]{1,0:T(8,128)(2,1)S(1)}, bf16[64,2560]{1,0:T(8,128)(2,1)S(1)}, bf16[64,2560]{1,0:T(8,128)(2,1)S(1)}) custom-call(bf16[128,1280]{1,0:T(8,128)(2,1)S(1)} %bitcast.15, bf16[1280,2560]{1,0:T(8,128)(2,1)S(1)} %bitcast.11, bf16[2560,1280]{1,0:T(8,128)(2,1)S(1)} %bitcast.13), custom_call_target="tpu_custom_call" | custom-call | flops 1677721600 | bytes 13107200 | tf_op jit(solution)/shard_map/expert_rows/pallas_call | solution.py:160
  41.8 0.0 copy-start.10
  41.8 0.7 copy-done.10
  42.5 0.0 copy-start.11
  42.5 0.7 copy-done.11
  43.2 0.0 copy-start.13
  43.3 0.7 copy-done.13
  44.0 3.5 %all-to-all-start.1 = ((bf16[16,8,1280]{2,1,0:T(8,128)(2,1)}), bf16[16,8,1280]{2,1,0:T(8,128)(2,1)S(1)}, u32[]{:S(2)}, u32[]{:S(2)}) async-start(bf16[16,8,1280]{2,1,0:T(8,128)(2,1)} %bitcast.19), calls=%async_computation.1 | async-start | bytes 655360 | tf_op jit(solution)/shard_map/all_to_all | solution.py:373
  47.5 1.6 %collective-permute-start = (bf16[128,1280]{1,0:T(8,128)(2,1)S(1)}, bf16[128,1280]{1,0:T(8,128)(2,1)}, u32[]{:S(2)}, u32[]{:S(2)}) collective-permute-start(bf16[128,1280]{1,0:T(8,128)(2,1)S(1)} %bitcast.16), channel_id=1, source_target_pairs={{0,16},{16,0},{1,17},{17,1},{2,18},{18,2},{3,19},{19,3},{4,20},{20... | collective-permute-start | bytes 983048 | tf_op jit(solution)/shard_map/ppermute | solution.py:371
  49.1 9.5 %all-to-all-done.1 = bf16[16,8,1280]{2,1,0:T(8,128)(2,1)S(1)} async-done(((bf16[16,8,1280]{2,1,0:T(8,128)(2,1)}), bf16[16,8,1280]{2,1,0:T(8,128)(2,1)S(1)}, u32[]{:S(2)}, u32[]{:S(2)}) %all-to-all-start.1) | async-done | bytes 327712 | tf_op jit(solution)/shard_map/all_to_all | solution.py:373
  58.6 0.0 copy-done.5
  58.6 0.0 copy-done.16
  58.6 1.7 %copy-done.7 = bf16[4,256,1280]{2,1,0:T(8,128)(2,1)S(1)} copy-done((bf16[4,256,1280]{2,1,0:T(8,128)(2,1)S(1)}, bf16[4,256,1280]{2,1,0:T(8,128)(2,1)}, u32[]{:S(2)}) %copy-start.7) | copy-done | bytes 2621464
  60.3 2.4 %logits_grads.1 = (bf16[4,32,256]{2,1,0:T(8,128)(2,1)S(1)}, bf16[4,32,1280]{2,1,0:T(8,128)(2,1)S(1)}, f32[16,1280]{1,0:T(8,128)S(1)}) custom-call(bf16[128,1280]{1,0:T(8,128)(2,1)S(1)} %bitcast.18, bf16[4,256,1280]{2,1,0:T(8,128)(2,1)S(1)} %copy-done.5, bf16[16,1280]{1,0:T(8,128)(2,1)S(1)} %bitcast.22, bf16[4,256,1280]{2,1,0:T(8,128)(2,1)S(1)} %copy-done.7, ...), custom_call_target="tpu_custom_call" | custom-call | flops 125829120 | bytes 5242880 | tf_op jit(solution)/shard_map/logits_grads/pallas_call | solution.py:306
  62.8 0.7 copy-done.8
  63.5 0.6 copy-done.17
  64.1 0.7 all_to_all.33
  64.9 3.2 %all-to-all-start.2 = ((f32[32,1,640]{2,1,0:T(1,128)}), f32[32,1,640]{2,1,0:T(1,128)S(1)}, u32[]{:S(2)}, u32[]{:S(2)}) async-start(f32[32,1,640]{2,1,0:T(1,128)} %all_to_all.33), calls=%async_computation.2 | async-start | bytes 163840 | tf_op jit(solution)/shard_map/all_to_all | solution.py:355
  68.0 7.6 %all-to-all-done.2 = f32[32,1,640]{2,1,0:T(1,128)S(1)} async-done(((f32[32,1,640]{2,1,0:T(1,128)}), f32[32,1,640]{2,1,0:T(1,128)S(1)}, u32[]{:S(2)}, u32[]{:S(2)}) %all-to-all-start.2) | async-done | bytes 81952 | tf_op jit(solution)/shard_map/all_to_all | solution.py:355
  75.6 0.1 reduce_sum.9
  75.7 0.7 broadcast_in_dim.12
  76.4 2.6 %all-to-all-start.3 = ((f32[32,1,640]{2,1,0:T(1,128)}), f32[32,1,640]{2,1,0:T(1,128)S(1)}, u32[]{:S(2)}, u32[]{:S(2)}) async-start(f32[32,1,640]{2,1,0:T(1,128)} %broadcast_in_dim.12), calls=%async_computation.3 | async-start | bytes 163840 | tf_op jit(solution)/shard_map/all_to_all | solution.py:358
  79.0 0.0 collective-permute-done.others
  79.0 0.0 copy-start.1
  79.0 2.9 %copy-done.1 = bf16[1,1280,2560]{2,1,0:T(8,128)(2,1)S(1)} copy-done((bf16[1,1280,2560]{2,1,0:T(8,128)(2,1)S(1)}, bf16[1,1280,2560]{2,1,0:T(8,128)(2,1)}, u32[]{:S(2)}) %copy-start.1) | copy-done | bytes 6553624
  81.8 2.9 %copy-done.3 = bf16[1,2560,1280]{2,1,0:T(8,128)(2,1)S(1)} copy-done((bf16[1,2560,1280]{2,1,0:T(8,128)(2,1)S(1)}, bf16[1,2560,1280]{2,1,0:T(8,128)(2,1)}, u32[]{:S(2)}) %copy-start.3) | copy-done | bytes 6553624
  84.7 1.0 copy-done.12
  85.7 1.0 copy-done.14
  86.6 13.2 %weight_grads.1 = (bf16[640,2560]{1,0:T(8,128)(2,1)}, bf16[1280,1280]{1,0:T(8,128)(2,1)}) custom-call(s32[1]{0:T(128)} %bitcast.8.mine, bf16[128,1280]{1,0:T(8,128)(2,1)S(1)} %bitcast.17, bf16[128,1280]{1,0:T(8,128)(2,1)} %collective-permute-done.others, bf16[1280,2560]{1,0:T(8,128)(2,1)S(1)} %bitcast.12, bf16[2560,1280]{1,0:T(8,128)(2,1)S(1)} %bitcast.14, ...), custom_call_target="tpu_custom_call" | custom-call | flops 1677721600 | bytes 19660800 | tf_op jit(solution)/shard_map/weight_grads/pallas_call | solution.py:237
  99.8 0.0 copy-done.9
  99.8 0.0 copy-done.18
  99.8 2.8 %tokens_grads.1 = bf16[4,256,1280]{2,1,0:T(8,128)(2,1)} custom-call(bf16[4,32,256]{2,1,0:T(8,128)(2,1)S(1)} %copy-done.18, bf16[4,32,1280]{2,1,0:T(8,128)(2,1)S(1)} %copy-done.9), custom_call_target="tpu_custom_call" | custom-call | flops 83886080 | bytes 2621440 | tf_op jit(solution)/shard_map/tokens_grads/pallas_call | solution.py:333
  102.6 0.0 all-to-all-done.3
  102.6 0.2 reduce.1
  102.8 0.7 reshape.29
  (9 shorter events, 0.0 us)
Async XLA Ops:
  0.6 1.7 %copy-start.4 = (bf16[4,256,1280]{2,1,0:T(8,128)(2,1)S(1)}, bf16[4,256,1280]{2,1,0:T(8,128)(2,1)}, u32[]{:S(2)}) copy-start(bf16[4,256,1280]{2,1,0:T(8,128)(2,1)} %tokens.3) | copy-start | bytes 7864324
  2.4 1.7 %copy-start.6 = (bf16[4,256,1280]{2,1,0:T(8,128)(2,1)S(1)}, bf16[4,256,1280]{2,1,0:T(8,128)(2,1)}, u32[]{:S(2)}) copy-start(bf16[4,256,1280]{2,1,0:T(8,128)(2,1)} %grads.3) | copy-start | bytes 7864324
  4.1 0.8 copy-start.15
  28.4 2.9 %copy-start = (bf16[1,1280,2560]{2,1,0:T(8,128)(2,1)S(1)}, bf16[1,1280,2560]{2,1,0:T(8,128)(2,1)}, u32[]{:S(2)}) copy-start(bf16[1,1280,2560]{2,1,0:T(8,128)(2,1)} %param.7) | copy-start | bytes 19660804
  31.3 2.9 %copy-start.2 = (bf16[1,2560,1280]{2,1,0:T(8,128)(2,1)S(1)}, bf16[1,2560,1280]{2,1,0:T(8,128)(2,1)}, u32[]{:S(2)}) copy-start(bf16[1,2560,1280]{2,1,0:T(8,128)(2,1)} %param.8) | copy-start | bytes 19660804
  34.2 24.4 %copy-start.5 = (bf16[4,256,1280]{2,1,0:T(8,128)(2,1)S(1)}, bf16[4,256,1280]{2,1,0:T(8,128)(2,1)}, u32[]{:S(2)}) copy-start(bf16[4,256,1280]{2,1,0:T(8,128)(2,1)} %tokens.3) | copy-start | bytes 7864324
  34.2 24.4 %copy-start.16 = (bf16[1280,16]{0,1:T(8,128)(2,1)S(1)}, bf16[1280,16]{0,1:T(8,128)(2,1)}, u32[]{:S(2)}) copy-start(bf16[1280,16]{0,1:T(8,128)(2,1)} %param.6) | copy-start | bytes 122884
  41.8 0.7 copy-start.10
  42.5 0.7 copy-start.11
  43.2 0.7 copy-start.13
  44.0 14.6 %all-to-all-start.1 = ((bf16[16,8,1280]{2,1,0:T(8,128)(2,1)}), bf16[16,8,1280]{2,1,0:T(8,128)(2,1)S(1)}, u32[]{:S(2)}, u32[]{:S(2)}) async-start(bf16[16,8,1280]{2,1,0:T(8,128)(2,1)} %bitcast.19), calls=%async_computation.1 | async-start | bytes 655360 | tf_op jit(solution)/shard_map/all_to_all | solution.py:373
  47.5 31.4 %collective-permute-start = (bf16[128,1280]{1,0:T(8,128)(2,1)S(1)}, bf16[128,1280]{1,0:T(8,128)(2,1)}, u32[]{:S(2)}, u32[]{:S(2)}) collective-permute-start(bf16[128,1280]{1,0:T(8,128)(2,1)S(1)} %bitcast.16), channel_id=1, source_target_pairs={{0,16},{16,0},{1,17},{17,1},{2,18},{18,2},{3,19},{19,3},{4,20},{20... | collective-permute-start | bytes 983048 | tf_op jit(solution)/shard_map/ppermute | solution.py:371
  58.6 1.7 %copy-start.7 = (bf16[4,256,1280]{2,1,0:T(8,128)(2,1)S(1)}, bf16[4,256,1280]{2,1,0:T(8,128)(2,1)}, u32[]{:S(2)}) copy-start(bf16[4,256,1280]{2,1,0:T(8,128)(2,1)} %grads.3) | copy-start | bytes 7864324
  62.8 0.7 copy-start.8
  63.5 0.6 copy-start.17
  64.9 10.8 %all-to-all-start.2 = ((f32[32,1,640]{2,1,0:T(1,128)}), f32[32,1,640]{2,1,0:T(1,128)S(1)}, u32[]{:S(2)}, u32[]{:S(2)}) async-start(f32[32,1,640]{2,1,0:T(1,128)} %all_to_all.33), calls=%async_computation.2 | async-start | bytes 163840 | tf_op jit(solution)/shard_map/all_to_all | solution.py:355
  76.4 26.2 %all-to-all-start.3 = ((f32[32,1,640]{2,1,0:T(1,128)}), f32[32,1,640]{2,1,0:T(1,128)S(1)}, u32[]{:S(2)}, u32[]{:S(2)}) async-start(f32[32,1,640]{2,1,0:T(1,128)} %broadcast_in_dim.12), calls=%async_computation.3 | async-start | bytes 163840 | tf_op jit(solution)/shard_map/all_to_all | solution.py:358
  79.0 2.9 %copy-start.1 = (bf16[1,1280,2560]{2,1,0:T(8,128)(2,1)S(1)}, bf16[1,1280,2560]{2,1,0:T(8,128)(2,1)}, u32[]{:S(2)}) copy-start(bf16[1,1280,2560]{2,1,0:T(8,128)(2,1)} %param.7) | copy-start | bytes 19660804
  81.8 2.9 %copy-start.3 = (bf16[1,2560,1280]{2,1,0:T(8,128)(2,1)S(1)}, bf16[1,2560,1280]{2,1,0:T(8,128)(2,1)}, u32[]{:S(2)}) copy-start(bf16[1,2560,1280]{2,1,0:T(8,128)(2,1)} %param.8) | copy-start | bytes 19660804
  84.7 1.0 copy-start.12
  85.7 1.0 copy-start.14
  86.6 13.2 %copy-start.9 = (bf16[4,32,1280]{2,1,0:T(8,128)(2,1)S(1)}, bf16[4,32,1280]{2,1,0:T(8,128)(2,1)}, u32[]{:S(2)}) copy-start(bf16[4,32,1280]{2,1,0:T(8,128)(2,1)} %copy-done.8) | copy-start | bytes 983044
  86.6 13.2 %copy-start.18 = (bf16[4,32,256]{2,1,0:T(8,128)(2,1)S(1)}, bf16[4,32,256]{2,1,0:T(8,128)(2,1)}, u32[]{:S(2)}) copy-start(bf16[4,32,256]{2,1,0:T(8,128)(2,1)} %copy-done.17) | copy-start | bytes 196612

commit v3 on v1

v3 whole, which is shorter than its diff:
```python
import math

import jax
import jax.numpy as jnp
from jax import lax
from jax.experimental import pallas as pl
from jax.experimental.pallas import tpu as pltpu
from jax.sharding import PartitionSpec as P

GELU_C = math.sqrt(2.0 / math.pi)
CUBIC = 0.044715
LOW = jnp.bfloat16
WIDE = jnp.float32
LANES = 128
FOLD = 2
VMEM_BYTES = 60 * 1024 * 1024
WHOLE = pl.BlockSpec(memory_space=pltpu.VMEM)
PLACE = pl.BlockSpec(memory_space=pl.ANY)


def call(kernel, name, flops, nbytes, exps=0, **kwargs):
    return pl.pallas_call(
        kernel,
        name=name,
        compiler_params=pltpu.CompilerParams(vmem_limit_bytes=VMEM_BYTES),
        cost_estimate=pl.CostEstimate(
            flops=flops, bytes_accessed=nbytes, transcendentals=exps
        ),
        **kwargs,
    )


def shaped(shape, dtype):
    return jax.ShapeDtypeStruct(shape, dtype)


def gelu_parts(values):
    square = values * values
    tangent = jnp.tanh(GELU_C * (values + CUBIC * square * values))
    half = 0.5 * (1.0 + tangent)
    slope = half + 0.5 * values * (1.0 - tangent * tangent) * GELU_C * (1.0 + 3.0 * CUBIC * square)
    return values * half, slope


def dot(left, right, over_left, over_right):
    return lax.dot_general(
        left, right, (((over_left,), (over_right,)), ((), ())), preferred_element_type=WIDE
    )


def softmax(values, axis):
    raised = jnp.exp(values - jnp.max(values, axis=axis, keepdims=True))
    return raised / jnp.sum(raised, axis=axis, keepdims=True)


def scratch_rows(shape):
    return pltpu.VMEM((shape[1] // LANES, shape[0], LANES), WIDE)


def load_rows(ref, array):
    for tile in range(ref.shape[0]):
        ref[tile] = array[:, tile * LANES : (tile + 1) * LANES].astype(WIDE)


def packed(ref):
    return jnp.concatenate([ref[tile] for tile in range(ref.shape[0])], axis=1).astype(LOW)


def take_part(ref, start, count, stride):
    picked = [ref[tile, pl.ds(start, count, stride=stride), :] for tile in range(ref.shape[0])]
    return jnp.concatenate(picked, axis=1)


def take(ref, start, count, stride):
    parts = [take_part(ref, start + part, count, stride) for part in range(FOLD)]
    return jnp.concatenate(parts, axis=1).astype(LOW)


def put(ref, start, count, stride, array):
    tiles = ref.shape[0]
    for part in range(FOLD):
        for tile in range(tiles):
            at = (part * tiles + tile) * LANES
            ref[tile, pl.ds(start + part, count, stride=stride), :] = array[:, at : at + LANES]


def start_copies(source, target, sems):
    copies = []
    for index in range(source.shape[0]):
        copy = pltpu.make_async_copy(source.at[index], target.at[index], sems.at[index])
        copy.start()
        copies.append(copy)
    return copies


def slot_in_kernel(tokens, params, sent, dispatch, combine, tokens_v, rows, sems):
    images = tokens.shape[0]
    slots = params.shape[0]
    copies = start_copies(tokens, tokens_v, sems)
    logits = []
    for image in range(images):
        copies[image].wait()
        logits.append(dot(params[...], tokens_v[image], 1, 1))
    for image in range(images):
        over_tokens = softmax(logits[image], 1)
        dispatch[image] = over_tokens
        value = dot(over_tokens.astype(LOW), tokens_v[image], 1, 0)
        put(rows, FOLD * image, slots, FOLD * images, value)
    for image in range(images):
        combine[image] = softmax(logits[image], 0)
    sent[...] = packed(rows)


def slot_in_rows(tokens, params):
    images, length, width = tokens.shape
    slots = params.shape[0]
    weights = shaped((images, slots, length), WIDE)
    rows = (slots * images * FOLD, width // FOLD)
    return call(
        slot_in_kernel,
        "slot_in",
        4 * images * slots * length * width,
        2 * images * length * width,
        2 * images * slots * length,
        out_shape=(shaped(rows, LOW), weights, weights),
        in_specs=[PLACE, WHOLE],
        out_specs=(WHOLE, WHOLE, WHOLE),
        scratch_shapes=[
            pltpu.VMEM(tokens.shape, LOW),
            scratch_rows(rows),
            pltpu.SemaphoreType.DMA((images,)),
        ],
    )(tokens, params)


def slot_grad_kernel(grads, combine, sent, grads_v, rows, sems):
    images = grads.shape[0]
    slots = combine.shape[1]
    copies = start_copies(grads, grads_v, sems)
    for image in range(images):
        copies[image].wait()
        value = dot(combine[image].astype(LOW), grads_v[image], 1, 0)
        put(rows, FOLD * image, slots, FOLD * images, value)
    sent[...] = packed(rows)


def slot_grad_rows(grads, combine):
    images, length, width = grads.shape
    slots = combine.shape[1]
    rows = (slots * images * FOLD, width // FOLD)
    return call(
        slot_grad_kernel,
        "slot_grad",
        2 * images * slots * length * width,
        2 * images * length * width,
        out_shape=shaped(rows, LOW),
        in_specs=[PLACE, WHOLE],
        out_specs=WHOLE,
        scratch_shapes=[
            pltpu.VMEM(grads.shape, LOW),
            scratch_rows(rows),
            pltpu.SemaphoreType.DMA((images,)),
        ],
    )(grads, combine)


def unfold(source, wide, low):
    load_rows(wide, source[...])
    low[...] = take(wide, 0, low.shape[0], FOLD)


def forward_kernel(rows, w_in, w_out, back, acts, slopes, wide, low, total):
    step = pl.program_id(0)

    @pl.when(step == 0)
    def _():
        unfold(rows, wide, low)
        total[...] = jnp.zeros_like(total)

    values, slope = gelu_parts(dot(low[...], w_in[...], 1, 0))
    values = values.astype(LOW)
    acts[...] = values
    slopes[...] = slope
    total[...] += dot(values, w_out[...], 1, 0)

    @pl.when(step == pl.num_programs(0) - 1)
    def _():
        put(wide, 0, low.shape[0], FOLD, total[...])
        back[...] = packed(wide)


def backward_kernel(rows, slopes, w_in, w_out, back, hidden, wide, low, total):
    step = pl.program_id(0)

    @pl.when(step == 0)
    def _():
        unfold(rows, wide, low)
        total[...] = jnp.zeros_like(total)

    values = (dot(low[...], w_out[...], 1, 1) * slopes[...]).astype(LOW)
    hidden[...] = values
    total[...] += dot(values, w_in[...], 1, 1)

    @pl.when(step == pl.num_programs(0) - 1)
    def _():
        put(wide, 0, low.shape[0], FOLD, total[...])
        back[...] = packed(wide)


def others_kernel(after, rows, grad_rows, w_in, w_out, acts, hidden, wide, low, low_grads):
    del after

    @pl.when(pl.program_id(0) == 0)
    def _():
        unfold(rows, wide, low)
        unfold(grad_rows, wide, low_grads)

    values, slope = gelu_parts(dot(low[...], w_in[...], 1, 0))
    acts[...] = values.astype(LOW)
    hidden[...] = (dot(low_grads[...], w_out[...], 1, 1) * slope).astype(LOW)


class Expert:
    def __init__(self, rows, w_in, w_out, tile):
        self.weights = (w_in, w_out)
        self.folded, part = rows.shape
        self.part = part
        self.width, self.hidden = w_in.shape
        self.count = self.folded // FOLD
        self.grid = (self.hidden // tile,)
        self.rows = pl.BlockSpec(rows.shape, lambda i: (0, 0))
        self.columns = pl.BlockSpec((self.count, tile), lambda i: (0, i))
        self.w_specs = [
            pl.BlockSpec((self.width, tile), lambda i: (0, i)),
            pl.BlockSpec((tile, self.width), lambda i: (i, 0)),
        ]
        self.back = shaped(rows.shape, LOW)
        self.kept = shaped((self.count, self.hidden), LOW)
        self.low = pltpu.VMEM((self.count, self.width), LOW)
        self.cost = (
            4 * self.count * self.hidden * self.width,
            4 * self.hidden * self.width,
            self.count * self.hidden,
        )
        self.wide = scratch_rows(rows.shape)
        self.total = pltpu.VMEM((self.count, self.width), WIDE)

    def forward(self, rows):
        return call(
            forward_kernel,
            "expert_forward",
            *self.cost,
            grid=self.grid,
            out_shape=(self.back, self.kept, shaped(self.kept.shape, WIDE)),
            in_specs=[self.rows, *self.w_specs],
            out_specs=(self.rows, self.columns, self.columns),
            scratch_shapes=[self.wide, self.low, self.total],
        )(rows, *self.weights)

    def backward(self, rows, slopes):
        return call(
            backward_kernel,
            "expert_backward",
            *self.cost,
            grid=self.grid,
            out_shape=(self.back, self.kept),
            in_specs=[self.rows, self.columns, *self.w_specs],
            out_specs=(self.rows, self.columns),
            scratch_shapes=[self.wide, self.low, self.total],
        )(rows, slopes, *self.weights)

    def others(self, after, rows, grad_rows):
        return call(
            others_kernel,
            "expert_others",
            *self.cost,
            grid=self.grid,
            out_shape=(self.kept, self.kept),
            in_specs=[PLACE, self.rows, self.rows, *self.w_specs],
            out_specs=(self.columns, self.columns),
            scratch_shapes=[self.wide, self.low, self.low],
        )(after, rows, grad_rows, *self.weights)


def weights_kernel(
    mine,
    after,
    rows,
    grad_rows,
    other_rows,
    other_grad_rows,
    acts,
    other_acts,
    hidden,
    other_hidden,
    grad_in,
    grad_out,
    wide,
    grads,
    turned,
):
    del after
    count = rows.shape[0] // FOLD

    @pl.when(pl.program_id(0) == 0)
    def _():
        left = []
        for source in (rows, other_rows):
            load_rows(wide, source[...])
            parts = [take_part(wide, part, count, FOLD) for part in range(FOLD)]
            left.append(jnp.where(mine[0] == 0, parts[0], parts[1]))
        turned[...] = jnp.concatenate(left, axis=0).T.astype(LOW)
        unfold(grad_rows, wide, grads.at[pl.ds(0, count)])
        unfold(other_grad_rows, wide, grads.at[pl.ds(count, count)])

    all_hidden = jnp.concatenate([hidden[...], other_hidden[...]], axis=0)
    grad_in[...] = dot(turned[...], all_hidden, 1, 0).astype(LOW)
    all_acts = jnp.concatenate([acts[...], other_acts[...]], axis=0)
    grad_out[...] = dot(all_acts, grads[...], 0, 0).astype(LOW)


def weight_grads(mine, after, rows, grad_rows, acts, hidden, steps, replicas):
    folded, part = rows[0].shape
    width = part * FOLD
    size = acts[0].shape[1]
    count = folded // FOLD
    in_tile, out_tile = size // steps, size // replicas // steps
    whole_rows = pl.BlockSpec((folded, part), lambda i, mine: (0, 0))
    acts_spec = pl.BlockSpec((count, out_tile), lambda i, mine: (0, mine[0] * steps + i))
    hidden_spec = pl.BlockSpec((count, in_tile), lambda i, mine: (0, i))
    return call(
        weights_kernel,
        "weight_grads",
        8 * count * size * width // replicas,
        4 * size * width // replicas,
        grid_spec=pltpu.PrefetchScalarGridSpec(
            num_scalar_prefetch=1,
            grid=(steps,),
            in_specs=[PLACE] + [whole_rows] * 4 + [acts_spec] * 2 + [hidden_spec] * 2,
            out_specs=(
                pl.BlockSpec((width // replicas, in_tile), lambda i, mine: (0, i)),
                pl.BlockSpec((out_tile, width), lambda i, mine: (i, 0)),
            ),
            scratch_shapes=[
                scratch_rows((folded, part)),
                pltpu.VMEM((2 * count, width), LOW),
                pltpu.VMEM((width // replicas, 2 * count), LOW),
            ],
        ),
        out_shape=(
            shaped((width // replicas, size), LOW),
            shaped((size // replicas, width), LOW),
        ),
    )(mine, after, rows[0], grad_rows[0], rows[1], grad_rows[1], *acts, *hidden)


def combine_kernel(after, back, grads, combine, part, grads_v, wide, sems):
    del after
    images, slots, _ = combine.shape
    copies = start_copies(grads, grads_v, sems)
    load_rows(wide, back[...])
    for image in range(images):
        slot_out = take(wide, FOLD * image, slots, FOLD * images)
        weights = combine[image]
        copies[image].wait()
        d_combine = dot(slot_out, grads_v[image], 1, 1)
        part[image] = weights * (
            d_combine - jnp.sum(weights * d_combine, axis=0, keepdims=True)
        )


def combine_part(after, back, grads, combine):
    images, length, width = grads.shape
    slots = combine.shape[1]
    return call(
        combine_kernel,
        "combine_part",
        2 * images * slots * length * width,
        2 * images * length * width,
        out_shape=shaped(combine.shape, WIDE),
        in_specs=[PLACE, WHOLE, PLACE, WHOLE],
        out_specs=WHOLE,
        scratch_shapes=[
            pltpu.VMEM(grads.shape, LOW),
            scratch_rows(back.shape),
            pltpu.SemaphoreType.DMA((images,)),
        ],
    )(after, back, grads, combine)


def logits_kernel(
    after, back, tokens, params, dispatch, part, left, right, local, tokens_v, wide, sems
):
    del after
    images, slots, _ = dispatch.shape
    copies = start_copies(tokens, tokens_v, sems)
    load_rows(wide, back[...])
    total = jnp.zeros(params.shape, WIDE)
    for image in range(images):
        d_slot_in = take(wide, FOLD * image, slots, FOLD * images)
        right[image, :slots, :] = d_slot_in
        right[image, slots:, :] = params[...]
        weights = dispatch[image]
        copies[image].wait()
        d_dispatch = dot(d_slot_in, tokens_v[image], 1, 1)
        d_logits = part[image] + weights * (
            d_dispatch - jnp.sum(weights * d_dispatch, axis=1, keepdims=True)
        )
        low = d_logits.astype(LOW)
        left[image, :slots, :] = weights.astype(LOW)
        left[image, slots:, :] = low
        total += dot(low, tokens_v[image], 1, 0)
    for slot in range(slots):
        local[slot] = total[slot : slot + 1, :]


def logits_grads(after, back, tokens, params, dispatch, part):
    images, length, width = tokens.shape
    slots = params.shape[0]
    return call(
        logits_kernel,
        "logits_grads",
        4 * images * slots * length * width,
        2 * images * length * width,
        out_shape=(
            shaped((images, 2 * slots, length), LOW),
            shaped((images, 2 * slots, width), LOW),
            shaped((slots, 1, width), WIDE),
        ),
        in_specs=[PLACE, WHOLE, PLACE, WHOLE, WHOLE, WHOLE],
        out_specs=(WHOLE,) * 3,
        scratch_shapes=[
            pltpu.VMEM(tokens.shape, LOW),
            scratch_rows(back.shape),
            pltpu.SemaphoreType.DMA((images,)),
        ],
    )(after, back, tokens, params, dispatch, part)


def tokens_kernel(after, left, right, out):
    del after
    out[0] = dot(left[0], right[0], 0, 0).astype(LOW)


def tokens_grads(after, left, right):
    images, deep, length = left.shape
    width = right.shape[2]
    return call(
        tokens_kernel,
        "tokens_grads",
        2 * images * deep * length * width,
        2 * images * length * width,
        grid=(images,),
        out_shape=shaped((images, length, width), LOW),
        in_specs=[
            PLACE,
            pl.BlockSpec((1, deep, length), lambda i: (i, 0, 0)),
            pl.BlockSpec((1, deep, width), lambda i: (i, 0, 0)),
        ],
        out_specs=pl.BlockSpec((1, length, width), lambda i: (i, 0, 0)),
    )(after, left, right)


def exchange(rows):
    return lax.all_to_all(rows, "exp", split_axis=0, concat_axis=0, tiled=True)


def body(tokens, slot_params, expert_in, expert_out, grad_out):
    params = slot_params.T
    replicas = lax.axis_size("rep")
    mine = lax.axis_index("rep").astype(jnp.int32).reshape(1)

    def swap(array):
        return lax.ppermute(array, "rep", [(i, (i + 1) % replicas) for i in range(replicas)])

    sent, dispatch, combine = slot_in_rows(tokens, params)
    rows = exchange(sent)
    grad_rows = exchange(slot_grad_rows(grad_out, combine))
    expert = Expert(rows, expert_in[0], expert_out[0], 512)
    other_rows = swap(rows)
    back, acts, slopes = expert.forward(rows)
    back = exchange(back)
    other_grad_rows = swap(grad_rows)
    d_back, hidden = expert.backward(grad_rows, slopes)
    part = combine_part(hidden, back, grad_out, combine)
    other_acts, other_hidden = expert.others(hidden, other_rows, other_grad_rows)
    d_back = exchange(d_back)
    left, right, local = logits_grads(other_hidden, d_back, tokens, params, dispatch, part)

    share = jnp.sum(exchange(local), axis=0, keepdims=True)
    grad_expert_in, grad_expert_out = weight_grads(
        mine,
        local,
        (rows, other_rows),
        (grad_rows, other_grad_rows),
        (acts, other_acts),
        (hidden, other_hidden),
        5,
        replicas,
    )
    share = share + swap(share)
    grad_params = exchange(jnp.broadcast_to(share, local.shape))
    grad_tokens = tokens_grads(share, left, right)
    return (
        grad_tokens,
        grad_params.reshape(params.shape).T,
        grad_expert_in[None],
        grad_expert_out[None],
    )


def solution(mesh):
    in_specs = (
        P(("rep", "exp"), None, None),
        P(),
        P("exp", None, None),
        P("exp", None, None),
        P(("rep", "exp"), None, None),
    )
    out_specs = (P(("rep", "exp"), None, None), P(), P("exp", "rep", None), P("exp", "rep", None))
    return jax.shard_map(body, mesh=mesh, in_specs=in_specs, out_specs=out_specs, check_vma=False)
```

time: 105 us -> 119 us (1.13)
  Pallas kernels: 0 us -> 54.8 us
  matrix products: 44.5 us -> 0 us
  local copies, waits for them, and re-layouts: 15.7 us -> 2.65 us
  blocking collectives: 0 us -> 12.9 us
  starting transfers between devices: 20.6 us -> 30 us
  other arithmetic: 4.18 us -> 0.66 us
  waiting for transfers between devices: 18.2 us -> 15.3 us
    pallas_call x0 -> x9, Pallas kernels: none -> 54.8 us  [the longest x1 9.59 us: backward(): call(backward_kernel, 'expert_backward', *self.cost, grid=self.grid, out_...]
    dot_general x16 -> x0, matrix products: 44.5 us -> none  [the longest x8 30 us: dot(): lax.dot_general(left, right, (contract, ((), ())), preferred_element_type...]
    all_to_all x4 -> x5, waiting for transfers between devices: 18.2 us -> 5 us  [exchange(): return lax.all_to_all(rows, 'exp', split_axis=0, concat_axis=0, tiled=True)]
    all_to_all x0 -> x1, blocking collectives: none -> 12.9 us  [exchange(): return lax.all_to_all(rows, 'exp', split_axis=0, concat_axis=0, tiled=True)]
    ppermute x1 -> x3, waiting for transfers between devices: 0.01 us -> 10.3 us  [swap(): lax.ppermute(array, 'rep', [(i, (i + 1) % replicas) for i in range(replic...]
    all_to_all x4 -> x5, starting transfers between devices: 19.1 us -> 26.4 us  [exchange(): return lax.all_to_all(rows, 'exp', split_axis=0, concat_axis=0, tiled=True)]
    reshape x7 -> x0, local copies, waits for them, and re-layouts: 7.23 us -> none  [the longest x1 1.62 us: body(): d_rows.reshape(slots, images, width)]
    slice x3 -> x0, local copies, waits for them, and re-layouts: 4.48 us -> none  [the longest x1 1.92 us: body(): others_in = others[:, :images].reshape(-1, width)]
  transfers between devices with their start and end apart: 5 -> 8, of which waited for: 3 -> 4; matrix products, arithmetic and copies ran while one was open for 35% -> 0% of each run, Pallas kernels for 0% -> 38%
where the time goes in v3:
time: 119 us; the launch traced here: 117 us
  Pallas kernels  54.8 us (46%)
  starting transfers between devices  30 us (25%)
  waiting for transfers between devices  15.3 us (13%)
  blocking collectives  12.9 us (11%)
  local copies, waits for them, and re-layouts  2.65 us (2%)
    all_to_all x5, starting transfers between devices, exchange(): return lax.all_to_all(rows, 'exp', split_axis=0, concat_axis=0, tiled=True)  26.4 us
    all_to_all x1, blocking collectives, exchange(): return lax.all_to_all(rows, 'exp', split_axis=0, concat_axis=0, tiled=True)  12.9 us
    ppermute x3, waiting for transfers between devices, swap(): lax.ppermute(array, 'rep', [(i, (i + 1) % replicas) for i in range(replic...  10.3 us
    pallas_call x1, Pallas kernels, backward(): call(backward_kernel, 'expert_backward', *self.cost, grid=self.grid, out_...  9.59 us
    pallas_call x1, Pallas kernels, others(): call(others_kernel, 'expert_others', *self.cost, grid=self.grid, out_shap...  8.38 us
    pallas_call x1, Pallas kernels, forward(): call(forward_kernel, 'expert_forward', *self.cost, grid=self.grid, out_sh...  8.37 us
    pallas_call x1, Pallas kernels, weight_grads(): call(weights_kernel, 'weight_grads', 8 * count * size * width // replicas...  6.22 us
    pallas_call x1, Pallas kernels, logits_grads(): call(logits_kernel, 'logits_grads', 4 * images * slots * length * width,...  5.27 us
  transfers between devices with their start and end apart: 8, of which 4 were waited for; matrix products, arithmetic and copies ran while one was open for 0% of the time, Pallas kernels for 38%

profile of v3, /device:TPU:0, one launch (start us, length us, event | category | flops | bytes accessed | tf_op | source)
XLA Modules:
  0.0 117.1 jit_solution(17241950909755383612)
XLA Ops:
  0.6 4.7 %slot_in.1 = (bf16[128,640]{1,0:T(8,128)(2,1)}, f32[4,16,256]{2,1,0:T(8,128)}, f32[4,16,256]{2,1,0:T(8,128)}) custom-call(bf16[4,256,1280]{2,1,0:T(8,128)(2,1)} %tokens.3, bf16[16,1280]{1,0:T(8,128)(2,1)} %bitcast.37), custom_call_target="tpu_custom_call" | custom-call | flops 83886080 | bytes 2621440 | tf_op jit(solution)/shard_map/slot_in/pallas_call | solution.py:119
  5.4 7.4 %all-to-all-start.1 = ((bf16[16,8,640]{2,1,0:T(8,128)(2,1)}), bf16[16,8,640]{2,1,0:T(8,128)(2,1)S(1)}, u32[]{:S(2)}, u32[]{:S(2)}) async-start(bf16[16,8,640]{2,1,0:T(8,128)(2,1)} %bitcast.36), calls=%async_computation.1 | async-start | bytes 327680 | tf_op jit(solution)/shard_map/all_to_all | solution.py:465
  12.8 3.5 %slot_grad.1 = bf16[128,640]{1,0:T(8,128)(2,1)} custom-call(bf16[4,256,1280]{2,1,0:T(8,128)(2,1)} %grads.3, f32[4,16,256]{2,1,0:T(8,128)} %get-tuple-element.19.combine), custom_call_target="tpu_custom_call" | custom-call | flops 41943040 | bytes 2621440 | tf_op jit(solution)/shard_map/slot_grad/pallas_call | solution.py:151
  16.3 4.9 %all-to-all-done.1 = bf16[16,8,640]{2,1,0:T(8,128)(2,1)S(1)} async-done(((bf16[16,8,640]{2,1,0:T(8,128)(2,1)}), bf16[16,8,640]{2,1,0:T(8,128)(2,1)S(1)}, u32[]{:S(2)}, u32[]{:S(2)}) %all-to-all-start.1) | async-done | bytes 163872 | tf_op jit(solution)/shard_map/all_to_all | solution.py:465
  21.2 0.0 copy-start.2
  21.3 3.5 %all-to-all-start = ((bf16[16,8,640]{2,1,0:T(8,128)(2,1)}), bf16[16,8,640]{2,1,0:T(8,128)(2,1)S(1)}, u32[]{:S(2)}, u32[]{:S(2)}) async-start(bf16[16,8,640]{2,1,0:T(8,128)(2,1)} %bitcast.27), calls=%async_computation | async-start | bytes 327680 | tf_op jit(solution)/shard_map/all_to_all | solution.py:465
  24.8 0.0 copy-done.2
  24.8 8.4 %expert_forward.1 = (bf16[128,640]{1,0:T(8,128)(2,1)}, bf16[64,2560]{1,0:T(8,128)(2,1)}, f32[64,2560]{1,0:T(8,128)}) custom-call(bf16[128,640]{1,0:T(8,128)(2,1)} %bitcast.28, bf16[1280,2560]{1,0:T(8,128)(2,1)} %bitcast.19, bf16[2560,1280]{1,0:T(8,128)(2,1)} %bitcast.22), custom_call_target="tpu_custom_call" | custom-call | flops 838860800 | bytes 13107200 | tf_op jit(solution)/shard_map/expert_forward/pallas_call | solution.py:249
  33.2 0.0 all-to-all-done
  33.2 0.0 copy-start.4
  33.2 5.9 %all-to-all-start.3 = ((bf16[16,8,640]{2,1,0:T(8,128)(2,1)}), bf16[16,8,640]{2,1,0:T(8,128)(2,1)S(1)}, u32[]{:S(2)}, u32[]{:S(2)}) async-start(bf16[16,8,640]{2,1,0:T(8,128)(2,1)} %bitcast.35), calls=%async_computation.3 | async-start | bytes 327680 | tf_op jit(solution)/shard_map/all_to_all | solution.py:465
  39.2 0.0 copy-done.4
  39.2 0.0 copy-start.3
  39.2 9.6 %expert_backward.1 = (bf16[128,640]{1,0:T(8,128)(2,1)}, bf16[64,2560]{1,0:T(8,128)(2,1)}) custom-call(bf16[128,640]{1,0:T(8,128)(2,1)} %bitcast.31, f32[64,2560]{1,0:T(8,128)} %get-tuple-element.21.slopes, bf16[1280,2560]{1,0:T(8,128)(2,1)} %bitcast.20, bf16[2560,1280]{1,0:T(8,128)(2,1)} %bitcast.23), custom_call_target="tpu_custom_call" | custom-call | flops 838860800 | bytes 13107200 | tf_op jit(solution)/shard_map/expert_backward/pallas_call | solution.py:261
  48.8 0.0 all-to-all-done.3
  48.8 0.0 copy-start
  48.8 6.0 %all-to-all-start.2 = ((bf16[16,8,640]{2,1,0:T(8,128)(2,1)}), bf16[16,8,640]{2,1,0:T(8,128)(2,1)S(1)}, u32[]{:S(2)}, u32[]{:S(2)}) async-start(bf16[16,8,640]{2,1,0:T(8,128)(2,1)} %bitcast.34), calls=%async_computation.2 | async-start | bytes 327680 | tf_op jit(solution)/shard_map/all_to_all | solution.py:465
  54.8 1.6 %collective-permute-start.1 = (bf16[128,640]{1,0:T(8,128)(2,1)}, bf16[128,640]{1,0:T(8,128)(2,1)S(1)}, u32[]{:S(2)}, u32[]{:S(2)}) collective-permute-start(bf16[128,640]{1,0:T(8,128)(2,1)} %bitcast.32), channel_id=1, source_target_pairs={{0,16},{16,0},{1,17},{17,1},{2,18},{18,2},{3,19},{19,3},{4,20},{20... | collective-permute-start | bytes 491528 | tf_op jit(solution)/shard_map/ppermute | solution.py:474
  56.4 0.0 copy-done.3
  56.4 0.5 collective-permute-start
  56.9 5.2 %collective-permute-done.1.grad_rows.other_grad_rows = bf16[128,640]{1,0:T(8,128)(2,1)S(1)} collective-permute-done((bf16[128,640]{1,0:T(8,128)(2,1)}, bf16[128,640]{1,0:T(8,128)(2,1)S(1)}, u32[]{:S(2)}, u32[]{:S(2)}) %collective-permute-start.1) | collective-permute-done | bytes 163872 | tf_op jit(solution)/shard_map/ppermute | solution.py:474
  62.1 0.0 copy-start.5
  62.1 2.9 %collective-permute-done.rows.other_rows = bf16[128,640]{1,0:T(8,128)(2,1)S(1)} collective-permute-done((bf16[128,640]{1,0:T(8,128)(2,1)S(1)}, bf16[128,640]{1,0:T(8,128)(2,1)S(1)}, u32[]{:S(2)}, u32[]{:S(2)}) %collective-permute-start) | collective-permute-done | bytes 163872 | tf_op jit(solution)/shard_map/ppermute | solution.py:474
  65.0 0.0 copy-start.6
  65.0 0.0 copy-done.5
  65.0 0.7 copy-done.6
  65.7 8.4 %expert_others.1 = (bf16[64,2560]{1,0:T(8,128)(2,1)}, bf16[64,2560]{1,0:T(8,128)(2,1)}) custom-call(bf16[64,2560]{1,0:T(8,128)(2,1)} %get-tuple-element.22.after.hidden, bf16[128,640]{1,0:T(8,128)(2,1)} %copy-done.6, bf16[128,640]{1,0:T(8,128)(2,1)} %copy-done.5, bf16[1280,2560]{1,0:T(8,128)(2,1)} %bitcast.21, bf16[2560,1280]{1,0:T(8,128)(2,1)} %bitcast.24), custom_call_target="tpu_custom_call" | custom-call | flops 838860800 | bytes 13107200 | tf_op jit(solution)/shard_map/expert_others/pallas_call | solution.py:273
  74.1 0.0 copy-done
  74.1 4.5 %combine_part.1.part = f32[4,16,256]{2,1,0:T(8,128)} custom-call(bf16[64,2560]{1,0:T(8,128)(2,1)} %get-tuple-element.22.after.hidden, bf16[128,640]{1,0:T(8,128)(2,1)} %bitcast.25, bf16[4,256,1280]{2,1,0:T(8,128)(2,1)} %grads.3, f32[4,16,256]{2,1,0:T(8,128)} %get-tuple-element.19.combine), custom_call_target="tpu_custom_call" | custom-call | flops 41943040 | bytes 2621440 | tf_op jit(solution)/shard_map/combine_part/pallas_call | solution.py:375
  78.6 0.0 all-to-all-done.2
  78.6 0.0 copy-start.1
  78.7 0.7 copy-done.1
  79.3 5.3 %logits_grads.1 = (bf16[4,32,256]{2,1,0:T(8,128)(2,1)}, bf16[4,32,1280]{2,1,0:T(8,128)(2,1)}, f32[16,1,1280]{2,1,0:T(1,128)}) custom-call(bf16[64,2560]{1,0:T(8,128)(2,1)} %get-tuple-element.23.after.other_hidden, bf16[128,640]{1,0:T(8,128)(2,1)} %bitcast.26, bf16[4,256,1280]{2,1,0:T(8,128)(2,1)} %tokens.3, bf16[16,1280]{1,0:T(8,128)(2,1)} %bitcast.38, ...), custom_call_target="tpu_custom_call" | custom-call | flops 83886080 | bytes 2621440 | tf_op jit(solution)/shard_map/logits_grads/pallas_call | solution.py:420
  84.6 12.9 %all_to_all.54 = f32[16,1,1280]{2,1,0:T(1,128)S(1)} all-to-all(f32[16,1,1280]{2,1,0:T(1,128)} %get-tuple-element.27.after), channel_id=1, replica_groups=mesh['rep'=2,'exp'=16] {'exp'}, dimensions={0} | all-to-all | bytes 163840 | tf_op jit(solution)/shard_map/all_to_all | solution.py:465
  97.5 0.1 reduce_sum.9
  97.6 1.6 %collective-permute-start.2 = (f32[1,1,1280]{2,1,0:T(1,128)S(1)}, f32[1,1,1280]{2,1,0:T(1,128)S(1)}, u32[]{:S(2)}, u32[]{:S(2)}) collective-permute-start(f32[1,1,1280]{2,1,0:T(1,128)S(1)} %broadcast_in_dim.16), channel_id=1, source_target_pairs={{0,16},{16,0},{1,17},{17,1},{2,18},{18,2},{3,19},{19,3},{4,20},{20... | collective-permute-start | bytes 15368 | tf_op jit(solution)/shard_map/ppermute | solution.py:474
  99.1 2.1 %collective-permute-done.2 = f32[1,1,1280]{2,1,0:T(1,128)S(1)} collective-permute-done((f32[1,1,1280]{2,1,0:T(1,128)S(1)}, f32[1,1,1280]{2,1,0:T(1,128)S(1)}, u32[]{:S(2)}, u32[]{:S(2)}) %collective-permute-start.2) | collective-permute-done | bytes 5152 | tf_op jit(solution)/shard_map/ppermute | solution.py:474
  101.3 0.6 fusion
  101.9 0.7 broadcast_in_dim.18
  102.5 3.5 %all-to-all-start.5 = ((f32[16,1,1280]{2,1,0:T(1,128)}), f32[16,1,1280]{2,1,0:T(1,128)S(1)}, u32[]{:S(2)}, u32[]{:S(2)}) async-start(f32[16,1,1280]{2,1,0:T(1,128)} %broadcast_in_dim.18), calls=%async_computation.5 | async-start | bytes 163840 | tf_op jit(solution)/shard_map/all_to_all | solution.py:465
  106.0 6.2 %weight_grads.1 = (bf16[640,2560]{1,0:T(8,128)(2,1)}, bf16[1280,1280]{1,0:T(8,128)(2,1)}) custom-call(s32[1]{0:T(128)} %bitcast.12.mine, f32[16,1,1280]{2,1,0:T(1,128)} %get-tuple-element.27.after, bf16[128,640]{1,0:T(8,128)(2,1)} %bitcast.29, bf16[128,640]{1,0:T(8,128)(2,1)} %bitcast.33, bf16[128,640]{1,0:T(8,128)(2,1)} %copy-done.6, ...), custom_call_target="tpu_custom_call" | custom-call | flops 838860800 | bytes 6553600 | tf_op jit(solution)/shard_map/weight_grads/pallas_call | solution.py:331
  112.3 4.2 %tokens_grads.1 = bf16[4,256,1280]{2,1,0:T(8,128)(2,1)} custom-call(f32[1,1,1280]{2,1,0:T(1,128)} %get-tuple-element.35.after, bf16[4,32,256]{2,1,0:T(8,128)(2,1)} %get-tuple-element.28.left, bf16[4,32,1280]{2,1,0:T(8,128)(2,1)} %get-tuple-element.29.right), custom_call_target="tpu_custom_call" | custom-call | flops 83886080 | bytes 2621440 | tf_op jit(solution)/shard_map/tokens_grads/pallas_call | solution.py:448
  116.5 0.0 all-to-all-done.5
  116.5 0.6 copy.11
  (1 shorter events, 0.0 us)
Async XLA Ops:
  5.4 15.9 %all-to-all-start.1 = ((bf16[16,8,640]{2,1,0:T(8,128)(2,1)}), bf16[16,8,640]{2,1,0:T(8,128)(2,1)S(1)}, u32[]{:S(2)}, u32[]{:S(2)}) async-start(bf16[16,8,640]{2,1,0:T(8,128)(2,1)} %bitcast.36), calls=%async_computation.1 | async-start | bytes 327680 | tf_op jit(solution)/shard_map/all_to_all | solution.py:465
  21.2 3.5 %copy-start.2 = (bf16[16,8,640]{2,1,0:T(8,128)(2,1)}, bf16[16,8,640]{2,1,0:T(8,128)(2,1)S(1)}, u32[]{:S(2)}) copy-start(bf16[16,8,640]{2,1,0:T(8,128)(2,1)S(1)} %all-to-all-done.1) | copy-start | bytes 491524
  21.3 12.0 %all-to-all-start = ((bf16[16,8,640]{2,1,0:T(8,128)(2,1)}), bf16[16,8,640]{2,1,0:T(8,128)(2,1)S(1)}, u32[]{:S(2)}, u32[]{:S(2)}) async-start(bf16[16,8,640]{2,1,0:T(8,128)(2,1)} %bitcast.27), calls=%async_computation | async-start | bytes 327680 | tf_op jit(solution)/shard_map/all_to_all | solution.py:465
  33.2 6.0 %copy-start.4 = (bf16[16,8,640]{2,1,0:T(8,128)(2,1)}, bf16[16,8,640]{2,1,0:T(8,128)(2,1)S(1)}, u32[]{:S(2)}) copy-start(bf16[16,8,640]{2,1,0:T(8,128)(2,1)S(1)} %all-to-all-done) | copy-start | bytes 491524
  33.2 15.6 %all-to-all-start.3 = ((bf16[16,8,640]{2,1,0:T(8,128)(2,1)}), bf16[16,8,640]{2,1,0:T(8,128)(2,1)S(1)}, u32[]{:S(2)}, u32[]{:S(2)}) async-start(bf16[16,8,640]{2,1,0:T(8,128)(2,1)} %bitcast.35), calls=%async_computation.3 | async-start | bytes 327680 | tf_op jit(solution)/shard_map/all_to_all | solution.py:465
  39.2 17.2 %copy-start.3 = (bf16[16,8,640]{2,1,0:T(8,128)(2,1)S(1)}, bf16[16,8,640]{2,1,0:T(8,128)(2,1)}, u32[]{:S(2)}) copy-start(bf16[16,8,640]{2,1,0:T(8,128)(2,1)} %copy-done.2) | copy-start | bytes 491524
  48.8 25.3 %copy-start = (bf16[16,8,640]{2,1,0:T(8,128)(2,1)}, bf16[16,8,640]{2,1,0:T(8,128)(2,1)S(1)}, u32[]{:S(2)}) copy-start(bf16[16,8,640]{2,1,0:T(8,128)(2,1)S(1)} %all-to-all-done.3) | copy-start | bytes 491524
  48.8 29.9 %all-to-all-start.2 = ((bf16[16,8,640]{2,1,0:T(8,128)(2,1)}), bf16[16,8,640]{2,1,0:T(8,128)(2,1)S(1)}, u32[]{:S(2)}, u32[]{:S(2)}) async-start(bf16[16,8,640]{2,1,0:T(8,128)(2,1)} %bitcast.34), calls=%async_computation.2 | async-start | bytes 327680 | tf_op jit(solution)/shard_map/all_to_all | solution.py:465
  54.8 7.3 %collective-permute-start.1 = (bf16[128,640]{1,0:T(8,128)(2,1)}, bf16[128,640]{1,0:T(8,128)(2,1)S(1)}, u32[]{:S(2)}, u32[]{:S(2)}) collective-permute-start(bf16[128,640]{1,0:T(8,128)(2,1)} %bitcast.32), channel_id=1, source_target_pairs={{0,16},{16,0},{1,17},{17,1},{2,18},{18,2},{3,19},{19,3},{4,20},{20... | collective-permute-start | bytes 491528 | tf_op jit(solution)/shard_map/ppermute | solution.py:474
  56.4 8.7 %collective-permute-start = (bf16[128,640]{1,0:T(8,128)(2,1)S(1)}, bf16[128,640]{1,0:T(8,128)(2,1)S(1)}, u32[]{:S(2)}, u32[]{:S(2)}) collective-permute-start(bf16[128,640]{1,0:T(8,128)(2,1)S(1)} %bitcast.30), channel_id=1, source_target_pairs={{0,16},{16,0},{1,17},{17,1},{2,18},{18,2},{3,19},{19,3},{4,20},{20... | collective-permute-start | bytes 491528 | tf_op jit(solution)/shard_map/ppermute | solution.py:474
  62.1 3.0 %copy-start.5 = (bf16[128,640]{1,0:T(8,128)(2,1)}, bf16[128,640]{1,0:T(8,128)(2,1)S(1)}, u32[]{:S(2)}) copy-start(bf16[128,640]{1,0:T(8,128)(2,1)S(1)} %collective-permute-done.1.grad_rows.other_grad_rows) | copy-start | bytes 491524
  65.0 0.7 copy-start.6
  78.6 0.7 copy-start.1
  97.6 3.7 %collective-permute-start.2 = (f32[1,1,1280]{2,1,0:T(1,128)S(1)}, f32[1,1,1280]{2,1,0:T(1,128)S(1)}, u32[]{:S(2)}, u32[]{:S(2)}) collective-permute-start(f32[1,1,1280]{2,1,0:T(1,128)S(1)} %broadcast_in_dim.16), channel_id=1, source_target_pairs={{0,16},{16,0},{1,17},{17,1},{2,18},{18,2},{3,19},{19,3},{4,20},{20... | collective-permute-start | bytes 15368 | tf_op jit(solution)/shard_map/ppermute | solution.py:474
  102.5 14.0 %all-to-all-start.5 = ((f32[16,1,1280]{2,1,0:T(1,128)}), f32[16,1,1280]{2,1,0:T(1,128)S(1)}, u32[]{:S(2)}, u32[]{:S(2)}) async-start(f32[16,1,1280]{2,1,0:T(1,128)} %broadcast_in_dim.18), calls=%async_computation.5 | async-start | bytes 163840 | tf_op jit(solution)/shard_map/all_to_all | solution.py:465

commit v4 on v3

v4 whole, which is shorter than its diff:
```python
import math

import jax
import jax.numpy as jnp
from jax import lax
from jax.experimental import pallas as pl
from jax.experimental.pallas import tpu as pltpu
from jax.sharding import PartitionSpec as P

GELU_C = math.sqrt(2.0 / math.pi)
CUBIC = 0.044715
LOW = jnp.bfloat16
WIDE = jnp.float32
LANES = 128
KINDS = 2
VMEM_BYTES = 60 * 1024 * 1024
WHOLE = pl.BlockSpec(memory_space=pltpu.VMEM)
FAR = pl.BlockSpec(memory_space=pltpu.HBM)
PLACE = pl.BlockSpec(memory_space=pl.ANY)


def call(kernel, name, flops, nbytes, exps=0, **kwargs):
    return pl.pallas_call(
        kernel,
        name=name,
        compiler_params=pltpu.CompilerParams(vmem_limit_bytes=VMEM_BYTES),
        cost_estimate=pl.CostEstimate(
            flops=flops, bytes_accessed=nbytes, transcendentals=exps
        ),
        **kwargs,
    )


def shaped(shape, dtype):
    return jax.ShapeDtypeStruct(shape, dtype)


def gelu_parts(values):
    square = values * values
    tangent = jnp.tanh(GELU_C * (values + CUBIC * square * values))
    half = 0.5 * (1.0 + tangent)
    slope = half + 0.5 * values * (1.0 - tangent * tangent) * GELU_C * (1.0 + 3.0 * CUBIC * square)
    return values * half, slope


def dot(left, right, over_left, over_right):
    return lax.dot_general(
        left, right, (((over_left,), (over_right,)), ((), ())), preferred_element_type=WIDE
    )


def softmax(values, axis):
    raised = jnp.exp(values - jnp.max(values, axis=axis, keepdims=True))
    return raised / jnp.sum(raised, axis=axis, keepdims=True)


def scratch_rows(shape):
    return pltpu.VMEM((shape[1] // LANES, shape[0], LANES), WIDE)


def load_rows(ref, array):
    for tile in range(ref.shape[0]):
        ref[tile] = array[:, tile * LANES : (tile + 1) * LANES].astype(WIDE)


def packed(ref):
    return jnp.concatenate([ref[tile] for tile in range(ref.shape[0])], axis=1).astype(LOW)


def take(ref, start, count, stride, first=0, tiles=None):
    tiles = ref.shape[0] if tiles is None else tiles
    picked = [ref[first + tile, pl.ds(start, count, stride=stride), :] for tile in range(tiles)]
    return jnp.concatenate(picked, axis=1)


def put(ref, start, count, stride, array):
    for tile in range(ref.shape[0]):
        ref[tile, pl.ds(start, count, stride=stride), :] = array[
            :, tile * LANES : (tile + 1) * LANES
        ]


def start_copies(source, target, sems):
    copies = []
    for index in range(source.shape[0]):
        copy = pltpu.make_async_copy(source.at[index], target.at[index], sems.at[index])
        copy.start()
        copies.append(copy)
    return copies


def gather_kernel(
    tokens, params, grads, sent, dispatch, combine, tokens_v, grads_v, rows, sems, grad_sems
):
    images = tokens.shape[0]
    slots = params.shape[0]
    stride = KINDS * images
    copies = start_copies(tokens, tokens_v, sems)
    grad_copies = start_copies(grads, grads_v, grad_sems)
    logits = []
    for image in range(images):
        copies[image].wait()
        logits.append(dot(params[...], tokens_v[image], 1, 1))
    over_slots = []
    for image in range(images):
        over_tokens = softmax(logits[image], 1)
        dispatch[image] = over_tokens
        put(
            rows, KINDS * image, slots, stride, dot(over_tokens.astype(LOW), tokens_v[image], 1, 0)
        )
        over_slots.append(softmax(logits[image], 0))
        combine[image] = over_slots[image]
    for image in range(images):
        grad_copies[image].wait()
        value = dot(over_slots[image].astype(LOW), grads_v[image], 1, 0)
        put(rows, KINDS * image + 1, slots, stride, value)
    sent[...] = packed(rows)


def gather(tokens, params, grads):
    images, length, width = tokens.shape
    slots = params.shape[0]
    weights = shaped((images, slots, length), WIDE)
    rows = (slots * images * KINDS, width)
    return call(
        gather_kernel,
        "gather_slots",
        6 * images * slots * length * width,
        4 * images * length * width,
        2 * images * slots * length,
        out_shape=(shaped(rows, LOW), weights, weights),
        in_specs=[FAR, WHOLE, FAR],
        out_specs=(WHOLE, WHOLE, WHOLE),
        scratch_shapes=[
            pltpu.VMEM(tokens.shape, LOW),
            pltpu.VMEM(grads.shape, LOW),
            scratch_rows(rows),
            pltpu.SemaphoreType.DMA((images,)),
            pltpu.SemaphoreType.DMA((images,)),
        ],
    )(tokens, params, grads)


def start_weights(w_in, w_out, w_in_v, w_out_v, sems):
    chunks, tile = w_out_v.shape[:2]
    copies = []
    for chunk in range(chunks):
        units = pl.ds(chunk * tile, tile)
        pair = (
            pltpu.make_async_copy(w_in.at[:, units], w_in_v.at[chunk], sems.at[0, chunk]),
            pltpu.make_async_copy(w_out.at[units, :], w_out_v.at[chunk], sems.at[1, chunk]),
        )
        for copy in pair:
            copy.start()
        copies.append(pair)
    return copies


def weight_scratch(width, hidden, tile):
    chunks = hidden // tile
    return [
        pltpu.VMEM((chunks, width, tile), LOW),
        pltpu.VMEM((chunks, tile, width), LOW),
        pltpu.SemaphoreType.DMA((2, chunks)),
    ]


def expert_kernel(rows, w_in, w_out, back, acts, hidden, w_in_v, w_out_v, sems, wide):
    copies = start_weights(w_in, w_out, w_in_v, w_out_v, sems)
    count = rows.shape[0] // KINDS
    chunks, tile = w_out_v.shape[:2]
    load_rows(wide, rows[...])
    rows_in = take(wide, 0, count, KINDS).astype(LOW)
    rows_grad = take(wide, 1, count, KINDS).astype(LOW)
    out = d_in = None
    for chunk in range(chunks):
        units = slice(chunk * tile, (chunk + 1) * tile)
        copies[chunk][0].wait()
        preact = dot(rows_in, w_in_v[chunk], 1, 0)
        copies[chunk][1].wait()
        d_acts = dot(rows_grad, w_out_v[chunk], 1, 1)
        values, slope = gelu_parts(preact)
        values = values.astype(LOW)
        d_hidden = (d_acts * slope).astype(LOW)
        acts[:, units] = values
        hidden[:, units] = d_hidden
        out_part = dot(values, w_out_v[chunk], 1, 0)
        d_in_part = dot(d_hidden, w_in_v[chunk], 1, 1)
        out = out_part if chunk == 0 else out + out_part
        d_in = d_in_part if chunk == 0 else d_in + d_in_part
    put(wide, 0, count, KINDS, out)
    put(wide, 1, count, KINDS, d_in)
    back[...] = packed(wide)


def expert(rows, w_in, w_out, tile):
    total, width = rows.shape
    hidden = w_in.shape[1]
    count = total // KINDS
    kept = shaped((count, hidden), LOW)
    return call(
        expert_kernel,
        "expert_rows",
        8 * count * hidden * width,
        4 * hidden * width,
        count * hidden,
        out_shape=(shaped(rows.shape, LOW), kept, kept),
        in_specs=[WHOLE, FAR, FAR],
        out_specs=(WHOLE,) * 3,
        scratch_shapes=[*weight_scratch(width, hidden, tile), scratch_rows(rows.shape)],
    )(rows, w_in, w_out)


def others_kernel(after, rows, w_in, w_out, acts, hidden, w_in_v, w_out_v, sems, wide):
    del after
    copies = start_weights(w_in, w_out, w_in_v, w_out_v, sems)
    count = rows.shape[0] // KINDS
    chunks, tile = w_out_v.shape[:2]
    load_rows(wide, rows[...])
    rows_in = take(wide, 0, count, KINDS).astype(LOW)
    rows_grad = take(wide, 1, count, KINDS).astype(LOW)
    for chunk in range(chunks):
        units = slice(chunk * tile, (chunk + 1) * tile)
        copies[chunk][0].wait()
        values, slope = gelu_parts(dot(rows_in, w_in_v[chunk], 1, 0))
        acts[:, units] = values.astype(LOW)
        copies[chunk][1].wait()
        d_acts = dot(rows_grad, w_out_v[chunk], 1, 1)
        hidden[:, units] = (d_acts * slope).astype(LOW)


def others_hidden(after, rows, w_in, w_out, tile):
    total, width = rows.shape
    hidden = w_in.shape[1]
    count = total // KINDS
    kept = shaped((count, hidden), LOW)
    return call(
        others_kernel,
        "others_hidden",
        64 * count * hidden * width,
        32 * hidden * width,
        count * hidden,
        out_shape=(kept, kept),
        in_specs=[PLACE, WHOLE, FAR, FAR],
        out_specs=(WHOLE,) * 2,
        scratch_shapes=[*weight_scratch(width, hidden, tile), scratch_rows(rows.shape)],
    )(after, rows, w_in, w_out)


def weights_kernel(
    mine, after, rows, other_rows, acts, other_acts, hidden, other_hidden, grad_in, grad_out,
    wide, grads, turned,
):
    del after
    count = rows.shape[0] // KINDS

    @pl.when(pl.program_id(0) == 0)
    def _():
        left, right = [], []
        tiles = turned.shape[0] // LANES
        for source in (rows, other_rows):
            load_rows(wide, source[...])
            left.append(take(wide, 0, count, KINDS, mine[0] * tiles, tiles))
            right.append(take(wide, 1, count, KINDS))
        turned[...] = jnp.concatenate(left, axis=0).T.astype(LOW)
        grads[...] = jnp.concatenate(right, axis=0).astype(LOW)

    all_hidden = jnp.concatenate([hidden[...], other_hidden[...]], axis=0)
    grad_in[...] = dot(turned[...], all_hidden, 1, 0).astype(LOW)
    all_acts = jnp.concatenate([acts[...], other_acts[...]], axis=0)
    grad_out[...] = dot(all_acts, grads[...], 0, 0).astype(LOW)


def weight_grads(mine, after, rows, acts, hidden, steps, replicas):
    total, width = rows[0].shape
    size = acts[0].shape[1]
    count = total // KINDS
    in_tile, out_tile = size // steps, size // replicas // steps
    whole_rows = pl.BlockSpec((total, width), lambda i, mine: (0, 0))
    acts_spec = pl.BlockSpec((count, out_tile), lambda i, mine: (0, mine[0] * steps + i))
    hidden_spec = pl.BlockSpec((count, in_tile), lambda i, mine: (0, i))
    return call(
        weights_kernel,
        "weight_grads",
        8 * count * size * width // replicas,
        4 * size * width // replicas,
        grid_spec=pltpu.PrefetchScalarGridSpec(
            num_scalar_prefetch=1,
            grid=(steps,),
            in_specs=[PLACE] + [whole_rows] * 2 + [acts_spec] * 2 + [hidden_spec] * 2,
            out_specs=(
                pl.BlockSpec((width // replicas, in_tile), lambda i, mine: (0, i)),
                pl.BlockSpec((out_tile, width), lambda i, mine: (i, 0)),
            ),
            scratch_shapes=[
                scratch_rows((total, width)),
                pltpu.VMEM((2 * count, width), LOW),
                pltpu.VMEM((width // replicas, 2 * count), LOW),
            ],
        ),
        out_shape=(
            shaped((width // replicas, size), LOW),
            shaped((size // replicas, width), LOW),
        ),
    )(mine, after, *rows, *acts, *hidden)


def logits_kernel(
    after, back, tokens, params, grads, dispatch, combine, left, right, local,
    tokens_v, grads_v, wide, sems, grad_sems,
):
    del after
    images, slots, _ = dispatch.shape
    grad_copies = start_copies(grads, grads_v, grad_sems)
    copies = start_copies(tokens, tokens_v, sems)
    load_rows(wide, back[...])
    stride = KINDS * images
    parts = []
    for image in range(images):
        slot_out = take(wide, KINDS * image, slots, stride).astype(LOW)
        weights = combine[image]
        grad_copies[image].wait()
        d_combine = dot(slot_out, grads_v[image], 1, 1)
        parts.append(
            weights * (d_combine - jnp.sum(weights * d_combine, axis=0, keepdims=True))
        )
    total = jnp.zeros(params.shape, WIDE)
    for image in range(images):
        d_slot_in = take(wide, KINDS * image + 1, slots, stride).astype(LOW)
        right[image, :slots, :] = d_slot_in
        right[image, slots:, :] = params[...]
        weights = dispatch[image]
        copies[image].wait()
        d_dispatch = dot(d_slot_in, tokens_v[image], 1, 1)
        d_logits = parts[image] + weights * (
            d_dispatch - jnp.sum(weights * d_dispatch, axis=1, keepdims=True)
        )
        low = d_logits.astype(LOW)
        left[image, :slots, :] = weights.astype(LOW)
        left[image, slots:, :] = low
        total += dot(low, tokens_v[image], 1, 0)
    pieces, _, size = local.shape
    for slot in range(slots):
        for piece in range(pieces // slots):
            local[slot * (pieces // slots) + piece] = total[
                slot : slot + 1, piece * size : (piece + 1) * size
            ]


def logits_grads(after, back, tokens, params, grads, dispatch, combine, pieces):
    images, length, width = tokens.shape
    slots = params.shape[0]
    return call(
        logits_kernel,
        "logits_grads",
        6 * images * slots * length * width,
        4 * images * length * width,
        out_shape=(
            shaped((images, 2 * slots, length), LOW),
            shaped((images, 2 * slots, width), LOW),
            shaped((pieces, 1, slots * width // pieces), WIDE),
        ),
        in_specs=[PLACE, WHOLE, FAR, WHOLE, FAR, WHOLE, WHOLE],
        out_specs=(WHOLE,) * 3,
        scratch_shapes=[
            pltpu.VMEM(tokens.shape, LOW),
            pltpu.VMEM(grads.shape, LOW),
            scratch_rows(back.shape),
            pltpu.SemaphoreType.DMA((images,)),
            pltpu.SemaphoreType.DMA((images,)),
        ],
    )(after, back, tokens, params, grads, dispatch, combine)


def tokens_kernel(after, left, right, out):
    del after
    out[0] = dot(left[0], right[0], 0, 0).astype(LOW)


def tokens_grads(after, left, right):
    images, deep, length = left.shape
    width = right.shape[2]
    return call(
        tokens_kernel,
        "tokens_grads",
        2 * images * deep * length * width,
        2 * images * length * width,
        grid=(images,),
        out_shape=shaped((images, length, width), LOW),
        in_specs=[
            PLACE,
            pl.BlockSpec((1, deep, length), lambda i: (i, 0, 0)),
            pl.BlockSpec((1, deep, width), lambda i: (i, 0, 0)),
        ],
        out_specs=pl.BlockSpec((1, length, width), lambda i: (i, 0, 0)),
    )(after, left, right)


def exchange(rows, axes):
    return lax.all_to_all(rows, axes, split_axis=0, concat_axis=0, tiled=True)


def body(tokens, slot_params, expert_in, expert_out, grad_out):
    params = slot_params.T
    weights = (expert_in[0], expert_out[0])
    replicas = lax.axis_size("rep")
    everyone = ("rep", "exp")
    mine = lax.axis_index("rep").astype(jnp.int32).reshape(1)

    sent, dispatch, combine = gather(tokens, params, grad_out)
    rows = exchange(sent, "exp")
    other_rows = lax.ppermute(rows, "rep", [(i, (i + 1) % replicas) for i in range(replicas)])
    back, acts, hidden = expert(rows, *weights, 512)
    other_acts, other_hidden = others_hidden(hidden, other_rows, *weights, 512)
    back = exchange(back, "exp")
    left, right, local = logits_grads(
        other_hidden, back, tokens, params, grad_out, dispatch, combine, lax.axis_size(everyone)
    )
    share = jnp.sum(exchange(local, everyone), axis=0, keepdims=True)
    grad_expert_in, grad_expert_out = weight_grads(
        mine, local, (rows, other_rows), (acts, other_acts), (hidden, other_hidden), 5, replicas
    )
    grad_params = exchange(jnp.broadcast_to(share, local.shape), everyone)
    grad_tokens = tokens_grads(share, left, right)
    return (
        grad_tokens,
        grad_params.reshape(params.shape).T,
        grad_expert_in[None],
        grad_expert_out[None],
    )


def solution(mesh):
    in_specs = (
        P(("rep", "exp"), None, None),
        P(),
        P("exp", None, None),
        P("exp", None, None),
        P(("rep", "exp"), None, None),
    )
    out_specs = (P(("rep", "exp"), None, None), P(), P("exp", "rep", None), P("exp", "rep", None))
    return jax.shard_map(body, mesh=mesh, in_specs=in_specs, out_specs=out_specs, check_vma=False)
```

time: 119 us -> 86.1 us (0.72)
  starting transfers between devices: 30 us -> 7.62 us
  blocking collectives: 12.9 us -> 28.7 us
  waiting for transfers between devices: 15.3 us -> 2.5 us
  Pallas kernels: 54.8 us -> 42 us
    all_to_all x5 -> x2, starting transfers between devices: 26.4 us -> 6.13 us  [exchange(): return lax.all_to_all(rows, axes, split_axis=0, concat_axis=0, tiled=True)]
    all_to_all x1 -> x2, blocking collectives: 12.9 us -> 28.7 us  [exchange(): return lax.all_to_all(rows, axes, split_axis=0, concat_axis=0, tiled=True)]
    pallas_call x7 -> x4, Pallas kernels: 44.4 us -> 31.6 us  [the longest x1 10.8 us: expert(): call(expert_kernel, 'expert_rows', 8 * count * hidden * width, 4 * hidden...]
    ppermute x3 -> x1, waiting for transfers between devices: 10.3 us -> 0.01 us  [body(): lax.ppermute(rows, 'rep', [(i, (i + 1) % replicas) for i in range(replica...]
    all_to_all x5 -> x2, waiting for transfers between devices: 5 us -> 2.49 us  [exchange(): return lax.all_to_all(rows, axes, split_axis=0, concat_axis=0, tiled=True)]
    ppermute x3 -> x1, starting transfers between devices: 3.65 us -> 1.49 us  [body(): lax.ppermute(rows, 'rep', [(i, (i + 1) % replicas) for i in range(replica...]
  transfers between devices with their start and end apart: 8 -> 3, of which waited for: 4 -> 1; matrix products, arithmetic and copies ran while one was open for 0% -> 1% of each run, Pallas kernels for 38% -> 34%
where the time goes in v4:
time: 86.1 us; the launch traced here: 85.2 us
  Pallas kernels  42 us (49%)
  blocking collectives  28.7 us (33%)
  starting transfers between devices  7.62 us (9%)
  local copies, waits for them, and re-layouts  3.36 us (4%)
  waiting for transfers between devices  2.5 us (3%)
    all_to_all x2, blocking collectives, exchange(): return lax.all_to_all(rows, axes, split_axis=0, concat_axis=0, tiled=True)  28.7 us
    pallas_call x1, Pallas kernels, expert(): call(expert_kernel, 'expert_rows', 8 * count * hidden * width, 4 * hidden...  10.8 us
    pallas_call x1, Pallas kernels, others_hidden(): call(others_kernel, 'others_hidden', 64 * count * hidden * width, 32 * hi...  7.83 us
    pallas_call x1, Pallas kernels, logits_grads(): call(logits_kernel, 'logits_grads', 6 * images * slots * length * width,...  7.3 us
    pallas_call x1, Pallas kernels, weight_grads(): call(weights_kernel, 'weight_grads', 8 * count * size * width // replicas...  6.18 us
    all_to_all x2, starting transfers between devices, exchange(): return lax.all_to_all(rows, axes, split_axis=0, concat_axis=0, tiled=True)  6.13 us
    pallas_call x1, Pallas kernels, gather(): call(gather_kernel, 'gather_slots', 6 * images * slots * length * width,...  5.71 us
    pallas_call x1, Pallas kernels, tokens_grads(): call(tokens_kernel, 'tokens_grads', 2 * images * deep * length * width, 2...  4.19 us
  transfers between devices with their start and end apart: 3, of which 1 were waited for; matrix products, arithmetic and copies ran while one was open for 1% of the time, Pallas kernels for 34%

profile of v4, /device:TPU:0, one launch (start us, length us, event | category | flops | bytes accessed | tf_op | source)
XLA Modules:
  0.0 85.2 jit_solution(8679711693919682202)
XLA Ops:
  0.6 5.7 %gather_slots.1 = (bf16[128,1280]{1,0:T(8,128)(2,1)}, f32[4,16,256]{2,1,0:T(8,128)}, f32[4,16,256]{2,1,0:T(8,128)}) custom-call(bf16[4,256,1280]{2,1,0:T(8,128)(2,1)} %tokens.3, bf16[16,1280]{1,0:T(8,128)(2,1)} %bitcast.21, bf16[4,256,1280]{2,1,0:T(8,128)(2,1)} %grads.3), custom_call_target="tpu_custom_call" | custom-call | flops 125829120 | bytes 5242880 | tf_op jit(solution)/shard_map/gather_slots/pallas_call | solution.py:125
  6.3 18.5 %all_to_all.32 = bf16[16,8,1280]{2,1,0:T(8,128)(2,1)S(1)} all-to-all(bf16[16,8,1280]{2,1,0:T(8,128)(2,1)} %bitcast.20), channel_id=1, replica_groups=mesh['rep'=2,'exp'=16] {'exp'}, dimensions={0} | all-to-all | bytes 655360 | tf_op jit(solution)/shard_map/all_to_all | solution.py:400
  24.8 0.0 copy-start
  24.8 1.5 %collective-permute-start = (bf16[128,1280]{1,0:T(8,128)(2,1)S(1)}, bf16[128,1280]{1,0:T(8,128)(2,1)S(1)}, u32[]{:S(2)}, u32[]{:S(2)}) collective-permute-start(bf16[128,1280]{1,0:T(8,128)(2,1)S(1)} %bitcast.15), channel_id=1, source_target_pairs={{0,16},{16,0},{1,17},{17,1},{2,18},{18,2},{3,19},{19,3},{4,20},{20... | collective-permute-start | bytes 983048 | tf_op jit(solution)/shard_map/ppermute | solution.py:412
  26.3 0.0 copy-done
  26.3 10.8 %expert_rows.1 = (bf16[128,1280]{1,0:T(8,128)(2,1)}, bf16[64,2560]{1,0:T(8,128)(2,1)}, bf16[64,2560]{1,0:T(8,128)(2,1)}) custom-call(bf16[128,1280]{1,0:T(8,128)(2,1)} %bitcast.16, bf16[1280,2560]{1,0:T(8,128)(2,1)} %bitcast.11, bf16[2560,1280]{1,0:T(8,128)(2,1)} %bitcast.13), custom_call_target="tpu_custom_call" | custom-call | flops 1677721600 | bytes 13107200 | tf_op jit(solution)/shard_map/expert_rows/pallas_call | solution.py:201
  37.1 3.6 %all-to-all-start.1 = ((bf16[16,8,1280]{2,1,0:T(8,128)(2,1)}), bf16[16,8,1280]{2,1,0:T(8,128)(2,1)S(1)}, u32[]{:S(2)}, u32[]{:S(2)}) async-start(bf16[16,8,1280]{2,1,0:T(8,128)(2,1)} %bitcast.19), calls=%async_computation.1 | async-start | bytes 655360 | tf_op jit(solution)/shard_map/all_to_all | solution.py:400
  40.7 0.0 collective-permute-done.rows.other_rows
  40.7 0.0 copy-start.2
  40.7 0.7 copy-done.2
  41.4 7.8 %others_hidden.1 = (bf16[64,2560]{1,0:T(8,128)(2,1)}, bf16[64,2560]{1,0:T(8,128)(2,1)}) custom-call(bf16[64,2560]{1,0:T(8,128)(2,1)} %get-tuple-element.18.after.hidden, bf16[128,1280]{1,0:T(8,128)(2,1)} %copy-done.2, bf16[1280,2560]{1,0:T(8,128)(2,1)} %bitcast.12, bf16[2560,1280]{1,0:T(8,128)(2,1)} %bitcast.14), custom_call_target="tpu_custom_call" | custom-call | flops 13421772800 | bytes 104857600 | tf_op jit(solution)/shard_map/others_hidden/pallas_call | solution.py:237
  49.2 2.5 %all-to-all-done.1 = bf16[16,8,1280]{2,1,0:T(8,128)(2,1)S(1)} async-done(((bf16[16,8,1280]{2,1,0:T(8,128)(2,1)}), bf16[16,8,1280]{2,1,0:T(8,128)(2,1)S(1)}, u32[]{:S(2)}, u32[]{:S(2)}) %all-to-all-start.1) | async-done | bytes 327712 | tf_op jit(solution)/shard_map/all_to_all | solution.py:400
  51.7 0.0 copy-start.1
  51.7 0.7 copy-done.1
  52.5 7.3 %logits_grads.1 = (bf16[4,32,256]{2,1,0:T(8,128)(2,1)}, bf16[4,32,1280]{2,1,0:T(8,128)(2,1)}, f32[32,1,640]{2,1,0:T(1,128)}) custom-call(bf16[64,2560]{1,0:T(8,128)(2,1)} %get-tuple-element.19.after.other_hidden, bf16[128,1280]{1,0:T(8,128)(2,1)} %bitcast.18, bf16[4,256,1280]{2,1,0:T(8,128)(2,1)} %tokens.3, bf16[16,1280]{1,0:T(8,128)(2,1)} %bitcast.22, ...), custom_call_target="tpu_custom_call" | custom-call | flops 125829120 | bytes 5242880 | tf_op jit(solution)/shard_map/logits_grads/pallas_call | solution.py:353
  59.8 10.3 %all_to_all.33 = f32[32,1,640]{2,1,0:T(1,128)S(1)} all-to-all(f32[32,1,640]{2,1,0:T(1,128)} %get-tuple-element.23.after), channel_id=1, replica_groups=mesh['rep'=2,'exp'=16] {'rep','exp'}, dimensions={0} | all-to-all | bytes 163840 | tf_op jit(solution)/shard_map/all_to_all | solution.py:400
  70.0 0.1 reduce_sum.9
  70.1 0.7 broadcast_in_dim.15
  70.8 2.6 %all-to-all-start.3 = ((f32[32,1,640]{2,1,0:T(1,128)}), f32[32,1,640]{2,1,0:T(1,128)S(1)}, u32[]{:S(2)}, u32[]{:S(2)}) async-start(f32[32,1,640]{2,1,0:T(1,128)} %broadcast_in_dim.15), calls=%async_computation.3 | async-start | bytes 163840 | tf_op jit(solution)/shard_map/all_to_all | solution.py:400
  73.3 6.2 %weight_grads.1 = (bf16[640,2560]{1,0:T(8,128)(2,1)}, bf16[1280,1280]{1,0:T(8,128)(2,1)}) custom-call(s32[1]{0:T(128)} %bitcast.8.mine, f32[32,1,640]{2,1,0:T(1,128)} %get-tuple-element.23.after, bf16[128,1280]{1,0:T(8,128)(2,1)} %bitcast.17, bf16[128,1280]{1,0:T(8,128)(2,1)} %copy-done.2, bf16[64,2560]{1,0:T(8,128)(2,1)} %get-tuple-element.26.acts, ...), custom_call_target="tpu_custom_call" | custom-call | flops 838860800 | bytes 6553600 | tf_op jit(solution)/shard_map/weight_grads/pallas_call | solution.py:282
  79.5 0.6 broadcast_in_dim.14.after
  80.1 4.2 %tokens_grads.1 = bf16[4,256,1280]{2,1,0:T(8,128)(2,1)} custom-call(f32[1,1,640]{2,1,0:T(1,128)} %broadcast_in_dim.14.after, bf16[4,32,256]{2,1,0:T(8,128)(2,1)} %get-tuple-element.24.left, bf16[4,32,1280]{2,1,0:T(8,128)(2,1)} %get-tuple-element.25.right), custom_call_target="tpu_custom_call" | custom-call | flops 83886080 | bytes 2621440 | tf_op jit(solution)/shard_map/tokens_grads/pallas_call | solution.py:383
  84.3 0.0 all-to-all-done.3
  84.3 0.2 reduce.1
  84.5 0.7 reshape.23
Async XLA Ops:
  24.8 1.5 %copy-start = (bf16[16,8,1280]{2,1,0:T(8,128)(2,1)}, bf16[16,8,1280]{2,1,0:T(8,128)(2,1)S(1)}, u32[]{:S(2)}) copy-start(bf16[16,8,1280]{2,1,0:T(8,128)(2,1)S(1)} %all_to_all.32) | copy-start | bytes 983044
  24.8 15.8 %collective-permute-start = (bf16[128,1280]{1,0:T(8,128)(2,1)S(1)}, bf16[128,1280]{1,0:T(8,128)(2,1)S(1)}, u32[]{:S(2)}, u32[]{:S(2)}) collective-permute-start(bf16[128,1280]{1,0:T(8,128)(2,1)S(1)} %bitcast.15), channel_id=1, source_target_pairs={{0,16},{16,0},{1,17},{17,1},{2,18},{18,2},{3,19},{19,3},{4,20},{20... | collective-permute-start | bytes 983048 | tf_op jit(solution)/shard_map/ppermute | solution.py:412
  37.1 14.6 %all-to-all-start.1 = ((bf16[16,8,1280]{2,1,0:T(8,128)(2,1)}), bf16[16,8,1280]{2,1,0:T(8,128)(2,1)S(1)}, u32[]{:S(2)}, u32[]{:S(2)}) async-start(bf16[16,8,1280]{2,1,0:T(8,128)(2,1)} %bitcast.19), calls=%async_computation.1 | async-start | bytes 655360 | tf_op jit(solution)/shard_map/all_to_all | solution.py:400
  40.7 0.7 copy-start.2
  51.7 0.7 copy-start.1
  70.8 13.5 %all-to-all-start.3 = ((f32[32,1,640]{2,1,0:T(1,128)}), f32[32,1,640]{2,1,0:T(1,128)S(1)}, u32[]{:S(2)}, u32[]{:S(2)}) async-start(f32[32,1,640]{2,1,0:T(1,128)} %broadcast_in_dim.15), calls=%async_computation.3 | async-start | bytes 163840 | tf_op jit(solution)/shard_map/all_to_all | solution.py:400

commit v5 on v4

--- a/solution.py
+++ b/solution.py
@@ -13,17 +13,17 @@
 WIDE = jnp.float32
 LANES = 128
 KINDS = 2
-VMEM_BYTES = 60 * 1024 * 1024
+ALONE = 60 * 1024 * 1024
+SHARED = 52 * 1024 * 1024
 WHOLE = pl.BlockSpec(memory_space=pltpu.VMEM)
-FAR = pl.BlockSpec(memory_space=pltpu.HBM)
 PLACE = pl.BlockSpec(memory_space=pl.ANY)
 
 
-def call(kernel, name, flops, nbytes, exps=0, **kwargs):
+def call(kernel, name, grant, flops, nbytes, exps=0, **kwargs):
     return pl.pallas_call(
         kernel,
         name=name,
-        compiler_params=pltpu.CompilerParams(vmem_limit_bytes=VMEM_BYTES),
+        compiler_params=pltpu.CompilerParams(vmem_limit_bytes=grant),
         cost_estimate=pl.CostEstimate(
             flops=flops, bytes_accessed=nbytes, transcendentals=exps
         ),
@@ -33,6 +33,9 @@
 
 def shaped(shape, dtype):
     return jax.ShapeDtypeStruct(shape, dtype)
+
+
+MARK = shaped((8, LANES), WIDE)
 
 
 def gelu_parts(values):
@@ -89,15 +92,24 @@
     return copies
 
 
+def start_copy(source, target, sem):
+    copy = pltpu.make_async_copy(source, target, sem)
+    copy.start()
+    return copy
+
+
 def gather_kernel(
-    tokens, params, grads, sent, dispatch, combine, tokens_v, grads_v, rows, sems, grad_sems
+    tokens, params_far, grads, sent_far, dispatch_far, combine_far,
+    tokens_v, grads_v, params, sent, dispatch, combine, rows, sems, grad_sems, more_sems,
 ):
     images = tokens.shape[0]
     slots = params.shape[0]
     stride = KINDS * images
+    params_copy = start_copy(params_far, params, more_sems.at[0])
     copies = start_copies(tokens, tokens_v, sems)
     grad_copies = start_copies(grads, grads_v, grad_sems)
     logits = []
+    params_copy.wait()
     for image in range(images):
         copies[image].wait()
         logits.append(dot(params[...], tokens_v[image], 1, 1))
@@ -110,11 +122,18 @@
         )
         over_slots.append(softmax(logits[image], 0))
         combine[image] = over_slots[image]
+    results = [
+        start_copy(dispatch, dispatch_far, more_sems.at[1]),
+        start_copy(combine, combine_far, more_sems.at[2]),
+    ]
     for image in range(images):
         grad_copies[image].wait()
         value = dot(over_slots[image].astype(LOW), grads_v[image], 1, 0)
         put(rows, KINDS * image + 1, slots, stride, value)
     sent[...] = packed(rows)
+    results.append(start_copy(sent, sent_far, more_sems.at[3]))
+    for copy in results:
+        copy.wait()
 
 
 def gather(tokens, params, grads):
@@ -125,18 +144,24 @@
     return call(
         gather_kernel,
         "gather_slots",
+        ALONE,
         6 * images * slots * length * width,
         4 * images * length * width,
         2 * images * slots * length,
         out_shape=(shaped(rows, LOW), weights, weights),
-        in_specs=[FAR, WHOLE, FAR],
-        out_specs=(WHOLE, WHOLE, WHOLE),
+        in_specs=[PLACE] * 3,
+        out_specs=(PLACE,) * 3,
         scratch_shapes=[
             pltpu.VMEM(tokens.shape, LOW),
             pltpu.VMEM(grads.shape, LOW),
+            pltpu.VMEM(params.shape, LOW),
+            pltpu.VMEM(rows, LOW),
+            pltpu.VMEM(weights.shape, WIDE),
+            pltpu.VMEM(weights.shape, WIDE),
             scratch_rows(rows),
             pltpu.SemaphoreType.DMA((images,)),
             pltpu.SemaphoreType.DMA((images,)),
+            pltpu.SemaphoreType.DMA((4,)),
         ],
     )(tokens, params, grads)
 
@@ -165,10 +190,16 @@
     ]
 
 
-def expert_kernel(rows, w_in, w_out, back, acts, hidden, w_in_v, w_out_v, sems, wide):
+def expert_kernel(
+    rows_far, w_in, w_out, back_far, acts_far, hidden_far, mark,
+    w_in_v, w_out_v, sems, wide, rows, back, acts, hidden, more_sems,
+):
+    del mark
+    rows_copy = start_copy(rows_far, rows, more_sems.at[0])
     copies = start_weights(w_in, w_out, w_in_v, w_out_v, sems)
     count = rows.shape[0] // KINDS
     chunks, tile = w_out_v.shape[:2]
+    rows_copy.wait()
     load_rows(wide, rows[...])
     rows_in = take(wide, 0, count, KINDS).astype(LOW)
     rows_grad = take(wide, 1, count, KINDS).astype(LOW)
@@ -188,9 +219,16 @@
         d_in_part = dot(d_hidden, w_in_v[chunk], 1, 1)
         out = out_part if chunk == 0 else out + out_part
         d_in = d_in_part if chunk == 0 else d_in + d_in_part
+    results = [
+        start_copy(acts, acts_far, more_sems.at[1]),
+        start_copy(hidden, hidden_far, more_sems.at[2]),
+    ]
     put(wide, 0, count, KINDS, out)
     put(wide, 1, count, KINDS, d_in)
     back[...] = packed(wide)
+    results.append(start_copy(back, back_far, more_sems.at[3]))
+    for copy in results:
+        copy.wait()
 
 
 def expert(rows, w_in, w_out, tile):
@@ -201,18 +239,27 @@
     return call(
         expert_kernel,
         "expert_rows",
+        ALONE,
         8 * count * hidden * width,
         4 * hidden * width,
         count * hidden,
-        out_shape=(shaped(rows.shape, LOW), kept, kept),
-        in_specs=[WHOLE, FAR, FAR],
-        out_specs=(WHOLE,) * 3,
-        scratch_shapes=[*weight_scratch(width, hidden, tile), scratch_rows(rows.shape)],
+        out_shape=(shaped(rows.shape, LOW), kept, kept, MARK),
+        in_specs=[PLACE] * 3,
+        out_specs=(PLACE,) * 4,
+        scratch_shapes=[
+            *weight_scratch(width, hidden, tile),
+            scratch_rows(rows.shape),
+            pltpu.VMEM(rows.shape, LOW),
+            pltpu.VMEM(rows.shape, LOW),
+            pltpu.VMEM(kept.shape, LOW),
+            pltpu.VMEM(kept.shape, LOW),
+            pltpu.SemaphoreType.DMA((4,)),
+        ],
     )(rows, w_in, w_out)
 
 
-def others_kernel(after, rows, w_in, w_out, acts, hidden, w_in_v, w_out_v, sems, wide):
-    del after
+def others_kernel(after, rows, w_in, w_out, acts, hidden, mark, w_in_v, w_out_v, sems, wide):
+    del after, mark
     copies = start_weights(w_in, w_out, w_in_v, w_out_v, sems)
     count = rows.shape[0] // KINDS
     chunks, tile = w_out_v.shape[:2]
@@ -237,21 +284,22 @@
     return call(
         others_kernel,
         "others_hidden",
+        SHARED,
         64 * count * hidden * width,
         32 * hidden * width,
         count * hidden,
-        out_shape=(kept, kept),
-        in_specs=[PLACE, WHOLE, FAR, FAR],
-        out_specs=(WHOLE,) * 2,
+        out_shape=(kept, kept, MARK),
+        in_specs=[PLACE, WHOLE, PLACE, PLACE],
+        out_specs=(WHOLE, WHOLE, PLACE),
         scratch_shapes=[*weight_scratch(width, hidden, tile), scratch_rows(rows.shape)],
     )(after, rows, w_in, w_out)
 
 
 def weights_kernel(
-    mine, after, rows, other_rows, acts, other_acts, hidden, other_hidden, grad_in, grad_out,
+    mine, after, rows, other_rows, acts, other_acts, hidden, other_hidden, grad_in, grad_out, mark,
     wide, grads, turned,
 ):
-    del after
+    del after, mark
     count = rows.shape[0] // KINDS
 
     @pl.when(pl.program_id(0) == 0)
@@ -282,6 +330,7 @@
     return call(
         weights_kernel,
         "weight_grads",
+        SHARED,
         8 * count * size * width // replicas,
         4 * size * width // replicas,
         grid_spec=pltpu.PrefetchScalarGridSpec(
@@ -291,6 +340,7 @@
             out_specs=(
                 pl.BlockSpec((width // replicas, in_tile), lambda i, mine: (0, i)),
                 pl.BlockSpec((out_tile, width), lambda i, mine: (i, 0)),
+                PLACE,
             ),
             scratch_shapes=[
                 scratch_rows((total, width)),
@@ -301,15 +351,16 @@
         out_shape=(
             shaped((width // replicas, size), LOW),
             shaped((size // replicas, width), LOW),
+            MARK,
         ),
     )(mine, after, *rows, *acts, *hidden)
 
 
 def logits_kernel(
-    after, back, tokens, params, grads, dispatch, combine, left, right, local,
+    after, back, tokens, params, grads, dispatch, combine, left, right, local, mark,
     tokens_v, grads_v, wide, sems, grad_sems,
 ):
-    del after
+    del after, mark
     images, slots, _ = dispatch.shape
     grad_copies = start_copies(grads, grads_v, grad_sems)
     copies = start_copies(tokens, tokens_v, sems)
@@ -353,15 +404,17 @@
     return call(
         logits_kernel,
         "logits_grads",
+        SHARED,
         6 * images * slots * length * width,
         4 * images * length * width,
         out_shape=(
             shaped((images, 2 * slots, length), LOW),
             shaped((images, 2 * slots, width), LOW),
             shaped((pieces, 1, slots * width // pieces), WIDE),
+            MARK,
         ),
-        in_specs=[PLACE, WHOLE, FAR, WHOLE, FAR, WHOLE, WHOLE],
-        out_specs=(WHOLE,) * 3,
+        in_specs=[PLACE, WHOLE, PLACE, WHOLE, PLACE, WHOLE, WHOLE],
+        out_specs=(WHOLE, WHOLE, WHOLE, PLACE),
         scratch_shapes=[
             pltpu.VMEM(tokens.shape, LOW),
             pltpu.VMEM(grads.shape, LOW),
@@ -383,6 +436,7 @@
     return call(
         tokens_kernel,
         "tokens_grads",
+        SHARED,
         2 * images * deep * length * width,
         2 * images * length * width,
         grid=(images,),
@@ -396,6 +450,24 @@
     )(after, left, right)
 
 
+def share_kernel(after, pieces, out, mark):
+    del after, mark
+    out[...] = jnp.broadcast_to(jnp.sum(pieces[...], axis=0, keepdims=True), out.shape)
+
+
+def share_of_sum(after, pieces):
+    return call(
+        share_kernel,
+        "share_of_sum",
+        SHARED,
+        pieces.size,
+        8 * pieces.size,
+        out_shape=(shaped(pieces.shape, WIDE), MARK),
+        in_specs=[PLACE, WHOLE],
+        out_specs=(WHOLE, PLACE),
+    )(after, pieces)
+
+
 def exchange(rows, axes):
     return lax.all_to_all(rows, axes, split_axis=0, concat_axis=0, tiled=True)
 
@@ -410,18 +482,26 @@
     sent, dispatch, combine = gather(tokens, params, grad_out)
     rows = exchange(sent, "exp")
     other_rows = lax.ppermute(rows, "rep", [(i, (i + 1) % replicas) for i in range(replicas)])
-    back, acts, hidden = expert(rows, *weights, 512)
-    other_acts, other_hidden = others_hidden(hidden, other_rows, *weights, 512)
+    back, acts, hidden, after_expert = expert(rows, *weights, 512)
+    other_acts, other_hidden, after_others = others_hidden(
+        after_expert, other_rows, *weights, 512
+    )
     back = exchange(back, "exp")
-    left, right, local = logits_grads(
-        other_hidden, back, tokens, params, grad_out, dispatch, combine, lax.axis_size(everyone)
-    )
-    share = jnp.sum(exchange(local, everyone), axis=0, keepdims=True)
-    grad_expert_in, grad_expert_out = weight_grads(
-        mine, local, (rows, other_rows), (acts, other_acts), (hidden, other_hidden), 5, replicas
-    )
-    grad_params = exchange(jnp.broadcast_to(share, local.shape), everyone)
-    grad_tokens = tokens_grads(share, left, right)
+    left, right, local, after_logits = logits_grads(
+        after_others, back, tokens, params, grad_out, dispatch, combine, lax.axis_size(everyone)
+    )
+    grad_expert_in, grad_expert_out, after_weights = weight_grads(
+        mine,
+        after_logits,
+        (rows, other_rows),
+        (acts, other_acts),
+        (hidden, other_hidden),
+        5,
+        replicas,
+    )
+    share, after_share = share_of_sum(after_weights, exchange(local, everyone))
+    grad_params = exchange(share, everyone)
+    grad_tokens = tokens_grads(after_share, left, right)
     return (
         grad_tokens,
         grad_params.reshape(params.shape).T,

time: 86.1 us -> 83.1 us (0.965)
  blocking collectives: 28.7 us -> 18.5 us
  waiting for transfers between devices: 2.5 us -> 12 us
  starting transfers between devices: 7.62 us -> 10.4 us
  Pallas kernels: 42 us -> 39.3 us
  local copies, waits for them, and re-layouts: 3.36 us -> 1.37 us
    all_to_all x2 -> x1, blocking collectives: 28.7 us -> 18.5 us  [exchange(): return lax.all_to_all(rows, axes, split_axis=0, concat_axis=0, tiled=True)]
    all_to_all x2 -> x3, waiting for transfers between devices: 2.49 us -> 12 us  [exchange(): return lax.all_to_all(rows, axes, split_axis=0, concat_axis=0, tiled=True)]
    all_to_all x2 -> x3, starting transfers between devices: 6.13 us -> 8.96 us  [exchange(): return lax.all_to_all(rows, axes, split_axis=0, concat_axis=0, tiled=True)]
    pallas_call x6 -> x7, Pallas kernels: 42 us -> 39.3 us  [the longest x1 13 us: expert(): call(expert_kernel, 'expert_rows', ALONE, 8 * count * hidden * width, 4 *...]
    broadcast_in_dim x2 -> x0, local copies, waits for them, and re-layouts: 1.26 us -> none  [the longest x1 0.68 us: body(): grad_params = exchange(jnp.broadcast_to(share, local.shape), everyone)]
  transfers between devices with their start and end apart: 3 -> 4, of which waited for: 1 -> 3; matrix products, arithmetic and copies ran while one was open for 1% -> 0% of each run, Pallas kernels for 34% -> 32%
where the time goes in v5:
time: 83.1 us; the launch traced here: 82.6 us
  Pallas kernels  39.3 us (47%)
  blocking collectives  18.5 us (22%)
  waiting for transfers between devices  12 us (14%)
  starting transfers between devices  10.4 us (13%)
  local copies, waits for them, and re-layouts  1.37 us (2%)
    all_to_all x1, blocking collectives, exchange(): return lax.all_to_all(rows, axes, split_axis=0, concat_axis=0, tiled=True)  18.5 us
    pallas_call x1, Pallas kernels, expert(): call(expert_kernel, 'expert_rows', ALONE, 8 * count * hidden * width, 4 *...  13 us
    all_to_all x3, waiting for transfers between devices, exchange(): return lax.all_to_all(rows, axes, split_axis=0, concat_axis=0, tiled=True)  12 us
    all_to_all x3, starting transfers between devices, exchange(): return lax.all_to_all(rows, axes, split_axis=0, concat_axis=0, tiled=True)  8.96 us
    pallas_call x1, Pallas kernels, logits_grads(): call(logits_kernel, 'logits_grads', SHARED, 6 * images * slots * length *...  6.3 us
    pallas_call x1, Pallas kernels, others_hidden(): call(others_kernel, 'others_hidden', SHARED, 64 * count * hidden * width,...  6.15 us
    pallas_call x1, Pallas kernels, gather(): call(gather_kernel, 'gather_slots', ALONE, 6 * images * slots * length *...  5.88 us
    pallas_call x1, Pallas kernels, weight_grads(): call(weights_kernel, 'weight_grads', SHARED, 8 * count * size * width //...  4.54 us
  transfers between devices with their start and end apart: 4, of which 3 were waited for; matrix products, arithmetic and copies ran while one was open for 0% of the time, Pallas kernels for 32%

profile of v5, /device:TPU:0, one launch (start us, length us, event | category | flops | bytes accessed | tf_op | source)
XLA Modules:
  0.0 82.6 jit_solution(17411871136283640664)
XLA Ops:
  0.6 5.9 %gather_slots.1 = (bf16[128,1280]{1,0:T(8,128)(2,1)}, f32[4,16,256]{2,1,0:T(8,128)}, f32[4,16,256]{2,1,0:T(8,128)}) custom-call(bf16[4,256,1280]{2,1,0:T(8,128)(2,1)} %tokens.3, bf16[16,1280]{1,0:T(8,128)(2,1)} %bitcast.15, bf16[4,256,1280]{2,1,0:T(8,128)(2,1)} %grads.3), custom_call_target="tpu_custom_call" | custom-call | flops 125829120 | bytes 5242880 | tf_op jit(solution)/shard_map/gather_slots/pallas_call | solution.py:144
  6.5 18.5 %all_to_all.32 = bf16[16,8,1280]{2,1,0:T(8,128)(2,1)S(1)} all-to-all(bf16[16,8,1280]{2,1,0:T(8,128)(2,1)} %bitcast.22), channel_id=1, replica_groups=mesh['rep'=2,'exp'=16] {'exp'}, dimensions={0} | all-to-all | bytes 655360 | tf_op jit(solution)/shard_map/all_to_all | solution.py:472
  25.0 0.0 copy-start
  25.0 1.5 %collective-permute-start = (bf16[128,1280]{1,0:T(8,128)(2,1)S(1)}, bf16[128,1280]{1,0:T(8,128)(2,1)S(1)}, u32[]{:S(2)}, u32[]{:S(2)}) collective-permute-start(bf16[128,1280]{1,0:T(8,128)(2,1)S(1)} %bitcast.11), channel_id=1, source_target_pairs={{0,16},{16,0},{1,17},{17,1},{2,18},{18,2},{3,19},{19,3},{4,20},{20... | collective-permute-start | bytes 983048 | tf_op jit(solution)/shard_map/ppermute | solution.py:484
  26.5 0.0 copy-done
  26.5 13.0 %expert_rows.1 = (bf16[128,1280]{1,0:T(8,128)(2,1)}, bf16[64,2560]{1,0:T(8,128)(2,1)}, bf16[64,2560]{1,0:T(8,128)(2,1)}, f32[8,128]{1,0:T(8,128)}) custom-call(bf16[128,1280]{1,0:T(8,128)(2,1)} %bitcast.12, bf16[1280,2560]{1,0:T(8,128)(2,1)} %bitcast.17, bf16[2560,1280]{1,0:T(8,128)(2,1)} %bitcast.19), custom_call_target="tpu_custom_call" | custom-call | flops 1677721600 | bytes 13107200 | tf_op jit(solution)/shard_map/expert_rows/pallas_call | solution.py:239
  39.5 3.6 %all-to-all-start.1 = ((bf16[16,8,1280]{2,1,0:T(8,128)(2,1)}), bf16[16,8,1280]{2,1,0:T(8,128)(2,1)S(1)}, u32[]{:S(2)}, u32[]{:S(2)}) async-start(bf16[16,8,1280]{2,1,0:T(8,128)(2,1)} %bitcast.21), calls=%async_computation.1 | async-start | bytes 655360 | tf_op jit(solution)/shard_map/all_to_all | solution.py:472
  43.1 0.0 collective-permute-done.rows.other_rows
  43.1 0.0 copy-start.7
  43.1 0.7 copy-done.7
  43.8 0.0 copy-start.2
  43.8 0.0 copy-start.3
  43.8 0.0 copy-start.4
  43.8 6.2 %others_hidden.1 = (bf16[64,2560]{1,0:T(8,128)(2,1)S(1)}, bf16[64,2560]{1,0:T(8,128)(2,1)S(1)}, f32[8,128]{1,0:T(8,128)S(1)}) custom-call(f32[8,128]{1,0:T(8,128)S(1)} %copy-done.7, bf16[128,1280]{1,0:T(8,128)(2,1)S(1)} %collective-permute-done.rows.other_rows, bf16[1280,2560]{1,0:T(8,128)(2,1)} %bitcast.18, bf16[2560,1280]{1,0:T(8,128)(2,1)} %bitcast.20), custom_call_target="tpu_custom_call" | custom-call | flops 13421772800 | bytes 104857600 | tf_op jit(solution)/shard_map/others_hidden/pallas_call | solution.py:284
  49.9 0.0 copy-start.1
  49.9 0.0 copy-start.5
  50.0 0.0 copy-start.6
  50.0 4.2 %all-to-all-done.1 = bf16[16,8,1280]{2,1,0:T(8,128)(2,1)S(1)} async-done(((bf16[16,8,1280]{2,1,0:T(8,128)(2,1)}), bf16[16,8,1280]{2,1,0:T(8,128)(2,1)S(1)}, u32[]{:S(2)}, u32[]{:S(2)}) %all-to-all-start.1) | async-done | bytes 327712 | tf_op jit(solution)/shard_map/all_to_all | solution.py:472
  54.1 0.0 copy-done.2
  54.1 0.0 copy-done.3
  54.1 0.0 copy-done.4
  54.1 6.3 %logits_grads.1 = (bf16[4,32,256]{2,1,0:T(8,128)(2,1)S(1)}, bf16[4,32,1280]{2,1,0:T(8,128)(2,1)S(1)}, f32[32,1,640]{2,1,0:T(1,128)}, f32[8,128]{1,0:T(8,128)S(1)}) custom-call(f32[8,128]{1,0:T(8,128)S(1)} %get-tuple-element.25.after, bf16[128,1280]{1,0:T(8,128)(2,1)S(1)} %bitcast.14, bf16[4,256,1280]{2,1,0:T(8,128)(2,1)} %tokens.3, ...), custom_call_target="tpu_custom_call" | custom-call | flops 125829120 | bytes 5242880 | tf_op jit(solution)/shard_map/logits_grads/pallas_call | solution.py:404
  60.5 2.6 %all-to-all-start.2 = ((f32[32,1,640]{2,1,0:T(1,128)}), f32[32,1,640]{2,1,0:T(1,128)S(1)}, u32[]{:S(2)}, u32[]{:S(2)}) async-start(f32[32,1,640]{2,1,0:T(1,128)} %get-tuple-element.35), calls=%async_computation.2 | async-start | bytes 163840 | tf_op jit(solution)/shard_map/all_to_all | solution.py:472
  63.1 0.0 copy-done.1
  63.1 0.0 copy-done.5
  63.1 0.0 copy-done.6
  63.1 4.5 %weight_grads.1 = (bf16[640,2560]{1,0:T(8,128)(2,1)}, bf16[1280,1280]{1,0:T(8,128)(2,1)}, f32[8,128]{1,0:T(8,128)S(1)}) custom-call(s32[1]{0:T(128)} %bitcast.mine, f32[8,128]{1,0:T(8,128)S(1)} %get-tuple-element.29.after, bf16[128,1280]{1,0:T(8,128)(2,1)S(1)} %bitcast.13, bf16[128,1280]{1,0:T(8,128)(2,1)S(1)} %collective-permute-done.rows.other_rows, ...), custom_call_target="tpu_custom_call" | custom-call | flops 838860800 | bytes 6553600 | tf_op jit(solution)/shard_map/weight_grads/pallas_call | solution.py:330
  67.6 3.0 %all-to-all-done.2.pieces = f32[32,1,640]{2,1,0:T(1,128)S(1)} async-done(((f32[32,1,640]{2,1,0:T(1,128)}), f32[32,1,640]{2,1,0:T(1,128)S(1)}, u32[]{:S(2)}, u32[]{:S(2)}) %all-to-all-start.2) | async-done | bytes 81952 | tf_op jit(solution)/shard_map/all_to_all | solution.py:472
  70.7 0.7 share_of_sum.1
  71.4 2.8 %all-to-all-start.3 = ((f32[32,1,640]{2,1,0:T(1,128)}), f32[32,1,640]{2,1,0:T(1,128)S(1)}, u32[]{:S(2)}, u32[]{:S(2)}) async-start(f32[32,1,640]{2,1,0:T(1,128)} %get-tuple-element.39), calls=%async_computation.3 | async-start | bytes 163840 | tf_op jit(solution)/shard_map/all_to_all | solution.py:472
  74.2 2.8 %tokens_grads.1 = bf16[4,256,1280]{2,1,0:T(8,128)(2,1)} custom-call(f32[8,128]{1,0:T(8,128)S(1)} %get-tuple-element.36.after, bf16[4,32,256]{2,1,0:T(8,128)(2,1)S(1)} %get-tuple-element.37.left, bf16[4,32,1280]{2,1,0:T(8,128)(2,1)S(1)} %get-tuple-element.38.right), custom_call_target="tpu_custom_call" | custom-call | flops 83886080 | bytes 2621440 | tf_op jit(solution)/shard_map/tokens_grads/pallas_call | solution.py:436
  76.9 4.8 %all-to-all-done.3 = f32[32,1,640]{2,1,0:T(1,128)S(1)} async-done(((f32[32,1,640]{2,1,0:T(1,128)}), f32[32,1,640]{2,1,0:T(1,128)S(1)}, u32[]{:S(2)}, u32[]{:S(2)}) %all-to-all-start.3) | async-done | bytes 81952 | tf_op jit(solution)/shard_map/all_to_all | solution.py:472
  81.8 0.2 reduce
  82.0 0.7 reshape.19
Async XLA Ops:
  25.0 1.5 %copy-start = (bf16[16,8,1280]{2,1,0:T(8,128)(2,1)}, bf16[16,8,1280]{2,1,0:T(8,128)(2,1)S(1)}, u32[]{:S(2)}) copy-start(bf16[16,8,1280]{2,1,0:T(8,128)(2,1)S(1)} %all_to_all.32) | copy-start | bytes 983044
  25.0 18.1 %collective-permute-start = (bf16[128,1280]{1,0:T(8,128)(2,1)S(1)}, bf16[128,1280]{1,0:T(8,128)(2,1)S(1)}, u32[]{:S(2)}, u32[]{:S(2)}) collective-permute-start(bf16[128,1280]{1,0:T(8,128)(2,1)S(1)} %bitcast.11), channel_id=1, source_target_pairs={{0,16},{16,0},{1,17},{17,1},{2,18},{18,2},{3,19},{19,3},{4,20},{20... | collective-permute-start | bytes 983048 | tf_op jit(solution)/shard_map/ppermute | solution.py:484
  39.5 14.6 %all-to-all-start.1 = ((bf16[16,8,1280]{2,1,0:T(8,128)(2,1)}), bf16[16,8,1280]{2,1,0:T(8,128)(2,1)S(1)}, u32[]{:S(2)}, u32[]{:S(2)}) async-start(bf16[16,8,1280]{2,1,0:T(8,128)(2,1)} %bitcast.21), calls=%async_computation.1 | async-start | bytes 655360 | tf_op jit(solution)/shard_map/all_to_all | solution.py:472
  43.1 0.7 copy-start.7
  43.8 10.4 %copy-start.2 = (bf16[1280,16]{0,1:T(8,128)(2,1)S(1)}, bf16[1280,16]{0,1:T(8,128)(2,1)}, u32[]{:S(2)}) copy-start(bf16[1280,16]{0,1:T(8,128)(2,1)} %param.6) | copy-start | bytes 122884
  43.8 10.4 %copy-start.3 = (f32[4,16,256]{2,1,0:T(8,128)S(1)}, f32[4,16,256]{2,1,0:T(8,128)}, u32[]{:S(2)}) copy-start(f32[4,16,256]{2,1,0:T(8,128)} %get-tuple-element.27.dispatch) | copy-start | bytes 196612
  43.8 10.4 %copy-start.4 = (f32[4,16,256]{2,1,0:T(8,128)S(1)}, f32[4,16,256]{2,1,0:T(8,128)}, u32[]{:S(2)}) copy-start(f32[4,16,256]{2,1,0:T(8,128)} %get-tuple-element.28.combine) | copy-start | bytes 196612
  49.9 13.1 %copy-start.1 = (bf16[16,8,1280]{2,1,0:T(8,128)(2,1)S(1)}, bf16[16,8,1280]{2,1,0:T(8,128)(2,1)}, u32[]{:S(2)}) copy-start(bf16[16,8,1280]{2,1,0:T(8,128)(2,1)} %copy-done) | copy-start | bytes 983044
  49.9 13.1 %copy-start.5 = (bf16[64,2560]{1,0:T(8,128)(2,1)S(1)}, bf16[64,2560]{1,0:T(8,128)(2,1)}, u32[]{:S(2)}) copy-start(bf16[64,2560]{1,0:T(8,128)(2,1)} %get-tuple-element.30.acts) | copy-start | bytes 983044
  50.0 13.1 %copy-start.6 = (bf16[64,2560]{1,0:T(8,128)(2,1)S(1)}, bf16[64,2560]{1,0:T(8,128)(2,1)}, u32[]{:S(2)}) copy-start(bf16[64,2560]{1,0:T(8,128)(2,1)} %get-tuple-element.32.hidden) | copy-start | bytes 983044
  60.5 10.2 %all-to-all-start.2 = ((f32[32,1,640]{2,1,0:T(1,128)}), f32[32,1,640]{2,1,0:T(1,128)S(1)}, u32[]{:S(2)}, u32[]{:S(2)}) async-start(f32[32,1,640]{2,1,0:T(1,128)} %get-tuple-element.35), calls=%async_computation.2 | async-start | bytes 163840 | tf_op jit(solution)/shard_map/all_to_all | solution.py:472
  71.4 10.4 %all-to-all-start.3 = ((f32[32,1,640]{2,1,0:T(1,128)}), f32[32,1,640]{2,1,0:T(1,128)S(1)}, u32[]{:S(2)}, u32[]{:S(2)}) async-start(f32[32,1,640]{2,1,0:T(1,128)} %get-tuple-element.39), calls=%async_computation.3 | async-start | bytes 163840 | tf_op jit(solution)/shard_map/all_to_all | solution.py:472

commit v6 on v5

--- a/solution.py
+++ b/solution.py
@@ -13,7 +13,6 @@
 WIDE = jnp.float32
 LANES = 128
 KINDS = 2
-ALONE = 60 * 1024 * 1024
 SHARED = 52 * 1024 * 1024
 WHOLE = pl.BlockSpec(memory_space=pltpu.VMEM)
 PLACE = pl.BlockSpec(memory_space=pl.ANY)
@@ -92,24 +91,15 @@
     return copies
 
 
-def start_copy(source, target, sem):
-    copy = pltpu.make_async_copy(source, target, sem)
-    copy.start()
-    return copy
-
-
 def gather_kernel(
-    tokens, params_far, grads, sent_far, dispatch_far, combine_far,
-    tokens_v, grads_v, params, sent, dispatch, combine, rows, sems, grad_sems, more_sems,
+    tokens, params, grads, sent, dispatch, combine, tokens_v, grads_v, rows, sems, grad_sems
 ):
     images = tokens.shape[0]
     slots = params.shape[0]
     stride = KINDS * images
-    params_copy = start_copy(params_far, params, more_sems.at[0])
     copies = start_copies(tokens, tokens_v, sems)
     grad_copies = start_copies(grads, grads_v, grad_sems)
     logits = []
-    params_copy.wait()
     for image in range(images):
         copies[image].wait()
         logits.append(dot(params[...], tokens_v[image], 1, 1))
@@ -122,18 +112,11 @@
         )
         over_slots.append(softmax(logits[image], 0))
         combine[image] = over_slots[image]
-    results = [
-        start_copy(dispatch, dispatch_far, more_sems.at[1]),
-        start_copy(combine, combine_far, more_sems.at[2]),
-    ]
     for image in range(images):
         grad_copies[image].wait()
         value = dot(over_slots[image].astype(LOW), grads_v[image], 1, 0)
         put(rows, KINDS * image + 1, slots, stride, value)
     sent[...] = packed(rows)
-    results.append(start_copy(sent, sent_far, more_sems.at[3]))
-    for copy in results:
-        copy.wait()
 
 
 def gather(tokens, params, grads):
@@ -144,24 +127,19 @@
     return call(
         gather_kernel,
         "gather_slots",
-        ALONE,
+        SHARED,
         6 * images * slots * length * width,
         4 * images * length * width,
         2 * images * slots * length,
         out_shape=(shaped(rows, LOW), weights, weights),
-        in_specs=[PLACE] * 3,
-        out_specs=(PLACE,) * 3,
+        in_specs=[PLACE, WHOLE, PLACE],
+        out_specs=(WHOLE, WHOLE, WHOLE),
         scratch_shapes=[
             pltpu.VMEM(tokens.shape, LOW),
             pltpu.VMEM(grads.shape, LOW),
-            pltpu.VMEM(params.shape, LOW),
-            pltpu.VMEM(rows, LOW),
-            pltpu.VMEM(weights.shape, WIDE),
-            pltpu.VMEM(weights.shape, WIDE),
             scratch_rows(rows),
             pltpu.SemaphoreType.DMA((images,)),
             pltpu.SemaphoreType.DMA((images,)),
-            pltpu.SemaphoreType.DMA((4,)),
         ],
     )(tokens, params, grads)
 
@@ -190,16 +168,11 @@
     ]
 
 
-def expert_kernel(
-    rows_far, w_in, w_out, back_far, acts_far, hidden_far, mark,
-    w_in_v, w_out_v, sems, wide, rows, back, acts, hidden, more_sems,
-):
+def expert_kernel(rows, w_in, w_out, back, acts, hidden, mark, w_in_v, w_out_v, sems, wide):
     del mark
-    rows_copy = start_copy(rows_far, rows, more_sems.at[0])
     copies = start_weights(w_in, w_out, w_in_v, w_out_v, sems)
     count = rows.shape[0] // KINDS
     chunks, tile = w_out_v.shape[:2]
-    rows_copy.wait()
     load_rows(wide, rows[...])
     rows_in = take(wide, 0, count, KINDS).astype(LOW)
     rows_grad = take(wide, 1, count, KINDS).astype(LOW)
@@ -219,16 +192,9 @@
         d_in_part = dot(d_hidden, w_in_v[chunk], 1, 1)
         out = out_part if chunk == 0 else out + out_part
         d_in = d_in_part if chunk == 0 else d_in + d_in_part
-    results = [
-        start_copy(acts, acts_far, more_sems.at[1]),
-        start_copy(hidden, hidden_far, more_sems.at[2]),
-    ]
     put(wide, 0, count, KINDS, out)
     put(wide, 1, count, KINDS, d_in)
     back[...] = packed(wide)
-    results.append(start_copy(back, back_far, more_sems.at[3]))
-    for copy in results:
-        copy.wait()
 
 
 def expert(rows, w_in, w_out, tile):
@@ -239,22 +205,14 @@
     return call(
         expert_kernel,
         "expert_rows",
-        ALONE,
+        SHARED,
         8 * count * hidden * width,
         4 * hidden * width,
         count * hidden,
         out_shape=(shaped(rows.shape, LOW), kept, kept, MARK),
-        in_specs=[PLACE] * 3,
-        out_specs=(PLACE,) * 4,
-        scratch_shapes=[
-            *weight_scratch(width, hidden, tile),
-            scratch_rows(rows.shape),
-            pltpu.VMEM(rows.shape, LOW),
-            pltpu.VMEM(rows.shape, LOW),
-            pltpu.VMEM(kept.shape, LOW),
-            pltpu.VMEM(kept.shape, LOW),
-            pltpu.SemaphoreType.DMA((4,)),
-        ],
+        in_specs=[WHOLE, PLACE, PLACE],
+        out_specs=(WHOLE, WHOLE, WHOLE, PLACE),
+        scratch_shapes=[*weight_scratch(width, hidden, tile), scratch_rows(rows.shape)],
     )(rows, w_in, w_out)
 
 

time: 83.1 us -> 78.7 us (0.947)
  Pallas kernels: 39.3 us -> 34.4 us
    pallas_call x2, Pallas kernels: 18.9 us -> 14 us  [the longest x1 9.79 us: expert(): call(expert_kernel, 'expert_rows', SHARED, 8 * count * hidden * width, 4...]
  transfers between devices with their start and end apart: 4 -> 4, of which waited for: 3 -> 3; matrix products, arithmetic and copies ran while one was open for 0% -> 0% of each run, Pallas kernels for 32% -> 30%
where the time goes in v6:
time: 78.7 us; the launch traced here: 78.3 us
  Pallas kernels  34.4 us (44%)
  blocking collectives  18.3 us (23%)
  waiting for transfers between devices  12.8 us (16%)
  starting transfers between devices  10.4 us (13%)
  local copies, waits for them, and re-layouts  1.44 us (2%)
    all_to_all x1, blocking collectives, exchange(): return lax.all_to_all(rows, axes, split_axis=0, concat_axis=0, tiled=True)  18.3 us
    all_to_all x3, waiting for transfers between devices, exchange(): return lax.all_to_all(rows, axes, split_axis=0, concat_axis=0, tiled=True)  12.8 us
    pallas_call x1, Pallas kernels, expert(): call(expert_kernel, 'expert_rows', SHARED, 8 * count * hidden * width, 4...  9.79 us
    all_to_all x3, starting transfers between devices, exchange(): return lax.all_to_all(rows, axes, split_axis=0, concat_axis=0, tiled=True)  8.93 us
    pallas_call x1, Pallas kernels, logits_grads(): call(logits_kernel, 'logits_grads', SHARED, 6 * images * slots * length *...  6.3 us
    pallas_call x1, Pallas kernels, others_hidden(): call(others_kernel, 'others_hidden', SHARED, 64 * count * hidden * width,...  6.13 us
    pallas_call x1, Pallas kernels, weight_grads(): call(weights_kernel, 'weight_grads', SHARED, 8 * count * size * width //...  4.55 us
    pallas_call x1, Pallas kernels, gather(): call(gather_kernel, 'gather_slots', SHARED, 6 * images * slots * length *...  4.2 us
  transfers between devices with their start and end apart: 4, of which 3 were waited for; matrix products, arithmetic and copies ran while one was open for 0% of the time, Pallas kernels for 30%

profile of v6, /device:TPU:0, one launch (start us, length us, event | category | flops | bytes accessed | tf_op | source)
XLA Modules:
  0.0 78.3 jit_solution(17010864151516224672)
XLA Ops:
  0.6 0.0 copy-start
  0.6 0.8 copy-done
  1.4 4.2 %gather_slots.1 = (bf16[128,1280]{1,0:T(8,128)(2,1)S(1)}, f32[4,16,256]{2,1,0:T(8,128)S(1)}, f32[4,16,256]{2,1,0:T(8,128)S(1)}) custom-call(bf16[4,256,1280]{2,1,0:T(8,128)(2,1)} %tokens.3, bf16[16,1280]{1,0:T(8,128)(2,1)S(1)} %bitcast.16, bf16[4,256,1280]{2,1,0:T(8,128)(2,1)} %grads.3), custom_call_target="tpu_custom_call" | custom-call | flops 125829120 | bytes 5242880 | tf_op jit(solution)/shard_map/gather_slots/pallas_call | solution.py:127
  5.6 18.3 %all_to_all.32 = bf16[16,8,1280]{2,1,0:T(8,128)(2,1)S(1)} all-to-all(bf16[16,8,1280]{2,1,0:T(8,128)(2,1)S(1)} %bitcast.15), channel_id=1, replica_groups=mesh['rep'=2,'exp'=16] {'exp'}, dimensions={0} | all-to-all | bytes 655360 | tf_op jit(solution)/shard_map/all_to_all | solution.py:430
  23.9 1.5 %collective-permute-start = (bf16[128,1280]{1,0:T(8,128)(2,1)S(1)}, bf16[128,1280]{1,0:T(8,128)(2,1)S(1)}, u32[]{:S(2)}, u32[]{:S(2)}) collective-permute-start(bf16[128,1280]{1,0:T(8,128)(2,1)S(1)} %bitcast.11), channel_id=1, source_target_pairs={{0,16},{16,0},{1,17},{17,1},{2,18},{18,2},{3,19},{19,3},{4,20},{20... | collective-permute-start | bytes 983048 | tf_op jit(solution)/shard_map/ppermute | solution.py:442
  25.4 9.8 %expert_rows.1 = (bf16[128,1280]{1,0:T(8,128)(2,1)}, bf16[64,2560]{1,0:T(8,128)(2,1)S(1)}, bf16[64,2560]{1,0:T(8,128)(2,1)S(1)}, f32[8,128]{1,0:T(8,128)S(1)}) custom-call(bf16[128,1280]{1,0:T(8,128)(2,1)S(1)} %bitcast.12, bf16[1280,2560]{1,0:T(8,128)(2,1)} %bitcast.18, bf16[2560,1280]{1,0:T(8,128)(2,1)} %bitcast.20), custom_call_target="tpu_custom_call" | custom-call | flops 1677721600 | bytes 13107200 | tf_op jit(solution)/shard_map/expert_rows/pallas_call | solution.py:205
  35.2 3.6 %all-to-all-start.1 = ((bf16[16,8,1280]{2,1,0:T(8,128)(2,1)}), bf16[16,8,1280]{2,1,0:T(8,128)(2,1)S(1)}, u32[]{:S(2)}, u32[]{:S(2)}) async-start(bf16[16,8,1280]{2,1,0:T(8,128)(2,1)} %bitcast.6), calls=%async_computation.1 | async-start | bytes 655360 | tf_op jit(solution)/shard_map/all_to_all | solution.py:430
  38.8 0.0 collective-permute-done.rows.other_rows
  38.8 0.0 copy-start.1
  38.8 6.1 %others_hidden.1 = (bf16[64,2560]{1,0:T(8,128)(2,1)S(1)}, bf16[64,2560]{1,0:T(8,128)(2,1)S(1)}, f32[8,128]{1,0:T(8,128)S(1)}) custom-call(f32[8,128]{1,0:T(8,128)S(1)} %get-tuple-element.24.after, bf16[128,1280]{1,0:T(8,128)(2,1)S(1)} %collective-permute-done.rows.other_rows, bf16[1280,2560]{1,0:T(8,128)(2,1)} %bitcast.19, bf16[2560,1280]{1,0:T(8,128)(2,1)} %bitcast.21), custom_call_target="tpu_custom_call" | custom-call | flops 13421772800 | bytes 104857600 | tf_op jit(solution)/shard_map/others_hidden/pallas_call | solution.py:242
  44.9 4.9 %all-to-all-done.1 = bf16[16,8,1280]{2,1,0:T(8,128)(2,1)S(1)} async-done(((bf16[16,8,1280]{2,1,0:T(8,128)(2,1)}), bf16[16,8,1280]{2,1,0:T(8,128)(2,1)S(1)}, u32[]{:S(2)}, u32[]{:S(2)}) %all-to-all-start.1) | async-done | bytes 327712 | tf_op jit(solution)/shard_map/all_to_all | solution.py:430
  49.8 0.0 copy-done.1
  49.8 6.3 %logits_grads.1 = (bf16[4,32,256]{2,1,0:T(8,128)(2,1)S(1)}, bf16[4,32,1280]{2,1,0:T(8,128)(2,1)S(1)}, f32[32,1,640]{2,1,0:T(1,128)}, f32[8,128]{1,0:T(8,128)S(1)}) custom-call(f32[8,128]{1,0:T(8,128)S(1)} %get-tuple-element.25.after, bf16[128,1280]{1,0:T(8,128)(2,1)S(1)} %bitcast.14, bf16[4,256,1280]{2,1,0:T(8,128)(2,1)} %tokens.3, ...), custom_call_target="tpu_custom_call" | custom-call | flops 125829120 | bytes 5242880 | tf_op jit(solution)/shard_map/logits_grads/pallas_call | solution.py:362
  56.1 2.6 %all-to-all-start.2 = ((f32[32,1,640]{2,1,0:T(1,128)}), f32[32,1,640]{2,1,0:T(1,128)S(1)}, u32[]{:S(2)}, u32[]{:S(2)}) async-start(f32[32,1,640]{2,1,0:T(1,128)} %get-tuple-element.35), calls=%async_computation.2 | async-start | bytes 163840 | tf_op jit(solution)/shard_map/all_to_all | solution.py:430
  58.7 4.6 %weight_grads.1 = (bf16[640,2560]{1,0:T(8,128)(2,1)}, bf16[1280,1280]{1,0:T(8,128)(2,1)}, f32[8,128]{1,0:T(8,128)S(1)}) custom-call(s32[1]{0:T(128)} %bitcast.mine, f32[8,128]{1,0:T(8,128)S(1)} %get-tuple-element.29.after, bf16[128,1280]{1,0:T(8,128)(2,1)S(1)} %bitcast.13, bf16[128,1280]{1,0:T(8,128)(2,1)S(1)} %collective-permute-done.rows.other_rows, ...), custom_call_target="tpu_custom_call" | custom-call | flops 838860800 | bytes 6553600 | tf_op jit(solution)/shard_map/weight_grads/pallas_call | solution.py:288
  63.3 3.0 %all-to-all-done.2.pieces = f32[32,1,640]{2,1,0:T(1,128)S(1)} async-done(((f32[32,1,640]{2,1,0:T(1,128)}), f32[32,1,640]{2,1,0:T(1,128)S(1)}, u32[]{:S(2)}, u32[]{:S(2)}) %all-to-all-start.2) | async-done | bytes 81952 | tf_op jit(solution)/shard_map/all_to_all | solution.py:430
  66.3 0.7 share_of_sum.1
  67.0 2.8 %all-to-all-start.3 = ((f32[32,1,640]{2,1,0:T(1,128)}), f32[32,1,640]{2,1,0:T(1,128)S(1)}, u32[]{:S(2)}, u32[]{:S(2)}) async-start(f32[32,1,640]{2,1,0:T(1,128)} %get-tuple-element.39), calls=%async_computation.3 | async-start | bytes 163840 | tf_op jit(solution)/shard_map/all_to_all | solution.py:430
  69.8 2.8 %tokens_grads.1 = bf16[4,256,1280]{2,1,0:T(8,128)(2,1)} custom-call(f32[8,128]{1,0:T(8,128)S(1)} %get-tuple-element.36.after, bf16[4,32,256]{2,1,0:T(8,128)(2,1)S(1)} %get-tuple-element.37.left, bf16[4,32,1280]{2,1,0:T(8,128)(2,1)S(1)} %get-tuple-element.38.right), custom_call_target="tpu_custom_call" | custom-call | flops 83886080 | bytes 2621440 | tf_op jit(solution)/shard_map/tokens_grads/pallas_call | solution.py:394
  72.6 4.8 %all-to-all-done.3 = f32[32,1,640]{2,1,0:T(1,128)S(1)} async-done(((f32[32,1,640]{2,1,0:T(1,128)}), f32[32,1,640]{2,1,0:T(1,128)S(1)}, u32[]{:S(2)}, u32[]{:S(2)}) %all-to-all-start.3) | async-done | bytes 81952 | tf_op jit(solution)/shard_map/all_to_all | solution.py:430
  77.4 0.2 reduce
  77.6 0.7 reshape.19
Async XLA Ops:
  0.6 0.8 copy-start
  23.9 14.9 %collective-permute-start = (bf16[128,1280]{1,0:T(8,128)(2,1)S(1)}, bf16[128,1280]{1,0:T(8,128)(2,1)S(1)}, u32[]{:S(2)}, u32[]{:S(2)}) collective-permute-start(bf16[128,1280]{1,0:T(8,128)(2,1)S(1)} %bitcast.11), channel_id=1, source_target_pairs={{0,16},{16,0},{1,17},{17,1},{2,18},{18,2},{3,19},{19,3},{4,20},{20... | collective-permute-start | bytes 983048 | tf_op jit(solution)/shard_map/ppermute | solution.py:442
  35.2 14.6 %all-to-all-start.1 = ((bf16[16,8,1280]{2,1,0:T(8,128)(2,1)}), bf16[16,8,1280]{2,1,0:T(8,128)(2,1)S(1)}, u32[]{:S(2)}, u32[]{:S(2)}) async-start(bf16[16,8,1280]{2,1,0:T(8,128)(2,1)} %bitcast.6), calls=%async_computation.1 | async-start | bytes 655360 | tf_op jit(solution)/shard_map/all_to_all | solution.py:430
  38.8 11.1 %copy-start.1 = (bf16[1280,16]{0,1:T(8,128)(2,1)S(1)}, bf16[1280,16]{0,1:T(8,128)(2,1)}, u32[]{:S(2)}) copy-start(bf16[1280,16]{0,1:T(8,128)(2,1)} %param.6) | copy-start | bytes 122884
  56.1 10.2 %all-to-all-start.2 = ((f32[32,1,640]{2,1,0:T(1,128)}), f32[32,1,640]{2,1,0:T(1,128)S(1)}, u32[]{:S(2)}, u32[]{:S(2)}) async-start(f32[32,1,640]{2,1,0:T(1,128)} %get-tuple-element.35), calls=%async_computation.2 | async-start | bytes 163840 | tf_op jit(solution)/shard_map/all_to_all | solution.py:430
  67.0 10.4 %all-to-all-start.3 = ((f32[32,1,640]{2,1,0:T(1,128)}), f32[32,1,640]{2,1,0:T(1,128)S(1)}, u32[]{:S(2)}, u32[]{:S(2)}) async-start(f32[32,1,640]{2,1,0:T(1,128)} %get-tuple-element.39), calls=%async_computation.3 | async-start | bytes 163840 | tf_op jit(solution)/shard_map/all_to_all | solution.py:430

commit v7 on v6

--- a/solution.py
+++ b/solution.py
@@ -12,6 +12,7 @@
 LOW = jnp.bfloat16
 WIDE = jnp.float32
 LANES = 128
+TILE = 8
 KINDS = 2
 SHARED = 52 * 1024 * 1024
 WHOLE = pl.BlockSpec(memory_space=pltpu.VMEM)
@@ -82,27 +83,22 @@
         ]
 
 
-def start_copies(source, target, sems):
-    copies = []
-    for index in range(source.shape[0]):
-        copy = pltpu.make_async_copy(source.at[index], target.at[index], sems.at[index])
-        copy.start()
-        copies.append(copy)
-    return copies
+def start_copy(source, target, sem):
+    copy = pltpu.make_async_copy(source, target, sem)
+    copy.start()
+    return copy
 
 
 def gather_kernel(
-    tokens, params, grads, sent, dispatch, combine, tokens_v, grads_v, rows, sems, grad_sems
+    tokens, params, grads, sent, dispatch, combine, tokens_v, grads_v, rows, sems
 ):
     images = tokens.shape[0]
     slots = params.shape[0]
     stride = KINDS * images
-    copies = start_copies(tokens, tokens_v, sems)
-    grad_copies = start_copies(grads, grads_v, grad_sems)
-    logits = []
-    for image in range(images):
-        copies[image].wait()
-        logits.append(dot(params[...], tokens_v[image], 1, 1))
+    tokens_copy = start_copy(tokens, tokens_v, sems.at[0])
+    grads_copy = start_copy(grads, grads_v, sems.at[1])
+    tokens_copy.wait()
+    logits = [dot(params[...], tokens_v[image], 1, 1) for image in range(images)]
     over_slots = []
     for image in range(images):
         over_tokens = softmax(logits[image], 1)
@@ -112,8 +108,8 @@
         )
         over_slots.append(softmax(logits[image], 0))
         combine[image] = over_slots[image]
+    grads_copy.wait()
     for image in range(images):
-        grad_copies[image].wait()
         value = dot(over_slots[image].astype(LOW), grads_v[image], 1, 0)
         put(rows, KINDS * image + 1, slots, stride, value)
     sent[...] = packed(rows)
@@ -138,8 +134,7 @@
             pltpu.VMEM(tokens.shape, LOW),
             pltpu.VMEM(grads.shape, LOW),
             scratch_rows(rows),
-            pltpu.SemaphoreType.DMA((images,)),
-            pltpu.SemaphoreType.DMA((images,)),
+            pltpu.SemaphoreType.DMA((2,)),
         ],
     )(tokens, params, grads)
 
@@ -177,21 +172,23 @@
     rows_in = take(wide, 0, count, KINDS).astype(LOW)
     rows_grad = take(wide, 1, count, KINDS).astype(LOW)
     out = d_in = None
-    for chunk in range(chunks):
-        units = slice(chunk * tile, (chunk + 1) * tile)
-        copies[chunk][0].wait()
-        preact = dot(rows_in, w_in_v[chunk], 1, 0)
-        copies[chunk][1].wait()
-        d_acts = dot(rows_grad, w_out_v[chunk], 1, 1)
-        values, slope = gelu_parts(preact)
-        values = values.astype(LOW)
-        d_hidden = (d_acts * slope).astype(LOW)
-        acts[:, units] = values
-        hidden[:, units] = d_hidden
-        out_part = dot(values, w_out_v[chunk], 1, 0)
-        d_in_part = dot(d_hidden, w_in_v[chunk], 1, 1)
-        out = out_part if chunk == 0 else out + out_part
-        d_in = d_in_part if chunk == 0 else d_in + d_in_part
+    held = None
+    for chunk in range(chunks + 1):
+        if chunk < chunks:
+            for copy in copies[chunk]:
+                copy.wait()
+            preact = dot(rows_in, w_in_v[chunk], 1, 0)
+            d_acts = dot(rows_grad, w_out_v[chunk], 1, 1)
+        if chunk > 0:
+            out_part = dot(held[0], w_out_v[chunk - 1], 1, 0)
+            d_in_part = dot(held[1], w_in_v[chunk - 1], 1, 1)
+            out = out_part if chunk == 1 else out + out_part
+            d_in = d_in_part if chunk == 1 else d_in + d_in_part
+        if chunk < chunks:
+            units = slice(chunk * tile, (chunk + 1) * tile)
+            values, slope = gelu_parts(preact)
+            held = (values.astype(LOW), (d_acts * slope).astype(LOW))
+            acts[:, units], hidden[:, units] = held
     put(wide, 0, count, KINDS, out)
     put(wide, 1, count, KINDS, d_in)
     back[...] = packed(wide)
@@ -316,44 +313,51 @@
 
 def logits_kernel(
     after, back, tokens, params, grads, dispatch, combine, left, right, local, mark,
-    tokens_v, grads_v, wide, sems, grad_sems,
+    tokens_v, grads_v, wide, sems,
 ):
     del after, mark
     images, slots, _ = dispatch.shape
-    grad_copies = start_copies(grads, grads_v, grad_sems)
-    copies = start_copies(tokens, tokens_v, sems)
+    grads_copy = start_copy(grads, grads_v, sems.at[0])
+    tokens_copy = start_copy(tokens, tokens_v, sems.at[1])
     load_rows(wide, back[...])
     stride = KINDS * images
+    d_slot_in = []
+    for image in range(images):
+        d_slot_in.append(take(wide, KINDS * image + 1, slots, stride).astype(LOW))
+        right[image, :slots, :] = d_slot_in[image]
+        right[image, slots:, :] = params[...]
+        left[image, :slots, :] = dispatch[image].astype(LOW)
+    local[...] = jnp.zeros_like(local)
+    grads_copy.wait()
     parts = []
     for image in range(images):
         slot_out = take(wide, KINDS * image, slots, stride).astype(LOW)
         weights = combine[image]
-        grad_copies[image].wait()
         d_combine = dot(slot_out, grads_v[image], 1, 1)
         parts.append(
             weights * (d_combine - jnp.sum(weights * d_combine, axis=0, keepdims=True))
         )
-    total = jnp.zeros(params.shape, WIDE)
+    tokens_copy.wait()
+    total = None
     for image in range(images):
-        d_slot_in = take(wide, KINDS * image + 1, slots, stride).astype(LOW)
-        right[image, :slots, :] = d_slot_in
-        right[image, slots:, :] = params[...]
         weights = dispatch[image]
-        copies[image].wait()
-        d_dispatch = dot(d_slot_in, tokens_v[image], 1, 1)
+        d_dispatch = dot(d_slot_in[image], tokens_v[image], 1, 1)
         d_logits = parts[image] + weights * (
             d_dispatch - jnp.sum(weights * d_dispatch, axis=1, keepdims=True)
         )
         low = d_logits.astype(LOW)
-        left[image, :slots, :] = weights.astype(LOW)
         left[image, slots:, :] = low
-        total += dot(low, tokens_v[image], 1, 0)
-    pieces, _, size = local.shape
-    for slot in range(slots):
-        for piece in range(pieces // slots):
-            local[slot * (pieces // slots) + piece] = total[
-                slot : slot + 1, piece * size : (piece + 1) * size
-            ]
+        part = dot(low, tokens_v[image], 1, 0)
+        total = part if image == 0 else total + part
+    for tile, (start, step) in enumerate(piece_rows(local, *params.shape)):
+        local[pl.ds(start, slots, stride=step), :] = total[:, tile * LANES : (tile + 1) * LANES]
+
+
+def piece_rows(pieces, slots, width):
+    per_slot = pieces.shape[0] // TILE // slots
+    used = width // LANES // per_slot
+    step = per_slot * TILE
+    return [(tile // used * TILE + tile % used, step) for tile in range(width // LANES)]
 
 
 def logits_grads(after, back, tokens, params, grads, dispatch, combine, pieces):
@@ -368,7 +372,7 @@
         out_shape=(
             shaped((images, 2 * slots, length), LOW),
             shaped((images, 2 * slots, width), LOW),
-            shaped((pieces, 1, slots * width // pieces), WIDE),
+            shaped((pieces * TILE, LANES), WIDE),
             MARK,
         ),
         in_specs=[PLACE, WHOLE, PLACE, WHOLE, PLACE, WHOLE, WHOLE],
@@ -377,8 +381,7 @@
             pltpu.VMEM(tokens.shape, LOW),
             pltpu.VMEM(grads.shape, LOW),
             scratch_rows(back.shape),
-            pltpu.SemaphoreType.DMA((images,)),
-            pltpu.SemaphoreType.DMA((images,)),
+            pltpu.SemaphoreType.DMA((2,)),
         ],
     )(after, back, tokens, params, grads, dispatch, combine)
 
@@ -410,7 +413,12 @@
 
 def share_kernel(after, pieces, out, mark):
     del after, mark
-    out[...] = jnp.broadcast_to(jnp.sum(pieces[...], axis=0, keepdims=True), out.shape)
+    rows = pieces.shape[0]
+    total = pieces[:TILE, :]
+    for row in range(TILE, rows, TILE):
+        total = total + pieces[row : row + TILE, :]
+    for row in range(0, rows, TILE):
+        out[row : row + TILE, :] = total
 
 
 def share_of_sum(after, pieces):
@@ -424,6 +432,25 @@
         in_specs=[PLACE, WHOLE],
         out_specs=(WHOLE, PLACE),
     )(after, pieces)
+
+
+def unpack_kernel(pieces, out):
+    slots, width = out.shape
+    for tile, (start, step) in enumerate(piece_rows(pieces, slots, width)):
+        out[:, tile * LANES : (tile + 1) * LANES] = pieces[pl.ds(start, slots, stride=step), :]
+
+
+def unpack(pieces, shape):
+    return call(
+        unpack_kernel,
+        "unpack_sum",
+        SHARED,
+        0,
+        8 * pieces.size,
+        out_shape=shaped(shape, WIDE),
+        in_specs=[WHOLE],
+        out_specs=WHOLE,
+    )(pieces)
 
 
 def exchange(rows, axes):
@@ -458,11 +485,11 @@
         replicas,
     )
     share, after_share = share_of_sum(after_weights, exchange(local, everyone))
-    grad_params = exchange(share, everyone)
+    grad_params = unpack(exchange(share, everyone), params.shape).T
     grad_tokens = tokens_grads(after_share, left, right)
     return (
         grad_tokens,
-        grad_params.reshape(params.shape).T,
+        grad_params,
         grad_expert_in[None],
         grad_expert_out[None],
     )

time: 78.7 us -> 77.5 us (0.985)
  Pallas kernels: 34.4 us -> 33.1 us
  waiting for transfers between devices: 12.8 us -> 14 us
    all_to_all x3, waiting for transfers between devices: 12.8 us -> 14 us  [exchange(): return lax.all_to_all(rows, axes, split_axis=0, concat_axis=0, tiled=True)]
    pallas_call x1, Pallas kernels: 6.3 us -> 5.25 us  [logits_grads(): call(logits_kernel, 'logits_grads', SHARED, 6 * images * slots * length *...]
where the time goes in v7:
time: 77.5 us; the launch traced here: 77.1 us
  Pallas kernels  33.1 us (43%)
  blocking collectives  18.3 us (24%)
  waiting for transfers between devices  14 us (18%)
  starting transfers between devices  10.2 us (13%)
  local copies, waits for them, and re-layouts  0.78 us (1%)
    all_to_all x1, blocking collectives, exchange(): return lax.all_to_all(rows, axes, split_axis=0, concat_axis=0, tiled=True)  18.3 us
    all_to_all x3, waiting for transfers between devices, exchange(): return lax.all_to_all(rows, axes, split_axis=0, concat_axis=0, tiled=True)  14 us
    pallas_call x1, Pallas kernels, expert(): call(expert_kernel, 'expert_rows', SHARED, 8 * count * hidden * width, 4...  9.54 us
    all_to_all x3, starting transfers between devices, exchange(): return lax.all_to_all(rows, axes, split_axis=0, concat_axis=0, tiled=True)  8.71 us
    pallas_call x1, Pallas kernels, others_hidden(): call(others_kernel, 'others_hidden', SHARED, 64 * count * hidden * width,...  6.13 us
    pallas_call x1, Pallas kernels, logits_grads(): call(logits_kernel, 'logits_grads', SHARED, 6 * images * slots * length *...  5.25 us
    pallas_call x1, Pallas kernels, weight_grads(): call(weights_kernel, 'weight_grads', SHARED, 8 * count * size * width //...  4.55 us
    pallas_call x1, Pallas kernels, gather(): call(gather_kernel, 'gather_slots', SHARED, 6 * images * slots * length *...  3.48 us
  transfers between devices with their start and end apart: 4, of which 3 were waited for; matrix products, arithmetic and copies ran while one was open for 0% of the time, Pallas kernels for 30%

profile of v7, /device:TPU:0, one launch (start us, length us, event | category | flops | bytes accessed | tf_op | source)
XLA Modules:
  0.0 77.1 jit_solution(5748737576547947562)
XLA Ops:
  0.6 0.0 copy-start
  0.6 0.8 copy-done
  1.4 3.5 %gather_slots.1 = (bf16[128,1280]{1,0:T(8,128)(2,1)S(1)}, f32[4,16,256]{2,1,0:T(8,128)S(1)}, f32[4,16,256]{2,1,0:T(8,128)S(1)}) custom-call(bf16[4,256,1280]{2,1,0:T(8,128)(2,1)} %tokens.3, bf16[16,1280]{1,0:T(8,128)(2,1)S(1)} %bitcast.22, bf16[4,256,1280]{2,1,0:T(8,128)(2,1)} %grads.3), custom_call_target="tpu_custom_call" | custom-call | flops 125829120 | bytes 5242880 | tf_op jit(solution)/shard_map/gather_slots/pallas_call | solution.py:123
  4.9 18.3 %all_to_all.44 = bf16[16,8,1280]{2,1,0:T(8,128)(2,1)S(1)} all-to-all(bf16[16,8,1280]{2,1,0:T(8,128)(2,1)S(1)} %bitcast.21), channel_id=1, replica_groups=mesh['rep'=2,'exp'=16] {'exp'}, dimensions={0} | all-to-all | bytes 655360 | tf_op jit(solution)/shard_map/all_to_all | solution.py:457
  23.2 1.5 %collective-permute-start = (bf16[128,1280]{1,0:T(8,128)(2,1)S(1)}, bf16[128,1280]{1,0:T(8,128)(2,1)S(1)}, u32[]{:S(2)}, u32[]{:S(2)}) collective-permute-start(bf16[128,1280]{1,0:T(8,128)(2,1)S(1)} %bitcast.15), channel_id=1, source_target_pairs={{0,16},{16,0},{1,17},{17,1},{2,18},{18,2},{3,19},{19,3},{4,20},{20... | collective-permute-start | bytes 983048 | tf_op jit(solution)/shard_map/ppermute | solution.py:469
  24.7 9.5 %expert_rows.1 = (bf16[128,1280]{1,0:T(8,128)(2,1)}, bf16[64,2560]{1,0:T(8,128)(2,1)S(1)}, bf16[64,2560]{1,0:T(8,128)(2,1)S(1)}, f32[8,128]{1,0:T(8,128)S(1)}) custom-call(bf16[128,1280]{1,0:T(8,128)(2,1)S(1)} %bitcast.16, bf16[1280,2560]{1,0:T(8,128)(2,1)} %bitcast.24, bf16[2560,1280]{1,0:T(8,128)(2,1)} %bitcast.26), custom_call_target="tpu_custom_call" | custom-call | flops 1677721600 | bytes 13107200 | tf_op jit(solution)/shard_map/expert_rows/pallas_call | solution.py:202
  34.2 3.6 %all-to-all-start.1 = ((bf16[16,8,1280]{2,1,0:T(8,128)(2,1)}), bf16[16,8,1280]{2,1,0:T(8,128)(2,1)S(1)}, u32[]{:S(2)}, u32[]{:S(2)}) async-start(bf16[16,8,1280]{2,1,0:T(8,128)(2,1)} %bitcast.6), calls=%async_computation.1 | async-start | bytes 655360 | tf_op jit(solution)/shard_map/all_to_all | solution.py:457
  37.8 0.0 collective-permute-done.rows.other_rows
  37.8 0.0 copy-start.1
  37.8 6.1 %others_hidden.1 = (bf16[64,2560]{1,0:T(8,128)(2,1)S(1)}, bf16[64,2560]{1,0:T(8,128)(2,1)S(1)}, f32[8,128]{1,0:T(8,128)S(1)}) custom-call(f32[8,128]{1,0:T(8,128)S(1)} %get-tuple-element.24.after, bf16[128,1280]{1,0:T(8,128)(2,1)S(1)} %collective-permute-done.rows.other_rows, bf16[1280,2560]{1,0:T(8,128)(2,1)} %bitcast.25, bf16[2560,1280]{1,0:T(8,128)(2,1)} %bitcast.27), custom_call_target="tpu_custom_call" | custom-call | flops 13421772800 | bytes 104857600 | tf_op jit(solution)/shard_map/others_hidden/pallas_call | solution.py:239
  43.9 4.9 %all-to-all-done.1 = bf16[16,8,1280]{2,1,0:T(8,128)(2,1)S(1)} async-done(((bf16[16,8,1280]{2,1,0:T(8,128)(2,1)}), bf16[16,8,1280]{2,1,0:T(8,128)(2,1)S(1)}, u32[]{:S(2)}, u32[]{:S(2)}) %all-to-all-start.1) | async-done | bytes 327712 | tf_op jit(solution)/shard_map/all_to_all | solution.py:457
  48.8 0.0 copy-done.1
  48.9 5.2 %logits_grads.1 = (bf16[4,32,256]{2,1,0:T(8,128)(2,1)S(1)}, bf16[4,32,1280]{2,1,0:T(8,128)(2,1)S(1)}, f32[256,128]{1,0:T(8,128)}, f32[8,128]{1,0:T(8,128)S(1)}) custom-call(f32[8,128]{1,0:T(8,128)S(1)} %get-tuple-element.25.after, bf16[128,1280]{1,0:T(8,128)(2,1)S(1)} %bitcast.18, bf16[4,256,1280]{2,1,0:T(8,128)(2,1)} %tokens.3, ...), custom_call_target="tpu_custom_call" | custom-call | flops 125829120 | bytes 5242880 | tf_op jit(solution)/shard_map/logits_grads/pallas_call | solution.py:366
  54.1 2.6 %all-to-all-start.2 = ((f32[32,8,128]{2,1,0:T(8,128)}), f32[32,8,128]{2,1,0:T(8,128)S(1)}, u32[]{:S(2)}, u32[]{:S(2)}) async-start(f32[32,8,128]{2,1,0:T(8,128)} %bitcast.8), calls=%async_computation.2 | async-start | bytes 262144 | tf_op jit(solution)/shard_map/all_to_all | solution.py:457
  56.7 4.5 %weight_grads.1 = (bf16[640,2560]{1,0:T(8,128)(2,1)}, bf16[1280,1280]{1,0:T(8,128)(2,1)}, f32[8,128]{1,0:T(8,128)S(1)}) custom-call(s32[1]{0:T(128)} %bitcast.mine, f32[8,128]{1,0:T(8,128)S(1)} %get-tuple-element.29.after, bf16[128,1280]{1,0:T(8,128)(2,1)S(1)} %bitcast.17, bf16[128,1280]{1,0:T(8,128)(2,1)S(1)} %collective-permute-done.rows.other_rows, ...), custom_call_target="tpu_custom_call" | custom-call | flops 838860800 | bytes 6553600 | tf_op jit(solution)/shard_map/weight_grads/pallas_call | solution.py:285
  61.3 3.7 %all-to-all-done.2 = f32[32,8,128]{2,1,0:T(8,128)S(1)} async-done(((f32[32,8,128]{2,1,0:T(8,128)}), f32[32,8,128]{2,1,0:T(8,128)S(1)}, u32[]{:S(2)}, u32[]{:S(2)}) %all-to-all-start.2) | async-done | bytes 131104 | tf_op jit(solution)/shard_map/all_to_all | solution.py:457
  64.9 0.7 share_of_sum.1
  65.6 2.6 %all-to-all-start.3 = ((f32[32,8,128]{2,1,0:T(8,128)}), f32[32,8,128]{2,1,0:T(8,128)S(1)}, u32[]{:S(2)}, u32[]{:S(2)}) async-start(f32[32,8,128]{2,1,0:T(8,128)} %bitcast.10), calls=%async_computation.3 | async-start | bytes 262144 | tf_op jit(solution)/shard_map/all_to_all | solution.py:457
  68.2 2.8 %tokens_grads.1 = bf16[4,256,1280]{2,1,0:T(8,128)(2,1)} custom-call(f32[8,128]{1,0:T(8,128)S(1)} %get-tuple-element.36.after, bf16[4,32,256]{2,1,0:T(8,128)(2,1)S(1)} %get-tuple-element.37.left, bf16[4,32,1280]{2,1,0:T(8,128)(2,1)S(1)} %get-tuple-element.38.right), custom_call_target="tpu_custom_call" | custom-call | flops 83886080 | bytes 2621440 | tf_op jit(solution)/shard_map/tokens_grads/pallas_call | solution.py:397
  71.0 5.5 %all-to-all-done.3 = f32[32,8,128]{2,1,0:T(8,128)S(1)} async-done(((f32[32,8,128]{2,1,0:T(8,128)}), f32[32,8,128]{2,1,0:T(8,128)S(1)}, u32[]{:S(2)}, u32[]{:S(2)}) %all-to-all-start.3) | async-done | bytes 131104 | tf_op jit(solution)/shard_map/all_to_all | solution.py:457
  76.4 0.7 unpack_sum.1
Async XLA Ops:
  0.6 0.8 %copy-start = (bf16[1280,16]{0,1:T(8,128)(2,1)S(1)}, bf16[1280,16]{0,1:T(8,128)(2,1)}, u32[]{:S(2)}) copy-start(bf16[1280,16]{0,1:T(8,128)(2,1)} %param.6) | copy-start | bytes 122884
  23.2 14.6 %collective-permute-start = (bf16[128,1280]{1,0:T(8,128)(2,1)S(1)}, bf16[128,1280]{1,0:T(8,128)(2,1)S(1)}, u32[]{:S(2)}, u32[]{:S(2)}) collective-permute-start(bf16[128,1280]{1,0:T(8,128)(2,1)S(1)} %bitcast.15), channel_id=1, source_target_pairs={{0,16},{16,0},{1,17},{17,1},{2,18},{18,2},{3,19},{19,3},{4,20},{20... | collective-permute-start | bytes 983048 | tf_op jit(solution)/shard_map/ppermute | solution.py:469
  34.2 14.6 %all-to-all-start.1 = ((bf16[16,8,1280]{2,1,0:T(8,128)(2,1)}), bf16[16,8,1280]{2,1,0:T(8,128)(2,1)S(1)}, u32[]{:S(2)}, u32[]{:S(2)}) async-start(bf16[16,8,1280]{2,1,0:T(8,128)(2,1)} %bitcast.6), calls=%async_computation.1 | async-start | bytes 655360 | tf_op jit(solution)/shard_map/all_to_all | solution.py:457
  37.8 11.1 %copy-start.1 = (bf16[1280,16]{0,1:T(8,128)(2,1)S(1)}, bf16[1280,16]{0,1:T(8,128)(2,1)}, u32[]{:S(2)}) copy-start(bf16[1280,16]{0,1:T(8,128)(2,1)} %param.6) | copy-start | bytes 122884
  54.1 10.8 %all-to-all-start.2 = ((f32[32,8,128]{2,1,0:T(8,128)}), f32[32,8,128]{2,1,0:T(8,128)S(1)}, u32[]{:S(2)}, u32[]{:S(2)}) async-start(f32[32,8,128]{2,1,0:T(8,128)} %bitcast.8), calls=%async_computation.2 | async-start | bytes 262144 | tf_op jit(solution)/shard_map/all_to_all | solution.py:457
  65.6 10.8 %all-to-all-start.3 = ((f32[32,8,128]{2,1,0:T(8,128)}), f32[32,8,128]{2,1,0:T(8,128)S(1)}, u32[]{:S(2)}, u32[]{:S(2)}) async-start(f32[32,8,128]{2,1,0:T(8,128)} %bitcast.10), calls=%async_computation.3 | async-start | bytes 262144 | tf_op jit(solution)/shard_map/all_to_all | solution.py:457

commit v8 on v7

--- a/solution.py
+++ b/solution.py
@@ -1,3 +1,4 @@
+import functools
 import math
 
 import jax
@@ -12,7 +13,6 @@
 LOW = jnp.bfloat16
 WIDE = jnp.float32
 LANES = 128
-TILE = 8
 KINDS = 2
 SHARED = 52 * 1024 * 1024
 WHOLE = pl.BlockSpec(memory_space=pltpu.VMEM)
@@ -139,56 +139,57 @@
     )(tokens, params, grads)
 
 
-def start_weights(w_in, w_out, w_in_v, w_out_v, sems):
-    chunks, tile = w_out_v.shape[:2]
+def chunks_of(hidden, tile):
+    edges = [0, *range(tile // 2, hidden, tile), hidden]
+    return [slice(first, last) for first, last in zip(edges, edges[1:])]
+
+
+def start_weights(w_in, w_out, w_in_v, w_out_v, sems, tile):
     copies = []
-    for chunk in range(chunks):
-        units = pl.ds(chunk * tile, tile)
-        pair = (
-            pltpu.make_async_copy(w_in.at[:, units], w_in_v.at[chunk], sems.at[0, chunk]),
-            pltpu.make_async_copy(w_out.at[units, :], w_out_v.at[chunk], sems.at[1, chunk]),
+    for chunk, units in enumerate(chunks_of(w_in.shape[1], tile)):
+        copies.append(
+            (
+                start_copy(w_in.at[:, units], w_in_v.at[:, units], sems.at[0, chunk]),
+                start_copy(w_out.at[units, :], w_out_v.at[units, :], sems.at[1, chunk]),
+            )
         )
-        for copy in pair:
-            copy.start()
-        copies.append(pair)
     return copies
 
 
 def weight_scratch(width, hidden, tile):
-    chunks = hidden // tile
     return [
-        pltpu.VMEM((chunks, width, tile), LOW),
-        pltpu.VMEM((chunks, tile, width), LOW),
-        pltpu.SemaphoreType.DMA((2, chunks)),
+        pltpu.VMEM((width, hidden), LOW),
+        pltpu.VMEM((hidden, width), LOW),
+        pltpu.SemaphoreType.DMA((2, len(chunks_of(hidden, tile)))),
     ]
 
 
-def expert_kernel(rows, w_in, w_out, back, acts, hidden, mark, w_in_v, w_out_v, sems, wide):
+def expert_kernel(
+    tile, rows, w_in, w_out, back, acts, hidden, mark, w_in_v, w_out_v, sems, wide
+):
     del mark
-    copies = start_weights(w_in, w_out, w_in_v, w_out_v, sems)
+    copies = start_weights(w_in, w_out, w_in_v, w_out_v, sems, tile)
     count = rows.shape[0] // KINDS
-    chunks, tile = w_out_v.shape[:2]
     load_rows(wide, rows[...])
     rows_in = take(wide, 0, count, KINDS).astype(LOW)
     rows_grad = take(wide, 1, count, KINDS).astype(LOW)
-    out = d_in = None
-    held = None
-    for chunk in range(chunks + 1):
-        if chunk < chunks:
-            for copy in copies[chunk]:
+    out = d_in = held = before = None
+    for pair, units in zip([*copies, None], [*chunks_of(w_in.shape[1], tile), None]):
+        if pair is not None:
+            for copy in pair:
                 copy.wait()
-            preact = dot(rows_in, w_in_v[chunk], 1, 0)
-            d_acts = dot(rows_grad, w_out_v[chunk], 1, 1)
-        if chunk > 0:
-            out_part = dot(held[0], w_out_v[chunk - 1], 1, 0)
-            d_in_part = dot(held[1], w_in_v[chunk - 1], 1, 1)
-            out = out_part if chunk == 1 else out + out_part
-            d_in = d_in_part if chunk == 1 else d_in + d_in_part
-        if chunk < chunks:
-            units = slice(chunk * tile, (chunk + 1) * tile)
+            preact = dot(rows_in, w_in_v[:, units], 1, 0)
+            d_acts = dot(rows_grad, w_out_v[units, :], 1, 1)
+        if before is not None:
+            out_part = dot(held[0], w_out_v[before, :], 1, 0)
+            d_in_part = dot(held[1], w_in_v[:, before], 1, 1)
+            out = out_part if out is None else out + out_part
+            d_in = d_in_part if d_in is None else d_in + d_in_part
+        if pair is not None:
             values, slope = gelu_parts(preact)
             held = (values.astype(LOW), (d_acts * slope).astype(LOW))
             acts[:, units], hidden[:, units] = held
+        before = units
     put(wide, 0, count, KINDS, out)
     put(wide, 1, count, KINDS, d_in)
     back[...] = packed(wide)
@@ -200,7 +201,7 @@
     count = total // KINDS
     kept = shaped((count, hidden), LOW)
     return call(
-        expert_kernel,
+        functools.partial(expert_kernel, tile),
         "expert_rows",
         SHARED,
         8 * count * hidden * width,
@@ -213,21 +214,21 @@
     )(rows, w_in, w_out)
 
 
-def others_kernel(after, rows, w_in, w_out, acts, hidden, mark, w_in_v, w_out_v, sems, wide):
+def others_kernel(
+    tile, after, rows, w_in, w_out, acts, hidden, mark, w_in_v, w_out_v, sems, wide
+):
     del after, mark
-    copies = start_weights(w_in, w_out, w_in_v, w_out_v, sems)
+    copies = start_weights(w_in, w_out, w_in_v, w_out_v, sems, tile)
     count = rows.shape[0] // KINDS
-    chunks, tile = w_out_v.shape[:2]
     load_rows(wide, rows[...])
     rows_in = take(wide, 0, count, KINDS).astype(LOW)
     rows_grad = take(wide, 1, count, KINDS).astype(LOW)
-    for chunk in range(chunks):
-        units = slice(chunk * tile, (chunk + 1) * tile)
-        copies[chunk][0].wait()
-        values, slope = gelu_parts(dot(rows_in, w_in_v[chunk], 1, 0))
+    for pair, units in zip(copies, chunks_of(w_in.shape[1], tile)):
+        for copy in pair:
+            copy.wait()
+        values, slope = gelu_parts(dot(rows_in, w_in_v[:, units], 1, 0))
         acts[:, units] = values.astype(LOW)
-        copies[chunk][1].wait()
-        d_acts = dot(rows_grad, w_out_v[chunk], 1, 1)
+        d_acts = dot(rows_grad, w_out_v[units, :], 1, 1)
         hidden[:, units] = (d_acts * slope).astype(LOW)
 
 
@@ -237,7 +238,7 @@
     count = total // KINDS
     kept = shaped((count, hidden), LOW)
     return call(
-        others_kernel,
+        functools.partial(others_kernel, tile),
         "others_hidden",
         SHARED,
         64 * count * hidden * width,
@@ -327,7 +328,6 @@
         right[image, :slots, :] = d_slot_in[image]
         right[image, slots:, :] = params[...]
         left[image, :slots, :] = dispatch[image].astype(LOW)
-    local[...] = jnp.zeros_like(local)
     grads_copy.wait()
     parts = []
     for image in range(images):
@@ -349,18 +349,11 @@
         left[image, slots:, :] = low
         part = dot(low, tokens_v[image], 1, 0)
         total = part if image == 0 else total + part
-    for tile, (start, step) in enumerate(piece_rows(local, *params.shape)):
-        local[pl.ds(start, slots, stride=step), :] = total[:, tile * LANES : (tile + 1) * LANES]
-
-
-def piece_rows(pieces, slots, width):
-    per_slot = pieces.shape[0] // TILE // slots
-    used = width // LANES // per_slot
-    step = per_slot * TILE
-    return [(tile // used * TILE + tile % used, step) for tile in range(width // LANES)]
-
-
-def logits_grads(after, back, tokens, params, grads, dispatch, combine, pieces):
+    for row in range(slots):
+        local[row] = total[row : row + 1, :]
+
+
+def logits_grads(after, back, tokens, params, grads, dispatch, combine):
     images, length, width = tokens.shape
     slots = params.shape[0]
     return call(
@@ -372,7 +365,7 @@
         out_shape=(
             shaped((images, 2 * slots, length), LOW),
             shaped((images, 2 * slots, width), LOW),
-            shaped((pieces * TILE, LANES), WIDE),
+            shaped((slots, 1, width), WIDE),
             MARK,
         ),
         in_specs=[PLACE, WHOLE, PLACE, WHOLE, PLACE, WHOLE, WHOLE],
@@ -411,46 +404,64 @@
     )(after, left, right)
 
 
-def share_kernel(after, pieces, out, mark):
+def share_kernel(after, parts, out, mark):
     del after, mark
-    rows = pieces.shape[0]
-    total = pieces[:TILE, :]
-    for row in range(TILE, rows, TILE):
-        total = total + pieces[row : row + TILE, :]
-    for row in range(0, rows, TILE):
-        out[row : row + TILE, :] = total
-
-
-def share_of_sum(after, pieces):
+    total = jnp.sum(parts[...], axis=0, keepdims=True)
+    out[...] = jnp.broadcast_to(total, out.shape)
+
+
+def share_of_sum(after, parts, copies):
+    shape = (copies, *parts.shape[1:])
     return call(
         share_kernel,
         "share_of_sum",
         SHARED,
-        pieces.size,
-        8 * pieces.size,
-        out_shape=(shaped(pieces.shape, WIDE), MARK),
+        parts.size,
+        8 * parts.size,
+        out_shape=(shaped(shape, WIDE), MARK),
         in_specs=[PLACE, WHOLE],
         out_specs=(WHOLE, PLACE),
-    )(after, pieces)
-
-
-def unpack_kernel(pieces, out):
-    slots, width = out.shape
-    for tile, (start, step) in enumerate(piece_rows(pieces, slots, width)):
-        out[:, tile * LANES : (tile + 1) * LANES] = pieces[pl.ds(start, slots, stride=step), :]
-
-
-def unpack(pieces, shape):
-    return call(
-        unpack_kernel,
-        "unpack_sum",
-        SHARED,
-        0,
-        8 * pieces.size,
+    )(after, parts)
+
+
+def total_kernel(shares, out):
+    slots = out.shape[0]
+    for slot in range(slots):
+        total = shares[slot]
+        for replica in range(1, shares.shape[0] // slots):
+            total = total + shares[replica * slots + slot]
+        out[slot : slot + 1, :] = total
+
+
+def total_of_shares(shares, shape):
+    return call(
+        total_kernel,
+        "total_of_shares",
+        SHARED,
+        shares.size,
+        8 * shares.size,
         out_shape=shaped(shape, WIDE),
         in_specs=[WHOLE],
         out_specs=WHOLE,
-    )(pieces)
+    )(shares)
+
+
+def copy_kernel(after, source, target):
+    del after
+    target[...] = source[...]
+
+
+def copy_after(after, array):
+    return call(
+        copy_kernel,
+        "copy_after",
+        SHARED,
+        0,
+        4 * array.size,
+        out_shape=shaped(array.shape, array.dtype),
+        in_specs=[PLACE, WHOLE],
+        out_specs=WHOLE,
+    )(after, array)
 
 
 def exchange(rows, axes):
@@ -466,26 +477,30 @@
 
     sent, dispatch, combine = gather(tokens, params, grad_out)
     rows = exchange(sent, "exp")
-    other_rows = lax.ppermute(rows, "rep", [(i, (i + 1) % replicas) for i in range(replicas)])
     back, acts, hidden, after_expert = expert(rows, *weights, 512)
+    back = exchange(back, "exp")
+    other_rows = lax.ppermute(
+        copy_after(after_expert, rows), "rep", [(i, (i + 1) % replicas) for i in range(replicas)]
+    )
+    left, right, local, after_logits = logits_grads(
+        after_expert, back, tokens, params, grad_out, dispatch, combine
+    )
     other_acts, other_hidden, after_others = others_hidden(
-        after_expert, other_rows, *weights, 512
-    )
-    back = exchange(back, "exp")
-    left, right, local, after_logits = logits_grads(
-        after_others, back, tokens, params, grad_out, dispatch, combine, lax.axis_size(everyone)
-    )
-    grad_expert_in, grad_expert_out, after_weights = weight_grads(
+        after_logits, other_rows, *weights, 512
+    )
+    share, after_share = share_of_sum(
+        after_others, exchange(local, "exp"), lax.axis_size(everyone)
+    )
+    grad_expert_in, grad_expert_out, _ = weight_grads(
         mine,
-        after_logits,
+        after_share,
         (rows, other_rows),
         (acts, other_acts),
         (hidden, other_hidden),
         5,
         replicas,
     )
-    share, after_share = share_of_sum(after_weights, exchange(local, everyone))
-    grad_params = unpack(exchange(share, everyone), params.shape).T
+    grad_params = total_of_shares(exchange(share, everyone), params.shape).T
     grad_tokens = tokens_grads(after_share, left, right)
     return (
         grad_tokens,

time: 77.5 us -> 78.2 us (level)
  starting transfers between devices: 10.2 us -> 13.2 us
  waiting for transfers between devices: 14 us -> 12 us
    all_to_all x3, starting transfers between devices: 8.71 us -> 11.7 us  [exchange(): return lax.all_to_all(rows, axes, split_axis=0, concat_axis=0, tiled=True)]
    all_to_all x3, waiting for transfers between devices: 14 us -> 12 us  [exchange(): return lax.all_to_all(rows, axes, split_axis=0, concat_axis=0, tiled=True)]
    pallas_call x4 -> x5, Pallas kernels: 17 us -> 16.7 us  [the longest x1 9.51 us: expert(): call(functools.partial(expert_kernel, tile), 'expert_rows', SHARED, 8 * c...]
  transfers between devices with their start and end apart: 4 -> 4, of which waited for: 3 -> 3; matrix products, arithmetic and copies ran while one was open for 0% -> 0% of each run, Pallas kernels for 30% -> 24%
where the time goes in v8:
time: 78.2 us; the launch traced here: 77.8 us
  Pallas kernels  32.7 us (42%)
  blocking collectives  18.3 us (23%)
  starting transfers between devices  13.2 us (17%)
  waiting for transfers between devices  12 us (15%)
    all_to_all x1, blocking collectives, exchange(): return lax.all_to_all(rows, axes, split_axis=0, concat_axis=0, tiled=True)  18.3 us
    all_to_all x3, waiting for transfers between devices, exchange(): return lax.all_to_all(rows, axes, split_axis=0, concat_axis=0, tiled=True)  12 us
    all_to_all x3, starting transfers between devices, exchange(): return lax.all_to_all(rows, axes, split_axis=0, concat_axis=0, tiled=True)  11.7 us
    pallas_call x1, Pallas kernels, expert(): call(functools.partial(expert_kernel, tile), 'expert_rows', SHARED, 8 * c...  9.51 us
    pallas_call x1, Pallas kernels, others_hidden(): call(functools.partial(others_kernel, tile), 'others_hidden', SHARED, 64...  5.81 us
    pallas_call x1, Pallas kernels, logits_grads(): call(logits_kernel, 'logits_grads', SHARED, 6 * images * slots * length *...  5.23 us
    pallas_call x1, Pallas kernels, weight_grads(): call(weights_kernel, 'weight_grads', SHARED, 8 * count * size * width //...  4.52 us
    pallas_call x1, Pallas kernels, gather(): call(gather_kernel, 'gather_slots', SHARED, 6 * images * slots * length *...  3.48 us
  transfers between devices with their start and end apart: 4, of which 3 were waited for; matrix products, arithmetic and copies ran while one was open for 0% of the time, Pallas kernels for 24%

profile of v8, /device:TPU:0, one launch (start us, length us, event | category | flops | bytes accessed | tf_op | source)
XLA Modules:
  0.0 77.8 jit_solution(7557480469906376332)
XLA Ops:
  0.6 0.0 copy-start
  0.6 0.8 copy-done
  1.4 3.5 %gather_slots.1 = (bf16[128,1280]{1,0:T(8,128)(2,1)S(1)}, f32[4,16,256]{2,1,0:T(8,128)S(1)}, f32[4,16,256]{2,1,0:T(8,128)S(1)}) custom-call(bf16[4,256,1280]{2,1,0:T(8,128)(2,1)} %tokens.3, bf16[16,1280]{1,0:T(8,128)(2,1)S(1)} %bitcast.16, bf16[4,256,1280]{2,1,0:T(8,128)(2,1)} %grads.3), custom_call_target="tpu_custom_call" | custom-call | flops 125829120 | bytes 5242880 | tf_op jit(solution)/shard_map/gather_slots/pallas_call | solution.py:123
  4.9 18.3 %all_to_all.32 = bf16[16,8,1280]{2,1,0:T(8,128)(2,1)S(1)} all-to-all(bf16[16,8,1280]{2,1,0:T(8,128)(2,1)S(1)} %bitcast.15), channel_id=1, replica_groups=mesh['rep'=2,'exp'=16] {'exp'}, dimensions={0} | all-to-all | bytes 655360 | tf_op jit(solution)/shard_map/all_to_all | solution.py:468
  23.2 0.0 copy-start.1
  23.2 9.5 %expert_rows.1 = (bf16[128,1280]{1,0:T(8,128)(2,1)}, bf16[64,2560]{1,0:T(8,128)(2,1)S(1)}, bf16[64,2560]{1,0:T(8,128)(2,1)S(1)}, f32[8,128]{1,0:T(8,128)S(1)}) custom-call(bf16[128,1280]{1,0:T(8,128)(2,1)S(1)} %bitcast.11, bf16[1280,2560]{1,0:T(8,128)(2,1)} %bitcast.18, bf16[2560,1280]{1,0:T(8,128)(2,1)} %bitcast.20), custom_call_target="tpu_custom_call" | custom-call | flops 1677721600 | bytes 13107200 | tf_op jit(solution)/shard_map/expert_rows/pallas_call | solution.py:203
  32.7 3.6 %all-to-all-start.1 = ((bf16[16,8,1280]{2,1,0:T(8,128)(2,1)}), bf16[16,8,1280]{2,1,0:T(8,128)(2,1)S(1)}, u32[]{:S(2)}, u32[]{:S(2)}) async-start(bf16[16,8,1280]{2,1,0:T(8,128)(2,1)} %bitcast.5), calls=%async_computation.1 | async-start | bytes 655360 | tf_op jit(solution)/shard_map/all_to_all | solution.py:468
  36.3 1.6 %collective-permute-start = (bf16[128,1280]{1,0:T(8,128)(2,1)S(1)}, bf16[128,1280]{1,0:T(8,128)(2,1)S(1)}, u32[]{:S(2)}, u32[]{:S(2)}) collective-permute-start(bf16[128,1280]{1,0:T(8,128)(2,1)S(1)} %copy_after.1), channel_id=1, source_target_pairs={{0,16},{16,0},{1,17},{17,1},{2,18},{18,2},{3,19},{19,3},{4,20},{20... | collective-permute-start | bytes 983048 | tf_op jit(solution)/shard_map/ppermute | solution.py:482
  37.9 9.5 %all-to-all-done.1 = bf16[16,8,1280]{2,1,0:T(8,128)(2,1)S(1)} async-done(((bf16[16,8,1280]{2,1,0:T(8,128)(2,1)}), bf16[16,8,1280]{2,1,0:T(8,128)(2,1)S(1)}, u32[]{:S(2)}, u32[]{:S(2)}) %all-to-all-start.1) | async-done | bytes 327712 | tf_op jit(solution)/shard_map/all_to_all | solution.py:468
  47.3 0.0 copy-done.1
  47.3 5.2 %logits_grads.1 = (bf16[4,32,256]{2,1,0:T(8,128)(2,1)S(1)}, bf16[4,32,1280]{2,1,0:T(8,128)(2,1)S(1)}, f32[16,1,1280]{2,1,0:T(1,128)}, f32[8,128]{1,0:T(8,128)S(1)}) custom-call(f32[8,128]{1,0:T(8,128)S(1)} %get-tuple-element.23.after, bf16[128,1280]{1,0:T(8,128)(2,1)S(1)} %bitcast.14, bf16[4,256,1280]{2,1,0:T(8,128)(2,1)} %tokens.3, ...), custom_call_target="tpu_custom_call" | custom-call | flops 125829120 | bytes 5242880 | tf_op jit(solution)/shard_map/logits_grads/pallas_call | solution.py:359
  52.6 3.5 %all-to-all-start.2 = ((f32[16,1,1280]{2,1,0:T(1,128)}), f32[16,1,1280]{2,1,0:T(1,128)S(1)}, u32[]{:S(2)}, u32[]{:S(2)}) async-start(f32[16,1,1280]{2,1,0:T(1,128)} %get-tuple-element.29), calls=%async_computation.2 | async-start | bytes 163840 | tf_op jit(solution)/shard_map/all_to_all | solution.py:468
  56.1 0.0 collective-permute-done.rows.other_rows
  56.1 5.8 %others_hidden.1 = (bf16[64,2560]{1,0:T(8,128)(2,1)S(1)}, bf16[64,2560]{1,0:T(8,128)(2,1)S(1)}, f32[8,128]{1,0:T(8,128)S(1)}) custom-call(f32[8,128]{1,0:T(8,128)S(1)} %get-tuple-element.27.after, bf16[128,1280]{1,0:T(8,128)(2,1)S(1)} %collective-permute-done.rows.other_rows, bf16[1280,2560]{1,0:T(8,128)(2,1)} %bitcast.19, bf16[2560,1280]{1,0:T(8,128)(2,1)} %bitcast.21), custom_call_target="tpu_custom_call" | custom-call | flops 13421772800 | bytes 104857600 | tf_op jit(solution)/shard_map/others_hidden/pallas_call | solution.py:240
  61.9 1.3 %all-to-all-done.2.parts = f32[16,1,1280]{2,1,0:T(1,128)S(1)} async-done(((f32[16,1,1280]{2,1,0:T(1,128)}), f32[16,1,1280]{2,1,0:T(1,128)S(1)}, u32[]{:S(2)}, u32[]{:S(2)}) %all-to-all-start.2) | async-done | bytes 81952 | tf_op jit(solution)/shard_map/all_to_all | solution.py:468
  63.2 0.7 share_of_sum.1
  63.9 4.6 %all-to-all-start.3 = ((f32[32,1,1280]{2,1,0:T(1,128)}), f32[32,1,1280]{2,1,0:T(1,128)S(1)}, u32[]{:S(2)}, u32[]{:S(2)}) async-start(f32[32,1,1280]{2,1,0:T(1,128)} %get-tuple-element.33), calls=%async_computation.3 | async-start | bytes 327680 | tf_op jit(solution)/shard_map/all_to_all | solution.py:468
  68.6 2.8 %tokens_grads.1 = bf16[4,256,1280]{2,1,0:T(8,128)(2,1)} custom-call(f32[8,128]{1,0:T(8,128)S(1)} %get-tuple-element.30.after, bf16[4,32,256]{2,1,0:T(8,128)(2,1)S(1)} %get-tuple-element.31.left, bf16[4,32,1280]{2,1,0:T(8,128)(2,1)S(1)} %get-tuple-element.32.right), custom_call_target="tpu_custom_call" | custom-call | flops 83886080 | bytes 2621440 | tf_op jit(solution)/shard_map/tokens_grads/pallas_call | solution.py:390
  71.3 4.5 %weight_grads.1 = (bf16[640,2560]{1,0:T(8,128)(2,1)}, bf16[1280,1280]{1,0:T(8,128)(2,1)}, f32[8,128]{1,0:T(8,128)}) custom-call(s32[1]{0:T(128)} %bitcast.8.mine, f32[8,128]{1,0:T(8,128)S(1)} %get-tuple-element.30.after, bf16[128,1280]{1,0:T(8,128)(2,1)S(1)} %bitcast.13, bf16[128,1280]{1,0:T(8,128)(2,1)S(1)} %collective-permute-done.rows.other_rows, ...), custom_call_target="tpu_custom_call" | custom-call | flops 838860800 | bytes 6553600 | tf_op jit(solution)/shard_map/weight_grads/pallas_call | solution.py:286
  75.8 1.3 %all-to-all-done.3.shares = f32[32,1,1280]{2,1,0:T(1,128)S(1)} async-done(((f32[32,1,1280]{2,1,0:T(1,128)}), f32[32,1,1280]{2,1,0:T(1,128)S(1)}, u32[]{:S(2)}, u32[]{:S(2)}) %all-to-all-start.3) | async-done | bytes 163872 | tf_op jit(solution)/shard_map/all_to_all | solution.py:468
  77.1 0.7 total_of_shares.1
  (1 shorter events, 0.0 us)
Async XLA Ops:
  0.6 0.8 %copy-start = (bf16[1280,16]{0,1:T(8,128)(2,1)S(1)}, bf16[1280,16]{0,1:T(8,128)(2,1)}, u32[]{:S(2)}) copy-start(bf16[1280,16]{0,1:T(8,128)(2,1)} %param.6) | copy-start | bytes 122884
  23.2 24.1 %copy-start.1 = (bf16[1280,16]{0,1:T(8,128)(2,1)S(1)}, bf16[1280,16]{0,1:T(8,128)(2,1)}, u32[]{:S(2)}) copy-start(bf16[1280,16]{0,1:T(8,128)(2,1)} %param.6) | copy-start | bytes 122884
  32.7 14.6 %all-to-all-start.1 = ((bf16[16,8,1280]{2,1,0:T(8,128)(2,1)}), bf16[16,8,1280]{2,1,0:T(8,128)(2,1)S(1)}, u32[]{:S(2)}, u32[]{:S(2)}) async-start(bf16[16,8,1280]{2,1,0:T(8,128)(2,1)} %bitcast.5), calls=%async_computation.1 | async-start | bytes 655360 | tf_op jit(solution)/shard_map/all_to_all | solution.py:468
  36.3 19.8 %collective-permute-start = (bf16[128,1280]{1,0:T(8,128)(2,1)S(1)}, bf16[128,1280]{1,0:T(8,128)(2,1)S(1)}, u32[]{:S(2)}, u32[]{:S(2)}) collective-permute-start(bf16[128,1280]{1,0:T(8,128)(2,1)S(1)} %copy_after.1), channel_id=1, source_target_pairs={{0,16},{16,0},{1,17},{17,1},{2,18},{18,2},{3,19},{19,3},{4,20},{20... | collective-permute-start | bytes 983048 | tf_op jit(solution)/shard_map/ppermute | solution.py:482
  52.6 10.6 %all-to-all-start.2 = ((f32[16,1,1280]{2,1,0:T(1,128)}), f32[16,1,1280]{2,1,0:T(1,128)S(1)}, u32[]{:S(2)}, u32[]{:S(2)}) async-start(f32[16,1,1280]{2,1,0:T(1,128)} %get-tuple-element.29), calls=%async_computation.2 | async-start | bytes 163840 | tf_op jit(solution)/shard_map/all_to_all | solution.py:468
  63.9 13.2 %all-to-all-start.3 = ((f32[32,1,1280]{2,1,0:T(1,128)}), f32[32,1,1280]{2,1,0:T(1,128)S(1)}, u32[]{:S(2)}, u32[]{:S(2)}) async-start(f32[32,1,1280]{2,1,0:T(1,128)} %get-tuple-element.33), calls=%async_computation.3 | async-start | bytes 327680 | tf_op jit(solution)/shard_map/all_to_all | solution.py:468

commit v9 on v8

--- a/solution.py
+++ b/solution.py
@@ -89,16 +89,29 @@
     return copy
 
 
+def start_halves(source, target, sems):
+    images = source.shape[0]
+    parts = []
+    for index, (first, last) in enumerate(((0, images // 2), (images // 2, images))):
+        part = pl.ds(first, last - first)
+        copy = start_copy(source.at[part], target.at[part], sems.at[index])
+        parts.append((copy, range(first, last)))
+    return parts
+
+
 def gather_kernel(
-    tokens, params, grads, sent, dispatch, combine, tokens_v, grads_v, rows, sems
+    tokens, params, grads, sent, dispatch, combine, mark, tokens_v, grads_v, rows, sems
 ):
+    del mark
     images = tokens.shape[0]
     slots = params.shape[0]
     stride = KINDS * images
-    tokens_copy = start_copy(tokens, tokens_v, sems.at[0])
-    grads_copy = start_copy(grads, grads_v, sems.at[1])
-    tokens_copy.wait()
-    logits = [dot(params[...], tokens_v[image], 1, 1) for image in range(images)]
+    halves = start_halves(tokens, tokens_v, sems)
+    grads_copy = start_copy(grads, grads_v, sems.at[2])
+    logits = []
+    for copy, half in halves:
+        copy.wait()
+        logits += [dot(params[...], tokens_v[image], 1, 1) for image in half]
     over_slots = []
     for image in range(images):
         over_tokens = softmax(logits[image], 1)
@@ -127,26 +140,26 @@
         6 * images * slots * length * width,
         4 * images * length * width,
         2 * images * slots * length,
-        out_shape=(shaped(rows, LOW), weights, weights),
+        out_shape=(shaped(rows, LOW), weights, weights, MARK),
         in_specs=[PLACE, WHOLE, PLACE],
-        out_specs=(WHOLE, WHOLE, WHOLE),
+        out_specs=(WHOLE, WHOLE, WHOLE, PLACE),
         scratch_shapes=[
             pltpu.VMEM(tokens.shape, LOW),
             pltpu.VMEM(grads.shape, LOW),
             scratch_rows(rows),
-            pltpu.SemaphoreType.DMA((2,)),
+            pltpu.SemaphoreType.DMA((3,)),
         ],
     )(tokens, params, grads)
 
 
-def chunks_of(hidden, tile):
-    edges = [0, *range(tile // 2, hidden, tile), hidden]
-    return [slice(first, last) for first, last in zip(edges, edges[1:])]
-
-
-def start_weights(w_in, w_out, w_in_v, w_out_v, sems, tile):
+def chunks_of(first, hidden, tile):
+    edges = [*range(first, hidden, tile), hidden]
+    return [slice(low, high) for low, high in zip(edges, edges[1:])]
+
+
+def start_weights(w_in, w_out, w_in_v, w_out_v, sems, chunks):
     copies = []
-    for chunk, units in enumerate(chunks_of(w_in.shape[1], tile)):
+    for chunk, units in enumerate(chunks):
         copies.append(
             (
                 start_copy(w_in.at[:, units], w_in_v.at[:, units], sems.at[0, chunk]),
@@ -156,74 +169,114 @@
     return copies
 
 
-def weight_scratch(width, hidden, tile):
+def weight_scratch(width, hidden, chunks):
     return [
         pltpu.VMEM((width, hidden), LOW),
         pltpu.VMEM((hidden, width), LOW),
-        pltpu.SemaphoreType.DMA((2, len(chunks_of(hidden, tile)))),
+        pltpu.SemaphoreType.DMA((2, len(chunks))),
     ]
 
 
+def fetch_kernel(after, w_in, w_out, first_in, first_out, sems):
+    del after
+    units = slice(0, first_out.shape[0])
+    copies = (
+        start_copy(w_in.at[:, units], first_in, sems.at[0]),
+        start_copy(w_out.at[units, :], first_out, sems.at[1]),
+    )
+    for copy in copies:
+        copy.wait()
+
+
+def fetch_first(after, w_in, w_out, count):
+    width = w_in.shape[0]
+    return call(
+        fetch_kernel,
+        "fetch_first",
+        SHARED,
+        0,
+        8 * count * width,
+        out_shape=(shaped((width, count), LOW), shaped((count, width), LOW)),
+        in_specs=[PLACE] * 3,
+        out_specs=(WHOLE,) * 2,
+        scratch_shapes=[pltpu.SemaphoreType.DMA((2,))],
+    )(after, w_in, w_out)
+
+
 def expert_kernel(
-    tile, rows, w_in, w_out, back, acts, hidden, mark, w_in_v, w_out_v, sems, wide
+    chunks, rows, first_in, first_out, w_in, w_out, back, acts, hidden, mark,
+    w_in_v, w_out_v, sems, wide,
 ):
     del mark
-    copies = start_weights(w_in, w_out, w_in_v, w_out_v, sems, tile)
+    copies = start_weights(w_in, w_out, w_in_v, w_out_v, sems, chunks)
     count = rows.shape[0] // KINDS
     load_rows(wide, rows[...])
     rows_in = take(wide, 0, count, KINDS).astype(LOW)
     rows_grad = take(wide, 1, count, KINDS).astype(LOW)
-    out = d_in = held = before = None
-    for pair, units in zip([*copies, None], [*chunks_of(w_in.shape[1], tile), None]):
+
+    def first_products(weight_in, weight_out):
+        return dot(rows_in, weight_in, 1, 0), dot(rows_grad, weight_out, 1, 1)
+
+    def second_products(held, weight_in, weight_out):
+        return dot(held[0], weight_out, 1, 0), dot(held[1], weight_in, 1, 1)
+
+    def hold(preact, d_acts, units):
+        values, slope = gelu_parts(preact)
+        held = (values.astype(LOW), (d_acts * slope).astype(LOW))
+        acts[:, units], hidden[:, units] = held
+        return held
+
+    held = hold(
+        *first_products(first_in[...], first_out[...]), slice(0, first_out.shape[0])
+    )
+    out, d_in = second_products(held, first_in[...], first_out[...])
+    before = None
+    for pair, units in zip([*copies, None], [*chunks, None]):
         if pair is not None:
             for copy in pair:
                 copy.wait()
-            preact = dot(rows_in, w_in_v[:, units], 1, 0)
-            d_acts = dot(rows_grad, w_out_v[units, :], 1, 1)
+            products = first_products(w_in_v[:, units], w_out_v[units, :])
         if before is not None:
-            out_part = dot(held[0], w_out_v[before, :], 1, 0)
-            d_in_part = dot(held[1], w_in_v[:, before], 1, 1)
-            out = out_part if out is None else out + out_part
-            d_in = d_in_part if d_in is None else d_in + d_in_part
+            parts = second_products(held, w_in_v[:, before], w_out_v[before, :])
+            out, d_in = out + parts[0], d_in + parts[1]
         if pair is not None:
-            values, slope = gelu_parts(preact)
-            held = (values.astype(LOW), (d_acts * slope).astype(LOW))
-            acts[:, units], hidden[:, units] = held
+            held = hold(*products, units)
         before = units
     put(wide, 0, count, KINDS, out)
     put(wide, 1, count, KINDS, d_in)
     back[...] = packed(wide)
 
 
-def expert(rows, w_in, w_out, tile):
+def expert(rows, first_in, first_out, w_in, w_out, tile):
     total, width = rows.shape
     hidden = w_in.shape[1]
     count = total // KINDS
     kept = shaped((count, hidden), LOW)
-    return call(
-        functools.partial(expert_kernel, tile),
+    chunks = chunks_of(first_out.shape[0], hidden, tile)
+    return call(
+        functools.partial(expert_kernel, chunks),
         "expert_rows",
-        SHARED,
+        50 * 1024 * 1024,
         8 * count * hidden * width,
         4 * hidden * width,
         count * hidden,
         out_shape=(shaped(rows.shape, LOW), kept, kept, MARK),
-        in_specs=[WHOLE, PLACE, PLACE],
+        in_specs=[WHOLE, WHOLE, WHOLE, PLACE, PLACE],
         out_specs=(WHOLE, WHOLE, WHOLE, PLACE),
-        scratch_shapes=[*weight_scratch(width, hidden, tile), scratch_rows(rows.shape)],
-    )(rows, w_in, w_out)
+        scratch_shapes=[*weight_scratch(width, hidden, chunks), scratch_rows(rows.shape)],
+    )(rows, first_in, first_out, w_in, w_out)
 
 
 def others_kernel(
-    tile, after, rows, w_in, w_out, acts, hidden, mark, w_in_v, w_out_v, sems, wide
+    chunks, after, rows, w_in, w_out, acts, hidden, mark, w_in_v, w_out_v, sems, wide
 ):
     del after, mark
-    copies = start_weights(w_in, w_out, w_in_v, w_out_v, sems, tile)
+    copies = start_weights(w_in, w_out, w_in_v, w_out_v, sems, chunks)
     count = rows.shape[0] // KINDS
     load_rows(wide, rows[...])
     rows_in = take(wide, 0, count, KINDS).astype(LOW)
     rows_grad = take(wide, 1, count, KINDS).astype(LOW)
-    for pair, units in zip(copies, chunks_of(w_in.shape[1], tile)):
+    for pair, units in zip(copies, chunks):
         for copy in pair:
             copy.wait()
         values, slope = gelu_parts(dot(rows_in, w_in_v[:, units], 1, 0))
@@ -237,8 +290,9 @@
     hidden = w_in.shape[1]
     count = total // KINDS
     kept = shaped((count, hidden), LOW)
-    return call(
-        functools.partial(others_kernel, tile),
+    chunks = chunks_of(0, hidden, tile)
+    return call(
+        functools.partial(others_kernel, chunks),
         "others_hidden",
         SHARED,
         64 * count * hidden * width,
@@ -247,7 +301,7 @@
         out_shape=(kept, kept, MARK),
         in_specs=[PLACE, WHOLE, PLACE, PLACE],
         out_specs=(WHOLE, WHOLE, PLACE),
-        scratch_shapes=[*weight_scratch(width, hidden, tile), scratch_rows(rows.shape)],
+        scratch_shapes=[*weight_scratch(width, hidden, chunks), scratch_rows(rows.shape)],
     )(after, rows, w_in, w_out)
 
 
@@ -312,14 +366,22 @@
     )(mine, after, *rows, *acts, *hidden)
 
 
+def put_pieces(pieces, array):
+    size = pieces.shape[2]
+    per_row = array.shape[1] // size
+    for piece in range(pieces.shape[0]):
+        row, at = piece // per_row, piece % per_row * size
+        pieces[piece] = array[row : row + 1, at : at + size]
+
+
 def logits_kernel(
     after, back, tokens, params, grads, dispatch, combine, left, right, local, mark,
     tokens_v, grads_v, wide, sems,
 ):
     del after, mark
     images, slots, _ = dispatch.shape
-    grads_copy = start_copy(grads, grads_v, sems.at[0])
-    tokens_copy = start_copy(tokens, tokens_v, sems.at[1])
+    halves = start_halves(tokens, tokens_v, sems)
+    grads_copy = start_copy(grads, grads_v, sems.at[2])
     load_rows(wide, back[...])
     stride = KINDS * images
     d_slot_in = []
@@ -328,32 +390,32 @@
         right[image, :slots, :] = d_slot_in[image]
         right[image, slots:, :] = params[...]
         left[image, :slots, :] = dispatch[image].astype(LOW)
+    parts = []
+    for copy, half in halves:
+        copy.wait()
+        for image in half:
+            weights = dispatch[image]
+            d_dispatch = dot(d_slot_in[image], tokens_v[image], 1, 1)
+            parts.append(
+                weights * (d_dispatch - jnp.sum(weights * d_dispatch, axis=1, keepdims=True))
+            )
     grads_copy.wait()
-    parts = []
+    total = None
     for image in range(images):
         slot_out = take(wide, KINDS * image, slots, stride).astype(LOW)
         weights = combine[image]
         d_combine = dot(slot_out, grads_v[image], 1, 1)
-        parts.append(
-            weights * (d_combine - jnp.sum(weights * d_combine, axis=0, keepdims=True))
-        )
-    tokens_copy.wait()
-    total = None
-    for image in range(images):
-        weights = dispatch[image]
-        d_dispatch = dot(d_slot_in[image], tokens_v[image], 1, 1)
         d_logits = parts[image] + weights * (
-            d_dispatch - jnp.sum(weights * d_dispatch, axis=1, keepdims=True)
+            d_combine - jnp.sum(weights * d_combine, axis=0, keepdims=True)
         )
         low = d_logits.astype(LOW)
         left[image, slots:, :] = low
         part = dot(low, tokens_v[image], 1, 0)
         total = part if image == 0 else total + part
-    for row in range(slots):
-        local[row] = total[row : row + 1, :]
-
-
-def logits_grads(after, back, tokens, params, grads, dispatch, combine):
+    put_pieces(local, total)
+
+
+def logits_grads(after, back, tokens, params, grads, dispatch, combine, pieces):
     images, length, width = tokens.shape
     slots = params.shape[0]
     return call(
@@ -365,7 +427,7 @@
         out_shape=(
             shaped((images, 2 * slots, length), LOW),
             shaped((images, 2 * slots, width), LOW),
-            shaped((slots, 1, width), WIDE),
+            shaped((pieces, 1, slots * width // pieces), WIDE),
             MARK,
         ),
         in_specs=[PLACE, WHOLE, PLACE, WHOLE, PLACE, WHOLE, WHOLE],
@@ -374,7 +436,7 @@
             pltpu.VMEM(tokens.shape, LOW),
             pltpu.VMEM(grads.shape, LOW),
             scratch_rows(back.shape),
-            pltpu.SemaphoreType.DMA((2,)),
+            pltpu.SemaphoreType.DMA((3,)),
         ],
     )(after, back, tokens, params, grads, dispatch, combine)
 
@@ -410,40 +472,38 @@
     out[...] = jnp.broadcast_to(total, out.shape)
 
 
-def share_of_sum(after, parts, copies):
-    shape = (copies, *parts.shape[1:])
+def share_of_sum(after, parts):
     return call(
         share_kernel,
         "share_of_sum",
         SHARED,
         parts.size,
         8 * parts.size,
-        out_shape=(shaped(shape, WIDE), MARK),
+        out_shape=(shaped(parts.shape, WIDE), MARK),
         in_specs=[PLACE, WHOLE],
         out_specs=(WHOLE, PLACE),
     )(after, parts)
 
 
-def total_kernel(shares, out):
-    slots = out.shape[0]
-    for slot in range(slots):
-        total = shares[slot]
-        for replica in range(1, shares.shape[0] // slots):
-            total = total + shares[replica * slots + slot]
-        out[slot : slot + 1, :] = total
-
-
-def total_of_shares(shares, shape):
-    return call(
-        total_kernel,
-        "total_of_shares",
-        SHARED,
-        shares.size,
-        8 * shares.size,
+def join_kernel(pieces, out):
+    size = pieces.shape[2]
+    per_row = out.shape[1] // size
+    for piece in range(pieces.shape[0]):
+        row, at = piece // per_row, piece % per_row * size
+        out[row : row + 1, at : at + size] = pieces[piece]
+
+
+def join(pieces, shape):
+    return call(
+        join_kernel,
+        "join_pieces",
+        SHARED,
+        0,
+        8 * pieces.size,
         out_shape=shaped(shape, WIDE),
         in_specs=[WHOLE],
         out_specs=WHOLE,
-    )(shares)
+    )(pieces)
 
 
 def copy_kernel(after, source, target):
@@ -475,22 +535,21 @@
     everyone = ("rep", "exp")
     mine = lax.axis_index("rep").astype(jnp.int32).reshape(1)
 
-    sent, dispatch, combine = gather(tokens, params, grad_out)
+    sent, dispatch, combine, after_gather = gather(tokens, params, grad_out)
     rows = exchange(sent, "exp")
-    back, acts, hidden, after_expert = expert(rows, *weights, 512)
+    first = fetch_first(after_gather, *weights, 256)
+    back, acts, hidden, after_expert = expert(rows, *first, *weights, 512)
     back = exchange(back, "exp")
     other_rows = lax.ppermute(
         copy_after(after_expert, rows), "rep", [(i, (i + 1) % replicas) for i in range(replicas)]
     )
     left, right, local, after_logits = logits_grads(
-        after_expert, back, tokens, params, grad_out, dispatch, combine
+        after_expert, back, tokens, params, grad_out, dispatch, combine, lax.axis_size(everyone)
     )
     other_acts, other_hidden, after_others = others_hidden(
         after_logits, other_rows, *weights, 512
     )
-    share, after_share = share_of_sum(
-        after_others, exchange(local, "exp"), lax.axis_size(everyone)
-    )
+    share, after_share = share_of_sum(after_others, exchange(local, everyone))
     grad_expert_in, grad_expert_out, _ = weight_grads(
         mine,
         after_share,
@@ -500,7 +559,7 @@
         5,
         replicas,
     )
-    grad_params = total_of_shares(exchange(share, everyone), params.shape).T
+    grad_params = join(exchange(share, everyone), params.shape).T
     grad_tokens = tokens_grads(after_share, left, right)
     return (
         grad_tokens,

time: 78.2 us -> 76.7 us (0.981)
  blocking collectives: 18.3 us -> 0 us
  waiting for transfers between devices: 12 us -> 21.5 us
  starting transfers between devices: 13.2 us -> 19.6 us
  Pallas kernels: 32.7 us -> 33.7 us
    all_to_all x1 -> x0, blocking collectives: 18.3 us -> none  [exchange(): return lax.all_to_all(rows, axes, split_axis=0, concat_axis=0, tiled=True)]
    all_to_all x3 -> x4, waiting for transfers between devices: 12 us -> 21.5 us  [exchange(): return lax.all_to_all(rows, axes, split_axis=0, concat_axis=0, tiled=True)]
    all_to_all x3 -> x4, starting transfers between devices: 11.7 us -> 18 us  [exchange(): return lax.all_to_all(rows, axes, split_axis=0, concat_axis=0, tiled=True)]
    pallas_call x3 -> x4, Pallas kernels: 16 us -> 16.8 us  [the longest x1 9.16 us: expert(): call(functools.partial(expert_kernel, chunks), 'expert_rows', 50 * 1024 *...]
  transfers between devices with their start and end apart: 4 -> 5, of which waited for: 3 -> 4; matrix products, arithmetic and copies ran while one was open for 0% -> 0% of each run, Pallas kernels for 24% -> 25%
where the time goes in v9:
time: 76.7 us; the launch traced here: 76.2 us
  Pallas kernels  33.7 us (44%)
  waiting for transfers between devices  21.5 us (28%)
  starting transfers between devices  19.6 us (26%)
  local copies, waits for them, and re-layouts  0.78 us (1%)
    all_to_all x4, waiting for transfers between devices, exchange(): return lax.all_to_all(rows, axes, split_axis=0, concat_axis=0, tiled=True)  21.5 us
    all_to_all x4, starting transfers between devices, exchange(): return lax.all_to_all(rows, axes, split_axis=0, concat_axis=0, tiled=True)  18 us
    pallas_call x1, Pallas kernels, expert(): call(functools.partial(expert_kernel, chunks), 'expert_rows', 50 * 1024 *...  9.16 us
    pallas_call x1, Pallas kernels, others_hidden(): call(functools.partial(others_kernel, chunks), 'others_hidden', SHARED, 6...  5.65 us
    pallas_call x1, Pallas kernels, logits_grads(): call(logits_kernel, 'logits_grads', SHARED, 6 * images * slots * length *...  4.96 us
    pallas_call x1, Pallas kernels, weight_grads(): call(weights_kernel, 'weight_grads', SHARED, 8 * count * size * width //...  4.52 us
    pallas_call x1, Pallas kernels, gather(): call(gather_kernel, 'gather_slots', SHARED, 6 * images * slots * length *...  3.91 us
    pallas_call x1, Pallas kernels, tokens_grads(): call(tokens_kernel, 'tokens_grads', SHARED, 2 * images * deep * length *...  2.77 us
  transfers between devices with their start and end apart: 5, of which 4 were waited for; matrix products, arithmetic and copies ran while one was open for 0% of the time, Pallas kernels for 25%

profile of v9, /device:TPU:0, one launch (start us, length us, event | category | flops | bytes accessed | tf_op | source)
XLA Modules:
  0.0 76.2 jit_solution(7924010253302824352)
XLA Ops:
  0.6 0.0 copy-start
  0.6 0.8 %copy-done = bf16[1280,16]{0,1:T(8,128)(2,1)S(1)} copy-done((bf16[1280,16]{0,1:T(8,128)(2,1)S(1)}, bf16[1280,16]{0,1:T(8,128)(2,1)}, u32[]{:S(2)}) %copy-start) | copy-done | bytes 40984
  1.4 3.9 %gather_slots.1 = (bf16[128,1280]{1,0:T(8,128)(2,1)}, f32[4,16,256]{2,1,0:T(8,128)S(1)}, f32[4,16,256]{2,1,0:T(8,128)S(1)}, f32[8,128]{1,0:T(8,128)S(1)}) custom-call(bf16[4,256,1280]{2,1,0:T(8,128)(2,1)} %tokens.3, bf16[16,1280]{1,0:T(8,128)(2,1)S(1)} %bitcast.15, bf16[4,256,1280]{2,1,0:T(8,128)(2,1)} %grads.3), custom_call_target="tpu_custom_call" | custom-call | flops 125829120 | bytes 5242880 | tf_op jit(solution)/shard_map/gather_slots/pallas_call | solution.py:136
  5.3 7.4 %all-to-all-start = ((bf16[16,8,1280]{2,1,0:T(8,128)(2,1)}), bf16[16,8,1280]{2,1,0:T(8,128)(2,1)S(1)}, u32[]{:S(2)}, u32[]{:S(2)}) async-start(bf16[16,8,1280]{2,1,0:T(8,128)(2,1)} %bitcast.1), calls=%async_computation | async-start | bytes 655360 | tf_op jit(solution)/shard_map/all_to_all | solution.py:528
  12.7 1.3 %fetch_first.1 = (bf16[1280,256]{1,0:T(8,128)(2,1)S(1)}, bf16[256,1280]{1,0:T(8,128)(2,1)S(1)}) custom-call(f32[8,128]{1,0:T(8,128)S(1)} %get-tuple-element.26.after, bf16[1280,2560]{1,0:T(8,128)(2,1)} %bitcast.17, bf16[2560,1280]{1,0:T(8,128)(2,1)} %bitcast.20), custom_call_target="tpu_custom_call" | custom-call | bytes 2621440 | tf_op jit(solution)/shard_map/fetch_first/pallas_call | solution.py:193
  14.1 9.8 %all-to-all-done = bf16[16,8,1280]{2,1,0:T(8,128)(2,1)S(1)} async-done(((bf16[16,8,1280]{2,1,0:T(8,128)(2,1)}), bf16[16,8,1280]{2,1,0:T(8,128)(2,1)S(1)}, u32[]{:S(2)}, u32[]{:S(2)}) %all-to-all-start) | async-done | bytes 327712 | tf_op jit(solution)/shard_map/all_to_all | solution.py:528
  23.8 0.0 copy-start.1
  23.8 9.2 %expert_rows.1 = (bf16[128,1280]{1,0:T(8,128)(2,1)}, bf16[64,2560]{1,0:T(8,128)(2,1)S(1)}, bf16[64,2560]{1,0:T(8,128)(2,1)S(1)}, f32[8,128]{1,0:T(8,128)S(1)}) custom-call(bf16[128,1280]{1,0:T(8,128)(2,1)S(1)} %bitcast.11, bf16[1280,256]{1,0:T(8,128)(2,1)S(1)} %get-tuple-element.27.first_in, bf16[256,1280]{1,0:T(8,128)(2,1)S(1)} %get-tuple-element.28.first_out, ...), custom_call_target="tpu_custom_call" | custom-call | flops 1677721600 | bytes 13107200 | tf_op jit(solution)/shard_map/expert_rows/pallas_call | solution.py:256
  33.0 3.6 %all-to-all-start.1 = ((bf16[16,8,1280]{2,1,0:T(8,128)(2,1)}), bf16[16,8,1280]{2,1,0:T(8,128)(2,1)S(1)}, u32[]{:S(2)}, u32[]{:S(2)}) async-start(bf16[16,8,1280]{2,1,0:T(8,128)(2,1)} %bitcast.5), calls=%async_computation.1 | async-start | bytes 655360 | tf_op jit(solution)/shard_map/all_to_all | solution.py:528
  36.6 1.6 %collective-permute-start = (bf16[128,1280]{1,0:T(8,128)(2,1)S(1)}, bf16[128,1280]{1,0:T(8,128)(2,1)S(1)}, u32[]{:S(2)}, u32[]{:S(2)}) collective-permute-start(bf16[128,1280]{1,0:T(8,128)(2,1)S(1)} %copy_after.1), channel_id=1, source_target_pairs={{0,16},{16,0},{1,17},{17,1},{2,18},{18,2},{3,19},{19,3},{4,20},{20... | collective-permute-start | bytes 983048 | tf_op jit(solution)/shard_map/ppermute | solution.py:543
  38.2 9.5 %all-to-all-done.1 = bf16[16,8,1280]{2,1,0:T(8,128)(2,1)S(1)} async-done(((bf16[16,8,1280]{2,1,0:T(8,128)(2,1)}), bf16[16,8,1280]{2,1,0:T(8,128)(2,1)S(1)}, u32[]{:S(2)}, u32[]{:S(2)}) %all-to-all-start.1) | async-done | bytes 327712 | tf_op jit(solution)/shard_map/all_to_all | solution.py:528
  47.6 0.0 copy-done.1
  47.6 5.0 %logits_grads.1 = (bf16[4,32,256]{2,1,0:T(8,128)(2,1)S(1)}, bf16[4,32,1280]{2,1,0:T(8,128)(2,1)S(1)}, f32[32,1,640]{2,1,0:T(1,128)}, f32[8,128]{1,0:T(8,128)S(1)}) custom-call(f32[8,128]{1,0:T(8,128)S(1)} %get-tuple-element.29.after, bf16[128,1280]{1,0:T(8,128)(2,1)S(1)} %bitcast.14, bf16[4,256,1280]{2,1,0:T(8,128)(2,1)} %tokens.3, ...), custom_call_target="tpu_custom_call" | custom-call | flops 125829120 | bytes 5242880 | tf_op jit(solution)/shard_map/logits_grads/pallas_call | solution.py:421
  52.6 3.2 %all-to-all-start.2 = ((f32[32,1,640]{2,1,0:T(1,128)}), f32[32,1,640]{2,1,0:T(1,128)S(1)}, u32[]{:S(2)}, u32[]{:S(2)}) async-start(f32[32,1,640]{2,1,0:T(1,128)} %get-tuple-element.35), calls=%async_computation.2 | async-start | bytes 163840 | tf_op jit(solution)/shard_map/all_to_all | solution.py:528
  55.8 0.0 collective-permute-done.rows.other_rows
  55.8 5.6 %others_hidden.1 = (bf16[64,2560]{1,0:T(8,128)(2,1)S(1)}, bf16[64,2560]{1,0:T(8,128)(2,1)S(1)}, f32[8,128]{1,0:T(8,128)S(1)}) custom-call(f32[8,128]{1,0:T(8,128)S(1)} %get-tuple-element.33.after, bf16[128,1280]{1,0:T(8,128)(2,1)S(1)} %collective-permute-done.rows.other_rows, bf16[1280,2560]{1,0:T(8,128)(2,1)} %bitcast.19, bf16[2560,1280]{1,0:T(8,128)(2,1)} %bitcast.22), custom_call_target="tpu_custom_call" | custom-call | flops 13421772800 | bytes 104857600 | tf_op jit(solution)/shard_map/others_hidden/pallas_call | solution.py:294
  61.4 1.9 %all-to-all-done.2.parts = f32[32,1,640]{2,1,0:T(1,128)S(1)} async-done(((f32[32,1,640]{2,1,0:T(1,128)}), f32[32,1,640]{2,1,0:T(1,128)S(1)}, u32[]{:S(2)}, u32[]{:S(2)}) %all-to-all-start.2) | async-done | bytes 81952 | tf_op jit(solution)/shard_map/all_to_all | solution.py:528
  63.4 0.7 share_of_sum.1
  64.1 3.9 %all-to-all-start.3 = ((f32[32,1,640]{2,1,0:T(1,128)}), f32[32,1,640]{2,1,0:T(1,128)S(1)}, u32[]{:S(2)}, u32[]{:S(2)}) async-start(f32[32,1,640]{2,1,0:T(1,128)} %get-tuple-element.39), calls=%async_computation.3 | async-start | bytes 163840 | tf_op jit(solution)/shard_map/all_to_all | solution.py:528
  68.0 2.8 %tokens_grads.1 = bf16[4,256,1280]{2,1,0:T(8,128)(2,1)} custom-call(f32[8,128]{1,0:T(8,128)S(1)} %get-tuple-element.36.after, bf16[4,32,256]{2,1,0:T(8,128)(2,1)S(1)} %get-tuple-element.37.left, bf16[4,32,1280]{2,1,0:T(8,128)(2,1)S(1)} %get-tuple-element.38.right), custom_call_target="tpu_custom_call" | custom-call | flops 83886080 | bytes 2621440 | tf_op jit(solution)/shard_map/tokens_grads/pallas_call | solution.py:452
  70.8 4.5 %weight_grads.1 = (bf16[640,2560]{1,0:T(8,128)(2,1)}, bf16[1280,1280]{1,0:T(8,128)(2,1)}, f32[8,128]{1,0:T(8,128)}) custom-call(s32[1]{0:T(128)} %bitcast.8.mine, f32[8,128]{1,0:T(8,128)S(1)} %get-tuple-element.36.after, bf16[128,1280]{1,0:T(8,128)(2,1)S(1)} %bitcast.13, bf16[128,1280]{1,0:T(8,128)(2,1)S(1)} %collective-permute-done.rows.other_rows, ...), custom_call_target="tpu_custom_call" | custom-call | flops 838860800 | bytes 6553600 | tf_op jit(solution)/shard_map/weight_grads/pallas_call | solution.py:340
  75.3 0.3 all-to-all-done.3.pieces
  75.6 0.7 join_pieces.1
  (1 shorter events, 0.0 us)
Async XLA Ops:
  0.6 0.8 %copy-start = (bf16[1280,16]{0,1:T(8,128)(2,1)S(1)}, bf16[1280,16]{0,1:T(8,128)(2,1)}, u32[]{:S(2)}) copy-start(bf16[1280,16]{0,1:T(8,128)(2,1)} %param.6) | copy-start | bytes 122884
  5.3 18.5 %all-to-all-start = ((bf16[16,8,1280]{2,1,0:T(8,128)(2,1)}), bf16[16,8,1280]{2,1,0:T(8,128)(2,1)S(1)}, u32[]{:S(2)}, u32[]{:S(2)}) async-start(bf16[16,8,1280]{2,1,0:T(8,128)(2,1)} %bitcast.1), calls=%async_computation | async-start | bytes 655360 | tf_op jit(solution)/shard_map/all_to_all | solution.py:528
  23.8 23.8 %copy-start.1 = (bf16[1280,16]{0,1:T(8,128)(2,1)S(1)}, bf16[1280,16]{0,1:T(8,128)(2,1)}, u32[]{:S(2)}) copy-start(bf16[1280,16]{0,1:T(8,128)(2,1)} %param.6) | copy-start | bytes 122884
  33.0 14.6 %all-to-all-start.1 = ((bf16[16,8,1280]{2,1,0:T(8,128)(2,1)}), bf16[16,8,1280]{2,1,0:T(8,128)(2,1)S(1)}, u32[]{:S(2)}, u32[]{:S(2)}) async-start(bf16[16,8,1280]{2,1,0:T(8,128)(2,1)} %bitcast.5), calls=%async_computation.1 | async-start | bytes 655360 | tf_op jit(solution)/shard_map/all_to_all | solution.py:528
  36.6 19.2 %collective-permute-start = (bf16[128,1280]{1,0:T(8,128)(2,1)S(1)}, bf16[128,1280]{1,0:T(8,128)(2,1)S(1)}, u32[]{:S(2)}, u32[]{:S(2)}) collective-permute-start(bf16[128,1280]{1,0:T(8,128)(2,1)S(1)} %copy_after.1), channel_id=1, source_target_pairs={{0,16},{16,0},{1,17},{17,1},{2,18},{18,2},{3,19},{19,3},{4,20},{20... | collective-permute-start | bytes 983048 | tf_op jit(solution)/shard_map/ppermute | solution.py:543
  52.6 10.8 %all-to-all-start.2 = ((f32[32,1,640]{2,1,0:T(1,128)}), f32[32,1,640]{2,1,0:T(1,128)S(1)}, u32[]{:S(2)}, u32[]{:S(2)}) async-start(f32[32,1,640]{2,1,0:T(1,128)} %get-tuple-element.35), calls=%async_computation.2 | async-start | bytes 163840 | tf_op jit(solution)/shard_map/all_to_all | solution.py:528
  64.1 11.5 %all-to-all-start.3 = ((f32[32,1,640]{2,1,0:T(1,128)}), f32[32,1,640]{2,1,0:T(1,128)S(1)}, u32[]{:S(2)}, u32[]{:S(2)}) async-start(f32[32,1,640]{2,1,0:T(1,128)} %get-tuple-element.39), calls=%async_computation.3 | async-start | bytes 163840 | tf_op jit(solution)/shard_map/all_to_all | solution.py:528

commit v10 on v9

--- a/solution.py
+++ b/solution.py
@@ -305,73 +305,92 @@
     )(after, rows, w_in, w_out)
 
 
-def weights_kernel(
-    mine, after, rows, other_rows, acts, other_acts, hidden, other_hidden, grad_in, grad_out, mark,
-    wide, grads, turned,
-):
-    del after, mark
+def grad_in_kernel(mine, rows, other_rows, hidden, other_hidden, grad, mark, wide, turned):
+    del mark
     count = rows.shape[0] // KINDS
 
     @pl.when(pl.program_id(0) == 0)
     def _():
-        left, right = [], []
+        left = []
         tiles = turned.shape[0] // LANES
         for source in (rows, other_rows):
             load_rows(wide, source[...])
             left.append(take(wide, 0, count, KINDS, mine[0] * tiles, tiles))
-            right.append(take(wide, 1, count, KINDS))
         turned[...] = jnp.concatenate(left, axis=0).T.astype(LOW)
-        grads[...] = jnp.concatenate(right, axis=0).astype(LOW)
 
     all_hidden = jnp.concatenate([hidden[...], other_hidden[...]], axis=0)
-    grad_in[...] = dot(turned[...], all_hidden, 1, 0).astype(LOW)
-    all_acts = jnp.concatenate([acts[...], other_acts[...]], axis=0)
-    grad_out[...] = dot(all_acts, grads[...], 0, 0).astype(LOW)
-
-
-def weight_grads(mine, after, rows, acts, hidden, steps, replicas):
+    grad[...] = dot(turned[...], all_hidden, 1, 0).astype(LOW)
+
+
+def grad_expert_in(mine, rows, hidden, steps, replicas):
     total, width = rows[0].shape
-    size = acts[0].shape[1]
+    size = hidden[0].shape[1]
     count = total // KINDS
-    in_tile, out_tile = size // steps, size // replicas // steps
     whole_rows = pl.BlockSpec((total, width), lambda i, mine: (0, 0))
-    acts_spec = pl.BlockSpec((count, out_tile), lambda i, mine: (0, mine[0] * steps + i))
-    hidden_spec = pl.BlockSpec((count, in_tile), lambda i, mine: (0, i))
-    return call(
-        weights_kernel,
-        "weight_grads",
-        SHARED,
-        8 * count * size * width // replicas,
-        4 * size * width // replicas,
+    units = pl.BlockSpec((count, size // steps), lambda i, mine: (0, i))
+    return call(
+        grad_in_kernel,
+        "grad_expert_in",
+        SHARED,
+        4 * count * size * width // replicas,
+        2 * size * width // replicas,
         grid_spec=pltpu.PrefetchScalarGridSpec(
             num_scalar_prefetch=1,
             grid=(steps,),
-            in_specs=[PLACE] + [whole_rows] * 2 + [acts_spec] * 2 + [hidden_spec] * 2,
+            in_specs=[whole_rows] * 2 + [units] * 2,
             out_specs=(
-                pl.BlockSpec((width // replicas, in_tile), lambda i, mine: (0, i)),
-                pl.BlockSpec((out_tile, width), lambda i, mine: (i, 0)),
+                pl.BlockSpec((width // replicas, size // steps), lambda i, mine: (0, i)),
                 PLACE,
             ),
             scratch_shapes=[
                 scratch_rows((total, width)),
-                pltpu.VMEM((2 * count, width), LOW),
                 pltpu.VMEM((width // replicas, 2 * count), LOW),
             ],
         ),
-        out_shape=(
-            shaped((width // replicas, size), LOW),
-            shaped((size // replicas, width), LOW),
-            MARK,
+        out_shape=(shaped((width // replicas, size), LOW), MARK),
+    )(mine, *rows, *hidden)
+
+
+def grad_out_kernel(mine, after, rows, other_rows, acts, other_acts, grad, wide, grads):
+    del mine, after
+    count = rows.shape[0] // KINDS
+
+    @pl.when(pl.program_id(0) == 0)
+    def _():
+        right = []
+        for source in (rows, other_rows):
+            load_rows(wide, source[...])
+            right.append(take(wide, 1, count, KINDS))
+        grads[...] = jnp.concatenate(right, axis=0).astype(LOW)
+
+    all_acts = jnp.concatenate([acts[...], other_acts[...]], axis=0)
+    grad[...] = dot(all_acts, grads[...], 0, 0).astype(LOW)
+
+
+def grad_expert_out(mine, after, rows, acts, steps, replicas):
+    total, width = rows[0].shape
+    size = acts[0].shape[1] // replicas
+    count = total // KINDS
+    whole_rows = pl.BlockSpec((total, width), lambda i, mine: (0, 0))
+    units = pl.BlockSpec((count, size // steps), lambda i, mine: (0, mine[0] * steps + i))
+    return call(
+        grad_out_kernel,
+        "grad_expert_out",
+        SHARED,
+        4 * count * size * width,
+        2 * size * width,
+        grid_spec=pltpu.PrefetchScalarGridSpec(
+            num_scalar_prefetch=1,
+            grid=(steps,),
+            in_specs=[PLACE] + [whole_rows] * 2 + [units] * 2,
+            out_specs=pl.BlockSpec((size // steps, width), lambda i, mine: (i, 0)),
+            scratch_shapes=[
+                scratch_rows((total, width)),
+                pltpu.VMEM((2 * count, width), LOW),
+            ],
         ),
-    )(mine, after, *rows, *acts, *hidden)
-
-
-def put_pieces(pieces, array):
-    size = pieces.shape[2]
-    per_row = array.shape[1] // size
-    for piece in range(pieces.shape[0]):
-        row, at = piece // per_row, piece % per_row * size
-        pieces[piece] = array[row : row + 1, at : at + size]
+        out_shape=shaped((size, width), LOW),
+    )(mine, after, *rows, *acts)
 
 
 def logits_kernel(
@@ -412,10 +431,10 @@
         left[image, slots:, :] = low
         part = dot(low, tokens_v[image], 1, 0)
         total = part if image == 0 else total + part
-    put_pieces(local, total)
-
-
-def logits_grads(after, back, tokens, params, grads, dispatch, combine, pieces):
+    local[...] = total.astype(LOW)
+
+
+def logits_grads(after, back, tokens, params, grads, dispatch, combine):
     images, length, width = tokens.shape
     slots = params.shape[0]
     return call(
@@ -427,7 +446,7 @@
         out_shape=(
             shaped((images, 2 * slots, length), LOW),
             shaped((images, 2 * slots, width), LOW),
-            shaped((pieces, 1, slots * width // pieces), WIDE),
+            shaped(params.shape, LOW),
             MARK,
         ),
         in_specs=[PLACE, WHOLE, PLACE, WHOLE, PLACE, WHOLE, WHOLE],
@@ -466,64 +485,6 @@
     )(after, left, right)
 
 
-def share_kernel(after, parts, out, mark):
-    del after, mark
-    total = jnp.sum(parts[...], axis=0, keepdims=True)
-    out[...] = jnp.broadcast_to(total, out.shape)
-
-
-def share_of_sum(after, parts):
-    return call(
-        share_kernel,
-        "share_of_sum",
-        SHARED,
-        parts.size,
-        8 * parts.size,
-        out_shape=(shaped(parts.shape, WIDE), MARK),
-        in_specs=[PLACE, WHOLE],
-        out_specs=(WHOLE, PLACE),
-    )(after, parts)
-
-
-def join_kernel(pieces, out):
-    size = pieces.shape[2]
-    per_row = out.shape[1] // size
-    for piece in range(pieces.shape[0]):
-        row, at = piece // per_row, piece % per_row * size
-        out[row : row + 1, at : at + size] = pieces[piece]
-
-
-def join(pieces, shape):
-    return call(
-        join_kernel,
-        "join_pieces",
-        SHARED,
-        0,
-        8 * pieces.size,
-        out_shape=shaped(shape, WIDE),
-        in_specs=[WHOLE],
-        out_specs=WHOLE,
-    )(pieces)
-
-
-def copy_kernel(after, source, target):
-    del after
-    target[...] = source[...]
-
-
-def copy_after(after, array):
-    return call(
-        copy_kernel,
-        "copy_after",
-        SHARED,
-        0,
-        4 * array.size,
-        out_shape=shaped(array.shape, array.dtype),
-        in_specs=[PLACE, WHOLE],
-        out_specs=WHOLE,
-    )(after, array)
-
-
 def exchange(rows, axes):
     return lax.all_to_all(rows, axes, split_axis=0, concat_axis=0, tiled=True)
 
@@ -532,41 +493,27 @@
     params = slot_params.T
     weights = (expert_in[0], expert_out[0])
     replicas = lax.axis_size("rep")
-    everyone = ("rep", "exp")
     mine = lax.axis_index("rep").astype(jnp.int32).reshape(1)
 
     sent, dispatch, combine, after_gather = gather(tokens, params, grad_out)
     rows = exchange(sent, "exp")
     first = fetch_first(after_gather, *weights, 256)
+    other_rows = lax.ppermute(rows, "rep", [(i, (i + 1) % replicas) for i in range(replicas)])
     back, acts, hidden, after_expert = expert(rows, *first, *weights, 512)
     back = exchange(back, "exp")
-    other_rows = lax.ppermute(
-        copy_after(after_expert, rows), "rep", [(i, (i + 1) % replicas) for i in range(replicas)]
+    other_acts, other_hidden, _ = others_hidden(after_expert, other_rows, *weights, 512)
+    grad_in, after_grad = grad_expert_in(
+        mine, (rows, other_rows), (hidden, other_hidden), 5, replicas
     )
     left, right, local, after_logits = logits_grads(
-        after_expert, back, tokens, params, grad_out, dispatch, combine, lax.axis_size(everyone)
-    )
-    other_acts, other_hidden, after_others = others_hidden(
-        after_logits, other_rows, *weights, 512
-    )
-    share, after_share = share_of_sum(after_others, exchange(local, everyone))
-    grad_expert_in, grad_expert_out, _ = weight_grads(
-        mine,
-        after_share,
-        (rows, other_rows),
-        (acts, other_acts),
-        (hidden, other_hidden),
-        5,
-        replicas,
-    )
-    grad_params = join(exchange(share, everyone), params.shape).T
-    grad_tokens = tokens_grads(after_share, left, right)
-    return (
-        grad_tokens,
-        grad_params,
-        grad_expert_in[None],
-        grad_expert_out[None],
-    )
+        after_grad, back, tokens, params, grad_out, dispatch, combine
+    )
+    grad_params = lax.psum(local, ("rep", "exp")).astype(WIDE).T
+    grad_outer = grad_expert_out(
+        mine, after_logits, (rows, other_rows), (acts, other_acts), 5, replicas
+    )
+    grad_tokens = tokens_grads(after_logits, left, right)
+    return (grad_tokens, grad_params, grad_in[None], grad_outer[None])
 
 
 def solution(mesh):

time: 76.7 us -> 100 us (1.30)
  blocking collectives: 0 us -> 57 us
  waiting for transfers between devices: 21.5 us -> 1.64 us
  starting transfers between devices: 19.6 us -> 5.05 us
    psum x0 -> x1, blocking collectives: none -> 38.7 us  [body(): grad_params = lax.psum(local, ('rep', 'exp')).astype(WIDE).T]
    all_to_all x4 -> x1, waiting for transfers between devices: 21.5 us -> 1.63 us  [exchange(): return lax.all_to_all(rows, axes, split_axis=0, concat_axis=0, tiled=True)]
    all_to_all x0 -> x1, blocking collectives: none -> 18.3 us  [exchange(): return lax.all_to_all(rows, axes, split_axis=0, concat_axis=0, tiled=True)]
    all_to_all x4 -> x1, starting transfers between devices: 18 us -> 3.56 us  [exchange(): return lax.all_to_all(rows, axes, split_axis=0, concat_axis=0, tiled=True)]
    pallas_call x4 -> x2, Pallas kernels: 5.9 us -> 7.45 us  [the longest x1 3.74 us: grad_expert_in(): call(grad_in_kernel, 'grad_expert_in', SHARED, 4 * count * size * width /...]
  transfers between devices with their start and end apart: 5 -> 2, of which waited for: 4 -> 1; matrix products, arithmetic and copies ran while one was open for 0% -> 0% of each run, Pallas kernels for 25% -> 20%
where the time goes in v10:
time: 100 us; the launch traced here: 99.6 us
  blocking collectives  57 us (57%)
  Pallas kernels  33.8 us (34%)
  starting transfers between devices  5.05 us (5%)
  waiting for transfers between devices  1.64 us (2%)
    psum x1, blocking collectives, body(): grad_params = lax.psum(local, ('rep', 'exp')).astype(WIDE).T  38.7 us
    all_to_all x1, blocking collectives, exchange(): return lax.all_to_all(rows, axes, split_axis=0, concat_axis=0, tiled=True)  18.3 us
    pallas_call x1, Pallas kernels, expert(): call(functools.partial(expert_kernel, chunks), 'expert_rows', 50 * 1024 *...  9.18 us
    pallas_call x1, Pallas kernels, others_hidden(): call(functools.partial(others_kernel, chunks), 'others_hidden', SHARED, 6...  5.66 us
    pallas_call x1, Pallas kernels, logits_grads(): call(logits_kernel, 'logits_grads', SHARED, 6 * images * slots * length *...  4.32 us
    pallas_call x1, Pallas kernels, grad_expert_in(): call(grad_in_kernel, 'grad_expert_in', SHARED, 4 * count * size * width /...  3.74 us
    pallas_call x1, Pallas kernels, grad_expert_out(): call(grad_out_kernel, 'grad_expert_out', SHARED, 4 * count * size * width...  3.71 us
    all_to_all x1, starting transfers between devices, exchange(): return lax.all_to_all(rows, axes, split_axis=0, concat_axis=0, tiled=True)  3.56 us
  transfers between devices with their start and end apart: 2, of which 1 were waited for; matrix products, arithmetic and copies ran while one was open for 0% of the time, Pallas kernels for 20%

profile of v10, /device:TPU:0, one launch (start us, length us, event | category | flops | bytes accessed | tf_op | source)
XLA Modules:
  0.0 99.6 jit_solution(6884924893549256919)
XLA Ops:
  0.6 0.0 copy-start
  0.6 0.8 copy-done
  1.4 3.2 %gather_slots.1 = (bf16[128,1280]{1,0:T(8,128)(2,1)S(1)}, f32[4,16,256]{2,1,0:T(8,128)S(1)}, f32[4,16,256]{2,1,0:T(8,128)S(1)}, f32[8,128]{1,0:T(8,128)S(1)}) custom-call(bf16[4,256,1280]{2,1,0:T(8,128)(2,1)} %tokens.3, bf16[16,1280]{1,0:T(8,128)(2,1)S(1)} %bitcast.17, bf16[4,256,1280]{2,1,0:T(8,128)(2,1)} %grads.3), custom_call_target="tpu_custom_call" | custom-call | flops 125829120 | bytes 5242880 | tf_op jit(solution)/shard_map/gather_slots/pallas_call | solution.py:136
  4.6 18.3 %all_to_all.22 = bf16[16,8,1280]{2,1,0:T(8,128)(2,1)S(1)} all-to-all(bf16[16,8,1280]{2,1,0:T(8,128)(2,1)S(1)} %bitcast.16), channel_id=1, replica_groups=mesh['rep'=2,'exp'=16] {'exp'}, dimensions={0} | all-to-all | bytes 655360 | tf_op jit(solution)/shard_map/all_to_all | solution.py:489
  22.9 1.5 %collective-permute-start = (bf16[128,1280]{1,0:T(8,128)(2,1)S(1)}, bf16[128,1280]{1,0:T(8,128)(2,1)S(1)}, u32[]{:S(2)}, u32[]{:S(2)}) collective-permute-start(bf16[128,1280]{1,0:T(8,128)(2,1)S(1)} %bitcast.11), channel_id=1, source_target_pairs={{0,16},{16,0},{1,17},{17,1},{2,18},{18,2},{3,19},{19,3},{4,20},{20... | collective-permute-start | bytes 983048 | tf_op jit(solution)/shard_map/ppermute | solution.py:501
  24.4 1.3 %fetch_first.1 = (bf16[1280,256]{1,0:T(8,128)(2,1)S(1)}, bf16[256,1280]{1,0:T(8,128)(2,1)S(1)}) custom-call(f32[8,128]{1,0:T(8,128)S(1)} %get-tuple-element.23.after, bf16[1280,2560]{1,0:T(8,128)(2,1)} %bitcast.20, bf16[2560,1280]{1,0:T(8,128)(2,1)} %bitcast.23), custom_call_target="tpu_custom_call" | custom-call | bytes 2621440 | tf_op jit(solution)/shard_map/fetch_first/pallas_call | solution.py:193
  25.7 9.2 %expert_rows.1 = (bf16[128,1280]{1,0:T(8,128)(2,1)}, bf16[64,2560]{1,0:T(8,128)(2,1)S(1)}, bf16[64,2560]{1,0:T(8,128)(2,1)S(1)}, f32[8,128]{1,0:T(8,128)S(1)}) custom-call(bf16[128,1280]{1,0:T(8,128)(2,1)S(1)} %bitcast.12, bf16[1280,256]{1,0:T(8,128)(2,1)S(1)} %get-tuple-element.24.first_in, bf16[256,1280]{1,0:T(8,128)(2,1)S(1)} %get-tuple-element.25.first_out, ...), custom_call_target="tpu_custom_call" | custom-call | flops 1677721600 | bytes 13107200 | tf_op jit(solution)/shard_map/expert_rows/pallas_call | solution.py:256
  34.9 3.6 %all-to-all-start.1 = ((bf16[16,8,1280]{2,1,0:T(8,128)(2,1)}), bf16[16,8,1280]{2,1,0:T(8,128)(2,1)S(1)}, u32[]{:S(2)}, u32[]{:S(2)}) async-start(bf16[16,8,1280]{2,1,0:T(8,128)(2,1)} %bitcast.6), calls=%async_computation.1 | async-start | bytes 655360 | tf_op jit(solution)/shard_map/all_to_all | solution.py:489
  38.5 0.0 collective-permute-done.rows.other_rows
  38.5 0.0 copy-start.1
  38.5 5.7 %others_hidden.1 = (bf16[64,2560]{1,0:T(8,128)(2,1)S(1)}, bf16[64,2560]{1,0:T(8,128)(2,1)S(1)}, f32[8,128]{1,0:T(8,128)}) custom-call(f32[8,128]{1,0:T(8,128)S(1)} %get-tuple-element.27.after, bf16[128,1280]{1,0:T(8,128)(2,1)S(1)} %collective-permute-done.rows.other_rows, bf16[1280,2560]{1,0:T(8,128)(2,1)} %bitcast.22, bf16[2560,1280]{1,0:T(8,128)(2,1)} %bitcast.25), custom_call_target="tpu_custom_call" | custom-call | flops 13421772800 | bytes 104857600 | tf_op jit(solution)/shard_map/others_hidden/pallas_call | solution.py:294
  44.1 3.7 %grad_expert_in.1 = (bf16[640,2560]{1,0:T(8,128)(2,1)}, f32[8,128]{1,0:T(8,128)S(1)}) custom-call(s32[1]{0:T(128)} %bitcast.mine, bf16[128,1280]{1,0:T(8,128)(2,1)S(1)} %bitcast.13, bf16[128,1280]{1,0:T(8,128)(2,1)S(1)} %collective-permute-done.rows.other_rows, bf16[64,2560]{1,0:T(8,128)(2,1)S(1)} %get-tuple-element.26.hidden, ...), custom_call_target="tpu_custom_call" | custom-call | flops 419430400 | bytes 3276800 | tf_op jit(solution)/shard_map/grad_expert_in/pallas_call | solution.py:331
  47.9 1.6 %all-to-all-done.1 = bf16[16,8,1280]{2,1,0:T(8,128)(2,1)S(1)} async-done(((bf16[16,8,1280]{2,1,0:T(8,128)(2,1)}), bf16[16,8,1280]{2,1,0:T(8,128)(2,1)S(1)}, u32[]{:S(2)}, u32[]{:S(2)}) %all-to-all-start.1) | async-done | bytes 327712 | tf_op jit(solution)/shard_map/all_to_all | solution.py:489
  49.5 0.0 copy-done.1
  49.5 4.3 %logits_grads.1 = (bf16[4,32,256]{2,1,0:T(8,128)(2,1)S(1)}, bf16[4,32,1280]{2,1,0:T(8,128)(2,1)S(1)}, bf16[16,1280]{1,0:T(8,128)(2,1)S(1)}, f32[8,128]{1,0:T(8,128)S(1)}) custom-call(f32[8,128]{1,0:T(8,128)S(1)} %get-tuple-element.29.after, bf16[128,1280]{1,0:T(8,128)(2,1)S(1)} %bitcast.15, bf16[4,256,1280]{2,1,0:T(8,128)(2,1)} %tokens.3, ...), custom_call_target="tpu_custom_call" | custom-call | flops 125829120 | bytes 5242880 | tf_op jit(solution)/shard_map/logits_grads/pallas_call | solution.py:440
  53.8 38.7 %psum.7 = bf16[1280,16]{0,1:T(8,128)(2,1)S(1)} all-reduce(bf16[1280,16]{0,1:T(8,128)(2,1)S(1)} %bitcast.19), channel_id=1, replica_groups=mesh['rep'=2,'exp'=16] {'rep','exp'}, use_global_device_ids=true, to_apply=%region_0.0 | all-reduce | flops 20480 | bytes 81920 | tf_op jit(solution)/shard_map/psum | solution.py:511
  92.5 0.6 transpose.11
  93.2 2.7 %tokens_grads.1 = bf16[4,256,1280]{2,1,0:T(8,128)(2,1)} custom-call(f32[8,128]{1,0:T(8,128)S(1)} %get-tuple-element.33.after, bf16[4,32,256]{2,1,0:T(8,128)(2,1)S(1)} %get-tuple-element.34.left, bf16[4,32,1280]{2,1,0:T(8,128)(2,1)S(1)} %get-tuple-element.35.right), custom_call_target="tpu_custom_call" | custom-call | flops 83886080 | bytes 2621440 | tf_op jit(solution)/shard_map/tokens_grads/pallas_call | solution.py:471
  95.9 3.7 %grad_expert_out.1 = bf16[1280,1280]{1,0:T(8,128)(2,1)} custom-call(s32[1]{0:T(128)} %bitcast.mine, f32[8,128]{1,0:T(8,128)S(1)} %get-tuple-element.33.after, bf16[128,1280]{1,0:T(8,128)(2,1)S(1)} %bitcast.14, bf16[128,1280]{1,0:T(8,128)(2,1)S(1)} %collective-permute-done.rows.other_rows, bf16[64,2560]{1,0:T(8,128)(2,1)S(1)} %get-tuple-element.38.acts, ...), custom_call_target="tpu_custom_call" | custom-call | flops 419430400 | bytes 3276800 | tf_op jit(solution)/shard_map/grad_expert_out/pallas_call | solution.py:376
Async XLA Ops:
  0.6 0.8 copy-start
  22.9 15.6 %collective-permute-start = (bf16[128,1280]{1,0:T(8,128)(2,1)S(1)}, bf16[128,1280]{1,0:T(8,128)(2,1)S(1)}, u32[]{:S(2)}, u32[]{:S(2)}) collective-permute-start(bf16[128,1280]{1,0:T(8,128)(2,1)S(1)} %bitcast.11), channel_id=1, source_target_pairs={{0,16},{16,0},{1,17},{17,1},{2,18},{18,2},{3,19},{19,3},{4,20},{20... | collective-permute-start | bytes 983048 | tf_op jit(solution)/shard_map/ppermute | solution.py:501
  34.9 14.6 %all-to-all-start.1 = ((bf16[16,8,1280]{2,1,0:T(8,128)(2,1)}), bf16[16,8,1280]{2,1,0:T(8,128)(2,1)S(1)}, u32[]{:S(2)}, u32[]{:S(2)}) async-start(bf16[16,8,1280]{2,1,0:T(8,128)(2,1)} %bitcast.6), calls=%async_computation.1 | async-start | bytes 655360 | tf_op jit(solution)/shard_map/all_to_all | solution.py:489
  38.5 11.1 %copy-start.1 = (bf16[1280,16]{0,1:T(8,128)(2,1)S(1)}, bf16[1280,16]{0,1:T(8,128)(2,1)}, u32[]{:S(2)}) copy-start(bf16[1280,16]{0,1:T(8,128)(2,1)} %param.6) | copy-start | bytes 122884

commit v11 on v9

--- a/solution.py
+++ b/solution.py
@@ -100,9 +100,8 @@
 
 
 def gather_kernel(
-    tokens, params, grads, sent, dispatch, combine, mark, tokens_v, grads_v, rows, sems
+    tokens, params, grads, sent, dispatch, combine, tokens_v, grads_v, rows, sems
 ):
-    del mark
     images = tokens.shape[0]
     slots = params.shape[0]
     stride = KINDS * images
@@ -140,9 +139,9 @@
         6 * images * slots * length * width,
         4 * images * length * width,
         2 * images * slots * length,
-        out_shape=(shaped(rows, LOW), weights, weights, MARK),
+        out_shape=(shaped(rows, LOW), weights, weights),
         in_specs=[PLACE, WHOLE, PLACE],
-        out_specs=(WHOLE, WHOLE, WHOLE, PLACE),
+        out_specs=(WHOLE, WHOLE, WHOLE),
         scratch_shapes=[
             pltpu.VMEM(tokens.shape, LOW),
             pltpu.VMEM(grads.shape, LOW),
@@ -177,35 +176,8 @@
     ]
 
 
-def fetch_kernel(after, w_in, w_out, first_in, first_out, sems):
-    del after
-    units = slice(0, first_out.shape[0])
-    copies = (
-        start_copy(w_in.at[:, units], first_in, sems.at[0]),
-        start_copy(w_out.at[units, :], first_out, sems.at[1]),
-    )
-    for copy in copies:
-        copy.wait()
-
-
-def fetch_first(after, w_in, w_out, count):
-    width = w_in.shape[0]
-    return call(
-        fetch_kernel,
-        "fetch_first",
-        SHARED,
-        0,
-        8 * count * width,
-        out_shape=(shaped((width, count), LOW), shaped((count, width), LOW)),
-        in_specs=[PLACE] * 3,
-        out_specs=(WHOLE,) * 2,
-        scratch_shapes=[pltpu.SemaphoreType.DMA((2,))],
-    )(after, w_in, w_out)
-
-
 def expert_kernel(
-    chunks, rows, first_in, first_out, w_in, w_out, back, acts, hidden, mark,
-    w_in_v, w_out_v, sems, wide,
+    chunks, rows, w_in, w_out, back, acts, hidden, mark, w_in_v, w_out_v, sems, wide
 ):
     del mark
     copies = start_weights(w_in, w_out, w_in_v, w_out_v, sems, chunks)
@@ -213,58 +185,46 @@
     load_rows(wide, rows[...])
     rows_in = take(wide, 0, count, KINDS).astype(LOW)
     rows_grad = take(wide, 1, count, KINDS).astype(LOW)
-
-    def first_products(weight_in, weight_out):
-        return dot(rows_in, weight_in, 1, 0), dot(rows_grad, weight_out, 1, 1)
-
-    def second_products(held, weight_in, weight_out):
-        return dot(held[0], weight_out, 1, 0), dot(held[1], weight_in, 1, 1)
-
-    def hold(preact, d_acts, units):
-        values, slope = gelu_parts(preact)
-        held = (values.astype(LOW), (d_acts * slope).astype(LOW))
-        acts[:, units], hidden[:, units] = held
-        return held
-
-    held = hold(
-        *first_products(first_in[...], first_out[...]), slice(0, first_out.shape[0])
-    )
-    out, d_in = second_products(held, first_in[...], first_out[...])
-    before = None
+    out = d_in = held = before = None
     for pair, units in zip([*copies, None], [*chunks, None]):
         if pair is not None:
             for copy in pair:
                 copy.wait()
-            products = first_products(w_in_v[:, units], w_out_v[units, :])
+            preact = dot(rows_in, w_in_v[:, units], 1, 0)
+            d_acts = dot(rows_grad, w_out_v[units, :], 1, 1)
         if before is not None:
-            parts = second_products(held, w_in_v[:, before], w_out_v[before, :])
-            out, d_in = out + parts[0], d_in + parts[1]
+            out_part = dot(held[0], w_out_v[before, :], 1, 0)
+            d_in_part = dot(held[1], w_in_v[:, before], 1, 1)
+            out = out_part if out is None else out + out_part
+            d_in = d_in_part if d_in is None else d_in + d_in_part
         if pair is not None:
-            held = hold(*products, units)
+            values, slope = gelu_parts(preact)
+            held = (values.astype(LOW), (d_acts * slope).astype(LOW))
+            acts[:, units], hidden[:, units] = held
         before = units
     put(wide, 0, count, KINDS, out)
     put(wide, 1, count, KINDS, d_in)
     back[...] = packed(wide)
 
 
-def expert(rows, first_in, first_out, w_in, w_out, tile):
+def expert(rows, w_in, w_out, tile):
     total, width = rows.shape
     hidden = w_in.shape[1]
     count = total // KINDS
     kept = shaped((count, hidden), LOW)
-    chunks = chunks_of(first_out.shape[0], hidden, tile)
+    chunks = chunks_of(0, hidden, tile)
     return call(
         functools.partial(expert_kernel, chunks),
         "expert_rows",
-        50 * 1024 * 1024,
+        SHARED,
         8 * count * hidden * width,
         4 * hidden * width,
         count * hidden,
         out_shape=(shaped(rows.shape, LOW), kept, kept, MARK),
-        in_specs=[WHOLE, WHOLE, WHOLE, PLACE, PLACE],
+        in_specs=[WHOLE, PLACE, PLACE],
         out_specs=(WHOLE, WHOLE, WHOLE, PLACE),
         scratch_shapes=[*weight_scratch(width, hidden, chunks), scratch_rows(rows.shape)],
-    )(rows, first_in, first_out, w_in, w_out)
+    )(rows, w_in, w_out)
 
 
 def others_kernel(
@@ -364,14 +324,6 @@
             MARK,
         ),
     )(mine, after, *rows, *acts, *hidden)
-
-
-def put_pieces(pieces, array):
-    size = pieces.shape[2]
-    per_row = array.shape[1] // size
-    for piece in range(pieces.shape[0]):
-        row, at = piece // per_row, piece % per_row * size
-        pieces[piece] = array[row : row + 1, at : at + size]
 
 
 def logits_kernel(
@@ -412,10 +364,10 @@
         left[image, slots:, :] = low
         part = dot(low, tokens_v[image], 1, 0)
         total = part if image == 0 else total + part
-    put_pieces(local, total)
-
-
-def logits_grads(after, back, tokens, params, grads, dispatch, combine, pieces):
+    local[...] = total.astype(LOW)
+
+
+def logits_grads(after, back, tokens, params, grads, dispatch, combine):
     images, length, width = tokens.shape
     slots = params.shape[0]
     return call(
@@ -427,7 +379,7 @@
         out_shape=(
             shaped((images, 2 * slots, length), LOW),
             shaped((images, 2 * slots, width), LOW),
-            shaped((pieces, 1, slots * width // pieces), WIDE),
+            shaped(params.shape, LOW),
             MARK,
         ),
         in_specs=[PLACE, WHOLE, PLACE, WHOLE, PLACE, WHOLE, WHOLE],
@@ -441,8 +393,8 @@
     )(after, back, tokens, params, grads, dispatch, combine)
 
 
-def tokens_kernel(after, left, right, out):
-    del after
+def tokens_kernel(after, left, right, out, mark):
+    del after, mark
     out[0] = dot(left[0], right[0], 0, 0).astype(LOW)
 
 
@@ -456,54 +408,43 @@
         2 * images * deep * length * width,
         2 * images * length * width,
         grid=(images,),
-        out_shape=shaped((images, length, width), LOW),
+        out_shape=(shaped((images, length, width), LOW), MARK),
         in_specs=[
             PLACE,
             pl.BlockSpec((1, deep, length), lambda i: (i, 0, 0)),
             pl.BlockSpec((1, deep, width), lambda i: (i, 0, 0)),
         ],
-        out_specs=pl.BlockSpec((1, length, width), lambda i: (i, 0, 0)),
+        out_specs=(pl.BlockSpec((1, length, width), lambda i: (i, 0, 0)), PLACE),
     )(after, left, right)
 
 
-def share_kernel(after, parts, out, mark):
-    del after, mark
-    total = jnp.sum(parts[...], axis=0, keepdims=True)
-    out[...] = jnp.broadcast_to(total, out.shape)
-
-
-def share_of_sum(after, parts):
-    return call(
-        share_kernel,
-        "share_of_sum",
-        SHARED,
-        parts.size,
-        8 * parts.size,
-        out_shape=(shaped(parts.shape, WIDE), MARK),
-        in_specs=[PLACE, WHOLE],
+def add_kernel(after, *refs):
+    del after
+    terms = [ref[...].astype(WIDE) for ref in refs[:-2]]
+    while len(terms) > 1:
+        terms = [left + right for left, right in zip(terms[::2], terms[1::2])]
+    refs[-2][...] = terms[0].astype(refs[-2].dtype)
+
+
+def add(after, terms, dtype):
+    return call(
+        add_kernel,
+        "add_terms",
+        SHARED,
+        len(terms) * terms[0].size,
+        2 * len(terms) * terms[0].size,
+        out_shape=(shaped(terms[0].shape, dtype), MARK),
+        in_specs=[PLACE] + [WHOLE] * len(terms),
         out_specs=(WHOLE, PLACE),
-    )(after, parts)
-
-
-def join_kernel(pieces, out):
-    size = pieces.shape[2]
-    per_row = out.shape[1] // size
-    for piece in range(pieces.shape[0]):
-        row, at = piece // per_row, piece % per_row * size
-        out[row : row + 1, at : at + size] = pieces[piece]
-
-
-def join(pieces, shape):
-    return call(
-        join_kernel,
-        "join_pieces",
-        SHARED,
-        0,
-        8 * pieces.size,
-        out_shape=shaped(shape, WIDE),
-        in_specs=[WHOLE],
-        out_specs=WHOLE,
-    )(pieces)
+    )(after, *terms)
+
+
+def terms_of_group(array, axis, distances):
+    count = lax.axis_size(axis)
+    return [array] + [
+        lax.ppermute(array, axis, [(i, i ^ distance) for i in range(count)])
+        for distance in distances
+    ]
 
 
 def copy_kernel(after, source, target):
@@ -532,41 +473,42 @@
     params = slot_params.T
     weights = (expert_in[0], expert_out[0])
     replicas = lax.axis_size("rep")
-    everyone = ("rep", "exp")
     mine = lax.axis_index("rep").astype(jnp.int32).reshape(1)
 
-    sent, dispatch, combine, after_gather = gather(tokens, params, grad_out)
+    sent, dispatch, combine = gather(tokens, params, grad_out)
     rows = exchange(sent, "exp")
-    first = fetch_first(after_gather, *weights, 256)
-    back, acts, hidden, after_expert = expert(rows, *first, *weights, 512)
+    back, acts, hidden, after_expert = expert(rows, *weights, 512)
     back = exchange(back, "exp")
     other_rows = lax.ppermute(
         copy_after(after_expert, rows), "rep", [(i, (i + 1) % replicas) for i in range(replicas)]
     )
-    left, right, local, after_logits = logits_grads(
-        after_expert, back, tokens, params, grad_out, dispatch, combine, lax.axis_size(everyone)
+    left, right, local, after = logits_grads(
+        after_expert, back, tokens, params, grad_out, dispatch, combine
     )
-    other_acts, other_hidden, after_others = others_hidden(
-        after_logits, other_rows, *weights, 512
-    )
-    share, after_share = share_of_sum(after_others, exchange(local, everyone))
-    grad_expert_in, grad_expert_out, _ = weight_grads(
+    bits = lax.axis_size("exp").bit_length() - 1
+    groups = [(1 << bit, 2 << bit, 3 << bit) for bit in range(0, bits - 1, 2)]
+    if bits % 2:
+        groups.append((1 << (bits - 1),))
+    terms = terms_of_group(local, "exp", groups[0])
+    grad_tokens, after = tokens_grads(after, left, right)
+    local, after = add(after, terms, LOW)
+    terms = terms_of_group(local, "exp", groups[1])
+    other_acts, other_hidden, after = others_hidden(after, other_rows, *weights, 512)
+    local, after = add(after, terms, LOW)
+    for distances in groups[2:]:
+        local, after = add(after, terms_of_group(local, "exp", distances), LOW)
+    terms = terms_of_group(local, "rep", (1,))
+    grad_expert_in, grad_expert_out, after = weight_grads(
         mine,
-        after_share,
+        after,
         (rows, other_rows),
         (acts, other_acts),
         (hidden, other_hidden),
         5,
         replicas,
     )
-    grad_params = join(exchange(share, everyone), params.shape).T
-    grad_tokens = tokens_grads(after_share, left, right)
-    return (
-        grad_tokens,
-        grad_params,
-        grad_expert_in[None],
-        grad_expert_out[None],
-    )
+    grad_params, _ = add(after, terms, WIDE)
+    return (grad_tokens, grad_params.T, grad_expert_in[None], grad_expert_out[None])
 
 
 def solution(mesh):

time: 76.7 us -> 73.3 us (0.956)
  blocking collectives: 0 us -> 18.3 us
  waiting for transfers between devices: 21.5 us -> 9.5 us
  starting transfers between devices: 19.6 us -> 13.1 us
  Pallas kernels: 33.7 us -> 30.7 us
    all_to_all x0 -> x1, blocking collectives: none -> 18.3 us  [exchange(): return lax.all_to_all(rows, axes, split_axis=0, concat_axis=0, tiled=True)]
    all_to_all x4 -> x1, starting transfers between devices: 18 us -> 3.56 us  [exchange(): return lax.all_to_all(rows, axes, split_axis=0, concat_axis=0, tiled=True)]
    all_to_all x4 -> x1, waiting for transfers between devices: 21.5 us -> 9.46 us  [exchange(): return lax.all_to_all(rows, axes, split_axis=0, concat_axis=0, tiled=True)]
    ppermute x0 -> x7, starting transfers between devices: none -> 7.95 us  [terms_of_group(): lax.ppermute(array, axis, [(i, i ^ distance) for i in range(count)])]
    pallas_call x4, Pallas kernels: 11.8 us -> 10.2 us  [the longest x1 9.54 us: expert(): call(functools.partial(expert_kernel, chunks), 'expert_rows', SHARED, 8 *...]
  transfers between devices with their start and end apart: 5 -> 9, of which waited for: 4 -> 1; matrix products, arithmetic and copies ran while one was open for 0% -> 0% of each run, Pallas kernels for 25% -> 24%
where the time goes in v11:
time: 73.3 us; the launch traced here: 73 us
  Pallas kernels  30.7 us (42%)
  blocking collectives  18.3 us (25%)
  starting transfers between devices  13.1 us (18%)
  waiting for transfers between devices  9.5 us (13%)
  local copies, waits for them, and re-layouts  0.78 us (1%)
  between operations  0.74 us (1%)
    all_to_all x1, blocking collectives, exchange(): return lax.all_to_all(rows, axes, split_axis=0, concat_axis=0, tiled=True)  18.3 us
    pallas_call x1, Pallas kernels, expert(): call(functools.partial(expert_kernel, chunks), 'expert_rows', SHARED, 8 *...  9.54 us
    all_to_all x1, waiting for transfers between devices, exchange(): return lax.all_to_all(rows, axes, split_axis=0, concat_axis=0, tiled=True)  9.46 us
    ppermute x7, starting transfers between devices, terms_of_group(): lax.ppermute(array, axis, [(i, i ^ distance) for i in range(count)])  7.95 us
    pallas_call x1, Pallas kernels, others_hidden(): call(functools.partial(others_kernel, chunks), 'others_hidden', SHARED, 6...  5.65 us
    pallas_call x1, Pallas kernels, weight_grads(): call(weights_kernel, 'weight_grads', SHARED, 8 * count * size * width //...  4.51 us
    pallas_call x1, Pallas kernels, logits_grads(): call(logits_kernel, 'logits_grads', SHARED, 6 * images * slots * length *...  4.32 us
    all_to_all x1, starting transfers between devices, exchange(): return lax.all_to_all(rows, axes, split_axis=0, concat_axis=0, tiled=True)  3.56 us
  transfers between devices with their start and end apart: 9, of which 1 were waited for; matrix products, arithmetic and copies ran while one was open for 0% of the time, Pallas kernels for 24%

profile of v11, /device:TPU:0, one launch (start us, length us, event | category | flops | bytes accessed | tf_op | source)
XLA Modules:
  0.0 73.0 jit_solution(6195748284960356313)
XLA Ops:
  0.6 0.0 copy-start
  0.6 0.8 %copy-done = bf16[1280,16]{0,1:T(8,128)(2,1)S(1)} copy-done((bf16[1280,16]{0,1:T(8,128)(2,1)S(1)}, bf16[1280,16]{0,1:T(8,128)(2,1)}, u32[]{:S(2)}) %copy-start) | copy-done | bytes 40984
  1.4 3.2 %gather_slots.1 = (bf16[128,1280]{1,0:T(8,128)(2,1)S(1)}, f32[4,16,256]{2,1,0:T(8,128)S(1)}, f32[4,16,256]{2,1,0:T(8,128)S(1)}) custom-call(bf16[4,256,1280]{2,1,0:T(8,128)(2,1)} %tokens.3, bf16[16,1280]{1,0:T(8,128)(2,1)S(1)} %bitcast.16, bf16[4,256,1280]{2,1,0:T(8,128)(2,1)} %grads.3), custom_call_target="tpu_custom_call" | custom-call | flops 125829120 | bytes 5242880 | tf_op jit(solution)/shard_map/gather_slots/pallas_call | solution.py:135
  4.6 18.3 %all_to_all.22 = bf16[16,8,1280]{2,1,0:T(8,128)(2,1)S(1)} all-to-all(bf16[16,8,1280]{2,1,0:T(8,128)(2,1)S(1)} %bitcast.15), channel_id=1, replica_groups=mesh['rep'=2,'exp'=16] {'exp'}, dimensions={0} | all-to-all | bytes 655360 | tf_op jit(solution)/shard_map/all_to_all | solution.py:469
  22.9 0.0 copy-start.1
  22.9 9.5 %expert_rows.1 = (bf16[128,1280]{1,0:T(8,128)(2,1)}, bf16[64,2560]{1,0:T(8,128)(2,1)S(1)}, bf16[64,2560]{1,0:T(8,128)(2,1)S(1)}, f32[8,128]{1,0:T(8,128)S(1)}) custom-call(bf16[128,1280]{1,0:T(8,128)(2,1)S(1)} %bitcast.11, bf16[1280,2560]{1,0:T(8,128)(2,1)} %bitcast.18, bf16[2560,1280]{1,0:T(8,128)(2,1)} %bitcast.20), custom_call_target="tpu_custom_call" | custom-call | flops 1677721600 | bytes 13107200 | tf_op jit(solution)/shard_map/expert_rows/pallas_call | solution.py:216
  32.4 3.6 %all-to-all-start.1 = ((bf16[16,8,1280]{2,1,0:T(8,128)(2,1)}), bf16[16,8,1280]{2,1,0:T(8,128)(2,1)S(1)}, u32[]{:S(2)}, u32[]{:S(2)}) async-start(bf16[16,8,1280]{2,1,0:T(8,128)(2,1)} %bitcast.5), calls=%async_computation.1 | async-start | bytes 655360 | tf_op jit(solution)/shard_map/all_to_all | solution.py:469
  36.0 1.6 %collective-permute-start.3 = (bf16[128,1280]{1,0:T(8,128)(2,1)S(1)}, bf16[128,1280]{1,0:T(8,128)(2,1)S(1)}, u32[]{:S(2)}, u32[]{:S(2)}) collective-permute-start(bf16[128,1280]{1,0:T(8,128)(2,1)S(1)} %copy_after.1), channel_id=1, source_target_pairs={{0,16},{16,0},{1,17},{17,1},{2,18},{18,2},{3,19},{19,3},{4,20},{20... | collective-permute-start | bytes 983048 | tf_op jit(solution)/shard_map/ppermute | solution.py:482
  37.6 9.5 %all-to-all-done.1 = bf16[16,8,1280]{2,1,0:T(8,128)(2,1)S(1)} async-done(((bf16[16,8,1280]{2,1,0:T(8,128)(2,1)}), bf16[16,8,1280]{2,1,0:T(8,128)(2,1)S(1)}, u32[]{:S(2)}, u32[]{:S(2)}) %all-to-all-start.1) | async-done | bytes 327712 | tf_op jit(solution)/shard_map/all_to_all | solution.py:469
  47.1 0.0 copy-done.1
  47.1 4.3 %logits_grads.1 = (bf16[4,32,256]{2,1,0:T(8,128)(2,1)S(1)}, bf16[4,32,1280]{2,1,0:T(8,128)(2,1)S(1)}, bf16[16,1280]{1,0:T(8,128)(2,1)S(1)}, f32[8,128]{1,0:T(8,128)S(1)}) custom-call(f32[8,128]{1,0:T(8,128)S(1)} %get-tuple-element.29.after, bf16[128,1280]{1,0:T(8,128)(2,1)S(1)} %bitcast.14, bf16[4,256,1280]{2,1,0:T(8,128)(2,1)} %tokens.3, ...), custom_call_target="tpu_custom_call" | custom-call | flops 125829120 | bytes 5242880 | tf_op jit(solution)/shard_map/logits_grads/pallas_call | solution.py:373
  51.4 0.1 collective-permute-start
  51.5 0.8 %collective-permute-start.1 = (bf16[16,1280]{1,0:T(8,128)(2,1)S(1)}, bf16[16,1280]{1,0:T(8,128)(2,1)S(1)}, u32[]{:S(2)}, u32[]{:S(2)}) collective-permute-start(bf16[16,1280]{1,0:T(8,128)(2,1)S(1)} %get-tuple-element.38.refs_0_), channel_id=1, source_target_pairs={{0,2},{1,3},{2,0},{3,1},{4,6},{5,7},{6,4},{7,5},{8,10},{9,11},{10,... | collective-permute-start | bytes 122888 | tf_op jit(solution)/shard_map/ppermute | solution.py:445
  52.2 1.1 %collective-permute-start.2 = (bf16[16,1280]{1,0:T(8,128)(2,1)S(1)}, bf16[16,1280]{1,0:T(8,128)(2,1)S(1)}, u32[]{:S(2)}, u32[]{:S(2)}) collective-permute-start(bf16[16,1280]{1,0:T(8,128)(2,1)S(1)} %get-tuple-element.38.refs_0_), channel_id=1, source_target_pairs={{0,3},{1,2},{2,1},{3,0},{4,7},{5,6},{6,5},{7,4},{8,11},{9,10},{10,... | collective-permute-start | bytes 122888 | tf_op jit(solution)/shard_map/ppermute | solution.py:445
  53.3 2.7 %tokens_grads.1 = (bf16[4,256,1280]{2,1,0:T(8,128)(2,1)}, f32[8,128]{1,0:T(8,128)S(1)}) custom-call(f32[8,128]{1,0:T(8,128)S(1)} %get-tuple-element.33.after, bf16[4,32,256]{2,1,0:T(8,128)(2,1)S(1)} %get-tuple-element.34.left, bf16[4,32,1280]{2,1,0:T(8,128)(2,1)S(1)} %get-tuple-element.35.right), custom_call_target="tpu_custom_call" | custom-call | flops 83886080 | bytes 2621440 | tf_op jit(solution)/shard_map/tokens_grads/pallas_call | solution.py:404
  56.1 0.0 collective-permute-done.refs_1_
  56.1 0.0 collective-permute-done.1.refs_2_
  56.1 0.0 collective-permute-done.2.refs_3_
  56.1 1.3 %collective-permute-start.4 = (bf16[16,1280]{1,0:T(8,128)(2,1)S(1)}, bf16[16,1280]{1,0:T(8,128)(2,1)S(1)}, u32[]{:S(2)}, u32[]{:S(2)}) collective-permute-start(bf16[16,1280]{1,0:T(8,128)(2,1)S(1)} %get-tuple-element.41.refs_0_), channel_id=1, source_target_pairs={{0,4},{1,5},{2,6},{3,7},{4,0},{5,1},{6,2},{7,3},{8,12},{9,13},{10,... | collective-permute-start | bytes 122888 | tf_op jit(solution)/shard_map/ppermute | solution.py:445
  57.5 0.9 %collective-permute-start.5 = (bf16[16,1280]{1,0:T(8,128)(2,1)S(1)}, bf16[16,1280]{1,0:T(8,128)(2,1)S(1)}, u32[]{:S(2)}, u32[]{:S(2)}) collective-permute-start(bf16[16,1280]{1,0:T(8,128)(2,1)S(1)} %get-tuple-element.41.refs_0_), channel_id=1, source_target_pairs={{0,8},{1,9},{2,10},{3,11},{4,12},{5,13},{6,14},{7,15},{8,0},{9,1},... | collective-permute-start | bytes 122888 | tf_op jit(solution)/shard_map/ppermute | solution.py:445
  58.4 2.2 %collective-permute-start.6 = (bf16[16,1280]{1,0:T(8,128)(2,1)S(1)}, bf16[16,1280]{1,0:T(8,128)(2,1)S(1)}, u32[]{:S(2)}, u32[]{:S(2)}) collective-permute-start(bf16[16,1280]{1,0:T(8,128)(2,1)S(1)} %get-tuple-element.41.refs_0_), channel_id=1, source_target_pairs={{0,12},{1,13},{2,14},{3,15},{4,8},{5,9},{6,10},{7,11},{8,4},{9,5},... | collective-permute-start | bytes 122888 | tf_op jit(solution)/shard_map/ppermute | solution.py:445
  60.6 0.0 collective-permute-done.3.rows.other_rows
  60.6 5.6 %others_hidden.1 = (bf16[64,2560]{1,0:T(8,128)(2,1)S(1)}, bf16[64,2560]{1,0:T(8,128)(2,1)S(1)}, f32[8,128]{1,0:T(8,128)S(1)}) custom-call(f32[8,128]{1,0:T(8,128)S(1)} %get-tuple-element.39.after, bf16[128,1280]{1,0:T(8,128)(2,1)S(1)} %collective-permute-done.3.rows.other_rows, bf16[1280,2560]{1,0:T(8,128)(2,1)} %bitcast.19, bf16[2560,1280]{1,0:T(8,128)(2,1)} %bitcast.21), custom_call_target="tpu_custom_call" | custom-call | flops 13421772800 | bytes 104857600 | tf_op jit(solution)/shard_map/others_hidden/pallas_call | solution.py:254
  66.2 0.0 collective-permute-done.4.refs_1_
  66.2 0.0 collective-permute-done.5.refs_2_
  66.3 0.0 collective-permute-done.6.refs_3_
  66.3 1.6 %collective-permute-start.7 = (bf16[16,1280]{1,0:T(8,128)(2,1)S(1)}, bf16[16,1280]{1,0:T(8,128)(2,1)S(1)}, u32[]{:S(2)}, u32[]{:S(2)}) collective-permute-start(bf16[16,1280]{1,0:T(8,128)(2,1)S(1)} %get-tuple-element.48.refs_0_), channel_id=1, source_target_pairs={{0,16},{16,0},{1,17},{17,1},{2,18},{18,2},{3,19},{19,3},{4,20},{20... | collective-permute-start | bytes 122888 | tf_op jit(solution)/shard_map/ppermute | solution.py:445
  67.9 4.5 %weight_grads.1 = (bf16[640,2560]{1,0:T(8,128)(2,1)}, bf16[1280,1280]{1,0:T(8,128)(2,1)}, f32[8,128]{1,0:T(8,128)S(1)}) custom-call(s32[1]{0:T(128)} %bitcast.7.mine, f32[8,128]{1,0:T(8,128)S(1)} %get-tuple-element.42.after, bf16[128,1280]{1,0:T(8,128)(2,1)S(1)} %bitcast.13, bf16[128,1280]{1,0:T(8,128)(2,1)S(1)} %collective-permute-done.3.rows.other_rows, ...), custom_call_target="tpu_custom_call" | custom-call | flops 838860800 | bytes 6553600 | tf_op jit(solution)/shard_map/weight_grads/pallas_call | solution.py:300
  72.4 0.0 collective-permute-done.7.refs_1_
  72.4 0.6 add_terms.5
  (3 shorter events, 0.1 us)
Async XLA Ops:
  0.6 0.8 %copy-start = (bf16[1280,16]{0,1:T(8,128)(2,1)S(1)}, bf16[1280,16]{0,1:T(8,128)(2,1)}, u32[]{:S(2)}) copy-start(bf16[1280,16]{0,1:T(8,128)(2,1)} %param.6) | copy-start | bytes 122884
  22.9 24.2 %copy-start.1 = (bf16[1280,16]{0,1:T(8,128)(2,1)S(1)}, bf16[1280,16]{0,1:T(8,128)(2,1)}, u32[]{:S(2)}) copy-start(bf16[1280,16]{0,1:T(8,128)(2,1)} %param.6) | copy-start | bytes 122884
  32.4 14.6 %all-to-all-start.1 = ((bf16[16,8,1280]{2,1,0:T(8,128)(2,1)}), bf16[16,8,1280]{2,1,0:T(8,128)(2,1)S(1)}, u32[]{:S(2)}, u32[]{:S(2)}) async-start(bf16[16,8,1280]{2,1,0:T(8,128)(2,1)} %bitcast.5), calls=%async_computation.1 | async-start | bytes 655360 | tf_op jit(solution)/shard_map/all_to_all | solution.py:469
  36.0 24.5 %collective-permute-start.3 = (bf16[128,1280]{1,0:T(8,128)(2,1)S(1)}, bf16[128,1280]{1,0:T(8,128)(2,1)S(1)}, u32[]{:S(2)}, u32[]{:S(2)}) collective-permute-start(bf16[128,1280]{1,0:T(8,128)(2,1)S(1)} %copy_after.1), channel_id=1, source_target_pairs={{0,16},{16,0},{1,17},{17,1},{2,18},{18,2},{3,19},{19,3},{4,20},{20... | collective-permute-start | bytes 983048 | tf_op jit(solution)/shard_map/ppermute | solution.py:482
  51.4 4.7 %collective-permute-start = (bf16[16,1280]{1,0:T(8,128)(2,1)S(1)}, bf16[16,1280]{1,0:T(8,128)(2,1)S(1)}, u32[]{:S(2)}, u32[]{:S(2)}) collective-permute-start(bf16[16,1280]{1,0:T(8,128)(2,1)S(1)} %get-tuple-element.38.refs_0_), channel_id=1, source_target_pairs={{0,1},{1,0},{2,3},{3,2},{4,5},{5,4},{6,7},{7,6},{8,9},{9,8},{10,11... | collective-permute-start | bytes 122888 | tf_op jit(solution)/shard_map/ppermute | solution.py:445
  51.5 4.6 %collective-permute-start.1 = (bf16[16,1280]{1,0:T(8,128)(2,1)S(1)}, bf16[16,1280]{1,0:T(8,128)(2,1)S(1)}, u32[]{:S(2)}, u32[]{:S(2)}) collective-permute-start(bf16[16,1280]{1,0:T(8,128)(2,1)S(1)} %get-tuple-element.38.refs_0_), channel_id=1, source_target_pairs={{0,2},{1,3},{2,0},{3,1},{4,6},{5,7},{6,4},{7,5},{8,10},{9,11},{10,... | collective-permute-start | bytes 122888 | tf_op jit(solution)/shard_map/ppermute | solution.py:445
  52.2 3.9 %collective-permute-start.2 = (bf16[16,1280]{1,0:T(8,128)(2,1)S(1)}, bf16[16,1280]{1,0:T(8,128)(2,1)S(1)}, u32[]{:S(2)}, u32[]{:S(2)}) collective-permute-start(bf16[16,1280]{1,0:T(8,128)(2,1)S(1)} %get-tuple-element.38.refs_0_), channel_id=1, source_target_pairs={{0,3},{1,2},{2,1},{3,0},{4,7},{5,6},{6,5},{7,4},{8,11},{9,10},{10,... | collective-permute-start | bytes 122888 | tf_op jit(solution)/shard_map/ppermute | solution.py:445
  56.1 10.1 %collective-permute-start.4 = (bf16[16,1280]{1,0:T(8,128)(2,1)S(1)}, bf16[16,1280]{1,0:T(8,128)(2,1)S(1)}, u32[]{:S(2)}, u32[]{:S(2)}) collective-permute-start(bf16[16,1280]{1,0:T(8,128)(2,1)S(1)} %get-tuple-element.41.refs_0_), channel_id=1, source_target_pairs={{0,4},{1,5},{2,6},{3,7},{4,0},{5,1},{6,2},{7,3},{8,12},{9,13},{10,... | collective-permute-start | bytes 122888 | tf_op jit(solution)/shard_map/ppermute | solution.py:445
  57.5 8.8 %collective-permute-start.5 = (bf16[16,1280]{1,0:T(8,128)(2,1)S(1)}, bf16[16,1280]{1,0:T(8,128)(2,1)S(1)}, u32[]{:S(2)}, u32[]{:S(2)}) collective-permute-start(bf16[16,1280]{1,0:T(8,128)(2,1)S(1)} %get-tuple-element.41.refs_0_), channel_id=1, source_target_pairs={{0,8},{1,9},{2,10},{3,11},{4,12},{5,13},{6,14},{7,15},{8,0},{9,1},... | collective-permute-start | bytes 122888 | tf_op jit(solution)/shard_map/ppermute | solution.py:445
  58.4 7.8 %collective-permute-start.6 = (bf16[16,1280]{1,0:T(8,128)(2,1)S(1)}, bf16[16,1280]{1,0:T(8,128)(2,1)S(1)}, u32[]{:S(2)}, u32[]{:S(2)}) collective-permute-start(bf16[16,1280]{1,0:T(8,128)(2,1)S(1)} %get-tuple-element.41.refs_0_), channel_id=1, source_target_pairs={{0,12},{1,13},{2,14},{3,15},{4,8},{5,9},{6,10},{7,11},{8,4},{9,5},... | collective-permute-start | bytes 122888 | tf_op jit(solution)/shard_map/ppermute | solution.py:445
  66.3 6.1 %collective-permute-start.7 = (bf16[16,1280]{1,0:T(8,128)(2,1)S(1)}, bf16[16,1280]{1,0:T(8,128)(2,1)S(1)}, u32[]{:S(2)}, u32[]{:S(2)}) collective-permute-start(bf16[16,1280]{1,0:T(8,128)(2,1)S(1)} %get-tuple-element.48.refs_0_), channel_id=1, source_target_pairs={{0,16},{16,0},{1,17},{17,1},{2,18},{18,2},{3,19},{19,3},{4,20},{20... | collective-permute-start | bytes 122888 | tf_op jit(solution)/shard_map/ppermute | solution.py:445

commit v12 on v11

--- a/solution.py
+++ b/solution.py
@@ -227,103 +227,107 @@
     )(rows, w_in, w_out)
 
 
-def others_kernel(
-    chunks, after, rows, w_in, w_out, acts, hidden, mark, w_in_v, w_out_v, sems, wide
-):
-    del after, mark
-    copies = start_weights(w_in, w_out, w_in_v, w_out_v, sems, chunks)
-    count = rows.shape[0] // KINDS
-    load_rows(wide, rows[...])
-    rows_in = take(wide, 0, count, KINDS).astype(LOW)
-    rows_grad = take(wide, 1, count, KINDS).astype(LOW)
-    for pair, units in zip(copies, chunks):
-        for copy in pair:
-            copy.wait()
-        values, slope = gelu_parts(dot(rows_in, w_in_v[:, units], 1, 0))
-        acts[:, units] = values.astype(LOW)
-        d_acts = dot(rows_grad, w_out_v[units, :], 1, 1)
-        hidden[:, units] = (d_acts * slope).astype(LOW)
-
-
-def others_hidden(after, rows, w_in, w_out, tile):
-    total, width = rows.shape
-    hidden = w_in.shape[1]
-    count = total // KINDS
-    kept = shaped((count, hidden), LOW)
-    chunks = chunks_of(0, hidden, tile)
-    return call(
-        functools.partial(others_kernel, chunks),
-        "others_hidden",
-        SHARED,
-        64 * count * hidden * width,
-        32 * hidden * width,
-        count * hidden,
-        out_shape=(kept, kept, MARK),
-        in_specs=[PLACE, WHOLE, PLACE, PLACE],
-        out_specs=(WHOLE, WHOLE, PLACE),
-        scratch_shapes=[*weight_scratch(width, hidden, chunks), scratch_rows(rows.shape)],
-    )(after, rows, w_in, w_out)
-
-
-def weights_kernel(
-    mine, after, rows, other_rows, acts, other_acts, hidden, other_hidden, grad_in, grad_out, mark,
-    wide, grads, turned,
+def replica_kernel(
+    chunks, mine, after, rows, other_rows, acts, hidden, w_in, w_out, grad_in, grad_out, mark,
+    w_in_v, w_out_v, grad_in_v, grad_out_v, wide, grads, turned, sems, in_sems, out_sems,
 ):
     del after, mark
     count = rows.shape[0] // KINDS
-
-    @pl.when(pl.program_id(0) == 0)
-    def _():
-        left, right = [], []
-        tiles = turned.shape[0] // LANES
-        for source in (rows, other_rows):
-            load_rows(wide, source[...])
-            left.append(take(wide, 0, count, KINDS, mine[0] * tiles, tiles))
-            right.append(take(wide, 1, count, KINDS))
-        turned[...] = jnp.concatenate(left, axis=0).T.astype(LOW)
-        grads[...] = jnp.concatenate(right, axis=0).astype(LOW)
-
-    all_hidden = jnp.concatenate([hidden[...], other_hidden[...]], axis=0)
-    grad_in[...] = dot(turned[...], all_hidden, 1, 0).astype(LOW)
-    all_acts = jnp.concatenate([acts[...], other_acts[...]], axis=0)
-    grad_out[...] = dot(all_acts, grads[...], 0, 0).astype(LOW)
-
-
-def weight_grads(mine, after, rows, acts, hidden, steps, replicas):
-    total, width = rows[0].shape
-    size = acts[0].shape[1]
+    size = w_in.shape[1]
+    half = grad_out.shape[0]
+    spans, copies = [], []
+    for chunk, units in enumerate(chunks):
+        start = pl.multiple_of(lax.rem(mine[0] * half + units.start, size), LANES)
+        span = pl.ds(start, units.stop - units.start)
+        spans.append(span)
+        copies.append(
+            (
+                start_copy(w_in.at[:, span], w_in_v.at[:, units], sems.at[0, chunk]),
+                start_copy(w_out.at[span, :], w_out_v.at[units, :], sems.at[1, chunk]),
+            )
+        )
+    left, right = [], []
+    tiles = turned.shape[0] // LANES
+    for source in (rows, other_rows):
+        load_rows(wide, source[...])
+        left.append(take(wide, 0, count, KINDS, mine[0] * tiles, tiles))
+        right.append(take(wide, 1, count, KINDS))
+    turned[...] = jnp.concatenate(left, axis=0).T.astype(LOW)
+    grads[...] = jnp.concatenate(right, axis=0).astype(LOW)
+    rows_in = take(wide, 0, count, KINDS).astype(LOW)
+    rows_grad = right[1].astype(LOW)
+    results = []
+    before = None
+    for chunk in range(len(chunks) + 1):
+        if chunk < len(chunks):
+            units = chunks[chunk]
+            for copy in copies[chunk]:
+                copy.wait()
+            preact = dot(rows_in, w_in_v[:, units], 1, 0)
+            d_acts = dot(rows_grad, w_out_v[units, :], 1, 1)
+        if before is not None:
+            past, span, all_acts, all_hidden = before
+            grad_in_v[:, past] = dot(turned[...], all_hidden, 1, 0).astype(LOW)
+            results.append(
+                start_copy(grad_in_v.at[:, past], grad_in.at[:, span], in_sems.at[chunk - 1])
+            )
+            if past.stop <= half:
+                grad_out_v[past, :] = dot(all_acts, grads[...], 0, 0).astype(LOW)
+                results.append(
+                    start_copy(
+                        grad_out_v.at[past, :], grad_out.at[past, :], out_sems.at[chunk - 1]
+                    )
+                )
+        if chunk < len(chunks):
+            span = spans[chunk]
+            values, slope = gelu_parts(preact)
+            all_acts = jnp.concatenate([acts[:, span], values.astype(LOW)], axis=0)
+            all_hidden = jnp.concatenate(
+                [hidden[:, span], (d_acts * slope).astype(LOW)], axis=0
+            )
+            before = (units, span, all_acts, all_hidden)
+    for copy in results:
+        copy.wait()
+
+
+def replica_grads(mine, after, rows, other_rows, acts, hidden, w_in, w_out, replicas, tile):
+    total, width = rows.shape
+    size = w_in.shape[1]
+    half = size // replicas
     count = total // KINDS
-    in_tile, out_tile = size // steps, size // replicas // steps
-    whole_rows = pl.BlockSpec((total, width), lambda i, mine: (0, 0))
-    acts_spec = pl.BlockSpec((count, out_tile), lambda i, mine: (0, mine[0] * steps + i))
-    hidden_spec = pl.BlockSpec((count, in_tile), lambda i, mine: (0, i))
-    return call(
-        weights_kernel,
-        "weight_grads",
-        SHARED,
-        8 * count * size * width // replicas,
-        4 * size * width // replicas,
-        grid_spec=pltpu.PrefetchScalarGridSpec(
-            num_scalar_prefetch=1,
-            grid=(steps,),
-            in_specs=[PLACE] + [whole_rows] * 2 + [acts_spec] * 2 + [hidden_spec] * 2,
-            out_specs=(
-                pl.BlockSpec((width // replicas, in_tile), lambda i, mine: (0, i)),
-                pl.BlockSpec((out_tile, width), lambda i, mine: (i, 0)),
-                PLACE,
-            ),
-            scratch_shapes=[
-                scratch_rows((total, width)),
-                pltpu.VMEM((2 * count, width), LOW),
-                pltpu.VMEM((width // replicas, 2 * count), LOW),
-            ],
-        ),
+    chunks = [
+        slice(part * half + units.start, part * half + units.stop)
+        for part in range(replicas)
+        for units in chunks_of(0, half, tile)
+    ]
+    return call(
+        functools.partial(replica_kernel, chunks),
+        "replica_grads",
+        SHARED,
+        64 * count * size * width,
+        32 * size * width,
+        count * size,
         out_shape=(
             shaped((width // replicas, size), LOW),
-            shaped((size // replicas, width), LOW),
+            shaped((half, width), LOW),
             MARK,
         ),
-    )(mine, after, *rows, *acts, *hidden)
+        in_specs=[pl.BlockSpec(memory_space=pltpu.SMEM), PLACE]
+        + [WHOLE] * 4
+        + [PLACE] * 2,
+        out_specs=(PLACE,) * 3,
+        scratch_shapes=[
+            *weight_scratch(width, size, chunks)[:2],
+            pltpu.VMEM((width // replicas, size), LOW),
+            pltpu.VMEM((half, width), LOW),
+            scratch_rows((total, width)),
+            pltpu.VMEM((2 * count, width), LOW),
+            pltpu.VMEM((width // replicas, 2 * count), LOW),
+            pltpu.SemaphoreType.DMA((2, len(chunks))),
+            pltpu.SemaphoreType.DMA((len(chunks),)),
+            pltpu.SemaphoreType.DMA((len(chunks),)),
+        ],
+    )(mine, after, rows, other_rows, acts, hidden, w_in, w_out)
 
 
 def logits_kernel(
@@ -447,24 +451,6 @@
     ]
 
 
-def copy_kernel(after, source, target):
-    del after
-    target[...] = source[...]
-
-
-def copy_after(after, array):
-    return call(
-        copy_kernel,
-        "copy_after",
-        SHARED,
-        0,
-        4 * array.size,
-        out_shape=shaped(array.shape, array.dtype),
-        in_specs=[PLACE, WHOLE],
-        out_specs=WHOLE,
-    )(after, array)
-
-
 def exchange(rows, axes):
     return lax.all_to_all(rows, axes, split_axis=0, concat_axis=0, tiled=True)
 
@@ -477,13 +463,14 @@
 
     sent, dispatch, combine = gather(tokens, params, grad_out)
     rows = exchange(sent, "exp")
-    back, acts, hidden, after_expert = expert(rows, *weights, 512)
+    other_rows = lax.ppermute(rows, "rep", [(i, (i + 1) % replicas) for i in range(replicas)])
+    back, acts, hidden, after = expert(rows, *weights, 512)
     back = exchange(back, "exp")
-    other_rows = lax.ppermute(
-        copy_after(after_expert, rows), "rep", [(i, (i + 1) % replicas) for i in range(replicas)]
+    grad_in, grad_outer, after = replica_grads(
+        mine, after, rows, other_rows, acts, hidden, *weights, replicas, 512
     )
     left, right, local, after = logits_grads(
-        after_expert, back, tokens, params, grad_out, dispatch, combine
+        after, back, tokens, params, grad_out, dispatch, combine
     )
     bits = lax.axis_size("exp").bit_length() - 1
     groups = [(1 << bit, 2 << bit, 3 << bit) for bit in range(0, bits - 1, 2)]
@@ -492,23 +479,10 @@
     terms = terms_of_group(local, "exp", groups[0])
     grad_tokens, after = tokens_grads(after, left, right)
     local, after = add(after, terms, LOW)
-    terms = terms_of_group(local, "exp", groups[1])
-    other_acts, other_hidden, after = others_hidden(after, other_rows, *weights, 512)
-    local, after = add(after, terms, LOW)
-    for distances in groups[2:]:
+    for distances in groups[1:]:
         local, after = add(after, terms_of_group(local, "exp", distances), LOW)
-    terms = terms_of_group(local, "rep", (1,))
-    grad_expert_in, grad_expert_out, after = weight_grads(
-        mine,
-        after,
-        (rows, other_rows),
-        (acts, other_acts),
-        (hidden, other_hidden),
-        5,
-        replicas,
-    )
-    grad_params, _ = add(after, terms, WIDE)
-    return (grad_tokens, grad_params.T, grad_expert_in[None], grad_expert_out[None])
+    grad_params, _ = add(after, terms_of_group(local, "rep", (1,)), WIDE)
+    return (grad_tokens, grad_params.T, grad_in[None], grad_outer[None])
 
 
 def solution(mesh):

time: 73.3 us -> 71.2 us (0.971)
  Pallas kernels: 30.7 us -> 29.3 us
  starting transfers between devices: 13.1 us -> 12.2 us
    ppermute x7, waiting for transfers between devices: 0.03 us -> 7.57 us  [terms_of_group(): lax.ppermute(array, axis, [(i, i ^ distance) for i in range(count)])]
    all_to_all x1, waiting for transfers between devices: 9.46 us -> 2.03 us  [exchange(): return lax.all_to_all(rows, axes, split_axis=0, concat_axis=0, tiled=True)]
    pallas_call x3 -> x1, Pallas kernels: 10.2 us -> 8.82 us  [replica_grads(): call(functools.partial(replica_kernel, chunks), 'replica_grads', SHARED,...]
    ppermute x7, starting transfers between devices: 7.95 us -> 6.98 us  [terms_of_group(): lax.ppermute(array, axis, [(i, i ^ distance) for i in range(count)])]
  transfers between devices with their start and end apart: 9 -> 9, of which waited for: 1 -> 4; matrix products, arithmetic and copies ran while one was open for 0% -> 0% of each run, Pallas kernels for 24% -> 30%
where the time goes in v12:
time: 71.2 us; the launch traced here: 70.9 us
  Pallas kernels  29.3 us (41%)
  blocking collectives  18.3 us (26%)
  starting transfers between devices  12.2 us (17%)
  waiting for transfers between devices  9.6 us (13%)
  local copies, waits for them, and re-layouts  0.78 us (1%)
  between operations  0.72 us (1%)
    all_to_all x1, blocking collectives, exchange(): return lax.all_to_all(rows, axes, split_axis=0, concat_axis=0, tiled=True)  18.3 us
    pallas_call x1, Pallas kernels, expert(): call(functools.partial(expert_kernel, chunks), 'expert_rows', SHARED, 8 *...  9.54 us
    pallas_call x1, Pallas kernels, replica_grads(): call(functools.partial(replica_kernel, chunks), 'replica_grads', SHARED,...  8.82 us
    ppermute x7, waiting for transfers between devices, terms_of_group(): lax.ppermute(array, axis, [(i, i ^ distance) for i in range(count)])  7.57 us
    ppermute x7, starting transfers between devices, terms_of_group(): lax.ppermute(array, axis, [(i, i ^ distance) for i in range(count)])  6.98 us
    pallas_call x1, Pallas kernels, logits_grads(): call(logits_kernel, 'logits_grads', SHARED, 6 * images * slots * length *...  4.32 us
    all_to_all x1, starting transfers between devices, exchange(): return lax.all_to_all(rows, axes, split_axis=0, concat_axis=0, tiled=True)  3.74 us
    pallas_call x1, Pallas kernels, gather(): call(gather_kernel, 'gather_slots', SHARED, 6 * images * slots * length *...  3.18 us
  transfers between devices with their start and end apart: 9, of which 4 were waited for; matrix products, arithmetic and copies ran while one was open for 0% of the time, Pallas kernels for 30%

profile of v12, /device:TPU:0, one launch (start us, length us, event | category | flops | bytes accessed | tf_op | source)
XLA Modules:
  0.0 70.9 jit_solution(5752000657651159247)
XLA Ops:
  0.6 0.0 copy-start
  0.6 0.8 %copy-done = bf16[1280,16]{0,1:T(8,128)(2,1)S(1)} copy-done((bf16[1280,16]{0,1:T(8,128)(2,1)S(1)}, bf16[1280,16]{0,1:T(8,128)(2,1)}, u32[]{:S(2)}) %copy-start) | copy-done | bytes 40984
  1.4 3.2 %gather_slots.1 = (bf16[128,1280]{1,0:T(8,128)(2,1)S(1)}, f32[4,16,256]{2,1,0:T(8,128)S(1)}, f32[4,16,256]{2,1,0:T(8,128)S(1)}) custom-call(bf16[4,256,1280]{2,1,0:T(8,128)(2,1)} %tokens.3, bf16[16,1280]{1,0:T(8,128)(2,1)S(1)} %bitcast.16, bf16[4,256,1280]{2,1,0:T(8,128)(2,1)} %grads.3), custom_call_target="tpu_custom_call" | custom-call | flops 125829120 | bytes 5242880 | tf_op jit(solution)/shard_map/gather_slots/pallas_call | solution.py:135
  4.6 18.3 %all_to_all.22 = bf16[16,8,1280]{2,1,0:T(8,128)(2,1)S(1)} all-to-all(bf16[16,8,1280]{2,1,0:T(8,128)(2,1)S(1)} %bitcast.15), channel_id=1, replica_groups=mesh['rep'=2,'exp'=16] {'exp'}, dimensions={0} | all-to-all | bytes 655360 | tf_op jit(solution)/shard_map/all_to_all | solution.py:455
  22.9 1.5 %collective-permute-start = (bf16[128,1280]{1,0:T(8,128)(2,1)S(1)}, bf16[128,1280]{1,0:T(8,128)(2,1)S(1)}, u32[]{:S(2)}, u32[]{:S(2)}) collective-permute-start(bf16[128,1280]{1,0:T(8,128)(2,1)S(1)} %bitcast.11), channel_id=1, source_target_pairs={{0,16},{16,0},{1,17},{17,1},{2,18},{18,2},{3,19},{19,3},{4,20},{20... | collective-permute-start | bytes 983048 | tf_op jit(solution)/shard_map/ppermute | solution.py:466
  24.4 9.5 %expert_rows.1 = (bf16[128,1280]{1,0:T(8,128)(2,1)}, bf16[64,2560]{1,0:T(8,128)(2,1)S(1)}, bf16[64,2560]{1,0:T(8,128)(2,1)S(1)}, f32[8,128]{1,0:T(8,128)S(1)}) custom-call(bf16[128,1280]{1,0:T(8,128)(2,1)S(1)} %bitcast.12, bf16[1280,2560]{1,0:T(8,128)(2,1)} %bitcast.18, bf16[2560,1280]{1,0:T(8,128)(2,1)} %bitcast.20), custom_call_target="tpu_custom_call" | custom-call | flops 1677721600 | bytes 13107200 | tf_op jit(solution)/shard_map/expert_rows/pallas_call | solution.py:216
  33.9 3.7 %all-to-all-start.1 = ((bf16[16,8,1280]{2,1,0:T(8,128)(2,1)}), bf16[16,8,1280]{2,1,0:T(8,128)(2,1)S(1)}, u32[]{:S(2)}, u32[]{:S(2)}) async-start(bf16[16,8,1280]{2,1,0:T(8,128)(2,1)} %bitcast.6), calls=%async_computation.1 | async-start | bytes 655360 | tf_op jit(solution)/shard_map/all_to_all | solution.py:455
  37.7 0.0 collective-permute-done.other_rows
  37.7 0.0 copy-start.1
  37.7 8.8 %replica_grads.1 = (bf16[640,2560]{1,0:T(8,128)(2,1)}, bf16[1280,1280]{1,0:T(8,128)(2,1)}, f32[8,128]{1,0:T(8,128)S(1)}) custom-call(s32[1]{0:T(128)} %bitcast.mine, f32[8,128]{1,0:T(8,128)S(1)} %get-tuple-element.26.after, bf16[128,1280]{1,0:T(8,128)(2,1)S(1)} %bitcast.13, bf16[128,1280]{1,0:T(8,128)(2,1)S(1)} %collective-permute-done.other_rows, ...), custom_call_target="tpu_custom_call" | custom-call | flops 13421772800 | bytes 104857600 | tf_op jit(solution)/shard_map/replica_grads/pallas_call | solution.py:303
  46.5 2.0 %all-to-all-done.1 = bf16[16,8,1280]{2,1,0:T(8,128)(2,1)S(1)} async-done(((bf16[16,8,1280]{2,1,0:T(8,128)(2,1)}), bf16[16,8,1280]{2,1,0:T(8,128)(2,1)S(1)}, u32[]{:S(2)}, u32[]{:S(2)}) %all-to-all-start.1) | async-done | bytes 327712 | tf_op jit(solution)/shard_map/all_to_all | solution.py:455
  48.6 0.0 copy-done.1
  48.6 4.3 %logits_grads.1 = (bf16[4,32,256]{2,1,0:T(8,128)(2,1)S(1)}, bf16[4,32,1280]{2,1,0:T(8,128)(2,1)S(1)}, bf16[16,1280]{1,0:T(8,128)(2,1)S(1)}, f32[8,128]{1,0:T(8,128)S(1)}) custom-call(f32[8,128]{1,0:T(8,128)S(1)} %get-tuple-element.29.after, bf16[128,1280]{1,0:T(8,128)(2,1)S(1)} %bitcast.14, bf16[4,256,1280]{2,1,0:T(8,128)(2,1)} %tokens.3, ...), custom_call_target="tpu_custom_call" | custom-call | flops 125829120 | bytes 5242880 | tf_op jit(solution)/shard_map/logits_grads/pallas_call | solution.py:377
  52.9 0.1 collective-permute-start.1
  53.0 0.8 %collective-permute-start.2 = (bf16[16,1280]{1,0:T(8,128)(2,1)S(1)}, bf16[16,1280]{1,0:T(8,128)(2,1)S(1)}, u32[]{:S(2)}, u32[]{:S(2)}) collective-permute-start(bf16[16,1280]{1,0:T(8,128)(2,1)S(1)} %get-tuple-element.38.refs_0_), channel_id=1, source_target_pairs={{0,2},{1,3},{2,0},{3,1},{4,6},{5,7},{6,4},{7,5},{8,10},{9,11},{10,... | collective-permute-start | bytes 122888 | tf_op jit(solution)/shard_map/ppermute | solution.py:449
  53.7 1.1 %collective-permute-start.3 = (bf16[16,1280]{1,0:T(8,128)(2,1)S(1)}, bf16[16,1280]{1,0:T(8,128)(2,1)S(1)}, u32[]{:S(2)}, u32[]{:S(2)}) collective-permute-start(bf16[16,1280]{1,0:T(8,128)(2,1)S(1)} %get-tuple-element.38.refs_0_), channel_id=1, source_target_pairs={{0,3},{1,2},{2,1},{3,0},{4,7},{5,6},{6,5},{7,4},{8,11},{9,10},{10,... | collective-permute-start | bytes 122888 | tf_op jit(solution)/shard_map/ppermute | solution.py:449
  54.8 2.7 %tokens_grads.1 = (bf16[4,256,1280]{2,1,0:T(8,128)(2,1)}, f32[8,128]{1,0:T(8,128)S(1)}) custom-call(f32[8,128]{1,0:T(8,128)S(1)} %get-tuple-element.33.after, bf16[4,32,256]{2,1,0:T(8,128)(2,1)S(1)} %get-tuple-element.34.left, bf16[4,32,1280]{2,1,0:T(8,128)(2,1)S(1)} %get-tuple-element.35.right), custom_call_target="tpu_custom_call" | custom-call | flops 83886080 | bytes 2621440 | tf_op jit(solution)/shard_map/tokens_grads/pallas_call | solution.py:408
  57.6 0.0 collective-permute-done.1.refs_1_
  57.6 0.0 collective-permute-done.2.refs_2_
  57.6 0.0 collective-permute-done.3.refs_3_
  57.6 1.1 %collective-permute-start.4 = (bf16[16,1280]{1,0:T(8,128)(2,1)S(1)}, bf16[16,1280]{1,0:T(8,128)(2,1)S(1)}, u32[]{:S(2)}, u32[]{:S(2)}) collective-permute-start(bf16[16,1280]{1,0:T(8,128)(2,1)S(1)} %get-tuple-element.40.refs_0_), channel_id=1, source_target_pairs={{0,4},{1,5},{2,6},{3,7},{4,0},{5,1},{6,2},{7,3},{8,12},{9,13},{10,... | collective-permute-start | bytes 122888 | tf_op jit(solution)/shard_map/ppermute | solution.py:449
  58.7 1.7 %collective-permute-start.5 = (bf16[16,1280]{1,0:T(8,128)(2,1)S(1)}, bf16[16,1280]{1,0:T(8,128)(2,1)S(1)}, u32[]{:S(2)}, u32[]{:S(2)}) collective-permute-start(bf16[16,1280]{1,0:T(8,128)(2,1)S(1)} %get-tuple-element.40.refs_0_), channel_id=1, source_target_pairs={{0,8},{1,9},{2,10},{3,11},{4,12},{5,13},{6,14},{7,15},{8,0},{9,1},... | collective-permute-start | bytes 122888 | tf_op jit(solution)/shard_map/ppermute | solution.py:449
  60.4 1.7 %collective-permute-start.6 = (bf16[16,1280]{1,0:T(8,128)(2,1)S(1)}, bf16[16,1280]{1,0:T(8,128)(2,1)S(1)}, u32[]{:S(2)}, u32[]{:S(2)}) collective-permute-start(bf16[16,1280]{1,0:T(8,128)(2,1)S(1)} %get-tuple-element.40.refs_0_), channel_id=1, source_target_pairs={{0,12},{1,13},{2,14},{3,15},{4,8},{5,9},{6,10},{7,11},{8,4},{9,5},... | collective-permute-start | bytes 122888 | tf_op jit(solution)/shard_map/ppermute | solution.py:449
  62.1 0.0 collective-permute-done.4.refs_1_
  62.1 2.8 %collective-permute-done.5.refs_2_ = bf16[16,1280]{1,0:T(8,128)(2,1)S(1)} collective-permute-done((bf16[16,1280]{1,0:T(8,128)(2,1)S(1)}, bf16[16,1280]{1,0:T(8,128)(2,1)S(1)}, u32[]{:S(2)}, u32[]{:S(2)}) %collective-permute-start.5) | collective-permute-done | bytes 40992 | tf_op jit(solution)/shard_map/ppermute | solution.py:449
  64.9 1.3 %collective-permute-done.6.refs_3_ = bf16[16,1280]{1,0:T(8,128)(2,1)S(1)} collective-permute-done((bf16[16,1280]{1,0:T(8,128)(2,1)S(1)}, bf16[16,1280]{1,0:T(8,128)(2,1)S(1)}, u32[]{:S(2)}, u32[]{:S(2)}) %collective-permute-start.6) | collective-permute-done | bytes 40992 | tf_op jit(solution)/shard_map/ppermute | solution.py:449
  66.2 0.6 collective-permute-start.7
  66.8 3.5 %collective-permute-done.7.refs_1_ = bf16[16,1280]{1,0:T(8,128)(2,1)S(1)} collective-permute-done((bf16[16,1280]{1,0:T(8,128)(2,1)S(1)}, bf16[16,1280]{1,0:T(8,128)(2,1)S(1)}, u32[]{:S(2)}, u32[]{:S(2)}) %collective-permute-start.7) | collective-permute-done | bytes 40992 | tf_op jit(solution)/shard_map/ppermute | solution.py:449
  70.2 0.6 add_terms.5
  (2 shorter events, 0.1 us)
Async XLA Ops:
  0.6 0.8 %copy-start = (bf16[1280,16]{0,1:T(8,128)(2,1)S(1)}, bf16[1280,16]{0,1:T(8,128)(2,1)}, u32[]{:S(2)}) copy-start(bf16[1280,16]{0,1:T(8,128)(2,1)} %param.6) | copy-start | bytes 122884
  22.9 14.8 %collective-permute-start = (bf16[128,1280]{1,0:T(8,128)(2,1)S(1)}, bf16[128,1280]{1,0:T(8,128)(2,1)S(1)}, u32[]{:S(2)}, u32[]{:S(2)}) collective-permute-start(bf16[128,1280]{1,0:T(8,128)(2,1)S(1)} %bitcast.11), channel_id=1, source_target_pairs={{0,16},{16,0},{1,17},{17,1},{2,18},{18,2},{3,19},{19,3},{4,20},{20... | collective-permute-start | bytes 983048 | tf_op jit(solution)/shard_map/ppermute | solution.py:466
  33.9 14.6 %all-to-all-start.1 = ((bf16[16,8,1280]{2,1,0:T(8,128)(2,1)}), bf16[16,8,1280]{2,1,0:T(8,128)(2,1)S(1)}, u32[]{:S(2)}, u32[]{:S(2)}) async-start(bf16[16,8,1280]{2,1,0:T(8,128)(2,1)} %bitcast.6), calls=%async_computation.1 | async-start | bytes 655360 | tf_op jit(solution)/shard_map/all_to_all | solution.py:455
  37.7 10.9 %copy-start.1 = (bf16[1280,16]{0,1:T(8,128)(2,1)S(1)}, bf16[1280,16]{0,1:T(8,128)(2,1)}, u32[]{:S(2)}) copy-start(bf16[1280,16]{0,1:T(8,128)(2,1)} %param.6) | copy-start | bytes 122884
  52.9 4.7 %collective-permute-start.1 = (bf16[16,1280]{1,0:T(8,128)(2,1)S(1)}, bf16[16,1280]{1,0:T(8,128)(2,1)S(1)}, u32[]{:S(2)}, u32[]{:S(2)}) collective-permute-start(bf16[16,1280]{1,0:T(8,128)(2,1)S(1)} %get-tuple-element.38.refs_0_), channel_id=1, source_target_pairs={{0,1},{1,0},{2,3},{3,2},{4,5},{5,4},{6,7},{7,6},{8,9},{9,8},{10,11... | collective-permute-start | bytes 122888 | tf_op jit(solution)/shard_map/ppermute | solution.py:449
  53.0 4.6 %collective-permute-start.2 = (bf16[16,1280]{1,0:T(8,128)(2,1)S(1)}, bf16[16,1280]{1,0:T(8,128)(2,1)S(1)}, u32[]{:S(2)}, u32[]{:S(2)}) collective-permute-start(bf16[16,1280]{1,0:T(8,128)(2,1)S(1)} %get-tuple-element.38.refs_0_), channel_id=1, source_target_pairs={{0,2},{1,3},{2,0},{3,1},{4,6},{5,7},{6,4},{7,5},{8,10},{9,11},{10,... | collective-permute-start | bytes 122888 | tf_op jit(solution)/shard_map/ppermute | solution.py:449
  53.7 3.9 %collective-permute-start.3 = (bf16[16,1280]{1,0:T(8,128)(2,1)S(1)}, bf16[16,1280]{1,0:T(8,128)(2,1)S(1)}, u32[]{:S(2)}, u32[]{:S(2)}) collective-permute-start(bf16[16,1280]{1,0:T(8,128)(2,1)S(1)} %get-tuple-element.38.refs_0_), channel_id=1, source_target_pairs={{0,3},{1,2},{2,1},{3,0},{4,7},{5,6},{6,5},{7,4},{8,11},{9,10},{10,... | collective-permute-start | bytes 122888 | tf_op jit(solution)/shard_map/ppermute | solution.py:449
  57.6 4.5 %collective-permute-start.4 = (bf16[16,1280]{1,0:T(8,128)(2,1)S(1)}, bf16[16,1280]{1,0:T(8,128)(2,1)S(1)}, u32[]{:S(2)}, u32[]{:S(2)}) collective-permute-start(bf16[16,1280]{1,0:T(8,128)(2,1)S(1)} %get-tuple-element.40.refs_0_), channel_id=1, source_target_pairs={{0,4},{1,5},{2,6},{3,7},{4,0},{5,1},{6,2},{7,3},{8,12},{9,13},{10,... | collective-permute-start | bytes 122888 | tf_op jit(solution)/shard_map/ppermute | solution.py:449
  58.7 6.2 %collective-permute-start.5 = (bf16[16,1280]{1,0:T(8,128)(2,1)S(1)}, bf16[16,1280]{1,0:T(8,128)(2,1)S(1)}, u32[]{:S(2)}, u32[]{:S(2)}) collective-permute-start(bf16[16,1280]{1,0:T(8,128)(2,1)S(1)} %get-tuple-element.40.refs_0_), channel_id=1, source_target_pairs={{0,8},{1,9},{2,10},{3,11},{4,12},{5,13},{6,14},{7,15},{8,0},{9,1},... | collective-permute-start | bytes 122888 | tf_op jit(solution)/shard_map/ppermute | solution.py:449
  60.4 5.8 %collective-permute-start.6 = (bf16[16,1280]{1,0:T(8,128)(2,1)S(1)}, bf16[16,1280]{1,0:T(8,128)(2,1)S(1)}, u32[]{:S(2)}, u32[]{:S(2)}) collective-permute-start(bf16[16,1280]{1,0:T(8,128)(2,1)S(1)} %get-tuple-element.40.refs_0_), channel_id=1, source_target_pairs={{0,12},{1,13},{2,14},{3,15},{4,8},{5,9},{6,10},{7,11},{8,4},{9,5},... | collective-permute-start | bytes 122888 | tf_op jit(solution)/shard_map/ppermute | solution.py:449
  66.2 4.1 %collective-permute-start.7 = (bf16[16,1280]{1,0:T(8,128)(2,1)S(1)}, bf16[16,1280]{1,0:T(8,128)(2,1)S(1)}, u32[]{:S(2)}, u32[]{:S(2)}) collective-permute-start(bf16[16,1280]{1,0:T(8,128)(2,1)S(1)} %get-tuple-element.42.refs_0_), channel_id=1, source_target_pairs={{0,16},{16,0},{1,17},{17,1},{2,18},{18,2},{3,19},{19,3},{4,20},{20... | collective-permute-start | bytes 122888 | tf_op jit(solution)/shard_map/ppermute | solution.py:449

commit v13 on v12

--- a/solution.py
+++ b/solution.py
@@ -15,6 +15,7 @@
 LANES = 128
 KINDS = 2
 SHARED = 52 * 1024 * 1024
+ROOMY = 50 * 1024 * 1024
 WHOLE = pl.BlockSpec(memory_space=pltpu.VMEM)
 PLACE = pl.BlockSpec(memory_space=pl.ANY)
 
@@ -100,13 +101,19 @@
 
 
 def gather_kernel(
-    tokens, params, grads, sent, dispatch, combine, tokens_v, grads_v, rows, sems
+    tokens, params, grads, w_in, w_out, sent, dispatch, combine, first_in, first_out,
+    tokens_v, grads_v, rows, sems,
 ):
     images = tokens.shape[0]
     slots = params.shape[0]
     stride = KINDS * images
     halves = start_halves(tokens, tokens_v, sems)
     grads_copy = start_copy(grads, grads_v, sems.at[2])
+    units = slice(0, first_out.shape[0])
+    weight_copies = (
+        start_copy(w_in.at[:, units], first_in, sems.at[3]),
+        start_copy(w_out.at[units, :], first_out, sems.at[4]),
+    )
     logits = []
     for copy, half in halves:
         copy.wait()
@@ -125,9 +132,11 @@
         value = dot(over_slots[image].astype(LOW), grads_v[image], 1, 0)
         put(rows, KINDS * image + 1, slots, stride, value)
     sent[...] = packed(rows)
-
-
-def gather(tokens, params, grads):
+    for copy in weight_copies:
+        copy.wait()
+
+
+def gather(tokens, params, grads, w_in, w_out, first):
     images, length, width = tokens.shape
     slots = params.shape[0]
     weights = shaped((images, slots, length), WIDE)
@@ -135,20 +144,26 @@
     return call(
         gather_kernel,
         "gather_slots",
-        SHARED,
+        ROOMY,
         6 * images * slots * length * width,
         4 * images * length * width,
         2 * images * slots * length,
-        out_shape=(shaped(rows, LOW), weights, weights),
-        in_specs=[PLACE, WHOLE, PLACE],
-        out_specs=(WHOLE, WHOLE, WHOLE),
+        out_shape=(
+            shaped(rows, LOW),
+            weights,
+            weights,
+            shaped((width, first), LOW),
+            shaped((first, width), LOW),
+        ),
+        in_specs=[PLACE, WHOLE, PLACE, PLACE, PLACE],
+        out_specs=(WHOLE,) * 5,
         scratch_shapes=[
             pltpu.VMEM(tokens.shape, LOW),
             pltpu.VMEM(grads.shape, LOW),
             scratch_rows(rows),
-            pltpu.SemaphoreType.DMA((3,)),
+            pltpu.SemaphoreType.DMA((5,)),
         ],
-    )(tokens, params, grads)
+    )(tokens, params, grads, w_in, w_out)
 
 
 def chunks_of(first, hidden, tile):
@@ -177,7 +192,8 @@
 
 
 def expert_kernel(
-    chunks, rows, w_in, w_out, back, acts, hidden, mark, w_in_v, w_out_v, sems, wide
+    chunks, rows, first_in, first_out, w_in, w_out, back, acts, hidden, mark,
+    w_in_v, w_out_v, sems, wide,
 ):
     del mark
     copies = start_weights(w_in, w_out, w_in_v, w_out_v, sems, chunks)
@@ -185,46 +201,58 @@
     load_rows(wide, rows[...])
     rows_in = take(wide, 0, count, KINDS).astype(LOW)
     rows_grad = take(wide, 1, count, KINDS).astype(LOW)
-    out = d_in = held = before = None
+
+    def first_products(weight_in, weight_out):
+        return dot(rows_in, weight_in, 1, 0), dot(rows_grad, weight_out, 1, 1)
+
+    def second_products(held, weight_in, weight_out):
+        return dot(held[0], weight_out, 1, 0), dot(held[1], weight_in, 1, 1)
+
+    def hold(preact, d_acts, units):
+        values, slope = gelu_parts(preact)
+        held = (values.astype(LOW), (d_acts * slope).astype(LOW))
+        acts[:, units], hidden[:, units] = held
+        return held
+
+    held = hold(
+        *first_products(first_in[...], first_out[...]), slice(0, first_out.shape[0])
+    )
+    out, d_in = second_products(held, first_in[...], first_out[...])
+    before = None
     for pair, units in zip([*copies, None], [*chunks, None]):
         if pair is not None:
             for copy in pair:
                 copy.wait()
-            preact = dot(rows_in, w_in_v[:, units], 1, 0)
-            d_acts = dot(rows_grad, w_out_v[units, :], 1, 1)
+            products = first_products(w_in_v[:, units], w_out_v[units, :])
         if before is not None:
-            out_part = dot(held[0], w_out_v[before, :], 1, 0)
-            d_in_part = dot(held[1], w_in_v[:, before], 1, 1)
-            out = out_part if out is None else out + out_part
-            d_in = d_in_part if d_in is None else d_in + d_in_part
+            parts = second_products(held, w_in_v[:, before], w_out_v[before, :])
+            out, d_in = out + parts[0], d_in + parts[1]
         if pair is not None:
-            values, slope = gelu_parts(preact)
-            held = (values.astype(LOW), (d_acts * slope).astype(LOW))
-            acts[:, units], hidden[:, units] = held
+            held = hold(*products, units)
         before = units
     put(wide, 0, count, KINDS, out)
     put(wide, 1, count, KINDS, d_in)
     back[...] = packed(wide)
 
 
-def expert(rows, w_in, w_out, tile):
+def expert(rows, first_in, first_out, w_in, w_out, tile):
     total, width = rows.shape
     hidden = w_in.shape[1]
     count = total // KINDS
     kept = shaped((count, hidden), LOW)
-    chunks = chunks_of(0, hidden, tile)
+    chunks = chunks_of(first_out.shape[0], hidden, tile)
     return call(
         functools.partial(expert_kernel, chunks),
         "expert_rows",
-        SHARED,
+        ROOMY,
         8 * count * hidden * width,
         4 * hidden * width,
         count * hidden,
         out_shape=(shaped(rows.shape, LOW), kept, kept, MARK),
-        in_specs=[WHOLE, PLACE, PLACE],
+        in_specs=[WHOLE, WHOLE, WHOLE, PLACE, PLACE],
         out_specs=(WHOLE, WHOLE, WHOLE, PLACE),
         scratch_shapes=[*weight_scratch(width, hidden, chunks), scratch_rows(rows.shape)],
-    )(rows, w_in, w_out)
+    )(rows, first_in, first_out, w_in, w_out)
 
 
 def replica_kernel(
@@ -461,10 +489,10 @@
     replicas = lax.axis_size("rep")
     mine = lax.axis_index("rep").astype(jnp.int32).reshape(1)
 
-    sent, dispatch, combine = gather(tokens, params, grad_out)
+    sent, dispatch, combine, *first = gather(tokens, params, grad_out, *weights, 512)
     rows = exchange(sent, "exp")
     other_rows = lax.ppermute(rows, "rep", [(i, (i + 1) % replicas) for i in range(replicas)])
-    back, acts, hidden, after = expert(rows, *weights, 512)
+    back, acts, hidden, after = expert(rows, *first, *weights, 512)
     back = exchange(back, "exp")
     grad_in, grad_outer, after = replica_grads(
         mine, after, rows, other_rows, acts, hidden, *weights, replicas, 512

time: 71.2 us -> 74.1 us (1.041)
  local copies, waits for them, and re-layouts: 0.78 us -> 4.16 us
    unnamed x4 -> x12, local copies, waits for them, and re-layouts: 0.78 us -> 4.16 us
    all_to_all x1, waiting for transfers between devices: 2.03 us -> 0.1 us  [exchange(): return lax.all_to_all(rows, axes, split_axis=0, concat_axis=0, tiled=True)]
    ppermute x7, waiting for transfers between devices: 7.57 us -> 9.48 us  [terms_of_group(): lax.ppermute(array, axis, [(i, i ^ distance) for i in range(count)])]
  transfers between devices with their start and end apart: 9 -> 9, of which waited for: 4 -> 5; matrix products, arithmetic and copies ran while one was open for 0% -> 0% of each run, Pallas kernels for 30% -> 28%
where the time goes in v13:
time: 74.1 us; the launch traced here: 73.7 us
  Pallas kernels  28.8 us (39%)
  blocking collectives  18.3 us (25%)
  starting transfers between devices  12.2 us (16%)
  waiting for transfers between devices  9.58 us (13%)
  local copies, waits for them, and re-layouts  4.16 us (6%)
    all_to_all x1, blocking collectives, exchange(): return lax.all_to_all(rows, axes, split_axis=0, concat_axis=0, tiled=True)  18.3 us
    ppermute x7, waiting for transfers between devices, terms_of_group(): lax.ppermute(array, axis, [(i, i ^ distance) for i in range(count)])  9.48 us
    pallas_call x1, Pallas kernels, expert(): call(functools.partial(expert_kernel, chunks), 'expert_rows', ROOMY, 8 *...  8.89 us
    pallas_call x1, Pallas kernels, replica_grads(): call(functools.partial(replica_kernel, chunks), 'replica_grads', SHARED,...  8.81 us
    ppermute x7, starting transfers between devices, terms_of_group(): lax.ppermute(array, axis, [(i, i ^ distance) for i in range(count)])  7 us
    pallas_call x1, Pallas kernels, logits_grads(): call(logits_kernel, 'logits_grads', SHARED, 6 * images * slots * length *...  4.32 us
    unnamed x12, local copies, waits for them, and re-layouts  4.16 us
    all_to_all x1, starting transfers between devices, exchange(): return lax.all_to_all(rows, axes, split_axis=0, concat_axis=0, tiled=True)  3.72 us
  transfers between devices with their start and end apart: 9, of which 5 were waited for; matrix products, arithmetic and copies ran while one was open for 0% of the time, Pallas kernels for 28%

profile of v13, /device:TPU:0, one launch (start us, length us, event | category | flops | bytes accessed | tf_op | source)
XLA Modules:
  0.0 73.7 jit_solution(17477222265925503406)
XLA Ops:
  0.6 0.0 copy-start
  0.6 0.8 %copy-done = bf16[1280,16]{0,1:T(8,128)(2,1)S(1)} copy-done((bf16[1280,16]{0,1:T(8,128)(2,1)S(1)}, bf16[1280,16]{0,1:T(8,128)(2,1)}, u32[]{:S(2)}) %copy-start) | copy-done | bytes 40984
  1.4 3.3 %gather_slots.1 = (bf16[128,1280]{1,0:T(8,128)(2,1)S(1)}, f32[4,16,256]{2,1,0:T(8,128)S(1)}, f32[4,16,256]{2,1,0:T(8,128)S(1)}, bf16[1280,512]{1,0:T(8,128)(2,1)S(1)}, bf16[512,1280]{1,0:T(8,128)(2,1)S(1)}) custom-call(bf16[4,256,1280]{2,1,0:T(8,128)(2,1)} %tokens.3, bf16[16,1280]{1,0:T(8,128)(2,1)S(1)} %bitcast.16, bf16[4,256,1280]{2,1,0:T(8,128)(2,1)} %grads.3, ...), custom_call_target="tpu_custom_call" | custom-call | flops 125829120 | bytes 5242880 | tf_op jit(solution)/shard_map/gather_slots/pallas_call | solution.py:144
  4.7 18.3 %all_to_all.22 = bf16[16,8,1280]{2,1,0:T(8,128)(2,1)S(1)} all-to-all(bf16[16,8,1280]{2,1,0:T(8,128)(2,1)S(1)} %bitcast.15), channel_id=1, replica_groups=mesh['rep'=2,'exp'=16] {'exp'}, dimensions={0} | all-to-all | bytes 655360 | tf_op jit(solution)/shard_map/all_to_all | solution.py:483
  23.0 1.5 %collective-permute-start = (bf16[128,1280]{1,0:T(8,128)(2,1)S(1)}, bf16[128,1280]{1,0:T(8,128)(2,1)S(1)}, u32[]{:S(2)}, u32[]{:S(2)}) collective-permute-start(bf16[128,1280]{1,0:T(8,128)(2,1)S(1)} %bitcast.12), channel_id=1, source_target_pairs={{0,16},{16,0},{1,17},{17,1},{2,18},{18,2},{3,19},{19,3},{4,20},{20... | collective-permute-start | bytes 983048 | tf_op jit(solution)/shard_map/ppermute | solution.py:494
  24.5 8.9 %expert_rows.1 = (bf16[128,1280]{1,0:T(8,128)(2,1)}, bf16[64,2560]{1,0:T(8,128)(2,1)S(1)}, bf16[64,2560]{1,0:T(8,128)(2,1)S(1)}, f32[8,128]{1,0:T(8,128)S(1)}) custom-call(bf16[128,1280]{1,0:T(8,128)(2,1)S(1)} %bitcast.13, bf16[1280,512]{1,0:T(8,128)(2,1)S(1)} %get-tuple-element.28.first_in, bf16[512,1280]{1,0:T(8,128)(2,1)S(1)} %get-tuple-element.29.first_out, ...), custom_call_target="tpu_custom_call" | custom-call | flops 1677721600 | bytes 13107200 | tf_op jit(solution)/shard_map/expert_rows/pallas_call | solution.py:244
  33.4 0.0 copy-start.2
  33.4 0.7 copy-done.2
  34.1 0.0 copy-start.4
  34.1 0.7 copy-done.4
  34.9 3.7 %all-to-all-start.1 = ((bf16[16,8,1280]{2,1,0:T(8,128)(2,1)}), bf16[16,8,1280]{2,1,0:T(8,128)(2,1)S(1)}, u32[]{:S(2)}, u32[]{:S(2)}) async-start(bf16[16,8,1280]{2,1,0:T(8,128)(2,1)} %bitcast.6), calls=%async_computation.1 | async-start | bytes 655360 | tf_op jit(solution)/shard_map/all_to_all | solution.py:483
  38.6 0.0 collective-permute-done.other_rows
  38.6 0.0 copy-start.3
  38.6 1.0 %copy-done.3 = bf16[64,2560]{1,0:T(8,128)(2,1)S(1)} copy-done((bf16[64,2560]{1,0:T(8,128)(2,1)S(1)}, bf16[64,2560]{1,0:T(8,128)(2,1)}, u32[]{:S(2)}) %copy-start.3) | copy-done | bytes 327704
  39.6 0.0 copy-start.5
  39.6 1.0 %copy-done.5 = bf16[64,2560]{1,0:T(8,128)(2,1)S(1)} copy-done((bf16[64,2560]{1,0:T(8,128)(2,1)S(1)}, bf16[64,2560]{1,0:T(8,128)(2,1)}, u32[]{:S(2)}) %copy-start.5) | copy-done | bytes 327704
  40.6 0.0 copy-start.1
  40.6 8.8 %replica_grads.1 = (bf16[640,2560]{1,0:T(8,128)(2,1)}, bf16[1280,1280]{1,0:T(8,128)(2,1)}, f32[8,128]{1,0:T(8,128)S(1)}) custom-call(s32[1]{0:T(128)} %bitcast.mine, f32[8,128]{1,0:T(8,128)S(1)} %get-tuple-element.30.after, bf16[128,1280]{1,0:T(8,128)(2,1)S(1)} %bitcast.14, bf16[128,1280]{1,0:T(8,128)(2,1)S(1)} %collective-permute-done.other_rows, ...), custom_call_target="tpu_custom_call" | custom-call | flops 13421772800 | bytes 104857600 | tf_op jit(solution)/shard_map/replica_grads/pallas_call | solution.py:331
  49.4 0.1 all-to-all-done.1
  49.5 0.0 copy-done.1
  49.5 4.3 %logits_grads.1 = (bf16[4,32,256]{2,1,0:T(8,128)(2,1)S(1)}, bf16[4,32,1280]{2,1,0:T(8,128)(2,1)S(1)}, bf16[16,1280]{1,0:T(8,128)(2,1)S(1)}, f32[8,128]{1,0:T(8,128)S(1)}) custom-call(f32[8,128]{1,0:T(8,128)S(1)} %get-tuple-element.33.after, bf16[128,1280]{1,0:T(8,128)(2,1)S(1)} %bitcast.11, bf16[4,256,1280]{2,1,0:T(8,128)(2,1)} %tokens.3, ...), custom_call_target="tpu_custom_call" | custom-call | flops 125829120 | bytes 5242880 | tf_op jit(solution)/shard_map/logits_grads/pallas_call | solution.py:405
  53.8 0.1 collective-permute-start.1
  53.9 1.7 %collective-permute-start.2 = (bf16[16,1280]{1,0:T(8,128)(2,1)S(1)}, bf16[16,1280]{1,0:T(8,128)(2,1)S(1)}, u32[]{:S(2)}, u32[]{:S(2)}) collective-permute-start(bf16[16,1280]{1,0:T(8,128)(2,1)S(1)} %get-tuple-element.42.refs_0_), channel_id=1, source_target_pairs={{0,2},{1,3},{2,0},{3,1},{4,6},{5,7},{6,4},{7,5},{8,10},{9,11},{10,... | collective-permute-start | bytes 122888 | tf_op jit(solution)/shard_map/ppermute | solution.py:477
  55.6 0.2 collective-permute-start.3
  55.7 2.7 %tokens_grads.1 = (bf16[4,256,1280]{2,1,0:T(8,128)(2,1)}, f32[8,128]{1,0:T(8,128)S(1)}) custom-call(f32[8,128]{1,0:T(8,128)S(1)} %get-tuple-element.37.after, bf16[4,32,256]{2,1,0:T(8,128)(2,1)S(1)} %get-tuple-element.38.left, bf16[4,32,1280]{2,1,0:T(8,128)(2,1)S(1)} %get-tuple-element.39.right), custom_call_target="tpu_custom_call" | custom-call | flops 83886080 | bytes 2621440 | tf_op jit(solution)/shard_map/tokens_grads/pallas_call | solution.py:436
  58.5 0.0 collective-permute-done.1.refs_1_
  58.5 0.0 collective-permute-done.2.refs_2_
  58.5 0.7 collective-permute-done.3.refs_3_
  59.2 1.6 %collective-permute-start.4 = (bf16[16,1280]{1,0:T(8,128)(2,1)S(1)}, bf16[16,1280]{1,0:T(8,128)(2,1)S(1)}, u32[]{:S(2)}, u32[]{:S(2)}) collective-permute-start(bf16[16,1280]{1,0:T(8,128)(2,1)S(1)} %get-tuple-element.44.refs_0_), channel_id=1, source_target_pairs={{0,4},{1,5},{2,6},{3,7},{4,0},{5,1},{6,2},{7,3},{8,12},{9,13},{10,... | collective-permute-start | bytes 122888 | tf_op jit(solution)/shard_map/ppermute | solution.py:477
  60.8 2.4 %collective-permute-start.5 = (bf16[16,1280]{1,0:T(8,128)(2,1)S(1)}, bf16[16,1280]{1,0:T(8,128)(2,1)S(1)}, u32[]{:S(2)}, u32[]{:S(2)}) collective-permute-start(bf16[16,1280]{1,0:T(8,128)(2,1)S(1)} %get-tuple-element.44.refs_0_), channel_id=1, source_target_pairs={{0,8},{1,9},{2,10},{3,11},{4,12},{5,13},{6,14},{7,15},{8,0},{9,1},... | collective-permute-start | bytes 122888 | tf_op jit(solution)/shard_map/ppermute | solution.py:477
  63.2 0.5 collective-permute-start.6
  63.7 0.0 collective-permute-done.4.refs_1_
  63.7 2.8 %collective-permute-done.5.refs_2_ = bf16[16,1280]{1,0:T(8,128)(2,1)S(1)} collective-permute-done((bf16[16,1280]{1,0:T(8,128)(2,1)S(1)}, bf16[16,1280]{1,0:T(8,128)(2,1)S(1)}, u32[]{:S(2)}, u32[]{:S(2)}) %collective-permute-start.5) | collective-permute-done | bytes 40992 | tf_op jit(solution)/shard_map/ppermute | solution.py:477
  66.5 2.5 %collective-permute-done.6.refs_3_ = bf16[16,1280]{1,0:T(8,128)(2,1)S(1)} collective-permute-done((bf16[16,1280]{1,0:T(8,128)(2,1)S(1)}, bf16[16,1280]{1,0:T(8,128)(2,1)S(1)}, u32[]{:S(2)}, u32[]{:S(2)}) %collective-permute-start.6) | collective-permute-done | bytes 40992 | tf_op jit(solution)/shard_map/ppermute | solution.py:477
  69.0 0.6 collective-permute-start.7
  69.6 3.5 %collective-permute-done.7.refs_1_ = bf16[16,1280]{1,0:T(8,128)(2,1)S(1)} collective-permute-done((bf16[16,1280]{1,0:T(8,128)(2,1)S(1)}, bf16[16,1280]{1,0:T(8,128)(2,1)S(1)}, u32[]{:S(2)}, u32[]{:S(2)}) %collective-permute-start.7) | collective-permute-done | bytes 40992 | tf_op jit(solution)/shard_map/ppermute | solution.py:477
  73.1 0.6 add_terms.5
  (2 shorter events, 0.1 us)
Async XLA Ops:
  0.6 0.8 %copy-start = (bf16[1280,16]{0,1:T(8,128)(2,1)S(1)}, bf16[1280,16]{0,1:T(8,128)(2,1)}, u32[]{:S(2)}) copy-start(bf16[1280,16]{0,1:T(8,128)(2,1)} %param.6) | copy-start | bytes 122884
  23.0 15.6 %collective-permute-start = (bf16[128,1280]{1,0:T(8,128)(2,1)S(1)}, bf16[128,1280]{1,0:T(8,128)(2,1)S(1)}, u32[]{:S(2)}, u32[]{:S(2)}) collective-permute-start(bf16[128,1280]{1,0:T(8,128)(2,1)S(1)} %bitcast.12), channel_id=1, source_target_pairs={{0,16},{16,0},{1,17},{17,1},{2,18},{18,2},{3,19},{19,3},{4,20},{20... | collective-permute-start | bytes 983048 | tf_op jit(solution)/shard_map/ppermute | solution.py:494
  33.4 0.7 copy-start.2
  34.1 0.7 copy-start.4
  34.9 14.6 %all-to-all-start.1 = ((bf16[16,8,1280]{2,1,0:T(8,128)(2,1)}), bf16[16,8,1280]{2,1,0:T(8,128)(2,1)S(1)}, u32[]{:S(2)}, u32[]{:S(2)}) async-start(bf16[16,8,1280]{2,1,0:T(8,128)(2,1)} %bitcast.6), calls=%async_computation.1 | async-start | bytes 655360 | tf_op jit(solution)/shard_map/all_to_all | solution.py:483
  38.6 1.0 %copy-start.3 = (bf16[64,2560]{1,0:T(8,128)(2,1)S(1)}, bf16[64,2560]{1,0:T(8,128)(2,1)}, u32[]{:S(2)}) copy-start(bf16[64,2560]{1,0:T(8,128)(2,1)} %copy-done.2) | copy-start | bytes 983044
  39.6 1.0 %copy-start.5 = (bf16[64,2560]{1,0:T(8,128)(2,1)S(1)}, bf16[64,2560]{1,0:T(8,128)(2,1)}, u32[]{:S(2)}) copy-start(bf16[64,2560]{1,0:T(8,128)(2,1)} %copy-done.4) | copy-start | bytes 983044
  40.6 8.9 %copy-start.1 = (bf16[1280,16]{0,1:T(8,128)(2,1)S(1)}, bf16[1280,16]{0,1:T(8,128)(2,1)}, u32[]{:S(2)}) copy-start(bf16[1280,16]{0,1:T(8,128)(2,1)} %param.6) | copy-start | bytes 122884
  53.8 4.7 %collective-permute-start.1 = (bf16[16,1280]{1,0:T(8,128)(2,1)S(1)}, bf16[16,1280]{1,0:T(8,128)(2,1)S(1)}, u32[]{:S(2)}, u32[]{:S(2)}) collective-permute-start(bf16[16,1280]{1,0:T(8,128)(2,1)S(1)} %get-tuple-element.42.refs_0_), channel_id=1, source_target_pairs={{0,1},{1,0},{2,3},{3,2},{4,5},{5,4},{6,7},{7,6},{8,9},{9,8},{10,11... | collective-permute-start | bytes 122888 | tf_op jit(solution)/shard_map/ppermute | solution.py:477
  53.9 4.6 %collective-permute-start.2 = (bf16[16,1280]{1,0:T(8,128)(2,1)S(1)}, bf16[16,1280]{1,0:T(8,128)(2,1)S(1)}, u32[]{:S(2)}, u32[]{:S(2)}) collective-permute-start(bf16[16,1280]{1,0:T(8,128)(2,1)S(1)} %get-tuple-element.42.refs_0_), channel_id=1, source_target_pairs={{0,2},{1,3},{2,0},{3,1},{4,6},{5,7},{6,4},{7,5},{8,10},{9,11},{10,... | collective-permute-start | bytes 122888 | tf_op jit(solution)/shard_map/ppermute | solution.py:477
  55.6 3.6 %collective-permute-start.3 = (bf16[16,1280]{1,0:T(8,128)(2,1)S(1)}, bf16[16,1280]{1,0:T(8,128)(2,1)S(1)}, u32[]{:S(2)}, u32[]{:S(2)}) collective-permute-start(bf16[16,1280]{1,0:T(8,128)(2,1)S(1)} %get-tuple-element.42.refs_0_), channel_id=1, source_target_pairs={{0,3},{1,2},{2,1},{3,0},{4,7},{5,6},{6,5},{7,4},{8,11},{9,10},{10,... | collective-permute-start | bytes 122888 | tf_op jit(solution)/shard_map/ppermute | solution.py:477
  59.2 4.5 %collective-permute-start.4 = (bf16[16,1280]{1,0:T(8,128)(2,1)S(1)}, bf16[16,1280]{1,0:T(8,128)(2,1)S(1)}, u32[]{:S(2)}, u32[]{:S(2)}) collective-permute-start(bf16[16,1280]{1,0:T(8,128)(2,1)S(1)} %get-tuple-element.44.refs_0_), channel_id=1, source_target_pairs={{0,4},{1,5},{2,6},{3,7},{4,0},{5,1},{6,2},{7,3},{8,12},{9,13},{10,... | collective-permute-start | bytes 122888 | tf_op jit(solution)/shard_map/ppermute | solution.py:477
  60.8 5.8 %collective-permute-start.5 = (bf16[16,1280]{1,0:T(8,128)(2,1)S(1)}, bf16[16,1280]{1,0:T(8,128)(2,1)S(1)}, u32[]{:S(2)}, u32[]{:S(2)}) collective-permute-start(bf16[16,1280]{1,0:T(8,128)(2,1)S(1)} %get-tuple-element.44.refs_0_), channel_id=1, source_target_pairs={{0,8},{1,9},{2,10},{3,11},{4,12},{5,13},{6,14},{7,15},{8,0},{9,1},... | collective-permute-start | bytes 122888 | tf_op jit(solution)/shard_map/ppermute | solution.py:477
  63.2 5.8 %collective-permute-start.6 = (bf16[16,1280]{1,0:T(8,128)(2,1)S(1)}, bf16[16,1280]{1,0:T(8,128)(2,1)S(1)}, u32[]{:S(2)}, u32[]{:S(2)}) collective-permute-start(bf16[16,1280]{1,0:T(8,128)(2,1)S(1)} %get-tuple-element.44.refs_0_), channel_id=1, source_target_pairs={{0,12},{1,13},{2,14},{3,15},{4,8},{5,9},{6,10},{7,11},{8,4},{9,5},... | collective-permute-start | bytes 122888 | tf_op jit(solution)/shard_map/ppermute | solution.py:477
  69.0 4.1 %collective-permute-start.7 = (bf16[16,1280]{1,0:T(8,128)(2,1)S(1)}, bf16[16,1280]{1,0:T(8,128)(2,1)S(1)}, u32[]{:S(2)}, u32[]{:S(2)}) collective-permute-start(bf16[16,1280]{1,0:T(8,128)(2,1)S(1)} %get-tuple-element.46.refs_0_), channel_id=1, source_target_pairs={{0,16},{16,0},{1,17},{17,1},{2,18},{18,2},{3,19},{19,3},{4,20},{20... | collective-permute-start | bytes 122888 | tf_op jit(solution)/shard_map/ppermute | solution.py:477

commit v14 on v13

--- a/solution.py
+++ b/solution.py
@@ -471,11 +471,15 @@
     )(after, *terms)
 
 
-def terms_of_group(array, axis, distances):
-    count = lax.axis_size(axis)
+def terms_of_group(array, bits):
+    axes = ("rep", "exp")
+    distances = [0]
+    for bit in bits:
+        distances += [distance + (1 << bit) for distance in distances]
+    count = lax.axis_size(axes)
     return [array] + [
-        lax.ppermute(array, axis, [(i, i ^ distance) for i in range(count)])
-        for distance in distances
+        lax.ppermute(array, axes, [(i, i ^ distance) for i in range(count)])
+        for distance in distances[1:]
     ]
 
 
@@ -489,7 +493,7 @@
     replicas = lax.axis_size("rep")
     mine = lax.axis_index("rep").astype(jnp.int32).reshape(1)
 
-    sent, dispatch, combine, *first = gather(tokens, params, grad_out, *weights, 512)
+    sent, dispatch, combine, *first = gather(tokens, params, grad_out, *weights, 256)
     rows = exchange(sent, "exp")
     other_rows = lax.ppermute(rows, "rep", [(i, (i + 1) % replicas) for i in range(replicas)])
     back, acts, hidden, after = expert(rows, *first, *weights, 512)
@@ -500,16 +504,15 @@
     left, right, local, after = logits_grads(
         after, back, tokens, params, grad_out, dispatch, combine
     )
-    bits = lax.axis_size("exp").bit_length() - 1
-    groups = [(1 << bit, 2 << bit, 3 << bit) for bit in range(0, bits - 1, 2)]
-    if bits % 2:
-        groups.append((1 << (bits - 1),))
-    terms = terms_of_group(local, "exp", groups[0])
+    exp_bits = lax.axis_size("exp").bit_length() - 1
+    rep_bits = replicas.bit_length() - 1
+    groups = [(0, 1, *range(exp_bits, exp_bits + rep_bits))]
+    groups += [range(bit, min(bit + 2, exp_bits)) for bit in range(2, exp_bits, 2)]
+    for bits in groups[:-1]:
+        local, after = add(after, terms_of_group(local, bits), LOW)
+    terms = terms_of_group(local, groups[-1])
     grad_tokens, after = tokens_grads(after, left, right)
-    local, after = add(after, terms, LOW)
-    for distances in groups[1:]:
-        local, after = add(after, terms_of_group(local, "exp", distances), LOW)
-    grad_params, _ = add(after, terms_of_group(local, "rep", (1,)), WIDE)
+    grad_params, _ = add(after, terms, WIDE)
     return (grad_tokens, grad_params.T, grad_in[None], grad_outer[None])
 
 

time: 74.1 us -> 70.1 us (0.946)
  waiting for transfers between devices: 9.58 us -> 5.23 us
  starting transfers between devices: 12.2 us -> 15.9 us
  local copies, waits for them, and re-layouts: 4.16 us -> 0.78 us
    ppermute x7 -> x10, waiting for transfers between devices: 9.48 us -> 3.19 us  [terms_of_group(): lax.ppermute(array, axes, [(i, i ^ distance) for i in range(count)])]
    ppermute x7 -> x10, starting transfers between devices: 7 us -> 10.6 us  [terms_of_group(): lax.ppermute(array, axes, [(i, i ^ distance) for i in range(count)])]
    unnamed x12 -> x4, local copies, waits for them, and re-layouts: 4.16 us -> 0.78 us
    all_to_all x1, waiting for transfers between devices: 0.1 us -> 2.04 us  [exchange(): return lax.all_to_all(rows, axes, split_axis=0, concat_axis=0, tiled=True)]
  transfers between devices with their start and end apart: 9 -> 12, of which waited for: 5 -> 5; matrix products, arithmetic and copies ran while one was open for 0% -> 0% of each run, Pallas kernels for 28% -> 30%
where the time goes in v14:
time: 70.1 us; the launch traced here: 69.8 us
  Pallas kernels  28.9 us (41%)
  blocking collectives  18.3 us (26%)
  starting transfers between devices  15.9 us (23%)
  waiting for transfers between devices  5.23 us (7%)
  local copies, waits for them, and re-layouts  0.78 us (1%)
  between operations  0.72 us (1%)
    all_to_all x1, blocking collectives, exchange(): return lax.all_to_all(rows, axes, split_axis=0, concat_axis=0, tiled=True)  18.3 us
    ppermute x10, starting transfers between devices, terms_of_group(): lax.ppermute(array, axes, [(i, i ^ distance) for i in range(count)])  10.6 us
    pallas_call x1, Pallas kernels, expert(): call(functools.partial(expert_kernel, chunks), 'expert_rows', ROOMY, 8 *...  9.16 us
    pallas_call x1, Pallas kernels, replica_grads(): call(functools.partial(replica_kernel, chunks), 'replica_grads', SHARED,...  8.81 us
    pallas_call x1, Pallas kernels, logits_grads(): call(logits_kernel, 'logits_grads', SHARED, 6 * images * slots * length *...  4.32 us
    all_to_all x1, starting transfers between devices, exchange(): return lax.all_to_all(rows, axes, split_axis=0, concat_axis=0, tiled=True)  3.74 us
    pallas_call x1, Pallas kernels, gather(): call(gather_kernel, 'gather_slots', ROOMY, 6 * images * slots * length *...  3.2 us
    ppermute x10, waiting for transfers between devices, terms_of_group(): lax.ppermute(array, axes, [(i, i ^ distance) for i in range(count)])  3.19 us
  transfers between devices with their start and end apart: 12, of which 5 were waited for; matrix products, arithmetic and copies ran while one was open for 0% of the time, Pallas kernels for 30%

profile of v14, /device:TPU:0, one launch (start us, length us, event | category | flops | bytes accessed | tf_op | source)
XLA Modules:
  0.0 69.8 jit_solution(4317594794867490465)
XLA Ops:
  0.6 0.0 copy-start
  0.6 0.8 %copy-done = bf16[1280,16]{0,1:T(8,128)(2,1)S(1)} copy-done((bf16[1280,16]{0,1:T(8,128)(2,1)S(1)}, bf16[1280,16]{0,1:T(8,128)(2,1)}, u32[]{:S(2)}) %copy-start) | copy-done | bytes 40984
  1.4 3.2 %gather_slots.1 = (bf16[128,1280]{1,0:T(8,128)(2,1)S(1)}, f32[4,16,256]{2,1,0:T(8,128)S(1)}, f32[4,16,256]{2,1,0:T(8,128)S(1)}, bf16[1280,256]{1,0:T(8,128)(2,1)S(1)}, bf16[256,1280]{1,0:T(8,128)(2,1)S(1)}) custom-call(bf16[4,256,1280]{2,1,0:T(8,128)(2,1)} %tokens.3, bf16[16,1280]{1,0:T(8,128)(2,1)S(1)} %bitcast.16, bf16[4,256,1280]{2,1,0:T(8,128)(2,1)} %grads.3, ...), custom_call_target="tpu_custom_call" | custom-call | flops 125829120 | bytes 5242880 | tf_op jit(solution)/shard_map/gather_slots/pallas_call | solution.py:144
  4.6 18.3 %all_to_all.22 = bf16[16,8,1280]{2,1,0:T(8,128)(2,1)S(1)} all-to-all(bf16[16,8,1280]{2,1,0:T(8,128)(2,1)S(1)} %bitcast.15), channel_id=1, replica_groups=mesh['rep'=2,'exp'=16] {'exp'}, dimensions={0} | all-to-all | bytes 655360 | tf_op jit(solution)/shard_map/all_to_all | solution.py:487
  22.9 1.5 %collective-permute-start = (bf16[128,1280]{1,0:T(8,128)(2,1)S(1)}, bf16[128,1280]{1,0:T(8,128)(2,1)S(1)}, u32[]{:S(2)}, u32[]{:S(2)}) collective-permute-start(bf16[128,1280]{1,0:T(8,128)(2,1)S(1)} %bitcast.12), channel_id=1, source_target_pairs={{0,16},{16,0},{1,17},{17,1},{2,18},{18,2},{3,19},{19,3},{4,20},{20... | collective-permute-start | bytes 983048 | tf_op jit(solution)/shard_map/ppermute | solution.py:498
  24.4 9.2 %expert_rows.1 = (bf16[128,1280]{1,0:T(8,128)(2,1)}, bf16[64,2560]{1,0:T(8,128)(2,1)S(1)}, bf16[64,2560]{1,0:T(8,128)(2,1)S(1)}, f32[8,128]{1,0:T(8,128)S(1)}) custom-call(bf16[128,1280]{1,0:T(8,128)(2,1)S(1)} %bitcast.13, bf16[1280,256]{1,0:T(8,128)(2,1)S(1)} %get-tuple-element.26.first_in, bf16[256,1280]{1,0:T(8,128)(2,1)S(1)} %get-tuple-element.27.first_out, ...), custom_call_target="tpu_custom_call" | custom-call | flops 1677721600 | bytes 13107200 | tf_op jit(solution)/shard_map/expert_rows/pallas_call | solution.py:244
  33.6 3.7 %all-to-all-start.1 = ((bf16[16,8,1280]{2,1,0:T(8,128)(2,1)}), bf16[16,8,1280]{2,1,0:T(8,128)(2,1)S(1)}, u32[]{:S(2)}, u32[]{:S(2)}) async-start(bf16[16,8,1280]{2,1,0:T(8,128)(2,1)} %bitcast.6), calls=%async_computation.1 | async-start | bytes 655360 | tf_op jit(solution)/shard_map/all_to_all | solution.py:487
  37.3 0.0 collective-permute-done.other_rows
  37.3 0.0 copy-start.1
  37.3 8.8 %replica_grads.1 = (bf16[640,2560]{1,0:T(8,128)(2,1)}, bf16[1280,1280]{1,0:T(8,128)(2,1)}, f32[8,128]{1,0:T(8,128)S(1)}) custom-call(s32[1]{0:T(128)} %bitcast.mine, f32[8,128]{1,0:T(8,128)S(1)} %get-tuple-element.28.after, bf16[128,1280]{1,0:T(8,128)(2,1)S(1)} %bitcast.14, bf16[128,1280]{1,0:T(8,128)(2,1)S(1)} %collective-permute-done.other_rows, ...), custom_call_target="tpu_custom_call" | custom-call | flops 13421772800 | bytes 104857600 | tf_op jit(solution)/shard_map/replica_grads/pallas_call | solution.py:331
  46.2 2.0 %all-to-all-done.1 = bf16[16,8,1280]{2,1,0:T(8,128)(2,1)S(1)} async-done(((bf16[16,8,1280]{2,1,0:T(8,128)(2,1)}), bf16[16,8,1280]{2,1,0:T(8,128)(2,1)S(1)}, u32[]{:S(2)}, u32[]{:S(2)}) %all-to-all-start.1) | async-done | bytes 327712 | tf_op jit(solution)/shard_map/all_to_all | solution.py:487
  48.2 0.0 copy-done.1
  48.2 4.3 %logits_grads.1 = (bf16[4,32,256]{2,1,0:T(8,128)(2,1)S(1)}, bf16[4,32,1280]{2,1,0:T(8,128)(2,1)S(1)}, bf16[16,1280]{1,0:T(8,128)(2,1)S(1)}, f32[8,128]{1,0:T(8,128)S(1)}) custom-call(f32[8,128]{1,0:T(8,128)S(1)} %get-tuple-element.31.after, bf16[128,1280]{1,0:T(8,128)(2,1)S(1)} %bitcast.11, bf16[4,256,1280]{2,1,0:T(8,128)(2,1)} %tokens.3, ...), custom_call_target="tpu_custom_call" | custom-call | flops 125829120 | bytes 5242880 | tf_op jit(solution)/shard_map/logits_grads/pallas_call | solution.py:405
  52.5 0.1 collective-permute-start.1
  52.6 0.8 %collective-permute-start.2 = (bf16[16,1280]{1,0:T(8,128)(2,1)S(1)}, bf16[16,1280]{1,0:T(8,128)(2,1)S(1)}, u32[]{:S(2)}, u32[]{:S(2)}) collective-permute-start(bf16[16,1280]{1,0:T(8,128)(2,1)S(1)} %get-tuple-element.36.refs_0_), channel_id=1, source_target_pairs={{0,2},{1,3},{2,0},{3,1},{4,6},{5,7},{6,4},{7,5},{8,10},{9,11},{10,... | collective-permute-start | bytes 122888 | tf_op jit(solution)/shard_map/ppermute | solution.py:481
  53.4 1.1 %collective-permute-start.3 = (bf16[16,1280]{1,0:T(8,128)(2,1)S(1)}, bf16[16,1280]{1,0:T(8,128)(2,1)S(1)}, u32[]{:S(2)}, u32[]{:S(2)}) collective-permute-start(bf16[16,1280]{1,0:T(8,128)(2,1)S(1)} %get-tuple-element.36.refs_0_), channel_id=1, source_target_pairs={{0,3},{1,2},{2,1},{3,0},{4,7},{5,6},{6,5},{7,4},{8,11},{9,10},{10,... | collective-permute-start | bytes 122888 | tf_op jit(solution)/shard_map/ppermute | solution.py:481
  54.5 0.5 collective-permute-start.4
  55.0 1.2 %collective-permute-start.5 = (bf16[16,1280]{1,0:T(8,128)(2,1)S(1)}, bf16[16,1280]{1,0:T(8,128)(2,1)S(1)}, u32[]{:S(2)}, u32[]{:S(2)}) collective-permute-start(bf16[16,1280]{1,0:T(8,128)(2,1)S(1)} %get-tuple-element.36.refs_0_), channel_id=1, source_target_pairs={{0,17},{1,16},{2,19},{3,18},{4,21},{5,20},{6,23},{7,22},{8,25},{9,... | collective-permute-start | bytes 122888 | tf_op jit(solution)/shard_map/ppermute | solution.py:481
  56.2 0.0 collective-permute-done.1.refs_1_
  56.2 0.7 collective-permute-start.6
  56.8 0.1 collective-permute-done.2.refs_2_
  57.0 1.9 %collective-permute-start.7 = (bf16[16,1280]{1,0:T(8,128)(2,1)S(1)}, bf16[16,1280]{1,0:T(8,128)(2,1)S(1)}, u32[]{:S(2)}, u32[]{:S(2)}) collective-permute-start(bf16[16,1280]{1,0:T(8,128)(2,1)S(1)} %get-tuple-element.36.refs_0_), channel_id=1, source_target_pairs={{0,19},{1,18},{2,17},{3,16},{4,23},{5,22},{6,21},{7,20},{8,27},{9,... | collective-permute-start | bytes 122888 | tf_op jit(solution)/shard_map/ppermute | solution.py:481
  58.9 0.0 collective-permute-done.3.refs_3_
  58.9 0.0 collective-permute-done.4.refs_4_
  58.9 0.0 collective-permute-done.5.refs_5_
  58.9 2.4 %collective-permute-done.6.refs_6_ = bf16[16,1280]{1,0:T(8,128)(2,1)S(1)} collective-permute-done((bf16[16,1280]{1,0:T(8,128)(2,1)S(1)}, bf16[16,1280]{1,0:T(8,128)(2,1)S(1)}, u32[]{:S(2)}, u32[]{:S(2)}) %collective-permute-start.6) | collective-permute-done | bytes 40992 | tf_op jit(solution)/shard_map/ppermute | solution.py:481
  61.3 0.5 collective-permute-done.7.refs_7_
  61.8 2.0 %collective-permute-start.10 = (bf16[16,1280]{1,0:T(8,128)(2,1)S(1)}, bf16[16,1280]{1,0:T(8,128)(2,1)S(1)}, u32[]{:S(2)}, u32[]{:S(2)}) collective-permute-start(bf16[16,1280]{1,0:T(8,128)(2,1)S(1)} %get-tuple-element.42.refs_0_), channel_id=1, source_target_pairs={{0,12},{1,13},{2,14},{3,15},{4,8},{5,9},{6,10},{7,11},{8,4},{9,5},... | collective-permute-start | bytes 122888 | tf_op jit(solution)/shard_map/ppermute | solution.py:481
  63.8 0.0 collective-permute-start.8
  63.8 2.4 %collective-permute-start.9 = (bf16[16,1280]{1,0:T(8,128)(2,1)S(1)}, bf16[16,1280]{1,0:T(8,128)(2,1)S(1)}, u32[]{:S(2)}, u32[]{:S(2)}) collective-permute-start(bf16[16,1280]{1,0:T(8,128)(2,1)S(1)} %get-tuple-element.42.refs_0_), channel_id=1, source_target_pairs={{0,8},{1,9},{2,10},{3,11},{4,12},{5,13},{6,14},{7,15},{8,0},{9,1},... | collective-permute-start | bytes 122888 | tf_op jit(solution)/shard_map/ppermute | solution.py:481
  66.2 2.7 %tokens_grads.1 = (bf16[4,256,1280]{2,1,0:T(8,128)(2,1)}, f32[8,128]{1,0:T(8,128)S(1)}) custom-call(f32[8,128]{1,0:T(8,128)S(1)} %get-tuple-element.37.after, bf16[4,32,256]{2,1,0:T(8,128)(2,1)S(1)} %get-tuple-element.38.left, bf16[4,32,1280]{2,1,0:T(8,128)(2,1)S(1)} %get-tuple-element.39.right), custom_call_target="tpu_custom_call" | custom-call | flops 83886080 | bytes 2621440 | tf_op jit(solution)/shard_map/tokens_grads/pallas_call | solution.py:436
  69.0 0.0 collective-permute-done.10.refs_3_
  69.0 0.0 collective-permute-done.8.refs_1_
  69.0 0.2 collective-permute-done.9.refs_2_
  69.2 0.7 add_terms.3
  (1 shorter events, 0.0 us)
Async XLA Ops:
  0.6 0.8 %copy-start = (bf16[1280,16]{0,1:T(8,128)(2,1)S(1)}, bf16[1280,16]{0,1:T(8,128)(2,1)}, u32[]{:S(2)}) copy-start(bf16[1280,16]{0,1:T(8,128)(2,1)} %param.6) | copy-start | bytes 122884
  22.9 14.4 %collective-permute-start = (bf16[128,1280]{1,0:T(8,128)(2,1)S(1)}, bf16[128,1280]{1,0:T(8,128)(2,1)S(1)}, u32[]{:S(2)}, u32[]{:S(2)}) collective-permute-start(bf16[128,1280]{1,0:T(8,128)(2,1)S(1)} %bitcast.12), channel_id=1, source_target_pairs={{0,16},{16,0},{1,17},{17,1},{2,18},{18,2},{3,19},{19,3},{4,20},{20... | collective-permute-start | bytes 983048 | tf_op jit(solution)/shard_map/ppermute | solution.py:498
  33.6 14.6 %all-to-all-start.1 = ((bf16[16,8,1280]{2,1,0:T(8,128)(2,1)}), bf16[16,8,1280]{2,1,0:T(8,128)(2,1)S(1)}, u32[]{:S(2)}, u32[]{:S(2)}) async-start(bf16[16,8,1280]{2,1,0:T(8,128)(2,1)} %bitcast.6), calls=%async_computation.1 | async-start | bytes 655360 | tf_op jit(solution)/shard_map/all_to_all | solution.py:487
  37.3 10.9 %copy-start.1 = (bf16[1280,16]{0,1:T(8,128)(2,1)S(1)}, bf16[1280,16]{0,1:T(8,128)(2,1)}, u32[]{:S(2)}) copy-start(bf16[1280,16]{0,1:T(8,128)(2,1)} %param.6) | copy-start | bytes 122884
  52.5 3.6 %collective-permute-start.1 = (bf16[16,1280]{1,0:T(8,128)(2,1)S(1)}, bf16[16,1280]{1,0:T(8,128)(2,1)S(1)}, u32[]{:S(2)}, u32[]{:S(2)}) collective-permute-start(bf16[16,1280]{1,0:T(8,128)(2,1)S(1)} %get-tuple-element.36.refs_0_), channel_id=1, source_target_pairs={{0,1},{1,0},{2,3},{3,2},{4,5},{5,4},{6,7},{7,6},{8,9},{9,8},{10,11... | collective-permute-start | bytes 122888 | tf_op jit(solution)/shard_map/ppermute | solution.py:481
  52.6 4.4 %collective-permute-start.2 = (bf16[16,1280]{1,0:T(8,128)(2,1)S(1)}, bf16[16,1280]{1,0:T(8,128)(2,1)S(1)}, u32[]{:S(2)}, u32[]{:S(2)}) collective-permute-start(bf16[16,1280]{1,0:T(8,128)(2,1)S(1)} %get-tuple-element.36.refs_0_), channel_id=1, source_target_pairs={{0,2},{1,3},{2,0},{3,1},{4,6},{5,7},{6,4},{7,5},{8,10},{9,11},{10,... | collective-permute-start | bytes 122888 | tf_op jit(solution)/shard_map/ppermute | solution.py:481
  53.4 5.5 %collective-permute-start.3 = (bf16[16,1280]{1,0:T(8,128)(2,1)S(1)}, bf16[16,1280]{1,0:T(8,128)(2,1)S(1)}, u32[]{:S(2)}, u32[]{:S(2)}) collective-permute-start(bf16[16,1280]{1,0:T(8,128)(2,1)S(1)} %get-tuple-element.36.refs_0_), channel_id=1, source_target_pairs={{0,3},{1,2},{2,1},{3,0},{4,7},{5,6},{6,5},{7,4},{8,11},{9,10},{10,... | collective-permute-start | bytes 122888 | tf_op jit(solution)/shard_map/ppermute | solution.py:481
  54.5 4.4 %collective-permute-start.4 = (bf16[16,1280]{1,0:T(8,128)(2,1)S(1)}, bf16[16,1280]{1,0:T(8,128)(2,1)S(1)}, u32[]{:S(2)}, u32[]{:S(2)}) collective-permute-start(bf16[16,1280]{1,0:T(8,128)(2,1)S(1)} %get-tuple-element.36.refs_0_), channel_id=1, source_target_pairs={{0,16},{1,17},{2,18},{3,19},{4,20},{5,21},{6,22},{7,23},{8,24},{9,... | collective-permute-start | bytes 122888 | tf_op jit(solution)/shard_map/ppermute | solution.py:481
  55.0 3.9 %collective-permute-start.5 = (bf16[16,1280]{1,0:T(8,128)(2,1)S(1)}, bf16[16,1280]{1,0:T(8,128)(2,1)S(1)}, u32[]{:S(2)}, u32[]{:S(2)}) collective-permute-start(bf16[16,1280]{1,0:T(8,128)(2,1)S(1)} %get-tuple-element.36.refs_0_), channel_id=1, source_target_pairs={{0,17},{1,16},{2,19},{3,18},{4,21},{5,20},{6,23},{7,22},{8,25},{9,... | collective-permute-start | bytes 122888 | tf_op jit(solution)/shard_map/ppermute | solution.py:481
  56.2 5.1 %collective-permute-start.6 = (bf16[16,1280]{1,0:T(8,128)(2,1)S(1)}, bf16[16,1280]{1,0:T(8,128)(2,1)S(1)}, u32[]{:S(2)}, u32[]{:S(2)}) collective-permute-start(bf16[16,1280]{1,0:T(8,128)(2,1)S(1)} %get-tuple-element.36.refs_0_), channel_id=1, source_target_pairs={{0,18},{1,19},{2,16},{3,17},{4,22},{5,23},{6,20},{7,21},{8,26},{9,... | collective-permute-start | bytes 122888 | tf_op jit(solution)/shard_map/ppermute | solution.py:481
  57.0 4.8 %collective-permute-start.7 = (bf16[16,1280]{1,0:T(8,128)(2,1)S(1)}, bf16[16,1280]{1,0:T(8,128)(2,1)S(1)}, u32[]{:S(2)}, u32[]{:S(2)}) collective-permute-start(bf16[16,1280]{1,0:T(8,128)(2,1)S(1)} %get-tuple-element.36.refs_0_), channel_id=1, source_target_pairs={{0,19},{1,18},{2,17},{3,16},{4,23},{5,22},{6,21},{7,20},{8,27},{9,... | collective-permute-start | bytes 122888 | tf_op jit(solution)/shard_map/ppermute | solution.py:481
  61.8 7.2 %collective-permute-start.10 = (bf16[16,1280]{1,0:T(8,128)(2,1)S(1)}, bf16[16,1280]{1,0:T(8,128)(2,1)S(1)}, u32[]{:S(2)}, u32[]{:S(2)}) collective-permute-start(bf16[16,1280]{1,0:T(8,128)(2,1)S(1)} %get-tuple-element.42.refs_0_), channel_id=1, source_target_pairs={{0,12},{1,13},{2,14},{3,15},{4,8},{5,9},{6,10},{7,11},{8,4},{9,5},... | collective-permute-start | bytes 122888 | tf_op jit(solution)/shard_map/ppermute | solution.py:481
  63.8 5.2 %collective-permute-start.8 = (bf16[16,1280]{1,0:T(8,128)(2,1)S(1)}, bf16[16,1280]{1,0:T(8,128)(2,1)S(1)}, u32[]{:S(2)}, u32[]{:S(2)}) collective-permute-start(bf16[16,1280]{1,0:T(8,128)(2,1)S(1)} %get-tuple-element.42.refs_0_), channel_id=1, source_target_pairs={{0,4},{1,5},{2,6},{3,7},{4,0},{5,1},{6,2},{7,3},{8,12},{9,13},{10,... | collective-permute-start | bytes 122888 | tf_op jit(solution)/shard_map/ppermute | solution.py:481
  63.8 5.3 %collective-permute-start.9 = (bf16[16,1280]{1,0:T(8,128)(2,1)S(1)}, bf16[16,1280]{1,0:T(8,128)(2,1)S(1)}, u32[]{:S(2)}, u32[]{:S(2)}) collective-permute-start(bf16[16,1280]{1,0:T(8,128)(2,1)S(1)} %get-tuple-element.42.refs_0_), channel_id=1, source_target_pairs={{0,8},{1,9},{2,10},{3,11},{4,12},{5,13},{6,14},{7,15},{8,0},{9,1},... | collective-permute-start | bytes 122888 | tf_op jit(solution)/shard_map/ppermute | solution.py:481

commit v15 on v14

--- a/solution.py
+++ b/solution.py
@@ -84,10 +84,14 @@
         ]
 
 
-def start_copy(source, target, sem):
+def start_copy(source, target, sem, priority=0):
     copy = pltpu.make_async_copy(source, target, sem)
-    copy.start()
+    copy.start(priority=priority)
     return copy
+
+
+def far(array):
+    return pltpu.with_memory_space_constraint(array, pltpu.HBM)
 
 
 def start_halves(source, target, sems):
@@ -101,12 +105,13 @@
 
 
 def gather_kernel(
-    tokens, params, grads, w_in, w_out, sent, dispatch, combine, first_in, first_out,
-    tokens_v, grads_v, rows, sems,
+    tokens, params_far, grads, w_in, w_out, sent, dispatch, combine, first_in, first_out,
+    tokens_v, grads_v, params, rows, sems,
 ):
     images = tokens.shape[0]
     slots = params.shape[0]
     stride = KINDS * images
+    params_copy = start_copy(params_far, params, sems.at[5], priority=1)
     halves = start_halves(tokens, tokens_v, sems)
     grads_copy = start_copy(grads, grads_v, sems.at[2])
     units = slice(0, first_out.shape[0])
@@ -115,6 +120,7 @@
         start_copy(w_out.at[units, :], first_out, sems.at[4]),
     )
     logits = []
+    params_copy.wait()
     for copy, half in halves:
         copy.wait()
         logits += [dot(params[...], tokens_v[image], 1, 1) for image in half]
@@ -155,15 +161,16 @@
             shaped((width, first), LOW),
             shaped((first, width), LOW),
         ),
-        in_specs=[PLACE, WHOLE, PLACE, PLACE, PLACE],
+        in_specs=[PLACE] * 5,
         out_specs=(WHOLE,) * 5,
         scratch_shapes=[
             pltpu.VMEM(tokens.shape, LOW),
             pltpu.VMEM(grads.shape, LOW),
+            pltpu.VMEM(params.shape, LOW),
             scratch_rows(rows),
-            pltpu.SemaphoreType.DMA((5,)),
+            pltpu.SemaphoreType.DMA((6,)),
         ],
-    )(tokens, params, grads, w_in, w_out)
+    )(tokens, far(params), grads, w_in, w_out)
 
 
 def chunks_of(first, hidden, tile):
@@ -256,8 +263,9 @@
 
 
 def replica_kernel(
-    chunks, mine, after, rows, other_rows, acts, hidden, w_in, w_out, grad_in, grad_out, mark,
-    w_in_v, w_out_v, grad_in_v, grad_out_v, wide, grads, turned, sems, in_sems, out_sems,
+    chunks, mine, after, rows, other_rows, acts, hidden, w_in, w_out, tokens,
+    grad_in, grad_out, tokens_half, mark,
+    w_in_v, w_out_v, grad_in_v, grad_out_v, wide, grads, turned, sems, in_sems, out_sems, half_sem,
 ):
     del after, mark
     count = rows.shape[0] // KINDS
@@ -274,6 +282,9 @@
                 start_copy(w_out.at[span, :], w_out_v.at[units, :], sems.at[1, chunk]),
             )
         )
+    results = [
+        start_copy(tokens.at[pl.ds(0, tokens_half.shape[0])], tokens_half, half_sem.at[0])
+    ]
     left, right = [], []
     tiles = turned.shape[0] // LANES
     for source in (rows, other_rows):
@@ -284,7 +295,6 @@
     grads[...] = jnp.concatenate(right, axis=0).astype(LOW)
     rows_in = take(wide, 0, count, KINDS).astype(LOW)
     rows_grad = right[1].astype(LOW)
-    results = []
     before = None
     for chunk in range(len(chunks) + 1):
         if chunk < len(chunks):
@@ -318,7 +328,9 @@
         copy.wait()
 
 
-def replica_grads(mine, after, rows, other_rows, acts, hidden, w_in, w_out, replicas, tile):
+def replica_grads(
+    mine, after, rows, other_rows, acts, hidden, w_in, w_out, tokens, replicas, tile
+):
     total, width = rows.shape
     size = w_in.shape[1]
     half = size // replicas
@@ -331,19 +343,20 @@
     return call(
         functools.partial(replica_kernel, chunks),
         "replica_grads",
-        SHARED,
+        ROOMY,
         64 * count * size * width,
         32 * size * width,
         count * size,
         out_shape=(
             shaped((width // replicas, size), LOW),
             shaped((half, width), LOW),
+            shaped((tokens.shape[0] // 2, *tokens.shape[1:]), LOW),
             MARK,
         ),
         in_specs=[pl.BlockSpec(memory_space=pltpu.SMEM), PLACE]
         + [WHOLE] * 4
-        + [PLACE] * 2,
-        out_specs=(PLACE,) * 3,
+        + [PLACE] * 3,
+        out_specs=(PLACE, PLACE, WHOLE, PLACE),
         scratch_shapes=[
             *weight_scratch(width, size, chunks)[:2],
             pltpu.VMEM((width // replicas, size), LOW),
@@ -354,18 +367,24 @@
             pltpu.SemaphoreType.DMA((2, len(chunks))),
             pltpu.SemaphoreType.DMA((len(chunks),)),
             pltpu.SemaphoreType.DMA((len(chunks),)),
+            pltpu.SemaphoreType.DMA((1,)),
         ],
-    )(mine, after, rows, other_rows, acts, hidden, w_in, w_out)
+    )(mine, after, rows, other_rows, acts, hidden, w_in, w_out, far(tokens))
 
 
 def logits_kernel(
-    after, back, tokens, params, grads, dispatch, combine, left, right, local, mark,
+    after, back, tokens, tokens_half, params, grads, dispatch, combine, left, right, local, mark,
     tokens_v, grads_v, wide, sems,
 ):
     del after, mark
     images, slots, _ = dispatch.shape
-    halves = start_halves(tokens, tokens_v, sems)
-    grads_copy = start_copy(grads, grads_v, sems.at[2])
+    ready = tokens_half.shape[0]
+    tokens_copy = start_copy(tokens.at[pl.ds(ready, images - ready)], tokens_v, sems.at[0])
+    grads_copy = start_copy(grads, grads_v, sems.at[1])
+
+    def tokens_of(image):
+        return tokens_half[image] if image < ready else tokens_v[image - ready]
+
     load_rows(wide, back[...])
     stride = KINDS * images
     d_slot_in = []
@@ -375,14 +394,14 @@
         right[image, slots:, :] = params[...]
         left[image, :slots, :] = dispatch[image].astype(LOW)
     parts = []
-    for copy, half in halves:
-        copy.wait()
-        for image in half:
-            weights = dispatch[image]
-            d_dispatch = dot(d_slot_in[image], tokens_v[image], 1, 1)
-            parts.append(
-                weights * (d_dispatch - jnp.sum(weights * d_dispatch, axis=1, keepdims=True))
-            )
+    for image in range(images):
+        if image == ready:
+            tokens_copy.wait()
+        weights = dispatch[image]
+        d_dispatch = dot(d_slot_in[image], tokens_of(image), 1, 1)
+        parts.append(
+            weights * (d_dispatch - jnp.sum(weights * d_dispatch, axis=1, keepdims=True))
+        )
     grads_copy.wait()
     total = None
     for image in range(images):
@@ -394,18 +413,18 @@
         )
         low = d_logits.astype(LOW)
         left[image, slots:, :] = low
-        part = dot(low, tokens_v[image], 1, 0)
+        part = dot(low, tokens_of(image), 1, 0)
         total = part if image == 0 else total + part
     local[...] = total.astype(LOW)
 
 
-def logits_grads(after, back, tokens, params, grads, dispatch, combine):
+def logits_grads(after, back, tokens, tokens_half, params, grads, dispatch, combine):
     images, length, width = tokens.shape
     slots = params.shape[0]
     return call(
         logits_kernel,
         "logits_grads",
-        SHARED,
+        ROOMY,
         6 * images * slots * length * width,
         4 * images * length * width,
         out_shape=(
@@ -414,15 +433,15 @@
             shaped(params.shape, LOW),
             MARK,
         ),
-        in_specs=[PLACE, WHOLE, PLACE, WHOLE, PLACE, WHOLE, WHOLE],
+        in_specs=[PLACE, WHOLE, PLACE, WHOLE, WHOLE, PLACE, WHOLE, WHOLE],
         out_specs=(WHOLE, WHOLE, WHOLE, PLACE),
         scratch_shapes=[
-            pltpu.VMEM(tokens.shape, LOW),
+            pltpu.VMEM((images - tokens_half.shape[0], length, width), LOW),
             pltpu.VMEM(grads.shape, LOW),
             scratch_rows(back.shape),
-            pltpu.SemaphoreType.DMA((3,)),
+            pltpu.SemaphoreType.DMA((2,)),
         ],
-    )(after, back, tokens, params, grads, dispatch, combine)
+    )(after, back, far(tokens), tokens_half, params, far(grads), dispatch, combine)
 
 
 def tokens_kernel(after, left, right, out, mark):
@@ -498,11 +517,11 @@
     other_rows = lax.ppermute(rows, "rep", [(i, (i + 1) % replicas) for i in range(replicas)])
     back, acts, hidden, after = expert(rows, *first, *weights, 512)
     back = exchange(back, "exp")
-    grad_in, grad_outer, after = replica_grads(
-        mine, after, rows, other_rows, acts, hidden, *weights, replicas, 512
+    grad_in, grad_outer, tokens_half, after = replica_grads(
+        mine, after, rows, other_rows, acts, hidden, *weights, tokens, replicas, 512
     )
     left, right, local, after = logits_grads(
-        after, back, tokens, params, grad_out, dispatch, combine
+        after, back, tokens, tokens_half, params, grad_out, dispatch, combine
     )
     exp_bits = lax.axis_size("exp").bit_length() - 1
     rep_bits = replicas.bit_length() - 1

time: 70.1 us -> 70.3 us (level)
  Pallas kernels: 28.9 us -> 30 us
  local copies, waits for them, and re-layouts: 0.78 us -> 0.01 us
    pallas_call x1, Pallas kernels: 3.2 us -> 4.64 us  [gather(): call(gather_kernel, 'gather_slots', ROOMY, 6 * images * slots * length *...]
    unnamed x4 -> x2, local copies, waits for them, and re-layouts: 0.78 us -> 0.01 us
where the time goes in v15:
time: 70.3 us; the launch traced here: 70.1 us
  Pallas kernels  30 us (43%)
  blocking collectives  18.3 us (26%)
  starting transfers between devices  15.9 us (23%)
  waiting for transfers between devices  5.2 us (7%)
  between operations  0.71 us (1%)
    all_to_all x1, blocking collectives, exchange(): return lax.all_to_all(rows, axes, split_axis=0, concat_axis=0, tiled=True)  18.3 us
    ppermute x10, starting transfers between devices, terms_of_group(): lax.ppermute(array, axes, [(i, i ^ distance) for i in range(count)])  10.6 us
    pallas_call x1, Pallas kernels, expert(): call(functools.partial(expert_kernel, chunks), 'expert_rows', ROOMY, 8 *...  9.16 us
    pallas_call x1, Pallas kernels, replica_grads(): call(functools.partial(replica_kernel, chunks), 'replica_grads', ROOMY, 6...  8.83 us
    pallas_call x1, Pallas kernels, gather(): call(gather_kernel, 'gather_slots', ROOMY, 6 * images * slots * length *...  4.64 us
    pallas_call x1, Pallas kernels, logits_grads(): call(logits_kernel, 'logits_grads', ROOMY, 6 * images * slots * length *...  3.92 us
    all_to_all x1, starting transfers between devices, exchange(): return lax.all_to_all(rows, axes, split_axis=0, concat_axis=0, tiled=True)  3.74 us
    ppermute x10, waiting for transfers between devices, terms_of_group(): lax.ppermute(array, axes, [(i, i ^ distance) for i in range(count)])  3.18 us
  transfers between devices with their start and end apart: 12, of which 5 were waited for; matrix products, arithmetic and copies ran while one was open for 0% of the time, Pallas kernels for 30%

profile of v15, /device:TPU:0, one launch (start us, length us, event | category | flops | bytes accessed | tf_op | source)
XLA Modules:
  0.0 70.1 jit_solution(639381421989703510)
XLA Ops:
  0.6 4.6 %gather_slots.1 = (bf16[128,1280]{1,0:T(8,128)(2,1)S(1)}, f32[4,16,256]{2,1,0:T(8,128)S(1)}, f32[4,16,256]{2,1,0:T(8,128)S(1)}, bf16[1280,256]{1,0:T(8,128)(2,1)S(1)}, bf16[256,1280]{1,0:T(8,128)(2,1)S(1)}) custom-call(bf16[4,256,1280]{2,1,0:T(8,128)(2,1)} %tokens.5, bf16[16,1280]{1,0:T(8,128)(2,1)} %bitcast.16, bf16[4,256,1280]{2,1,0:T(8,128)(2,1)} %grads.3, ...), custom_call_target="tpu_custom_call" | custom-call | flops 125829120 | bytes 5242880 | tf_op jit(solution)/shard_map/gather_slots/pallas_call | solution.py:150
  5.3 18.3 %all_to_all.22 = bf16[16,8,1280]{2,1,0:T(8,128)(2,1)S(1)} all-to-all(bf16[16,8,1280]{2,1,0:T(8,128)(2,1)S(1)} %bitcast.15), channel_id=1, replica_groups=mesh['rep'=2,'exp'=16] {'exp'}, dimensions={0} | all-to-all | bytes 655360 | tf_op jit(solution)/shard_map/all_to_all | solution.py:506
  23.6 1.5 %collective-permute-start = (bf16[128,1280]{1,0:T(8,128)(2,1)S(1)}, bf16[128,1280]{1,0:T(8,128)(2,1)S(1)}, u32[]{:S(2)}, u32[]{:S(2)}) collective-permute-start(bf16[128,1280]{1,0:T(8,128)(2,1)S(1)} %bitcast.12), channel_id=1, source_target_pairs={{0,16},{16,0},{1,17},{17,1},{2,18},{18,2},{3,19},{19,3},{4,20},{20... | collective-permute-start | bytes 983048 | tf_op jit(solution)/shard_map/ppermute | solution.py:517
  25.1 9.2 %expert_rows.1 = (bf16[128,1280]{1,0:T(8,128)(2,1)}, bf16[64,2560]{1,0:T(8,128)(2,1)S(1)}, bf16[64,2560]{1,0:T(8,128)(2,1)S(1)}, f32[8,128]{1,0:T(8,128)S(1)}) custom-call(bf16[128,1280]{1,0:T(8,128)(2,1)S(1)} %bitcast.13, bf16[1280,256]{1,0:T(8,128)(2,1)S(1)} %get-tuple-element.27.first_in, bf16[256,1280]{1,0:T(8,128)(2,1)S(1)} %get-tuple-element.28.first_out, ...), custom_call_target="tpu_custom_call" | custom-call | flops 1677721600 | bytes 13107200 | tf_op jit(solution)/shard_map/expert_rows/pallas_call | solution.py:251
  34.2 3.7 %all-to-all-start.1 = ((bf16[16,8,1280]{2,1,0:T(8,128)(2,1)}), bf16[16,8,1280]{2,1,0:T(8,128)(2,1)S(1)}, u32[]{:S(2)}, u32[]{:S(2)}) async-start(bf16[16,8,1280]{2,1,0:T(8,128)(2,1)} %bitcast.6), calls=%async_computation.1 | async-start | bytes 655360 | tf_op jit(solution)/shard_map/all_to_all | solution.py:506
  38.0 0.0 collective-permute-done.other_rows
  38.0 0.0 copy-start
  38.0 8.8 %replica_grads.1 = (bf16[640,2560]{1,0:T(8,128)(2,1)}, bf16[1280,1280]{1,0:T(8,128)(2,1)}, bf16[2,256,1280]{2,1,0:T(8,128)(2,1)S(1)}, f32[8,128]{1,0:T(8,128)S(1)}) custom-call(s32[1]{0:T(128)} %bitcast.mine, f32[8,128]{1,0:T(8,128)S(1)} %get-tuple-element.29.after, bf16[128,1280]{1,0:T(8,128)(2,1)S(1)} %bitcast.14, ...), custom_call_target="tpu_custom_call" | custom-call | flops 13421772800 | bytes 104857600 | tf_op jit(solution)/shard_map/replica_grads/pallas_call | solution.py:343
  46.8 2.0 %all-to-all-done.1 = bf16[16,8,1280]{2,1,0:T(8,128)(2,1)S(1)} async-done(((bf16[16,8,1280]{2,1,0:T(8,128)(2,1)}), bf16[16,8,1280]{2,1,0:T(8,128)(2,1)S(1)}, u32[]{:S(2)}, u32[]{:S(2)}) %all-to-all-start.1) | async-done | bytes 327712 | tf_op jit(solution)/shard_map/all_to_all | solution.py:506
  48.8 0.0 copy-done
  48.8 3.9 %logits_grads.1 = (bf16[4,32,256]{2,1,0:T(8,128)(2,1)S(1)}, bf16[4,32,1280]{2,1,0:T(8,128)(2,1)S(1)}, bf16[16,1280]{1,0:T(8,128)(2,1)S(1)}, f32[8,128]{1,0:T(8,128)S(1)}) custom-call(f32[8,128]{1,0:T(8,128)S(1)} %get-tuple-element.32.after, bf16[128,1280]{1,0:T(8,128)(2,1)S(1)} %bitcast.11, bf16[4,256,1280]{2,1,0:T(8,128)(2,1)} %tokens.5, ...), custom_call_target="tpu_custom_call" | custom-call | flops 125829120 | bytes 5242880 | tf_op jit(solution)/shard_map/logits_grads/pallas_call | solution.py:424
  52.8 0.1 collective-permute-start.1
  52.8 0.8 %collective-permute-start.2 = (bf16[16,1280]{1,0:T(8,128)(2,1)S(1)}, bf16[16,1280]{1,0:T(8,128)(2,1)S(1)}, u32[]{:S(2)}, u32[]{:S(2)}) collective-permute-start(bf16[16,1280]{1,0:T(8,128)(2,1)S(1)} %get-tuple-element.38.refs_0_), channel_id=1, source_target_pairs={{0,2},{1,3},{2,0},{3,1},{4,6},{5,7},{6,4},{7,5},{8,10},{9,11},{10,... | collective-permute-start | bytes 122888 | tf_op jit(solution)/shard_map/ppermute | solution.py:500
  53.6 1.1 %collective-permute-start.3 = (bf16[16,1280]{1,0:T(8,128)(2,1)S(1)}, bf16[16,1280]{1,0:T(8,128)(2,1)S(1)}, u32[]{:S(2)}, u32[]{:S(2)}) collective-permute-start(bf16[16,1280]{1,0:T(8,128)(2,1)S(1)} %get-tuple-element.38.refs_0_), channel_id=1, source_target_pairs={{0,3},{1,2},{2,1},{3,0},{4,7},{5,6},{6,5},{7,4},{8,11},{9,10},{10,... | collective-permute-start | bytes 122888 | tf_op jit(solution)/shard_map/ppermute | solution.py:500
  54.7 0.5 collective-permute-start.4
  55.2 1.2 %collective-permute-start.5 = (bf16[16,1280]{1,0:T(8,128)(2,1)S(1)}, bf16[16,1280]{1,0:T(8,128)(2,1)S(1)}, u32[]{:S(2)}, u32[]{:S(2)}) collective-permute-start(bf16[16,1280]{1,0:T(8,128)(2,1)S(1)} %get-tuple-element.38.refs_0_), channel_id=1, source_target_pairs={{0,17},{1,16},{2,19},{3,18},{4,21},{5,20},{6,23},{7,22},{8,25},{9,... | collective-permute-start | bytes 122888 | tf_op jit(solution)/shard_map/ppermute | solution.py:500
  56.4 0.0 collective-permute-done.1.refs_1_
  56.4 0.7 collective-permute-start.6
  57.1 0.1 collective-permute-done.2.refs_2_
  57.2 1.9 %collective-permute-start.7 = (bf16[16,1280]{1,0:T(8,128)(2,1)S(1)}, bf16[16,1280]{1,0:T(8,128)(2,1)S(1)}, u32[]{:S(2)}, u32[]{:S(2)}) collective-permute-start(bf16[16,1280]{1,0:T(8,128)(2,1)S(1)} %get-tuple-element.38.refs_0_), channel_id=1, source_target_pairs={{0,19},{1,18},{2,17},{3,16},{4,23},{5,22},{6,21},{7,20},{8,27},{9,... | collective-permute-start | bytes 122888 | tf_op jit(solution)/shard_map/ppermute | solution.py:500
  59.1 0.0 collective-permute-done.3.refs_3_
  59.1 0.0 collective-permute-done.4.refs_4_
  59.1 0.0 collective-permute-done.5.refs_5_
  59.1 2.4 %collective-permute-done.6.refs_6_ = bf16[16,1280]{1,0:T(8,128)(2,1)S(1)} collective-permute-done((bf16[16,1280]{1,0:T(8,128)(2,1)S(1)}, bf16[16,1280]{1,0:T(8,128)(2,1)S(1)}, u32[]{:S(2)}, u32[]{:S(2)}) %collective-permute-start.6) | collective-permute-done | bytes 40992 | tf_op jit(solution)/shard_map/ppermute | solution.py:500
  61.5 0.5 collective-permute-done.7.refs_7_
  62.0 2.0 %collective-permute-start.10 = (bf16[16,1280]{1,0:T(8,128)(2,1)S(1)}, bf16[16,1280]{1,0:T(8,128)(2,1)S(1)}, u32[]{:S(2)}, u32[]{:S(2)}) collective-permute-start(bf16[16,1280]{1,0:T(8,128)(2,1)S(1)} %get-tuple-element.44.refs_0_), channel_id=1, source_target_pairs={{0,12},{1,13},{2,14},{3,15},{4,8},{5,9},{6,10},{7,11},{8,4},{9,5},... | collective-permute-start | bytes 122888 | tf_op jit(solution)/shard_map/ppermute | solution.py:500
  64.1 0.0 collective-permute-start.8
  64.1 2.4 %collective-permute-start.9 = (bf16[16,1280]{1,0:T(8,128)(2,1)S(1)}, bf16[16,1280]{1,0:T(8,128)(2,1)S(1)}, u32[]{:S(2)}, u32[]{:S(2)}) collective-permute-start(bf16[16,1280]{1,0:T(8,128)(2,1)S(1)} %get-tuple-element.44.refs_0_), channel_id=1, source_target_pairs={{0,8},{1,9},{2,10},{3,11},{4,12},{5,13},{6,14},{7,15},{8,0},{9,1},... | collective-permute-start | bytes 122888 | tf_op jit(solution)/shard_map/ppermute | solution.py:500
  66.5 2.7 %tokens_grads.1 = (bf16[4,256,1280]{2,1,0:T(8,128)(2,1)}, f32[8,128]{1,0:T(8,128)S(1)}) custom-call(f32[8,128]{1,0:T(8,128)S(1)} %get-tuple-element.39.after, bf16[4,32,256]{2,1,0:T(8,128)(2,1)S(1)} %get-tuple-element.40.left, bf16[4,32,1280]{2,1,0:T(8,128)(2,1)S(1)} %get-tuple-element.41.right), custom_call_target="tpu_custom_call" | custom-call | flops 83886080 | bytes 2621440 | tf_op jit(solution)/shard_map/tokens_grads/pallas_call | solution.py:455
  69.2 0.0 collective-permute-done.10.refs_3_
  69.2 0.0 collective-permute-done.8.refs_1_
  69.2 0.2 collective-permute-done.9.refs_2_
  69.4 0.7 add_terms.3
  (1 shorter events, 0.0 us)
Async XLA Ops:
  23.6 14.4 %collective-permute-start = (bf16[128,1280]{1,0:T(8,128)(2,1)S(1)}, bf16[128,1280]{1,0:T(8,128)(2,1)S(1)}, u32[]{:S(2)}, u32[]{:S(2)}) collective-permute-start(bf16[128,1280]{1,0:T(8,128)(2,1)S(1)} %bitcast.12), channel_id=1, source_target_pairs={{0,16},{16,0},{1,17},{17,1},{2,18},{18,2},{3,19},{19,3},{4,20},{20... | collective-permute-start | bytes 983048 | tf_op jit(solution)/shard_map/ppermute | solution.py:517
  34.2 14.6 %all-to-all-start.1 = ((bf16[16,8,1280]{2,1,0:T(8,128)(2,1)}), bf16[16,8,1280]{2,1,0:T(8,128)(2,1)S(1)}, u32[]{:S(2)}, u32[]{:S(2)}) async-start(bf16[16,8,1280]{2,1,0:T(8,128)(2,1)} %bitcast.6), calls=%async_computation.1 | async-start | bytes 655360 | tf_op jit(solution)/shard_map/all_to_all | solution.py:506
  38.0 10.9 %copy-start = (bf16[1280,16]{0,1:T(8,128)(2,1)S(1)}, bf16[1280,16]{0,1:T(8,128)(2,1)}, u32[]{:S(2)}) copy-start(bf16[1280,16]{0,1:T(8,128)(2,1)} %param.6) | copy-start | bytes 122884
  52.8 3.6 %collective-permute-start.1 = (bf16[16,1280]{1,0:T(8,128)(2,1)S(1)}, bf16[16,1280]{1,0:T(8,128)(2,1)S(1)}, u32[]{:S(2)}, u32[]{:S(2)}) collective-permute-start(bf16[16,1280]{1,0:T(8,128)(2,1)S(1)} %get-tuple-element.38.refs_0_), channel_id=1, source_target_pairs={{0,1},{1,0},{2,3},{3,2},{4,5},{5,4},{6,7},{7,6},{8,9},{9,8},{10,11... | collective-permute-start | bytes 122888 | tf_op jit(solution)/shard_map/ppermute | solution.py:500
  52.8 4.4 %collective-permute-start.2 = (bf16[16,1280]{1,0:T(8,128)(2,1)S(1)}, bf16[16,1280]{1,0:T(8,128)(2,1)S(1)}, u32[]{:S(2)}, u32[]{:S(2)}) collective-permute-start(bf16[16,1280]{1,0:T(8,128)(2,1)S(1)} %get-tuple-element.38.refs_0_), channel_id=1, source_target_pairs={{0,2},{1,3},{2,0},{3,1},{4,6},{5,7},{6,4},{7,5},{8,10},{9,11},{10,... | collective-permute-start | bytes 122888 | tf_op jit(solution)/shard_map/ppermute | solution.py:500
  53.6 5.5 %collective-permute-start.3 = (bf16[16,1280]{1,0:T(8,128)(2,1)S(1)}, bf16[16,1280]{1,0:T(8,128)(2,1)S(1)}, u32[]{:S(2)}, u32[]{:S(2)}) collective-permute-start(bf16[16,1280]{1,0:T(8,128)(2,1)S(1)} %get-tuple-element.38.refs_0_), channel_id=1, source_target_pairs={{0,3},{1,2},{2,1},{3,0},{4,7},{5,6},{6,5},{7,4},{8,11},{9,10},{10,... | collective-permute-start | bytes 122888 | tf_op jit(solution)/shard_map/ppermute | solution.py:500
  54.7 4.4 %collective-permute-start.4 = (bf16[16,1280]{1,0:T(8,128)(2,1)S(1)}, bf16[16,1280]{1,0:T(8,128)(2,1)S(1)}, u32[]{:S(2)}, u32[]{:S(2)}) collective-permute-start(bf16[16,1280]{1,0:T(8,128)(2,1)S(1)} %get-tuple-element.38.refs_0_), channel_id=1, source_target_pairs={{0,16},{1,17},{2,18},{3,19},{4,20},{5,21},{6,22},{7,23},{8,24},{9,... | collective-permute-start | bytes 122888 | tf_op jit(solution)/shard_map/ppermute | solution.py:500
  55.2 3.9 %collective-permute-start.5 = (bf16[16,1280]{1,0:T(8,128)(2,1)S(1)}, bf16[16,1280]{1,0:T(8,128)(2,1)S(1)}, u32[]{:S(2)}, u32[]{:S(2)}) collective-permute-start(bf16[16,1280]{1,0:T(8,128)(2,1)S(1)} %get-tuple-element.38.refs_0_), channel_id=1, source_target_pairs={{0,17},{1,16},{2,19},{3,18},{4,21},{5,20},{6,23},{7,22},{8,25},{9,... | collective-permute-start | bytes 122888 | tf_op jit(solution)/shard_map/ppermute | solution.py:500
  56.4 5.1 %collective-permute-start.6 = (bf16[16,1280]{1,0:T(8,128)(2,1)S(1)}, bf16[16,1280]{1,0:T(8,128)(2,1)S(1)}, u32[]{:S(2)}, u32[]{:S(2)}) collective-permute-start(bf16[16,1280]{1,0:T(8,128)(2,1)S(1)} %get-tuple-element.38.refs_0_), channel_id=1, source_target_pairs={{0,18},{1,19},{2,16},{3,17},{4,22},{5,23},{6,20},{7,21},{8,26},{9,... | collective-permute-start | bytes 122888 | tf_op jit(solution)/shard_map/ppermute | solution.py:500
  57.2 4.8 %collective-permute-start.7 = (bf16[16,1280]{1,0:T(8,128)(2,1)S(1)}, bf16[16,1280]{1,0:T(8,128)(2,1)S(1)}, u32[]{:S(2)}, u32[]{:S(2)}) collective-permute-start(bf16[16,1280]{1,0:T(8,128)(2,1)S(1)} %get-tuple-element.38.refs_0_), channel_id=1, source_target_pairs={{0,19},{1,18},{2,17},{3,16},{4,23},{5,22},{6,21},{7,20},{8,27},{9,... | collective-permute-start | bytes 122888 | tf_op jit(solution)/shard_map/ppermute | solution.py:500
  62.0 7.2 %collective-permute-start.10 = (bf16[16,1280]{1,0:T(8,128)(2,1)S(1)}, bf16[16,1280]{1,0:T(8,128)(2,1)S(1)}, u32[]{:S(2)}, u32[]{:S(2)}) collective-permute-start(bf16[16,1280]{1,0:T(8,128)(2,1)S(1)} %get-tuple-element.44.refs_0_), channel_id=1, source_target_pairs={{0,12},{1,13},{2,14},{3,15},{4,8},{5,9},{6,10},{7,11},{8,4},{9,5},... | collective-permute-start | bytes 122888 | tf_op jit(solution)/shard_map/ppermute | solution.py:500
  64.1 5.2 %collective-permute-start.8 = (bf16[16,1280]{1,0:T(8,128)(2,1)S(1)}, bf16[16,1280]{1,0:T(8,128)(2,1)S(1)}, u32[]{:S(2)}, u32[]{:S(2)}) collective-permute-start(bf16[16,1280]{1,0:T(8,128)(2,1)S(1)} %get-tuple-element.44.refs_0_), channel_id=1, source_target_pairs={{0,4},{1,5},{2,6},{3,7},{4,0},{5,1},{6,2},{7,3},{8,12},{9,13},{10,... | collective-permute-start | bytes 122888 | tf_op jit(solution)/shard_map/ppermute | solution.py:500
  64.1 5.3 %collective-permute-start.9 = (bf16[16,1280]{1,0:T(8,128)(2,1)S(1)}, bf16[16,1280]{1,0:T(8,128)(2,1)S(1)}, u32[]{:S(2)}, u32[]{:S(2)}) collective-permute-start(bf16[16,1280]{1,0:T(8,128)(2,1)S(1)} %get-tuple-element.44.refs_0_), channel_id=1, source_target_pairs={{0,8},{1,9},{2,10},{3,11},{4,12},{5,13},{6,14},{7,15},{8,0},{9,1},... | collective-permute-start | bytes 122888 | tf_op jit(solution)/shard_map/ppermute | solution.py:500

commit v16 on v15

--- a/solution.py
+++ b/solution.py
@@ -84,9 +84,9 @@
         ]
 
 
-def start_copy(source, target, sem, priority=0):
+def start_copy(source, target, sem):
     copy = pltpu.make_async_copy(source, target, sem)
-    copy.start(priority=priority)
+    copy.start()
     return copy
 
 
@@ -105,13 +105,12 @@
 
 
 def gather_kernel(
-    tokens, params_far, grads, w_in, w_out, sent, dispatch, combine, first_in, first_out,
-    tokens_v, grads_v, params, rows, sems,
+    tokens, params, grads, w_in, w_out, sent, dispatch, combine, first_in, first_out,
+    tokens_v, grads_v, rows, sems,
 ):
     images = tokens.shape[0]
     slots = params.shape[0]
     stride = KINDS * images
-    params_copy = start_copy(params_far, params, sems.at[5], priority=1)
     halves = start_halves(tokens, tokens_v, sems)
     grads_copy = start_copy(grads, grads_v, sems.at[2])
     units = slice(0, first_out.shape[0])
@@ -120,7 +119,6 @@
         start_copy(w_out.at[units, :], first_out, sems.at[4]),
     )
     logits = []
-    params_copy.wait()
     for copy, half in halves:
         copy.wait()
         logits += [dot(params[...], tokens_v[image], 1, 1) for image in half]
@@ -161,16 +159,15 @@
             shaped((width, first), LOW),
             shaped((first, width), LOW),
         ),
-        in_specs=[PLACE] * 5,
+        in_specs=[PLACE, WHOLE, PLACE, PLACE, PLACE],
         out_specs=(WHOLE,) * 5,
         scratch_shapes=[
             pltpu.VMEM(tokens.shape, LOW),
             pltpu.VMEM(grads.shape, LOW),
-            pltpu.VMEM(params.shape, LOW),
             scratch_rows(rows),
-            pltpu.SemaphoreType.DMA((6,)),
+            pltpu.SemaphoreType.DMA((5,)),
         ],
-    )(tokens, far(params), grads, w_in, w_out)
+    )(tokens, params, grads, w_in, w_out)
 
 
 def chunks_of(first, hidden, tile):

time: 70.3 us -> 69.7 us (level)
  Pallas kernels: 30 us -> 28.6 us
  local copies, waits for them, and re-layouts: 0.01 us -> 0.78 us
    pallas_call x1, Pallas kernels: 4.64 us -> 3.2 us  [gather(): call(gather_kernel, 'gather_slots', ROOMY, 6 * images * slots * length *...]
    unnamed x2 -> x4, local copies, waits for them, and re-layouts: 0.01 us -> 0.78 us
where the time goes in v16:
time: 69.7 us; the launch traced here: 69.4 us
  Pallas kernels  28.6 us (41%)
  blocking collectives  18.3 us (26%)
  starting transfers between devices  15.9 us (23%)
  waiting for transfers between devices  5.2 us (7%)
  local copies, waits for them, and re-layouts  0.78 us (1%)
  between operations  0.72 us (1%)
    all_to_all x1, blocking collectives, exchange(): return lax.all_to_all(rows, axes, split_axis=0, concat_axis=0, tiled=True)  18.3 us
    ppermute x10, starting transfers between devices, terms_of_group(): lax.ppermute(array, axes, [(i, i ^ distance) for i in range(count)])  10.6 us
    pallas_call x1, Pallas kernels, expert(): call(functools.partial(expert_kernel, chunks), 'expert_rows', ROOMY, 8 *...  9.16 us
    pallas_call x1, Pallas kernels, replica_grads(): call(functools.partial(replica_kernel, chunks), 'replica_grads', ROOMY, 6...  8.83 us
    pallas_call x1, Pallas kernels, logits_grads(): call(logits_kernel, 'logits_grads', ROOMY, 6 * images * slots * length *...  3.92 us
    all_to_all x1, starting transfers between devices, exchange(): return lax.all_to_all(rows, axes, split_axis=0, concat_axis=0, tiled=True)  3.74 us
    pallas_call x1, Pallas kernels, gather(): call(gather_kernel, 'gather_slots', ROOMY, 6 * images * slots * length *...  3.2 us
    ppermute x10, waiting for transfers between devices, terms_of_group(): lax.ppermute(array, axes, [(i, i ^ distance) for i in range(count)])  3.18 us
  transfers between devices with their start and end apart: 12, of which 5 were waited for; matrix products, arithmetic and copies ran while one was open for 0% of the time, Pallas kernels for 30%

profile of v16, /device:TPU:0, one launch (start us, length us, event | category | flops | bytes accessed | tf_op | source)
XLA Modules:
  0.0 69.4 jit_solution(7545891394185532571)
XLA Ops:
  0.6 0.0 copy-start
  0.6 0.8 %copy-done = bf16[1280,16]{0,1:T(8,128)(2,1)S(1)} copy-done((bf16[1280,16]{0,1:T(8,128)(2,1)S(1)}, bf16[1280,16]{0,1:T(8,128)(2,1)}, u32[]{:S(2)}) %copy-start) | copy-done | bytes 40984
  1.4 3.2 %gather_slots.1 = (bf16[128,1280]{1,0:T(8,128)(2,1)S(1)}, f32[4,16,256]{2,1,0:T(8,128)S(1)}, f32[4,16,256]{2,1,0:T(8,128)S(1)}, bf16[1280,256]{1,0:T(8,128)(2,1)S(1)}, bf16[256,1280]{1,0:T(8,128)(2,1)S(1)}) custom-call(bf16[4,256,1280]{2,1,0:T(8,128)(2,1)} %tokens.5, bf16[16,1280]{1,0:T(8,128)(2,1)S(1)} %bitcast.16, bf16[4,256,1280]{2,1,0:T(8,128)(2,1)} %grads.3, ...), custom_call_target="tpu_custom_call" | custom-call | flops 125829120 | bytes 5242880 | tf_op jit(solution)/shard_map/gather_slots/pallas_call | solution.py:148
  4.6 18.3 %all_to_all.22 = bf16[16,8,1280]{2,1,0:T(8,128)(2,1)S(1)} all-to-all(bf16[16,8,1280]{2,1,0:T(8,128)(2,1)S(1)} %bitcast.15), channel_id=1, replica_groups=mesh['rep'=2,'exp'=16] {'exp'}, dimensions={0} | all-to-all | bytes 655360 | tf_op jit(solution)/shard_map/all_to_all | solution.py:503
  22.9 1.5 %collective-permute-start = (bf16[128,1280]{1,0:T(8,128)(2,1)S(1)}, bf16[128,1280]{1,0:T(8,128)(2,1)S(1)}, u32[]{:S(2)}, u32[]{:S(2)}) collective-permute-start(bf16[128,1280]{1,0:T(8,128)(2,1)S(1)} %bitcast.12), channel_id=1, source_target_pairs={{0,16},{16,0},{1,17},{17,1},{2,18},{18,2},{3,19},{19,3},{4,20},{20... | collective-permute-start | bytes 983048 | tf_op jit(solution)/shard_map/ppermute | solution.py:514
  24.4 9.2 %expert_rows.1 = (bf16[128,1280]{1,0:T(8,128)(2,1)}, bf16[64,2560]{1,0:T(8,128)(2,1)S(1)}, bf16[64,2560]{1,0:T(8,128)(2,1)S(1)}, f32[8,128]{1,0:T(8,128)S(1)}) custom-call(bf16[128,1280]{1,0:T(8,128)(2,1)S(1)} %bitcast.13, bf16[1280,256]{1,0:T(8,128)(2,1)S(1)} %get-tuple-element.27.first_in, bf16[256,1280]{1,0:T(8,128)(2,1)S(1)} %get-tuple-element.28.first_out, ...), custom_call_target="tpu_custom_call" | custom-call | flops 1677721600 | bytes 13107200 | tf_op jit(solution)/shard_map/expert_rows/pallas_call | solution.py:248
  33.6 3.7 %all-to-all-start.1 = ((bf16[16,8,1280]{2,1,0:T(8,128)(2,1)}), bf16[16,8,1280]{2,1,0:T(8,128)(2,1)S(1)}, u32[]{:S(2)}, u32[]{:S(2)}) async-start(bf16[16,8,1280]{2,1,0:T(8,128)(2,1)} %bitcast.6), calls=%async_computation.1 | async-start | bytes 655360 | tf_op jit(solution)/shard_map/all_to_all | solution.py:503
  37.3 0.0 collective-permute-done.other_rows
  37.3 0.0 copy-start.1
  37.3 8.8 %replica_grads.1 = (bf16[640,2560]{1,0:T(8,128)(2,1)}, bf16[1280,1280]{1,0:T(8,128)(2,1)}, bf16[2,256,1280]{2,1,0:T(8,128)(2,1)S(1)}, f32[8,128]{1,0:T(8,128)S(1)}) custom-call(s32[1]{0:T(128)} %bitcast.mine, f32[8,128]{1,0:T(8,128)S(1)} %get-tuple-element.29.after, bf16[128,1280]{1,0:T(8,128)(2,1)S(1)} %bitcast.14, ...), custom_call_target="tpu_custom_call" | custom-call | flops 13421772800 | bytes 104857600 | tf_op jit(solution)/shard_map/replica_grads/pallas_call | solution.py:340
  46.2 2.0 %all-to-all-done.1 = bf16[16,8,1280]{2,1,0:T(8,128)(2,1)S(1)} async-done(((bf16[16,8,1280]{2,1,0:T(8,128)(2,1)}), bf16[16,8,1280]{2,1,0:T(8,128)(2,1)S(1)}, u32[]{:S(2)}, u32[]{:S(2)}) %all-to-all-start.1) | async-done | bytes 327712 | tf_op jit(solution)/shard_map/all_to_all | solution.py:503
  48.2 0.0 copy-done.1
  48.2 3.9 %logits_grads.1 = (bf16[4,32,256]{2,1,0:T(8,128)(2,1)S(1)}, bf16[4,32,1280]{2,1,0:T(8,128)(2,1)S(1)}, bf16[16,1280]{1,0:T(8,128)(2,1)S(1)}, f32[8,128]{1,0:T(8,128)S(1)}) custom-call(f32[8,128]{1,0:T(8,128)S(1)} %get-tuple-element.32.after, bf16[128,1280]{1,0:T(8,128)(2,1)S(1)} %bitcast.11, bf16[4,256,1280]{2,1,0:T(8,128)(2,1)} %tokens.5, ...), custom_call_target="tpu_custom_call" | custom-call | flops 125829120 | bytes 5242880 | tf_op jit(solution)/shard_map/logits_grads/pallas_call | solution.py:421
  52.1 0.1 collective-permute-start.1
  52.2 0.8 %collective-permute-start.2 = (bf16[16,1280]{1,0:T(8,128)(2,1)S(1)}, bf16[16,1280]{1,0:T(8,128)(2,1)S(1)}, u32[]{:S(2)}, u32[]{:S(2)}) collective-permute-start(bf16[16,1280]{1,0:T(8,128)(2,1)S(1)} %get-tuple-element.38.refs_0_), channel_id=1, source_target_pairs={{0,2},{1,3},{2,0},{3,1},{4,6},{5,7},{6,4},{7,5},{8,10},{9,11},{10,... | collective-permute-start | bytes 122888 | tf_op jit(solution)/shard_map/ppermute | solution.py:497
  53.0 1.1 %collective-permute-start.3 = (bf16[16,1280]{1,0:T(8,128)(2,1)S(1)}, bf16[16,1280]{1,0:T(8,128)(2,1)S(1)}, u32[]{:S(2)}, u32[]{:S(2)}) collective-permute-start(bf16[16,1280]{1,0:T(8,128)(2,1)S(1)} %get-tuple-element.38.refs_0_), channel_id=1, source_target_pairs={{0,3},{1,2},{2,1},{3,0},{4,7},{5,6},{6,5},{7,4},{8,11},{9,10},{10,... | collective-permute-start | bytes 122888 | tf_op jit(solution)/shard_map/ppermute | solution.py:497
  54.1 0.5 collective-permute-start.4
  54.6 1.2 %collective-permute-start.5 = (bf16[16,1280]{1,0:T(8,128)(2,1)S(1)}, bf16[16,1280]{1,0:T(8,128)(2,1)S(1)}, u32[]{:S(2)}, u32[]{:S(2)}) collective-permute-start(bf16[16,1280]{1,0:T(8,128)(2,1)S(1)} %get-tuple-element.38.refs_0_), channel_id=1, source_target_pairs={{0,17},{1,16},{2,19},{3,18},{4,21},{5,20},{6,23},{7,22},{8,25},{9,... | collective-permute-start | bytes 122888 | tf_op jit(solution)/shard_map/ppermute | solution.py:497
  55.8 0.0 collective-permute-done.1.refs_1_
  55.8 0.7 collective-permute-start.6
  56.4 0.1 collective-permute-done.2.refs_2_
  56.6 1.9 %collective-permute-start.7 = (bf16[16,1280]{1,0:T(8,128)(2,1)S(1)}, bf16[16,1280]{1,0:T(8,128)(2,1)S(1)}, u32[]{:S(2)}, u32[]{:S(2)}) collective-permute-start(bf16[16,1280]{1,0:T(8,128)(2,1)S(1)} %get-tuple-element.38.refs_0_), channel_id=1, source_target_pairs={{0,19},{1,18},{2,17},{3,16},{4,23},{5,22},{6,21},{7,20},{8,27},{9,... | collective-permute-start | bytes 122888 | tf_op jit(solution)/shard_map/ppermute | solution.py:497
  58.5 0.0 collective-permute-done.3.refs_3_
  58.5 0.0 collective-permute-done.4.refs_4_
  58.5 0.0 collective-permute-done.5.refs_5_
  58.5 2.4 %collective-permute-done.6.refs_6_ = bf16[16,1280]{1,0:T(8,128)(2,1)S(1)} collective-permute-done((bf16[16,1280]{1,0:T(8,128)(2,1)S(1)}, bf16[16,1280]{1,0:T(8,128)(2,1)S(1)}, u32[]{:S(2)}, u32[]{:S(2)}) %collective-permute-start.6) | collective-permute-done | bytes 40992 | tf_op jit(solution)/shard_map/ppermute | solution.py:497
  60.9 0.5 collective-permute-done.7.refs_7_
  61.4 2.0 %collective-permute-start.10 = (bf16[16,1280]{1,0:T(8,128)(2,1)S(1)}, bf16[16,1280]{1,0:T(8,128)(2,1)S(1)}, u32[]{:S(2)}, u32[]{:S(2)}) collective-permute-start(bf16[16,1280]{1,0:T(8,128)(2,1)S(1)} %get-tuple-element.44.refs_0_), channel_id=1, source_target_pairs={{0,12},{1,13},{2,14},{3,15},{4,8},{5,9},{6,10},{7,11},{8,4},{9,5},... | collective-permute-start | bytes 122888 | tf_op jit(solution)/shard_map/ppermute | solution.py:497
  63.4 0.0 collective-permute-start.8
  63.4 2.4 %collective-permute-start.9 = (bf16[16,1280]{1,0:T(8,128)(2,1)S(1)}, bf16[16,1280]{1,0:T(8,128)(2,1)S(1)}, u32[]{:S(2)}, u32[]{:S(2)}) collective-permute-start(bf16[16,1280]{1,0:T(8,128)(2,1)S(1)} %get-tuple-element.44.refs_0_), channel_id=1, source_target_pairs={{0,8},{1,9},{2,10},{3,11},{4,12},{5,13},{6,14},{7,15},{8,0},{9,1},... | collective-permute-start | bytes 122888 | tf_op jit(solution)/shard_map/ppermute | solution.py:497
  65.8 2.7 %tokens_grads.1 = (bf16[4,256,1280]{2,1,0:T(8,128)(2,1)}, f32[8,128]{1,0:T(8,128)S(1)}) custom-call(f32[8,128]{1,0:T(8,128)S(1)} %get-tuple-element.39.after, bf16[4,32,256]{2,1,0:T(8,128)(2,1)S(1)} %get-tuple-element.40.left, bf16[4,32,1280]{2,1,0:T(8,128)(2,1)S(1)} %get-tuple-element.41.right), custom_call_target="tpu_custom_call" | custom-call | flops 83886080 | bytes 2621440 | tf_op jit(solution)/shard_map/tokens_grads/pallas_call | solution.py:452
  68.6 0.0 collective-permute-done.10.refs_3_
  68.6 0.0 collective-permute-done.8.refs_1_
  68.6 0.2 collective-permute-done.9.refs_2_
  68.8 0.7 add_terms.3
  (1 shorter events, 0.0 us)
Async XLA Ops:
  0.6 0.8 %copy-start = (bf16[1280,16]{0,1:T(8,128)(2,1)S(1)}, bf16[1280,16]{0,1:T(8,128)(2,1)}, u32[]{:S(2)}) copy-start(bf16[1280,16]{0,1:T(8,128)(2,1)} %param.6) | copy-start | bytes 122884
  22.9 14.4 %collective-permute-start = (bf16[128,1280]{1,0:T(8,128)(2,1)S(1)}, bf16[128,1280]{1,0:T(8,128)(2,1)S(1)}, u32[]{:S(2)}, u32[]{:S(2)}) collective-permute-start(bf16[128,1280]{1,0:T(8,128)(2,1)S(1)} %bitcast.12), channel_id=1, source_target_pairs={{0,16},{16,0},{1,17},{17,1},{2,18},{18,2},{3,19},{19,3},{4,20},{20... | collective-permute-start | bytes 983048 | tf_op jit(solution)/shard_map/ppermute | solution.py:514
  33.6 14.6 %all-to-all-start.1 = ((bf16[16,8,1280]{2,1,0:T(8,128)(2,1)}), bf16[16,8,1280]{2,1,0:T(8,128)(2,1)S(1)}, u32[]{:S(2)}, u32[]{:S(2)}) async-start(bf16[16,8,1280]{2,1,0:T(8,128)(2,1)} %bitcast.6), calls=%async_computation.1 | async-start | bytes 655360 | tf_op jit(solution)/shard_map/all_to_all | solution.py:503
  37.3 10.9 %copy-start.1 = (bf16[1280,16]{0,1:T(8,128)(2,1)S(1)}, bf16[1280,16]{0,1:T(8,128)(2,1)}, u32[]{:S(2)}) copy-start(bf16[1280,16]{0,1:T(8,128)(2,1)} %param.6) | copy-start | bytes 122884
  52.1 3.6 %collective-permute-start.1 = (bf16[16,1280]{1,0:T(8,128)(2,1)S(1)}, bf16[16,1280]{1,0:T(8,128)(2,1)S(1)}, u32[]{:S(2)}, u32[]{:S(2)}) collective-permute-start(bf16[16,1280]{1,0:T(8,128)(2,1)S(1)} %get-tuple-element.38.refs_0_), channel_id=1, source_target_pairs={{0,1},{1,0},{2,3},{3,2},{4,5},{5,4},{6,7},{7,6},{8,9},{9,8},{10,11... | collective-permute-start | bytes 122888 | tf_op jit(solution)/shard_map/ppermute | solution.py:497
  52.2 4.4 %collective-permute-start.2 = (bf16[16,1280]{1,0:T(8,128)(2,1)S(1)}, bf16[16,1280]{1,0:T(8,128)(2,1)S(1)}, u32[]{:S(2)}, u32[]{:S(2)}) collective-permute-start(bf16[16,1280]{1,0:T(8,128)(2,1)S(1)} %get-tuple-element.38.refs_0_), channel_id=1, source_target_pairs={{0,2},{1,3},{2,0},{3,1},{4,6},{5,7},{6,4},{7,5},{8,10},{9,11},{10,... | collective-permute-start | bytes 122888 | tf_op jit(solution)/shard_map/ppermute | solution.py:497
  53.0 5.5 %collective-permute-start.3 = (bf16[16,1280]{1,0:T(8,128)(2,1)S(1)}, bf16[16,1280]{1,0:T(8,128)(2,1)S(1)}, u32[]{:S(2)}, u32[]{:S(2)}) collective-permute-start(bf16[16,1280]{1,0:T(8,128)(2,1)S(1)} %get-tuple-element.38.refs_0_), channel_id=1, source_target_pairs={{0,3},{1,2},{2,1},{3,0},{4,7},{5,6},{6,5},{7,4},{8,11},{9,10},{10,... | collective-permute-start | bytes 122888 | tf_op jit(solution)/shard_map/ppermute | solution.py:497
  54.1 4.4 %collective-permute-start.4 = (bf16[16,1280]{1,0:T(8,128)(2,1)S(1)}, bf16[16,1280]{1,0:T(8,128)(2,1)S(1)}, u32[]{:S(2)}, u32[]{:S(2)}) collective-permute-start(bf16[16,1280]{1,0:T(8,128)(2,1)S(1)} %get-tuple-element.38.refs_0_), channel_id=1, source_target_pairs={{0,16},{1,17},{2,18},{3,19},{4,20},{5,21},{6,22},{7,23},{8,24},{9,... | collective-permute-start | bytes 122888 | tf_op jit(solution)/shard_map/ppermute | solution.py:497
  54.6 3.9 %collective-permute-start.5 = (bf16[16,1280]{1,0:T(8,128)(2,1)S(1)}, bf16[16,1280]{1,0:T(8,128)(2,1)S(1)}, u32[]{:S(2)}, u32[]{:S(2)}) collective-permute-start(bf16[16,1280]{1,0:T(8,128)(2,1)S(1)} %get-tuple-element.38.refs_0_), channel_id=1, source_target_pairs={{0,17},{1,16},{2,19},{3,18},{4,21},{5,20},{6,23},{7,22},{8,25},{9,... | collective-permute-start | bytes 122888 | tf_op jit(solution)/shard_map/ppermute | solution.py:497
  55.8 5.1 %collective-permute-start.6 = (bf16[16,1280]{1,0:T(8,128)(2,1)S(1)}, bf16[16,1280]{1,0:T(8,128)(2,1)S(1)}, u32[]{:S(2)}, u32[]{:S(2)}) collective-permute-start(bf16[16,1280]{1,0:T(8,128)(2,1)S(1)} %get-tuple-element.38.refs_0_), channel_id=1, source_target_pairs={{0,18},{1,19},{2,16},{3,17},{4,22},{5,23},{6,20},{7,21},{8,26},{9,... | collective-permute-start | bytes 122888 | tf_op jit(solution)/shard_map/ppermute | solution.py:497
  56.6 4.8 %collective-permute-start.7 = (bf16[16,1280]{1,0:T(8,128)(2,1)S(1)}, bf16[16,1280]{1,0:T(8,128)(2,1)S(1)}, u32[]{:S(2)}, u32[]{:S(2)}) collective-permute-start(bf16[16,1280]{1,0:T(8,128)(2,1)S(1)} %get-tuple-element.38.refs_0_), channel_id=1, source_target_pairs={{0,19},{1,18},{2,17},{3,16},{4,23},{5,22},{6,21},{7,20},{8,27},{9,... | collective-permute-start | bytes 122888 | tf_op jit(solution)/shard_map/ppermute | solution.py:497
  61.4 7.2 %collective-permute-start.10 = (bf16[16,1280]{1,0:T(8,128)(2,1)S(1)}, bf16[16,1280]{1,0:T(8,128)(2,1)S(1)}, u32[]{:S(2)}, u32[]{:S(2)}) collective-permute-start(bf16[16,1280]{1,0:T(8,128)(2,1)S(1)} %get-tuple-element.44.refs_0_), channel_id=1, source_target_pairs={{0,12},{1,13},{2,14},{3,15},{4,8},{5,9},{6,10},{7,11},{8,4},{9,5},... | collective-permute-start | bytes 122888 | tf_op jit(solution)/shard_map/ppermute | solution.py:497
  63.4 5.2 %collective-permute-start.8 = (bf16[16,1280]{1,0:T(8,128)(2,1)S(1)}, bf16[16,1280]{1,0:T(8,128)(2,1)S(1)}, u32[]{:S(2)}, u32[]{:S(2)}) collective-permute-start(bf16[16,1280]{1,0:T(8,128)(2,1)S(1)} %get-tuple-element.44.refs_0_), channel_id=1, source_target_pairs={{0,4},{1,5},{2,6},{3,7},{4,0},{5,1},{6,2},{7,3},{8,12},{9,13},{10,... | collective-permute-start | bytes 122888 | tf_op jit(solution)/shard_map/ppermute | solution.py:497
  63.4 5.3 %collective-permute-start.9 = (bf16[16,1280]{1,0:T(8,128)(2,1)S(1)}, bf16[16,1280]{1,0:T(8,128)(2,1)S(1)}, u32[]{:S(2)}, u32[]{:S(2)}) collective-permute-start(bf16[16,1280]{1,0:T(8,128)(2,1)S(1)} %get-tuple-element.44.refs_0_), channel_id=1, source_target_pairs={{0,8},{1,9},{2,10},{3,11},{4,12},{5,13},{6,14},{7,15},{8,0},{9,1},... | collective-permute-start | bytes 122888 | tf_op jit(solution)/shard_map/ppermute | solution.py:497

commit v17 on v16

--- a/solution.py
+++ b/solution.py
@@ -376,42 +376,51 @@
     del after, mark
     images, slots, _ = dispatch.shape
     ready = tokens_half.shape[0]
-    tokens_copy = start_copy(tokens.at[pl.ds(ready, images - ready)], tokens_v, sems.at[0])
-    grads_copy = start_copy(grads, grads_v, sems.at[1])
+    early, late = pl.ds(0, ready), pl.ds(ready, images - ready)
+    copies = (
+        (start_copy(grads.at[early], grads_v.at[early], sems.at[0]),),
+        (
+            start_copy(tokens.at[late], tokens_v, sems.at[1]),
+            start_copy(grads.at[late], grads_v.at[late], sems.at[2]),
+        ),
+    )
 
     def tokens_of(image):
         return tokens_half[image] if image < ready else tokens_v[image - ready]
 
     load_rows(wide, back[...])
     stride = KINDS * images
-    d_slot_in = []
+    slot_out, d_slot_in = [], []
     for image in range(images):
+        slot_out.append(take(wide, KINDS * image, slots, stride).astype(LOW))
         d_slot_in.append(take(wide, KINDS * image + 1, slots, stride).astype(LOW))
         right[image, :slots, :] = d_slot_in[image]
         right[image, slots:, :] = params[...]
         left[image, :slots, :] = dispatch[image].astype(LOW)
-    parts = []
-    for image in range(images):
-        if image == ready:
-            tokens_copy.wait()
+
+    def dispatch_part(image):
         weights = dispatch[image]
         d_dispatch = dot(d_slot_in[image], tokens_of(image), 1, 1)
-        parts.append(
-            weights * (d_dispatch - jnp.sum(weights * d_dispatch, axis=1, keepdims=True))
-        )
-    grads_copy.wait()
+        return weights * (d_dispatch - jnp.sum(weights * d_dispatch, axis=1, keepdims=True))
+
+    def combine_part(image):
+        weights = combine[image]
+        d_combine = dot(slot_out[image], grads_v[image], 1, 1)
+        return weights * (d_combine - jnp.sum(weights * d_combine, axis=0, keepdims=True))
+
+    parts = [dispatch_part(image) for image in range(ready)]
     total = None
-    for image in range(images):
-        slot_out = take(wide, KINDS * image, slots, stride).astype(LOW)
-        weights = combine[image]
-        d_combine = dot(slot_out, grads_v[image], 1, 1)
-        d_logits = parts[image] + weights * (
-            d_combine - jnp.sum(weights * d_combine, axis=0, keepdims=True)
-        )
-        low = d_logits.astype(LOW)
-        left[image, slots:, :] = low
-        part = dot(low, tokens_of(image), 1, 0)
-        total = part if image == 0 else total + part
+    for pair, half in zip(copies, (range(ready), range(ready, images))):
+        for copy in pair:
+            copy.wait()
+        for image in half:
+            if image >= ready:
+                parts.append(dispatch_part(image))
+        lows = [(parts[image] + combine_part(image)).astype(LOW) for image in half]
+        for image, low in zip(half, lows):
+            left[image, slots:, :] = low
+            part = dot(low, tokens_of(image), 1, 0)
+            total = part if total is None else total + part
     local[...] = total.astype(LOW)
 
 
@@ -436,7 +445,7 @@
             pltpu.VMEM((images - tokens_half.shape[0], length, width), LOW),
             pltpu.VMEM(grads.shape, LOW),
             scratch_rows(back.shape),
-            pltpu.SemaphoreType.DMA((2,)),
+            pltpu.SemaphoreType.DMA((3,)),
         ],
     )(after, back, far(tokens), tokens_half, params, far(grads), dispatch, combine)
 
@@ -468,7 +477,7 @@
 
 def add_kernel(after, *refs):
     del after
-    terms = [ref[...].astype(WIDE) for ref in refs[:-2]]
+    terms = [ref[...].astype(WIDE) for ref in reversed(refs[:-2])]
     while len(terms) > 1:
         terms = [left + right for left, right in zip(terms[::2], terms[1::2])]
     refs[-2][...] = terms[0].astype(refs[-2].dtype)
@@ -484,7 +493,7 @@
         out_shape=(shaped(terms[0].shape, dtype), MARK),
         in_specs=[PLACE] + [WHOLE] * len(terms),
         out_specs=(WHOLE, PLACE),
-    )(after, *terms)
+    )(after, *reversed(terms))
 
 
 def terms_of_group(array, bits):
@@ -493,10 +502,11 @@
     for bit in bits:
         distances += [distance + (1 << bit) for distance in distances]
     count = lax.axis_size(axes)
-    return [array] + [
+    terms = [
         lax.ppermute(array, axes, [(i, i ^ distance) for i in range(count)])
-        for distance in distances[1:]
+        for distance in reversed(distances[1:])
     ]
+    return [array, *reversed(terms)]
 
 
 def exchange(rows, axes):

time: 69.7 us -> 69.6 us (level)
  waiting for transfers between devices: 5.2 us -> 6.54 us
  starting transfers between devices: 15.9 us -> 15.1 us
  Pallas kernels: 28.6 us -> 27.9 us
    ppermute x10, waiting for transfers between devices: 3.18 us -> 4.52 us  [terms_of_group(): lax.ppermute(array, axes, [(i, i ^ distance) for i in range(count)])]
    ppermute x10, starting transfers between devices: 10.6 us -> 9.87 us  [terms_of_group(): lax.ppermute(array, axes, [(i, i ^ distance) for i in range(count)])]
  transfers between devices with their start and end apart: 12 -> 12, of which waited for: 5 -> 6; matrix products, arithmetic and copies ran while one was open for 0% -> 0% of each run, Pallas kernels for 30% -> 30%
where the time goes in v17:
time: 69.6 us; the launch traced here: 69.3 us
  Pallas kernels  27.9 us (40%)
  blocking collectives  18.3 us (26%)
  starting transfers between devices  15.1 us (22%)
  waiting for transfers between devices  6.54 us (9%)
  local copies, waits for them, and re-layouts  0.78 us (1%)
  between operations  0.71 us (1%)
    all_to_all x1, blocking collectives, exchange(): return lax.all_to_all(rows, axes, split_axis=0, concat_axis=0, tiled=True)  18.3 us
    ppermute x10, starting transfers between devices, terms_of_group(): lax.ppermute(array, axes, [(i, i ^ distance) for i in range(count)])  9.87 us
    pallas_call x1, Pallas kernels, expert(): call(functools.partial(expert_kernel, chunks), 'expert_rows', ROOMY, 8 *...  9.16 us
    pallas_call x1, Pallas kernels, replica_grads(): call(functools.partial(replica_kernel, chunks), 'replica_grads', ROOMY, 6...  8.83 us
    ppermute x10, waiting for transfers between devices, terms_of_group(): lax.ppermute(array, axes, [(i, i ^ distance) for i in range(count)])  4.52 us
    all_to_all x1, starting transfers between devices, exchange(): return lax.all_to_all(rows, axes, split_axis=0, concat_axis=0, tiled=True)  3.74 us
    pallas_call x1, Pallas kernels, logits_grads(): call(logits_kernel, 'logits_grads', ROOMY, 6 * images * slots * length *...  3.22 us
    pallas_call x1, Pallas kernels, gather(): call(gather_kernel, 'gather_slots', ROOMY, 6 * images * slots * length *...  3.2 us
  transfers between devices with their start and end apart: 12, of which 6 were waited for; matrix products, arithmetic and copies ran while one was open for 0% of the time, Pallas kernels for 30%

profile of v17, /device:TPU:0, one launch (start us, length us, event | category | flops | bytes accessed | tf_op | source)
XLA Modules:
  0.0 69.3 jit_solution(13856712997627572998)
XLA Ops:
  0.6 0.0 copy-start
  0.6 0.8 %copy-done = bf16[1280,16]{0,1:T(8,128)(2,1)S(1)} copy-done((bf16[1280,16]{0,1:T(8,128)(2,1)S(1)}, bf16[1280,16]{0,1:T(8,128)(2,1)}, u32[]{:S(2)}) %copy-start) | copy-done | bytes 40984
  1.4 3.2 %gather_slots.1 = (bf16[128,1280]{1,0:T(8,128)(2,1)S(1)}, f32[4,16,256]{2,1,0:T(8,128)S(1)}, f32[4,16,256]{2,1,0:T(8,128)S(1)}, bf16[1280,256]{1,0:T(8,128)(2,1)S(1)}, bf16[256,1280]{1,0:T(8,128)(2,1)S(1)}) custom-call(bf16[4,256,1280]{2,1,0:T(8,128)(2,1)} %tokens.5, bf16[16,1280]{1,0:T(8,128)(2,1)S(1)} %bitcast.16, bf16[4,256,1280]{2,1,0:T(8,128)(2,1)} %grads.3, ...), custom_call_target="tpu_custom_call" | custom-call | flops 125829120 | bytes 5242880 | tf_op jit(solution)/shard_map/gather_slots/pallas_call | solution.py:148
  4.6 18.3 %all_to_all.22 = bf16[16,8,1280]{2,1,0:T(8,128)(2,1)S(1)} all-to-all(bf16[16,8,1280]{2,1,0:T(8,128)(2,1)S(1)} %bitcast.15), channel_id=1, replica_groups=mesh['rep'=2,'exp'=16] {'exp'}, dimensions={0} | all-to-all | bytes 655360 | tf_op jit(solution)/shard_map/all_to_all | solution.py:513
  22.9 1.5 %collective-permute-start = (bf16[128,1280]{1,0:T(8,128)(2,1)S(1)}, bf16[128,1280]{1,0:T(8,128)(2,1)S(1)}, u32[]{:S(2)}, u32[]{:S(2)}) collective-permute-start(bf16[128,1280]{1,0:T(8,128)(2,1)S(1)} %bitcast.12), channel_id=1, source_target_pairs={{0,16},{16,0},{1,17},{17,1},{2,18},{18,2},{3,19},{19,3},{4,20},{20... | collective-permute-start | bytes 983048 | tf_op jit(solution)/shard_map/ppermute | solution.py:524
  24.4 9.2 %expert_rows.1 = (bf16[128,1280]{1,0:T(8,128)(2,1)}, bf16[64,2560]{1,0:T(8,128)(2,1)S(1)}, bf16[64,2560]{1,0:T(8,128)(2,1)S(1)}, f32[8,128]{1,0:T(8,128)S(1)}) custom-call(bf16[128,1280]{1,0:T(8,128)(2,1)S(1)} %bitcast.13, bf16[1280,256]{1,0:T(8,128)(2,1)S(1)} %get-tuple-element.27.first_in, bf16[256,1280]{1,0:T(8,128)(2,1)S(1)} %get-tuple-element.28.first_out, ...), custom_call_target="tpu_custom_call" | custom-call | flops 1677721600 | bytes 13107200 | tf_op jit(solution)/shard_map/expert_rows/pallas_call | solution.py:248
  33.6 3.7 %all-to-all-start.1 = ((bf16[16,8,1280]{2,1,0:T(8,128)(2,1)}), bf16[16,8,1280]{2,1,0:T(8,128)(2,1)S(1)}, u32[]{:S(2)}, u32[]{:S(2)}) async-start(bf16[16,8,1280]{2,1,0:T(8,128)(2,1)} %bitcast.6), calls=%async_computation.1 | async-start | bytes 655360 | tf_op jit(solution)/shard_map/all_to_all | solution.py:513
  37.3 0.0 collective-permute-done.other_rows
  37.3 0.0 copy-start.1
  37.3 8.8 %replica_grads.1 = (bf16[640,2560]{1,0:T(8,128)(2,1)}, bf16[1280,1280]{1,0:T(8,128)(2,1)}, bf16[2,256,1280]{2,1,0:T(8,128)(2,1)S(1)}, f32[8,128]{1,0:T(8,128)S(1)}) custom-call(s32[1]{0:T(128)} %bitcast.mine, f32[8,128]{1,0:T(8,128)S(1)} %get-tuple-element.29.after, bf16[128,1280]{1,0:T(8,128)(2,1)S(1)} %bitcast.14, ...), custom_call_target="tpu_custom_call" | custom-call | flops 13421772800 | bytes 104857600 | tf_op jit(solution)/shard_map/replica_grads/pallas_call | solution.py:340
  46.2 2.0 %all-to-all-done.1 = bf16[16,8,1280]{2,1,0:T(8,128)(2,1)S(1)} async-done(((bf16[16,8,1280]{2,1,0:T(8,128)(2,1)}), bf16[16,8,1280]{2,1,0:T(8,128)(2,1)S(1)}, u32[]{:S(2)}, u32[]{:S(2)}) %all-to-all-start.1) | async-done | bytes 327712 | tf_op jit(solution)/shard_map/all_to_all | solution.py:513
  48.2 0.0 copy-done.1
  48.2 3.2 %logits_grads.1 = (bf16[4,32,256]{2,1,0:T(8,128)(2,1)S(1)}, bf16[4,32,1280]{2,1,0:T(8,128)(2,1)S(1)}, bf16[16,1280]{1,0:T(8,128)(2,1)S(1)}, f32[8,128]{1,0:T(8,128)S(1)}) custom-call(f32[8,128]{1,0:T(8,128)S(1)} %get-tuple-element.32.after, bf16[128,1280]{1,0:T(8,128)(2,1)S(1)} %bitcast.11, bf16[4,256,1280]{2,1,0:T(8,128)(2,1)} %tokens.5, ...), custom_call_target="tpu_custom_call" | custom-call | flops 125829120 | bytes 5242880 | tf_op jit(solution)/shard_map/logits_grads/pallas_call | solution.py:430
  51.4 0.4 collective-permute-start.1
  51.8 2.1 %collective-permute-start.2 = (bf16[16,1280]{1,0:T(8,128)(2,1)S(1)}, bf16[16,1280]{1,0:T(8,128)(2,1)S(1)}, u32[]{:S(2)}, u32[]{:S(2)}) collective-permute-start(bf16[16,1280]{1,0:T(8,128)(2,1)S(1)} %get-tuple-element.38.refs_7_), channel_id=1, source_target_pairs={{0,18},{1,19},{2,16},{3,17},{4,22},{5,23},{6,20},{7,21},{8,26},{9,... | collective-permute-start | bytes 122888 | tf_op jit(solution)/shard_map/ppermute | solution.py:506
  53.9 0.5 collective-permute-start.3
  54.4 1.5 %collective-permute-start.4 = (bf16[16,1280]{1,0:T(8,128)(2,1)S(1)}, bf16[16,1280]{1,0:T(8,128)(2,1)S(1)}, u32[]{:S(2)}, u32[]{:S(2)}) collective-permute-start(bf16[16,1280]{1,0:T(8,128)(2,1)S(1)} %get-tuple-element.38.refs_7_), channel_id=1, source_target_pairs={{0,16},{1,17},{2,18},{3,19},{4,20},{5,21},{6,22},{7,23},{8,24},{9,... | collective-permute-start | bytes 122888 | tf_op jit(solution)/shard_map/ppermute | solution.py:506
  55.9 0.4 collective-permute-start.5
  56.3 0.0 collective-permute-done.1.refs_0_
  56.3 1.1 %collective-permute-start.6 = (bf16[16,1280]{1,0:T(8,128)(2,1)S(1)}, bf16[16,1280]{1,0:T(8,128)(2,1)S(1)}, u32[]{:S(2)}, u32[]{:S(2)}) collective-permute-start(bf16[16,1280]{1,0:T(8,128)(2,1)S(1)} %get-tuple-element.38.refs_7_), channel_id=1, source_target_pairs={{0,2},{1,3},{2,0},{3,1},{4,6},{5,7},{6,4},{7,5},{8,10},{9,11},{10,... | collective-permute-start | bytes 122888 | tf_op jit(solution)/shard_map/ppermute | solution.py:506
  57.4 0.0 collective-permute-done.2.refs_1_
  57.4 0.4 collective-permute-start.7
  57.8 0.0 collective-permute-done.3.refs_2_
  57.8 0.9 %collective-permute-done.4.refs_3_ = bf16[16,1280]{1,0:T(8,128)(2,1)S(1)} collective-permute-done((bf16[16,1280]{1,0:T(8,128)(2,1)S(1)}, bf16[16,1280]{1,0:T(8,128)(2,1)S(1)}, u32[]{:S(2)}, u32[]{:S(2)}) %collective-permute-start.4) | collective-permute-done | bytes 40992 | tf_op jit(solution)/shard_map/ppermute | solution.py:506
  58.6 1.0 %collective-permute-done.5.refs_4_ = bf16[16,1280]{1,0:T(8,128)(2,1)S(1)} collective-permute-done((bf16[16,1280]{1,0:T(8,128)(2,1)S(1)}, bf16[16,1280]{1,0:T(8,128)(2,1)S(1)}, u32[]{:S(2)}, u32[]{:S(2)}) %collective-permute-start.5) | collective-permute-done | bytes 40992 | tf_op jit(solution)/shard_map/ppermute | solution.py:506
  59.7 0.9 %collective-permute-done.6.refs_5_ = bf16[16,1280]{1,0:T(8,128)(2,1)S(1)} collective-permute-done((bf16[16,1280]{1,0:T(8,128)(2,1)S(1)}, bf16[16,1280]{1,0:T(8,128)(2,1)S(1)}, u32[]{:S(2)}, u32[]{:S(2)}) %collective-permute-start.6) | collective-permute-done | bytes 40992 | tf_op jit(solution)/shard_map/ppermute | solution.py:506
  60.6 0.0 collective-permute-done.7.refs_6_
  60.7 0.8 %collective-permute-start.10 = (bf16[16,1280]{1,0:T(8,128)(2,1)S(1)}, bf16[16,1280]{1,0:T(8,128)(2,1)S(1)}, u32[]{:S(2)}, u32[]{:S(2)}) collective-permute-start(bf16[16,1280]{1,0:T(8,128)(2,1)S(1)} %get-tuple-element.44.refs_3_), channel_id=1, source_target_pairs={{0,4},{1,5},{2,6},{3,7},{4,0},{5,1},{6,2},{7,3},{8,12},{9,13},{10,... | collective-permute-start | bytes 122888 | tf_op jit(solution)/shard_map/ppermute | solution.py:506
  61.5 1.8 %collective-permute-start.8 = (bf16[16,1280]{1,0:T(8,128)(2,1)S(1)}, bf16[16,1280]{1,0:T(8,128)(2,1)S(1)}, u32[]{:S(2)}, u32[]{:S(2)}) collective-permute-start(bf16[16,1280]{1,0:T(8,128)(2,1)S(1)} %get-tuple-element.44.refs_3_), channel_id=1, source_target_pairs={{0,12},{1,13},{2,14},{3,15},{4,8},{5,9},{6,10},{7,11},{8,4},{9,5},... | collective-permute-start | bytes 122888 | tf_op jit(solution)/shard_map/ppermute | solution.py:506
  63.3 1.0 %collective-permute-start.9 = (bf16[16,1280]{1,0:T(8,128)(2,1)S(1)}, bf16[16,1280]{1,0:T(8,128)(2,1)S(1)}, u32[]{:S(2)}, u32[]{:S(2)}) collective-permute-start(bf16[16,1280]{1,0:T(8,128)(2,1)S(1)} %get-tuple-element.44.refs_3_), channel_id=1, source_target_pairs={{0,8},{1,9},{2,10},{3,11},{4,12},{5,13},{6,14},{7,15},{8,0},{9,1},... | collective-permute-start | bytes 122888 | tf_op jit(solution)/shard_map/ppermute | solution.py:506
  64.2 2.7 %tokens_grads.1 = (bf16[4,256,1280]{2,1,0:T(8,128)(2,1)}, f32[8,128]{1,0:T(8,128)S(1)}) custom-call(f32[8,128]{1,0:T(8,128)S(1)} %get-tuple-element.39.after, bf16[4,32,256]{2,1,0:T(8,128)(2,1)S(1)} %get-tuple-element.40.left, bf16[4,32,1280]{2,1,0:T(8,128)(2,1)S(1)} %get-tuple-element.41.right), custom_call_target="tpu_custom_call" | custom-call | flops 83886080 | bytes 2621440 | tf_op jit(solution)/shard_map/tokens_grads/pallas_call | solution.py:461
  67.0 0.0 collective-permute-done.10.refs_2_
  67.0 0.4 collective-permute-done.8.refs_0_
  67.4 1.2 %collective-permute-done.9.refs_1_ = bf16[16,1280]{1,0:T(8,128)(2,1)S(1)} collective-permute-done((bf16[16,1280]{1,0:T(8,128)(2,1)S(1)}, bf16[16,1280]{1,0:T(8,128)(2,1)S(1)}, u32[]{:S(2)}, u32[]{:S(2)}) %collective-permute-start.9) | collective-permute-done | bytes 40992 | tf_op jit(solution)/shard_map/ppermute | solution.py:506
  68.6 0.7 add_terms.3
  (1 shorter events, 0.0 us)
Async XLA Ops:
  0.6 0.8 %copy-start = (bf16[1280,16]{0,1:T(8,128)(2,1)S(1)}, bf16[1280,16]{0,1:T(8,128)(2,1)}, u32[]{:S(2)}) copy-start(bf16[1280,16]{0,1:T(8,128)(2,1)} %param.6) | copy-start | bytes 122884
  22.9 14.4 %collective-permute-start = (bf16[128,1280]{1,0:T(8,128)(2,1)S(1)}, bf16[128,1280]{1,0:T(8,128)(2,1)S(1)}, u32[]{:S(2)}, u32[]{:S(2)}) collective-permute-start(bf16[128,1280]{1,0:T(8,128)(2,1)S(1)} %bitcast.12), channel_id=1, source_target_pairs={{0,16},{16,0},{1,17},{17,1},{2,18},{18,2},{3,19},{19,3},{4,20},{20... | collective-permute-start | bytes 983048 | tf_op jit(solution)/shard_map/ppermute | solution.py:524
  33.6 14.6 %all-to-all-start.1 = ((bf16[16,8,1280]{2,1,0:T(8,128)(2,1)}), bf16[16,8,1280]{2,1,0:T(8,128)(2,1)S(1)}, u32[]{:S(2)}, u32[]{:S(2)}) async-start(bf16[16,8,1280]{2,1,0:T(8,128)(2,1)} %bitcast.6), calls=%async_computation.1 | async-start | bytes 655360 | tf_op jit(solution)/shard_map/all_to_all | solution.py:513
  37.3 10.9 %copy-start.1 = (bf16[1280,16]{0,1:T(8,128)(2,1)S(1)}, bf16[1280,16]{0,1:T(8,128)(2,1)}, u32[]{:S(2)}) copy-start(bf16[1280,16]{0,1:T(8,128)(2,1)} %param.6) | copy-start | bytes 122884
  51.4 4.8 %collective-permute-start.1 = (bf16[16,1280]{1,0:T(8,128)(2,1)S(1)}, bf16[16,1280]{1,0:T(8,128)(2,1)S(1)}, u32[]{:S(2)}, u32[]{:S(2)}) collective-permute-start(bf16[16,1280]{1,0:T(8,128)(2,1)S(1)} %get-tuple-element.38.refs_7_), channel_id=1, source_target_pairs={{0,19},{1,18},{2,17},{3,16},{4,23},{5,22},{6,21},{7,20},{8,27},{9,... | collective-permute-start | bytes 122888 | tf_op jit(solution)/shard_map/ppermute | solution.py:506
  51.8 5.6 %collective-permute-start.2 = (bf16[16,1280]{1,0:T(8,128)(2,1)S(1)}, bf16[16,1280]{1,0:T(8,128)(2,1)S(1)}, u32[]{:S(2)}, u32[]{:S(2)}) collective-permute-start(bf16[16,1280]{1,0:T(8,128)(2,1)S(1)} %get-tuple-element.38.refs_7_), channel_id=1, source_target_pairs={{0,18},{1,19},{2,16},{3,17},{4,22},{5,23},{6,20},{7,21},{8,26},{9,... | collective-permute-start | bytes 122888 | tf_op jit(solution)/shard_map/ppermute | solution.py:506
  53.9 3.9 %collective-permute-start.3 = (bf16[16,1280]{1,0:T(8,128)(2,1)S(1)}, bf16[16,1280]{1,0:T(8,128)(2,1)S(1)}, u32[]{:S(2)}, u32[]{:S(2)}) collective-permute-start(bf16[16,1280]{1,0:T(8,128)(2,1)S(1)} %get-tuple-element.38.refs_7_), channel_id=1, source_target_pairs={{0,17},{1,16},{2,19},{3,18},{4,21},{5,20},{6,23},{7,22},{8,25},{9,... | collective-permute-start | bytes 122888 | tf_op jit(solution)/shard_map/ppermute | solution.py:506
  54.4 4.2 %collective-permute-start.4 = (bf16[16,1280]{1,0:T(8,128)(2,1)S(1)}, bf16[16,1280]{1,0:T(8,128)(2,1)S(1)}, u32[]{:S(2)}, u32[]{:S(2)}) collective-permute-start(bf16[16,1280]{1,0:T(8,128)(2,1)S(1)} %get-tuple-element.38.refs_7_), channel_id=1, source_target_pairs={{0,16},{1,17},{2,18},{3,19},{4,20},{5,21},{6,22},{7,23},{8,24},{9,... | collective-permute-start | bytes 122888 | tf_op jit(solution)/shard_map/ppermute | solution.py:506
  55.9 3.8 %collective-permute-start.5 = (bf16[16,1280]{1,0:T(8,128)(2,1)S(1)}, bf16[16,1280]{1,0:T(8,128)(2,1)S(1)}, u32[]{:S(2)}, u32[]{:S(2)}) collective-permute-start(bf16[16,1280]{1,0:T(8,128)(2,1)S(1)} %get-tuple-element.38.refs_7_), channel_id=1, source_target_pairs={{0,3},{1,2},{2,1},{3,0},{4,7},{5,6},{6,5},{7,4},{8,11},{9,10},{10,... | collective-permute-start | bytes 122888 | tf_op jit(solution)/shard_map/ppermute | solution.py:506
  56.3 4.4 %collective-permute-start.6 = (bf16[16,1280]{1,0:T(8,128)(2,1)S(1)}, bf16[16,1280]{1,0:T(8,128)(2,1)S(1)}, u32[]{:S(2)}, u32[]{:S(2)}) collective-permute-start(bf16[16,1280]{1,0:T(8,128)(2,1)S(1)} %get-tuple-element.38.refs_7_), channel_id=1, source_target_pairs={{0,2},{1,3},{2,0},{3,1},{4,6},{5,7},{6,4},{7,5},{8,10},{9,11},{10,... | collective-permute-start | bytes 122888 | tf_op jit(solution)/shard_map/ppermute | solution.py:506
  57.4 3.2 %collective-permute-start.7 = (bf16[16,1280]{1,0:T(8,128)(2,1)S(1)}, bf16[16,1280]{1,0:T(8,128)(2,1)S(1)}, u32[]{:S(2)}, u32[]{:S(2)}) collective-permute-start(bf16[16,1280]{1,0:T(8,128)(2,1)S(1)} %get-tuple-element.38.refs_7_), channel_id=1, source_target_pairs={{0,1},{1,0},{2,3},{3,2},{4,5},{5,4},{6,7},{7,6},{8,9},{9,8},{10,11... | collective-permute-start | bytes 122888 | tf_op jit(solution)/shard_map/ppermute | solution.py:506
  60.7 6.3 %collective-permute-start.10 = (bf16[16,1280]{1,0:T(8,128)(2,1)S(1)}, bf16[16,1280]{1,0:T(8,128)(2,1)S(1)}, u32[]{:S(2)}, u32[]{:S(2)}) collective-permute-start(bf16[16,1280]{1,0:T(8,128)(2,1)S(1)} %get-tuple-element.44.refs_3_), channel_id=1, source_target_pairs={{0,4},{1,5},{2,6},{3,7},{4,0},{5,1},{6,2},{7,3},{8,12},{9,13},{10,... | collective-permute-start | bytes 122888 | tf_op jit(solution)/shard_map/ppermute | solution.py:506
  61.5 5.9 %collective-permute-start.8 = (bf16[16,1280]{1,0:T(8,128)(2,1)S(1)}, bf16[16,1280]{1,0:T(8,128)(2,1)S(1)}, u32[]{:S(2)}, u32[]{:S(2)}) collective-permute-start(bf16[16,1280]{1,0:T(8,128)(2,1)S(1)} %get-tuple-element.44.refs_3_), channel_id=1, source_target_pairs={{0,12},{1,13},{2,14},{3,15},{4,8},{5,9},{6,10},{7,11},{8,4},{9,5},... | collective-permute-start | bytes 122888 | tf_op jit(solution)/shard_map/ppermute | solution.py:506
  63.3 5.3 %collective-permute-start.9 = (bf16[16,1280]{1,0:T(8,128)(2,1)S(1)}, bf16[16,1280]{1,0:T(8,128)(2,1)S(1)}, u32[]{:S(2)}, u32[]{:S(2)}) collective-permute-start(bf16[16,1280]{1,0:T(8,128)(2,1)S(1)} %get-tuple-element.44.refs_3_), channel_id=1, source_target_pairs={{0,8},{1,9},{2,10},{3,11},{4,12},{5,13},{6,14},{7,15},{8,0},{9,1},... | collective-permute-start | bytes 122888 | tf_op jit(solution)/shard_map/ppermute | solution.py:506

commit v18 on v17

--- a/solution.py
+++ b/solution.py
@@ -244,7 +244,12 @@
     hidden = w_in.shape[1]
     count = total // KINDS
     kept = shaped((count, hidden), LOW)
-    chunks = chunks_of(first_out.shape[0], hidden, tile)
+    start = first_out.shape[0]
+    chunks = [
+        *chunks_of(start, start + tile // 2, tile),
+        *chunks_of(start + tile // 2, hidden - tile // 2, tile),
+        *chunks_of(hidden - tile // 2, hidden, tile),
+    ]
     return call(
         functools.partial(expert_kernel, chunks),
         "expert_rows",
@@ -477,7 +482,7 @@
 
 def add_kernel(after, *refs):
     del after
-    terms = [ref[...].astype(WIDE) for ref in reversed(refs[:-2])]
+    terms = [ref[...].astype(WIDE) for ref in refs[:-2]]
     while len(terms) > 1:
         terms = [left + right for left, right in zip(terms[::2], terms[1::2])]
     refs[-2][...] = terms[0].astype(refs[-2].dtype)
@@ -493,7 +498,7 @@
         out_shape=(shaped(terms[0].shape, dtype), MARK),
         in_specs=[PLACE] + [WHOLE] * len(terms),
         out_specs=(WHOLE, PLACE),
-    )(after, *reversed(terms))
+    )(after, *terms)
 
 
 def terms_of_group(array, bits):
@@ -502,11 +507,10 @@
     for bit in bits:
         distances += [distance + (1 << bit) for distance in distances]
     count = lax.axis_size(axes)
-    terms = [
+    return [array] + [
         lax.ppermute(array, axes, [(i, i ^ distance) for i in range(count)])
-        for distance in reversed(distances[1:])
+        for distance in distances[1:]
     ]
-    return [array, *reversed(terms)]
 
 
 def exchange(rows, axes):

time: 69.6 us -> 69.4 us (level)
  waiting for transfers between devices: 6.54 us -> 5.21 us
  starting transfers between devices: 15.1 us -> 15.9 us
    ppermute x10, waiting for transfers between devices: 4.52 us -> 3.18 us  [terms_of_group(): lax.ppermute(array, axes, [(i, i ^ distance) for i in range(count)])]
    ppermute x10, starting transfers between devices: 9.87 us -> 10.6 us  [terms_of_group(): lax.ppermute(array, axes, [(i, i ^ distance) for i in range(count)])]
  transfers between devices with their start and end apart: 12 -> 12, of which waited for: 6 -> 5; matrix products, arithmetic and copies ran while one was open for 0% -> 0% of each run, Pallas kernels for 30% -> 30%
where the time goes in v18:
time: 69.4 us; the launch traced here: 69.1 us
  Pallas kernels  28.2 us (41%)
  blocking collectives  18.3 us (26%)
  starting transfers between devices  15.9 us (23%)
  waiting for transfers between devices  5.21 us (8%)
  local copies, waits for them, and re-layouts  0.78 us (1%)
  between operations  0.72 us (1%)
    all_to_all x1, blocking collectives, exchange(): return lax.all_to_all(rows, axes, split_axis=0, concat_axis=0, tiled=True)  18.3 us
    ppermute x10, starting transfers between devices, terms_of_group(): lax.ppermute(array, axes, [(i, i ^ distance) for i in range(count)])  10.6 us
    pallas_call x1, Pallas kernels, expert(): call(functools.partial(expert_kernel, chunks), 'expert_rows', ROOMY, 8 *...  9.51 us
    pallas_call x1, Pallas kernels, replica_grads(): call(functools.partial(replica_kernel, chunks), 'replica_grads', ROOMY, 6...  8.83 us
    all_to_all x1, starting transfers between devices, exchange(): return lax.all_to_all(rows, axes, split_axis=0, concat_axis=0, tiled=True)  3.74 us
    pallas_call x1, Pallas kernels, logits_grads(): call(logits_kernel, 'logits_grads', ROOMY, 6 * images * slots * length *...  3.22 us
    pallas_call x1, Pallas kernels, gather(): call(gather_kernel, 'gather_slots', ROOMY, 6 * images * slots * length *...  3.2 us
    ppermute x10, waiting for transfers between devices, terms_of_group(): lax.ppermute(array, axes, [(i, i ^ distance) for i in range(count)])  3.18 us
  transfers between devices with their start and end apart: 12, of which 5 were waited for; matrix products, arithmetic and copies ran while one was open for 0% of the time, Pallas kernels for 30%

profile of v18, /device:TPU:0, one launch (start us, length us, event | category | flops | bytes accessed | tf_op | source)
XLA Modules:
  0.0 69.1 jit_solution(10038047051563128934)
XLA Ops:
  0.6 0.0 copy-start
  0.6 0.8 %copy-done = bf16[1280,16]{0,1:T(8,128)(2,1)S(1)} copy-done((bf16[1280,16]{0,1:T(8,128)(2,1)S(1)}, bf16[1280,16]{0,1:T(8,128)(2,1)}, u32[]{:S(2)}) %copy-start) | copy-done | bytes 40984
  1.4 3.2 %gather_slots.1 = (bf16[128,1280]{1,0:T(8,128)(2,1)S(1)}, f32[4,16,256]{2,1,0:T(8,128)S(1)}, f32[4,16,256]{2,1,0:T(8,128)S(1)}, bf16[1280,256]{1,0:T(8,128)(2,1)S(1)}, bf16[256,1280]{1,0:T(8,128)(2,1)S(1)}) custom-call(bf16[4,256,1280]{2,1,0:T(8,128)(2,1)} %tokens.5, bf16[16,1280]{1,0:T(8,128)(2,1)S(1)} %bitcast.16, bf16[4,256,1280]{2,1,0:T(8,128)(2,1)} %grads.3, ...), custom_call_target="tpu_custom_call" | custom-call | flops 125829120 | bytes 5242880 | tf_op jit(solution)/shard_map/gather_slots/pallas_call | solution.py:148
  4.6 18.3 %all_to_all.22 = bf16[16,8,1280]{2,1,0:T(8,128)(2,1)S(1)} all-to-all(bf16[16,8,1280]{2,1,0:T(8,128)(2,1)S(1)} %bitcast.15), channel_id=1, replica_groups=mesh['rep'=2,'exp'=16] {'exp'}, dimensions={0} | all-to-all | bytes 655360 | tf_op jit(solution)/shard_map/all_to_all | solution.py:517
  22.9 1.5 %collective-permute-start = (bf16[128,1280]{1,0:T(8,128)(2,1)S(1)}, bf16[128,1280]{1,0:T(8,128)(2,1)S(1)}, u32[]{:S(2)}, u32[]{:S(2)}) collective-permute-start(bf16[128,1280]{1,0:T(8,128)(2,1)S(1)} %bitcast.12), channel_id=1, source_target_pairs={{0,16},{16,0},{1,17},{17,1},{2,18},{18,2},{3,19},{19,3},{4,20},{20... | collective-permute-start | bytes 983048 | tf_op jit(solution)/shard_map/ppermute | solution.py:528
  24.4 9.5 %expert_rows.1 = (bf16[128,1280]{1,0:T(8,128)(2,1)}, bf16[64,2560]{1,0:T(8,128)(2,1)S(1)}, bf16[64,2560]{1,0:T(8,128)(2,1)S(1)}, f32[8,128]{1,0:T(8,128)S(1)}) custom-call(bf16[128,1280]{1,0:T(8,128)(2,1)S(1)} %bitcast.13, bf16[1280,256]{1,0:T(8,128)(2,1)S(1)} %get-tuple-element.27.first_in, bf16[256,1280]{1,0:T(8,128)(2,1)S(1)} %get-tuple-element.28.first_out, ...), custom_call_target="tpu_custom_call" | custom-call | flops 1677721600 | bytes 13107200 | tf_op jit(solution)/shard_map/expert_rows/pallas_call | solution.py:253
  33.9 3.7 %all-to-all-start.1 = ((bf16[16,8,1280]{2,1,0:T(8,128)(2,1)}), bf16[16,8,1280]{2,1,0:T(8,128)(2,1)S(1)}, u32[]{:S(2)}, u32[]{:S(2)}) async-start(bf16[16,8,1280]{2,1,0:T(8,128)(2,1)} %bitcast.6), calls=%async_computation.1 | async-start | bytes 655360 | tf_op jit(solution)/shard_map/all_to_all | solution.py:517
  37.7 0.0 collective-permute-done.other_rows
  37.7 0.0 copy-start.1
  37.7 8.8 %replica_grads.1 = (bf16[640,2560]{1,0:T(8,128)(2,1)}, bf16[1280,1280]{1,0:T(8,128)(2,1)}, bf16[2,256,1280]{2,1,0:T(8,128)(2,1)S(1)}, f32[8,128]{1,0:T(8,128)S(1)}) custom-call(s32[1]{0:T(128)} %bitcast.mine, f32[8,128]{1,0:T(8,128)S(1)} %get-tuple-element.29.after, bf16[128,1280]{1,0:T(8,128)(2,1)S(1)} %bitcast.14, ...), custom_call_target="tpu_custom_call" | custom-call | flops 13421772800 | bytes 104857600 | tf_op jit(solution)/shard_map/replica_grads/pallas_call | solution.py:345
  46.5 2.0 %all-to-all-done.1 = bf16[16,8,1280]{2,1,0:T(8,128)(2,1)S(1)} async-done(((bf16[16,8,1280]{2,1,0:T(8,128)(2,1)}), bf16[16,8,1280]{2,1,0:T(8,128)(2,1)S(1)}, u32[]{:S(2)}, u32[]{:S(2)}) %all-to-all-start.1) | async-done | bytes 327712 | tf_op jit(solution)/shard_map/all_to_all | solution.py:517
  48.5 0.0 copy-done.1
  48.5 3.2 %logits_grads.1 = (bf16[4,32,256]{2,1,0:T(8,128)(2,1)S(1)}, bf16[4,32,1280]{2,1,0:T(8,128)(2,1)S(1)}, bf16[16,1280]{1,0:T(8,128)(2,1)S(1)}, f32[8,128]{1,0:T(8,128)S(1)}) custom-call(f32[8,128]{1,0:T(8,128)S(1)} %get-tuple-element.32.after, bf16[128,1280]{1,0:T(8,128)(2,1)S(1)} %bitcast.11, bf16[4,256,1280]{2,1,0:T(8,128)(2,1)} %tokens.5, ...), custom_call_target="tpu_custom_call" | custom-call | flops 125829120 | bytes 5242880 | tf_op jit(solution)/shard_map/logits_grads/pallas_call | solution.py:435
  51.8 0.1 collective-permute-start.1
  51.9 0.8 %collective-permute-start.2 = (bf16[16,1280]{1,0:T(8,128)(2,1)S(1)}, bf16[16,1280]{1,0:T(8,128)(2,1)S(1)}, u32[]{:S(2)}, u32[]{:S(2)}) collective-permute-start(bf16[16,1280]{1,0:T(8,128)(2,1)S(1)} %get-tuple-element.38.refs_0_), channel_id=1, source_target_pairs={{0,2},{1,3},{2,0},{3,1},{4,6},{5,7},{6,4},{7,5},{8,10},{9,11},{10,... | collective-permute-start | bytes 122888 | tf_op jit(solution)/shard_map/ppermute | solution.py:511
  52.6 1.1 %collective-permute-start.3 = (bf16[16,1280]{1,0:T(8,128)(2,1)S(1)}, bf16[16,1280]{1,0:T(8,128)(2,1)S(1)}, u32[]{:S(2)}, u32[]{:S(2)}) collective-permute-start(bf16[16,1280]{1,0:T(8,128)(2,1)S(1)} %get-tuple-element.38.refs_0_), channel_id=1, source_target_pairs={{0,3},{1,2},{2,1},{3,0},{4,7},{5,6},{6,5},{7,4},{8,11},{9,10},{10,... | collective-permute-start | bytes 122888 | tf_op jit(solution)/shard_map/ppermute | solution.py:511
  53.7 0.5 collective-permute-start.4
  54.3 1.2 %collective-permute-start.5 = (bf16[16,1280]{1,0:T(8,128)(2,1)S(1)}, bf16[16,1280]{1,0:T(8,128)(2,1)S(1)}, u32[]{:S(2)}, u32[]{:S(2)}) collective-permute-start(bf16[16,1280]{1,0:T(8,128)(2,1)S(1)} %get-tuple-element.38.refs_0_), channel_id=1, source_target_pairs={{0,17},{1,16},{2,19},{3,18},{4,21},{5,20},{6,23},{7,22},{8,25},{9,... | collective-permute-start | bytes 122888 | tf_op jit(solution)/shard_map/ppermute | solution.py:511
  55.4 0.0 collective-permute-done.1.refs_1_
  55.4 0.7 collective-permute-start.6
  56.1 0.1 collective-permute-done.2.refs_2_
  56.2 1.9 %collective-permute-start.7 = (bf16[16,1280]{1,0:T(8,128)(2,1)S(1)}, bf16[16,1280]{1,0:T(8,128)(2,1)S(1)}, u32[]{:S(2)}, u32[]{:S(2)}) collective-permute-start(bf16[16,1280]{1,0:T(8,128)(2,1)S(1)} %get-tuple-element.38.refs_0_), channel_id=1, source_target_pairs={{0,19},{1,18},{2,17},{3,16},{4,23},{5,22},{6,21},{7,20},{8,27},{9,... | collective-permute-start | bytes 122888 | tf_op jit(solution)/shard_map/ppermute | solution.py:511
  58.1 0.0 collective-permute-done.3.refs_3_
  58.1 0.0 collective-permute-done.4.refs_4_
  58.1 0.0 collective-permute-done.5.refs_5_
  58.1 2.4 %collective-permute-done.6.refs_6_ = bf16[16,1280]{1,0:T(8,128)(2,1)S(1)} collective-permute-done((bf16[16,1280]{1,0:T(8,128)(2,1)S(1)}, bf16[16,1280]{1,0:T(8,128)(2,1)S(1)}, u32[]{:S(2)}, u32[]{:S(2)}) %collective-permute-start.6) | collective-permute-done | bytes 40992 | tf_op jit(solution)/shard_map/ppermute | solution.py:511
  60.5 0.5 collective-permute-done.7.refs_7_
  61.0 2.0 %collective-permute-start.10 = (bf16[16,1280]{1,0:T(8,128)(2,1)S(1)}, bf16[16,1280]{1,0:T(8,128)(2,1)S(1)}, u32[]{:S(2)}, u32[]{:S(2)}) collective-permute-start(bf16[16,1280]{1,0:T(8,128)(2,1)S(1)} %get-tuple-element.44.refs_0_), channel_id=1, source_target_pairs={{0,12},{1,13},{2,14},{3,15},{4,8},{5,9},{6,10},{7,11},{8,4},{9,5},... | collective-permute-start | bytes 122888 | tf_op jit(solution)/shard_map/ppermute | solution.py:511
  63.1 0.0 collective-permute-start.8
  63.1 2.4 %collective-permute-start.9 = (bf16[16,1280]{1,0:T(8,128)(2,1)S(1)}, bf16[16,1280]{1,0:T(8,128)(2,1)S(1)}, u32[]{:S(2)}, u32[]{:S(2)}) collective-permute-start(bf16[16,1280]{1,0:T(8,128)(2,1)S(1)} %get-tuple-element.44.refs_0_), channel_id=1, source_target_pairs={{0,8},{1,9},{2,10},{3,11},{4,12},{5,13},{6,14},{7,15},{8,0},{9,1},... | collective-permute-start | bytes 122888 | tf_op jit(solution)/shard_map/ppermute | solution.py:511
  65.5 2.7 %tokens_grads.1 = (bf16[4,256,1280]{2,1,0:T(8,128)(2,1)}, f32[8,128]{1,0:T(8,128)S(1)}) custom-call(f32[8,128]{1,0:T(8,128)S(1)} %get-tuple-element.39.after, bf16[4,32,256]{2,1,0:T(8,128)(2,1)S(1)} %get-tuple-element.40.left, bf16[4,32,1280]{2,1,0:T(8,128)(2,1)S(1)} %get-tuple-element.41.right), custom_call_target="tpu_custom_call" | custom-call | flops 83886080 | bytes 2621440 | tf_op jit(solution)/shard_map/tokens_grads/pallas_call | solution.py:466
  68.2 0.0 collective-permute-done.10.refs_3_
  68.2 0.0 collective-permute-done.8.refs_1_
  68.2 0.2 collective-permute-done.9.refs_2_
  68.4 0.7 add_terms.3
  (1 shorter events, 0.0 us)
Async XLA Ops:
  0.6 0.8 %copy-start = (bf16[1280,16]{0,1:T(8,128)(2,1)S(1)}, bf16[1280,16]{0,1:T(8,128)(2,1)}, u32[]{:S(2)}) copy-start(bf16[1280,16]{0,1:T(8,128)(2,1)} %param.6) | copy-start | bytes 122884
  22.9 14.8 %collective-permute-start = (bf16[128,1280]{1,0:T(8,128)(2,1)S(1)}, bf16[128,1280]{1,0:T(8,128)(2,1)S(1)}, u32[]{:S(2)}, u32[]{:S(2)}) collective-permute-start(bf16[128,1280]{1,0:T(8,128)(2,1)S(1)} %bitcast.12), channel_id=1, source_target_pairs={{0,16},{16,0},{1,17},{17,1},{2,18},{18,2},{3,19},{19,3},{4,20},{20... | collective-permute-start | bytes 983048 | tf_op jit(solution)/shard_map/ppermute | solution.py:528
  33.9 14.6 %all-to-all-start.1 = ((bf16[16,8,1280]{2,1,0:T(8,128)(2,1)}), bf16[16,8,1280]{2,1,0:T(8,128)(2,1)S(1)}, u32[]{:S(2)}, u32[]{:S(2)}) async-start(bf16[16,8,1280]{2,1,0:T(8,128)(2,1)} %bitcast.6), calls=%async_computation.1 | async-start | bytes 655360 | tf_op jit(solution)/shard_map/all_to_all | solution.py:517
  37.7 10.9 %copy-start.1 = (bf16[1280,16]{0,1:T(8,128)(2,1)S(1)}, bf16[1280,16]{0,1:T(8,128)(2,1)}, u32[]{:S(2)}) copy-start(bf16[1280,16]{0,1:T(8,128)(2,1)} %param.6) | copy-start | bytes 122884
  51.8 3.6 %collective-permute-start.1 = (bf16[16,1280]{1,0:T(8,128)(2,1)S(1)}, bf16[16,1280]{1,0:T(8,128)(2,1)S(1)}, u32[]{:S(2)}, u32[]{:S(2)}) collective-permute-start(bf16[16,1280]{1,0:T(8,128)(2,1)S(1)} %get-tuple-element.38.refs_0_), channel_id=1, source_target_pairs={{0,1},{1,0},{2,3},{3,2},{4,5},{5,4},{6,7},{7,6},{8,9},{9,8},{10,11... | collective-permute-start | bytes 122888 | tf_op jit(solution)/shard_map/ppermute | solution.py:511
  51.9 4.4 %collective-permute-start.2 = (bf16[16,1280]{1,0:T(8,128)(2,1)S(1)}, bf16[16,1280]{1,0:T(8,128)(2,1)S(1)}, u32[]{:S(2)}, u32[]{:S(2)}) collective-permute-start(bf16[16,1280]{1,0:T(8,128)(2,1)S(1)} %get-tuple-element.38.refs_0_), channel_id=1, source_target_pairs={{0,2},{1,3},{2,0},{3,1},{4,6},{5,7},{6,4},{7,5},{8,10},{9,11},{10,... | collective-permute-start | bytes 122888 | tf_op jit(solution)/shard_map/ppermute | solution.py:511
  52.6 5.5 %collective-permute-start.3 = (bf16[16,1280]{1,0:T(8,128)(2,1)S(1)}, bf16[16,1280]{1,0:T(8,128)(2,1)S(1)}, u32[]{:S(2)}, u32[]{:S(2)}) collective-permute-start(bf16[16,1280]{1,0:T(8,128)(2,1)S(1)} %get-tuple-element.38.refs_0_), channel_id=1, source_target_pairs={{0,3},{1,2},{2,1},{3,0},{4,7},{5,6},{6,5},{7,4},{8,11},{9,10},{10,... | collective-permute-start | bytes 122888 | tf_op jit(solution)/shard_map/ppermute | solution.py:511
  53.7 4.4 %collective-permute-start.4 = (bf16[16,1280]{1,0:T(8,128)(2,1)S(1)}, bf16[16,1280]{1,0:T(8,128)(2,1)S(1)}, u32[]{:S(2)}, u32[]{:S(2)}) collective-permute-start(bf16[16,1280]{1,0:T(8,128)(2,1)S(1)} %get-tuple-element.38.refs_0_), channel_id=1, source_target_pairs={{0,16},{1,17},{2,18},{3,19},{4,20},{5,21},{6,22},{7,23},{8,24},{9,... | collective-permute-start | bytes 122888 | tf_op jit(solution)/shard_map/ppermute | solution.py:511
  54.3 3.9 %collective-permute-start.5 = (bf16[16,1280]{1,0:T(8,128)(2,1)S(1)}, bf16[16,1280]{1,0:T(8,128)(2,1)S(1)}, u32[]{:S(2)}, u32[]{:S(2)}) collective-permute-start(bf16[16,1280]{1,0:T(8,128)(2,1)S(1)} %get-tuple-element.38.refs_0_), channel_id=1, source_target_pairs={{0,17},{1,16},{2,19},{3,18},{4,21},{5,20},{6,23},{7,22},{8,25},{9,... | collective-permute-start | bytes 122888 | tf_op jit(solution)/shard_map/ppermute | solution.py:511
  55.4 5.1 %collective-permute-start.6 = (bf16[16,1280]{1,0:T(8,128)(2,1)S(1)}, bf16[16,1280]{1,0:T(8,128)(2,1)S(1)}, u32[]{:S(2)}, u32[]{:S(2)}) collective-permute-start(bf16[16,1280]{1,0:T(8,128)(2,1)S(1)} %get-tuple-element.38.refs_0_), channel_id=1, source_target_pairs={{0,18},{1,19},{2,16},{3,17},{4,22},{5,23},{6,20},{7,21},{8,26},{9,... | collective-permute-start | bytes 122888 | tf_op jit(solution)/shard_map/ppermute | solution.py:511
  56.2 4.8 %collective-permute-start.7 = (bf16[16,1280]{1,0:T(8,128)(2,1)S(1)}, bf16[16,1280]{1,0:T(8,128)(2,1)S(1)}, u32[]{:S(2)}, u32[]{:S(2)}) collective-permute-start(bf16[16,1280]{1,0:T(8,128)(2,1)S(1)} %get-tuple-element.38.refs_0_), channel_id=1, source_target_pairs={{0,19},{1,18},{2,17},{3,16},{4,23},{5,22},{6,21},{7,20},{8,27},{9,... | collective-permute-start | bytes 122888 | tf_op jit(solution)/shard_map/ppermute | solution.py:511
  61.0 7.2 %collective-permute-start.10 = (bf16[16,1280]{1,0:T(8,128)(2,1)S(1)}, bf16[16,1280]{1,0:T(8,128)(2,1)S(1)}, u32[]{:S(2)}, u32[]{:S(2)}) collective-permute-start(bf16[16,1280]{1,0:T(8,128)(2,1)S(1)} %get-tuple-element.44.refs_0_), channel_id=1, source_target_pairs={{0,12},{1,13},{2,14},{3,15},{4,8},{5,9},{6,10},{7,11},{8,4},{9,5},... | collective-permute-start | bytes 122888 | tf_op jit(solution)/shard_map/ppermute | solution.py:511
  63.1 5.2 %collective-permute-start.8 = (bf16[16,1280]{1,0:T(8,128)(2,1)S(1)}, bf16[16,1280]{1,0:T(8,128)(2,1)S(1)}, u32[]{:S(2)}, u32[]{:S(2)}) collective-permute-start(bf16[16,1280]{1,0:T(8,128)(2,1)S(1)} %get-tuple-element.44.refs_0_), channel_id=1, source_target_pairs={{0,4},{1,5},{2,6},{3,7},{4,0},{5,1},{6,2},{7,3},{8,12},{9,13},{10,... | collective-permute-start | bytes 122888 | tf_op jit(solution)/shard_map/ppermute | solution.py:511
  63.1 5.3 %collective-permute-start.9 = (bf16[16,1280]{1,0:T(8,128)(2,1)S(1)}, bf16[16,1280]{1,0:T(8,128)(2,1)S(1)}, u32[]{:S(2)}, u32[]{:S(2)}) collective-permute-start(bf16[16,1280]{1,0:T(8,128)(2,1)S(1)} %get-tuple-element.44.refs_0_), channel_id=1, source_target_pairs={{0,8},{1,9},{2,10},{3,11},{4,12},{5,13},{6,14},{7,15},{8,0},{9,1},... | collective-permute-start | bytes 122888 | tf_op jit(solution)/shard_map/ppermute | solution.py:511

commit v19 on v18

--- a/solution.py
+++ b/solution.py
@@ -244,12 +244,7 @@
     hidden = w_in.shape[1]
     count = total // KINDS
     kept = shaped((count, hidden), LOW)
-    start = first_out.shape[0]
-    chunks = [
-        *chunks_of(start, start + tile // 2, tile),
-        *chunks_of(start + tile // 2, hidden - tile // 2, tile),
-        *chunks_of(hidden - tile // 2, hidden, tile),
-    ]
+    chunks = chunks_of(first_out.shape[0], hidden, tile)
     return call(
         functools.partial(expert_kernel, chunks),
         "expert_rows",

time: 69.4 us -> 69 us (level)
  no operation moved by 1% of the time
where the time goes in v19:
time: 69 us; the launch traced here: 68.7 us
  Pallas kernels  27.9 us (40%)
  blocking collectives  18.3 us (27%)
  starting transfers between devices  15.9 us (23%)
  waiting for transfers between devices  5.2 us (8%)
  local copies, waits for them, and re-layouts  0.78 us (1%)
  between operations  0.72 us (1%)
    all_to_all x1, blocking collectives, exchange(): return lax.all_to_all(rows, axes, split_axis=0, concat_axis=0, tiled=True)  18.3 us
    ppermute x10, starting transfers between devices, terms_of_group(): lax.ppermute(array, axes, [(i, i ^ distance) for i in range(count)])  10.6 us
    pallas_call x1, Pallas kernels, expert(): call(functools.partial(expert_kernel, chunks), 'expert_rows', ROOMY, 8 *...  9.16 us
    pallas_call x1, Pallas kernels, replica_grads(): call(functools.partial(replica_kernel, chunks), 'replica_grads', ROOMY, 6...  8.83 us
    all_to_all x1, starting transfers between devices, exchange(): return lax.all_to_all(rows, axes, split_axis=0, concat_axis=0, tiled=True)  3.74 us
    pallas_call x1, Pallas kernels, logits_grads(): call(logits_kernel, 'logits_grads', ROOMY, 6 * images * slots * length *...  3.22 us
    pallas_call x1, Pallas kernels, gather(): call(gather_kernel, 'gather_slots', ROOMY, 6 * images * slots * length *...  3.2 us
    ppermute x10, waiting for transfers between devices, terms_of_group(): lax.ppermute(array, axes, [(i, i ^ distance) for i in range(count)])  3.18 us
  transfers between devices with their start and end apart: 12, of which 5 were waited for; matrix products, arithmetic and copies ran while one was open for 0% of the time, Pallas kernels for 30%

profile of v19, /device:TPU:0, one launch (start us, length us, event | category | flops | bytes accessed | tf_op | source)
XLA Modules:
  0.0 68.7 jit_solution(3866497548231657783)
XLA Ops:
  0.6 0.0 copy-start
  0.6 0.8 %copy-done = bf16[1280,16]{0,1:T(8,128)(2,1)S(1)} copy-done((bf16[1280,16]{0,1:T(8,128)(2,1)S(1)}, bf16[1280,16]{0,1:T(8,128)(2,1)}, u32[]{:S(2)}) %copy-start) | copy-done | bytes 40984
  1.4 3.2 %gather_slots.1 = (bf16[128,1280]{1,0:T(8,128)(2,1)S(1)}, f32[4,16,256]{2,1,0:T(8,128)S(1)}, f32[4,16,256]{2,1,0:T(8,128)S(1)}, bf16[1280,256]{1,0:T(8,128)(2,1)S(1)}, bf16[256,1280]{1,0:T(8,128)(2,1)S(1)}) custom-call(bf16[4,256,1280]{2,1,0:T(8,128)(2,1)} %tokens.5, bf16[16,1280]{1,0:T(8,128)(2,1)S(1)} %bitcast.16, bf16[4,256,1280]{2,1,0:T(8,128)(2,1)} %grads.3, ...), custom_call_target="tpu_custom_call" | custom-call | flops 125829120 | bytes 5242880 | tf_op jit(solution)/shard_map/gather_slots/pallas_call | solution.py:148
  4.6 18.3 %all_to_all.22 = bf16[16,8,1280]{2,1,0:T(8,128)(2,1)S(1)} all-to-all(bf16[16,8,1280]{2,1,0:T(8,128)(2,1)S(1)} %bitcast.15), channel_id=1, replica_groups=mesh['rep'=2,'exp'=16] {'exp'}, dimensions={0} | all-to-all | bytes 655360 | tf_op jit(solution)/shard_map/all_to_all | solution.py:512
  22.9 1.5 %collective-permute-start = (bf16[128,1280]{1,0:T(8,128)(2,1)S(1)}, bf16[128,1280]{1,0:T(8,128)(2,1)S(1)}, u32[]{:S(2)}, u32[]{:S(2)}) collective-permute-start(bf16[128,1280]{1,0:T(8,128)(2,1)S(1)} %bitcast.12), channel_id=1, source_target_pairs={{0,16},{16,0},{1,17},{17,1},{2,18},{18,2},{3,19},{19,3},{4,20},{20... | collective-permute-start | bytes 983048 | tf_op jit(solution)/shard_map/ppermute | solution.py:523
  24.4 9.2 %expert_rows.1 = (bf16[128,1280]{1,0:T(8,128)(2,1)}, bf16[64,2560]{1,0:T(8,128)(2,1)S(1)}, bf16[64,2560]{1,0:T(8,128)(2,1)S(1)}, f32[8,128]{1,0:T(8,128)S(1)}) custom-call(bf16[128,1280]{1,0:T(8,128)(2,1)S(1)} %bitcast.13, bf16[1280,256]{1,0:T(8,128)(2,1)S(1)} %get-tuple-element.27.first_in, bf16[256,1280]{1,0:T(8,128)(2,1)S(1)} %get-tuple-element.28.first_out, ...), custom_call_target="tpu_custom_call" | custom-call | flops 1677721600 | bytes 13107200 | tf_op jit(solution)/shard_map/expert_rows/pallas_call | solution.py:248
  33.6 3.7 %all-to-all-start.1 = ((bf16[16,8,1280]{2,1,0:T(8,128)(2,1)}), bf16[16,8,1280]{2,1,0:T(8,128)(2,1)S(1)}, u32[]{:S(2)}, u32[]{:S(2)}) async-start(bf16[16,8,1280]{2,1,0:T(8,128)(2,1)} %bitcast.6), calls=%async_computation.1 | async-start | bytes 655360 | tf_op jit(solution)/shard_map/all_to_all | solution.py:512
  37.3 0.0 collective-permute-done.other_rows
  37.3 0.0 copy-start.1
  37.3 8.8 %replica_grads.1 = (bf16[640,2560]{1,0:T(8,128)(2,1)}, bf16[1280,1280]{1,0:T(8,128)(2,1)}, bf16[2,256,1280]{2,1,0:T(8,128)(2,1)S(1)}, f32[8,128]{1,0:T(8,128)S(1)}) custom-call(s32[1]{0:T(128)} %bitcast.mine, f32[8,128]{1,0:T(8,128)S(1)} %get-tuple-element.29.after, bf16[128,1280]{1,0:T(8,128)(2,1)S(1)} %bitcast.14, ...), custom_call_target="tpu_custom_call" | custom-call | flops 13421772800 | bytes 104857600 | tf_op jit(solution)/shard_map/replica_grads/pallas_call | solution.py:340
  46.2 2.0 %all-to-all-done.1 = bf16[16,8,1280]{2,1,0:T(8,128)(2,1)S(1)} async-done(((bf16[16,8,1280]{2,1,0:T(8,128)(2,1)}), bf16[16,8,1280]{2,1,0:T(8,128)(2,1)S(1)}, u32[]{:S(2)}, u32[]{:S(2)}) %all-to-all-start.1) | async-done | bytes 327712 | tf_op jit(solution)/shard_map/all_to_all | solution.py:512
  48.2 0.0 copy-done.1
  48.2 3.2 %logits_grads.1 = (bf16[4,32,256]{2,1,0:T(8,128)(2,1)S(1)}, bf16[4,32,1280]{2,1,0:T(8,128)(2,1)S(1)}, bf16[16,1280]{1,0:T(8,128)(2,1)S(1)}, f32[8,128]{1,0:T(8,128)S(1)}) custom-call(f32[8,128]{1,0:T(8,128)S(1)} %get-tuple-element.32.after, bf16[128,1280]{1,0:T(8,128)(2,1)S(1)} %bitcast.11, bf16[4,256,1280]{2,1,0:T(8,128)(2,1)} %tokens.5, ...), custom_call_target="tpu_custom_call" | custom-call | flops 125829120 | bytes 5242880 | tf_op jit(solution)/shard_map/logits_grads/pallas_call | solution.py:430
  51.4 0.1 collective-permute-start.1
  51.5 0.8 %collective-permute-start.2 = (bf16[16,1280]{1,0:T(8,128)(2,1)S(1)}, bf16[16,1280]{1,0:T(8,128)(2,1)S(1)}, u32[]{:S(2)}, u32[]{:S(2)}) collective-permute-start(bf16[16,1280]{1,0:T(8,128)(2,1)S(1)} %get-tuple-element.38.refs_0_), channel_id=1, source_target_pairs={{0,2},{1,3},{2,0},{3,1},{4,6},{5,7},{6,4},{7,5},{8,10},{9,11},{10,... | collective-permute-start | bytes 122888 | tf_op jit(solution)/shard_map/ppermute | solution.py:506
  52.3 1.1 %collective-permute-start.3 = (bf16[16,1280]{1,0:T(8,128)(2,1)S(1)}, bf16[16,1280]{1,0:T(8,128)(2,1)S(1)}, u32[]{:S(2)}, u32[]{:S(2)}) collective-permute-start(bf16[16,1280]{1,0:T(8,128)(2,1)S(1)} %get-tuple-element.38.refs_0_), channel_id=1, source_target_pairs={{0,3},{1,2},{2,1},{3,0},{4,7},{5,6},{6,5},{7,4},{8,11},{9,10},{10,... | collective-permute-start | bytes 122888 | tf_op jit(solution)/shard_map/ppermute | solution.py:506
  53.4 0.5 collective-permute-start.4
  53.9 1.2 %collective-permute-start.5 = (bf16[16,1280]{1,0:T(8,128)(2,1)S(1)}, bf16[16,1280]{1,0:T(8,128)(2,1)S(1)}, u32[]{:S(2)}, u32[]{:S(2)}) collective-permute-start(bf16[16,1280]{1,0:T(8,128)(2,1)S(1)} %get-tuple-element.38.refs_0_), channel_id=1, source_target_pairs={{0,17},{1,16},{2,19},{3,18},{4,21},{5,20},{6,23},{7,22},{8,25},{9,... | collective-permute-start | bytes 122888 | tf_op jit(solution)/shard_map/ppermute | solution.py:506
  55.1 0.0 collective-permute-done.1.refs_1_
  55.1 0.7 collective-permute-start.6
  55.8 0.1 collective-permute-done.2.refs_2_
  55.9 1.9 %collective-permute-start.7 = (bf16[16,1280]{1,0:T(8,128)(2,1)S(1)}, bf16[16,1280]{1,0:T(8,128)(2,1)S(1)}, u32[]{:S(2)}, u32[]{:S(2)}) collective-permute-start(bf16[16,1280]{1,0:T(8,128)(2,1)S(1)} %get-tuple-element.38.refs_0_), channel_id=1, source_target_pairs={{0,19},{1,18},{2,17},{3,16},{4,23},{5,22},{6,21},{7,20},{8,27},{9,... | collective-permute-start | bytes 122888 | tf_op jit(solution)/shard_map/ppermute | solution.py:506
  57.8 0.0 collective-permute-done.3.refs_3_
  57.8 0.0 collective-permute-done.4.refs_4_
  57.8 0.0 collective-permute-done.5.refs_5_
  57.8 2.4 %collective-permute-done.6.refs_6_ = bf16[16,1280]{1,0:T(8,128)(2,1)S(1)} collective-permute-done((bf16[16,1280]{1,0:T(8,128)(2,1)S(1)}, bf16[16,1280]{1,0:T(8,128)(2,1)S(1)}, u32[]{:S(2)}, u32[]{:S(2)}) %collective-permute-start.6) | collective-permute-done | bytes 40992 | tf_op jit(solution)/shard_map/ppermute | solution.py:506
  60.2 0.5 collective-permute-done.7.refs_7_
  60.7 2.0 %collective-permute-start.10 = (bf16[16,1280]{1,0:T(8,128)(2,1)S(1)}, bf16[16,1280]{1,0:T(8,128)(2,1)S(1)}, u32[]{:S(2)}, u32[]{:S(2)}) collective-permute-start(bf16[16,1280]{1,0:T(8,128)(2,1)S(1)} %get-tuple-element.44.refs_0_), channel_id=1, source_target_pairs={{0,12},{1,13},{2,14},{3,15},{4,8},{5,9},{6,10},{7,11},{8,4},{9,5},... | collective-permute-start | bytes 122888 | tf_op jit(solution)/shard_map/ppermute | solution.py:506
  62.7 0.0 collective-permute-start.8
  62.7 2.4 %collective-permute-start.9 = (bf16[16,1280]{1,0:T(8,128)(2,1)S(1)}, bf16[16,1280]{1,0:T(8,128)(2,1)S(1)}, u32[]{:S(2)}, u32[]{:S(2)}) collective-permute-start(bf16[16,1280]{1,0:T(8,128)(2,1)S(1)} %get-tuple-element.44.refs_0_), channel_id=1, source_target_pairs={{0,8},{1,9},{2,10},{3,11},{4,12},{5,13},{6,14},{7,15},{8,0},{9,1},... | collective-permute-start | bytes 122888 | tf_op jit(solution)/shard_map/ppermute | solution.py:506
  65.2 2.7 %tokens_grads.1 = (bf16[4,256,1280]{2,1,0:T(8,128)(2,1)}, f32[8,128]{1,0:T(8,128)S(1)}) custom-call(f32[8,128]{1,0:T(8,128)S(1)} %get-tuple-element.39.after, bf16[4,32,256]{2,1,0:T(8,128)(2,1)S(1)} %get-tuple-element.40.left, bf16[4,32,1280]{2,1,0:T(8,128)(2,1)S(1)} %get-tuple-element.41.right), custom_call_target="tpu_custom_call" | custom-call | flops 83886080 | bytes 2621440 | tf_op jit(solution)/shard_map/tokens_grads/pallas_call | solution.py:461
  67.9 0.0 collective-permute-done.10.refs_3_
  67.9 0.0 collective-permute-done.8.refs_1_
  67.9 0.2 collective-permute-done.9.refs_2_
  68.1 0.7 add_terms.3
  (1 shorter events, 0.0 us)
Async XLA Ops:
  0.6 0.8 %copy-start = (bf16[1280,16]{0,1:T(8,128)(2,1)S(1)}, bf16[1280,16]{0,1:T(8,128)(2,1)}, u32[]{:S(2)}) copy-start(bf16[1280,16]{0,1:T(8,128)(2,1)} %param.6) | copy-start | bytes 122884
  22.9 14.4 %collective-permute-start = (bf16[128,1280]{1,0:T(8,128)(2,1)S(1)}, bf16[128,1280]{1,0:T(8,128)(2,1)S(1)}, u32[]{:S(2)}, u32[]{:S(2)}) collective-permute-start(bf16[128,1280]{1,0:T(8,128)(2,1)S(1)} %bitcast.12), channel_id=1, source_target_pairs={{0,16},{16,0},{1,17},{17,1},{2,18},{18,2},{3,19},{19,3},{4,20},{20... | collective-permute-start | bytes 983048 | tf_op jit(solution)/shard_map/ppermute | solution.py:523
  33.6 14.6 %all-to-all-start.1 = ((bf16[16,8,1280]{2,1,0:T(8,128)(2,1)}), bf16[16,8,1280]{2,1,0:T(8,128)(2,1)S(1)}, u32[]{:S(2)}, u32[]{:S(2)}) async-start(bf16[16,8,1280]{2,1,0:T(8,128)(2,1)} %bitcast.6), calls=%async_computation.1 | async-start | bytes 655360 | tf_op jit(solution)/shard_map/all_to_all | solution.py:512
  37.3 10.9 %copy-start.1 = (bf16[1280,16]{0,1:T(8,128)(2,1)S(1)}, bf16[1280,16]{0,1:T(8,128)(2,1)}, u32[]{:S(2)}) copy-start(bf16[1280,16]{0,1:T(8,128)(2,1)} %param.6) | copy-start | bytes 122884
  51.4 3.6 %collective-permute-start.1 = (bf16[16,1280]{1,0:T(8,128)(2,1)S(1)}, bf16[16,1280]{1,0:T(8,128)(2,1)S(1)}, u32[]{:S(2)}, u32[]{:S(2)}) collective-permute-start(bf16[16,1280]{1,0:T(8,128)(2,1)S(1)} %get-tuple-element.38.refs_0_), channel_id=1, source_target_pairs={{0,1},{1,0},{2,3},{3,2},{4,5},{5,4},{6,7},{7,6},{8,9},{9,8},{10,11... | collective-permute-start | bytes 122888 | tf_op jit(solution)/shard_map/ppermute | solution.py:506
  51.5 4.4 %collective-permute-start.2 = (bf16[16,1280]{1,0:T(8,128)(2,1)S(1)}, bf16[16,1280]{1,0:T(8,128)(2,1)S(1)}, u32[]{:S(2)}, u32[]{:S(2)}) collective-permute-start(bf16[16,1280]{1,0:T(8,128)(2,1)S(1)} %get-tuple-element.38.refs_0_), channel_id=1, source_target_pairs={{0,2},{1,3},{2,0},{3,1},{4,6},{5,7},{6,4},{7,5},{8,10},{9,11},{10,... | collective-permute-start | bytes 122888 | tf_op jit(solution)/shard_map/ppermute | solution.py:506
  52.3 5.5 %collective-permute-start.3 = (bf16[16,1280]{1,0:T(8,128)(2,1)S(1)}, bf16[16,1280]{1,0:T(8,128)(2,1)S(1)}, u32[]{:S(2)}, u32[]{:S(2)}) collective-permute-start(bf16[16,1280]{1,0:T(8,128)(2,1)S(1)} %get-tuple-element.38.refs_0_), channel_id=1, source_target_pairs={{0,3},{1,2},{2,1},{3,0},{4,7},{5,6},{6,5},{7,4},{8,11},{9,10},{10,... | collective-permute-start | bytes 122888 | tf_op jit(solution)/shard_map/ppermute | solution.py:506
  53.4 4.4 %collective-permute-start.4 = (bf16[16,1280]{1,0:T(8,128)(2,1)S(1)}, bf16[16,1280]{1,0:T(8,128)(2,1)S(1)}, u32[]{:S(2)}, u32[]{:S(2)}) collective-permute-start(bf16[16,1280]{1,0:T(8,128)(2,1)S(1)} %get-tuple-element.38.refs_0_), channel_id=1, source_target_pairs={{0,16},{1,17},{2,18},{3,19},{4,20},{5,21},{6,22},{7,23},{8,24},{9,... | collective-permute-start | bytes 122888 | tf_op jit(solution)/shard_map/ppermute | solution.py:506
  53.9 3.9 %collective-permute-start.5 = (bf16[16,1280]{1,0:T(8,128)(2,1)S(1)}, bf16[16,1280]{1,0:T(8,128)(2,1)S(1)}, u32[]{:S(2)}, u32[]{:S(2)}) collective-permute-start(bf16[16,1280]{1,0:T(8,128)(2,1)S(1)} %get-tuple-element.38.refs_0_), channel_id=1, source_target_pairs={{0,17},{1,16},{2,19},{3,18},{4,21},{5,20},{6,23},{7,22},{8,25},{9,... | collective-permute-start | bytes 122888 | tf_op jit(solution)/shard_map/ppermute | solution.py:506
  55.1 5.1 %collective-permute-start.6 = (bf16[16,1280]{1,0:T(8,128)(2,1)S(1)}, bf16[16,1280]{1,0:T(8,128)(2,1)S(1)}, u32[]{:S(2)}, u32[]{:S(2)}) collective-permute-start(bf16[16,1280]{1,0:T(8,128)(2,1)S(1)} %get-tuple-element.38.refs_0_), channel_id=1, source_target_pairs={{0,18},{1,19},{2,16},{3,17},{4,22},{5,23},{6,20},{7,21},{8,26},{9,... | collective-permute-start | bytes 122888 | tf_op jit(solution)/shard_map/ppermute | solution.py:506
  55.9 4.8 %collective-permute-start.7 = (bf16[16,1280]{1,0:T(8,128)(2,1)S(1)}, bf16[16,1280]{1,0:T(8,128)(2,1)S(1)}, u32[]{:S(2)}, u32[]{:S(2)}) collective-permute-start(bf16[16,1280]{1,0:T(8,128)(2,1)S(1)} %get-tuple-element.38.refs_0_), channel_id=1, source_target_pairs={{0,19},{1,18},{2,17},{3,16},{4,23},{5,22},{6,21},{7,20},{8,27},{9,... | collective-permute-start | bytes 122888 | tf_op jit(solution)/shard_map/ppermute | solution.py:506
  60.7 7.2 %collective-permute-start.10 = (bf16[16,1280]{1,0:T(8,128)(2,1)S(1)}, bf16[16,1280]{1,0:T(8,128)(2,1)S(1)}, u32[]{:S(2)}, u32[]{:S(2)}) collective-permute-start(bf16[16,1280]{1,0:T(8,128)(2,1)S(1)} %get-tuple-element.44.refs_0_), channel_id=1, source_target_pairs={{0,12},{1,13},{2,14},{3,15},{4,8},{5,9},{6,10},{7,11},{8,4},{9,5},... | collective-permute-start | bytes 122888 | tf_op jit(solution)/shard_map/ppermute | solution.py:506
  62.7 5.2 %collective-permute-start.8 = (bf16[16,1280]{1,0:T(8,128)(2,1)S(1)}, bf16[16,1280]{1,0:T(8,128)(2,1)S(1)}, u32[]{:S(2)}, u32[]{:S(2)}) collective-permute-start(bf16[16,1280]{1,0:T(8,128)(2,1)S(1)} %get-tuple-element.44.refs_0_), channel_id=1, source_target_pairs={{0,4},{1,5},{2,6},{3,7},{4,0},{5,1},{6,2},{7,3},{8,12},{9,13},{10,... | collective-permute-start | bytes 122888 | tf_op jit(solution)/shard_map/ppermute | solution.py:506
  62.7 5.3 %collective-permute-start.9 = (bf16[16,1280]{1,0:T(8,128)(2,1)S(1)}, bf16[16,1280]{1,0:T(8,128)(2,1)S(1)}, u32[]{:S(2)}, u32[]{:S(2)}) collective-permute-start(bf16[16,1280]{1,0:T(8,128)(2,1)S(1)} %get-tuple-element.44.refs_0_), channel_id=1, source_target_pairs={{0,8},{1,9},{2,10},{3,11},{4,12},{5,13},{6,14},{7,15},{8,0},{9,1},... | collective-permute-start | bytes 122888 | tf_op jit(solution)/shard_map/ppermute | solution.py:506

commit v20 on v18

--- a/solution.py
+++ b/solution.py
@@ -246,9 +246,8 @@
     kept = shaped((count, hidden), LOW)
     start = first_out.shape[0]
     chunks = [
-        *chunks_of(start, start + tile // 2, tile),
-        *chunks_of(start + tile // 2, hidden - tile // 2, tile),
-        *chunks_of(hidden - tile // 2, hidden, tile),
+        slice(start, start + tile),
+        *chunks_of(start + tile, hidden, tile + tile // 2),
     ]
     return call(
         functools.partial(expert_kernel, chunks),

time: 69.4 us -> 69.5 us (level)
  transfers between devices with their start and end apart: 12 -> 12, of which waited for: 5 -> 5; matrix products, arithmetic and copies ran while one was open for 0% -> 0% of each run, Pallas kernels for 30% -> 31%
where the time goes in v20:
time: 69.5 us; the launch traced here: 69.1 us
  Pallas kernels  28.3 us (41%)
  blocking collectives  18.3 us (26%)
  starting transfers between devices  15.9 us (23%)
  waiting for transfers between devices  5.21 us (7%)
  local copies, waits for them, and re-layouts  0.78 us (1%)
  between operations  0.72 us (1%)
    all_to_all x1, blocking collectives, exchange(): return lax.all_to_all(rows, axes, split_axis=0, concat_axis=0, tiled=True)  18.3 us
    ppermute x10, starting transfers between devices, terms_of_group(): lax.ppermute(array, axes, [(i, i ^ distance) for i in range(count)])  10.6 us
    pallas_call x1, Pallas kernels, expert(): call(functools.partial(expert_kernel, chunks), 'expert_rows', ROOMY, 8 *...  9.57 us
    pallas_call x1, Pallas kernels, replica_grads(): call(functools.partial(replica_kernel, chunks), 'replica_grads', ROOMY, 6...  8.83 us
    all_to_all x1, starting transfers between devices, exchange(): return lax.all_to_all(rows, axes, split_axis=0, concat_axis=0, tiled=True)  3.74 us
    pallas_call x1, Pallas kernels, logits_grads(): call(logits_kernel, 'logits_grads', ROOMY, 6 * images * slots * length *...  3.22 us
    pallas_call x1, Pallas kernels, gather(): call(gather_kernel, 'gather_slots', ROOMY, 6 * images * slots * length *...  3.2 us
    ppermute x10, waiting for transfers between devices, terms_of_group(): lax.ppermute(array, axes, [(i, i ^ distance) for i in range(count)])  3.18 us
  transfers between devices with their start and end apart: 12, of which 5 were waited for; matrix products, arithmetic and copies ran while one was open for 0% of the time, Pallas kernels for 31%

profile of v20, /device:TPU:0, one launch (start us, length us, event | category | flops | bytes accessed | tf_op | source)
XLA Modules:
  0.0 69.1 jit_solution(17694946508443848749)
XLA Ops:
  0.6 0.0 copy-start
  0.6 0.8 %copy-done = bf16[1280,16]{0,1:T(8,128)(2,1)S(1)} copy-done((bf16[1280,16]{0,1:T(8,128)(2,1)S(1)}, bf16[1280,16]{0,1:T(8,128)(2,1)}, u32[]{:S(2)}) %copy-start) | copy-done | bytes 40984
  1.4 3.2 %gather_slots.1 = (bf16[128,1280]{1,0:T(8,128)(2,1)S(1)}, f32[4,16,256]{2,1,0:T(8,128)S(1)}, f32[4,16,256]{2,1,0:T(8,128)S(1)}, bf16[1280,256]{1,0:T(8,128)(2,1)S(1)}, bf16[256,1280]{1,0:T(8,128)(2,1)S(1)}) custom-call(bf16[4,256,1280]{2,1,0:T(8,128)(2,1)} %tokens.5, bf16[16,1280]{1,0:T(8,128)(2,1)S(1)} %bitcast.16, bf16[4,256,1280]{2,1,0:T(8,128)(2,1)} %grads.3, ...), custom_call_target="tpu_custom_call" | custom-call | flops 125829120 | bytes 5242880 | tf_op jit(solution)/shard_map/gather_slots/pallas_call | solution.py:148
  4.6 18.3 %all_to_all.22 = bf16[16,8,1280]{2,1,0:T(8,128)(2,1)S(1)} all-to-all(bf16[16,8,1280]{2,1,0:T(8,128)(2,1)S(1)} %bitcast.15), channel_id=1, replica_groups=mesh['rep'=2,'exp'=16] {'exp'}, dimensions={0} | all-to-all | bytes 655360 | tf_op jit(solution)/shard_map/all_to_all | solution.py:516
  22.9 1.5 %collective-permute-start = (bf16[128,1280]{1,0:T(8,128)(2,1)S(1)}, bf16[128,1280]{1,0:T(8,128)(2,1)S(1)}, u32[]{:S(2)}, u32[]{:S(2)}) collective-permute-start(bf16[128,1280]{1,0:T(8,128)(2,1)S(1)} %bitcast.12), channel_id=1, source_target_pairs={{0,16},{16,0},{1,17},{17,1},{2,18},{18,2},{3,19},{19,3},{4,20},{20... | collective-permute-start | bytes 983048 | tf_op jit(solution)/shard_map/ppermute | solution.py:527
  24.4 9.6 %expert_rows.1 = (bf16[128,1280]{1,0:T(8,128)(2,1)}, bf16[64,2560]{1,0:T(8,128)(2,1)S(1)}, bf16[64,2560]{1,0:T(8,128)(2,1)S(1)}, f32[8,128]{1,0:T(8,128)S(1)}) custom-call(bf16[128,1280]{1,0:T(8,128)(2,1)S(1)} %bitcast.13, bf16[1280,256]{1,0:T(8,128)(2,1)S(1)} %get-tuple-element.27.first_in, bf16[256,1280]{1,0:T(8,128)(2,1)S(1)} %get-tuple-element.28.first_out, ...), custom_call_target="tpu_custom_call" | custom-call | flops 1677721600 | bytes 13107200 | tf_op jit(solution)/shard_map/expert_rows/pallas_call | solution.py:252
  34.0 3.7 %all-to-all-start.1 = ((bf16[16,8,1280]{2,1,0:T(8,128)(2,1)}), bf16[16,8,1280]{2,1,0:T(8,128)(2,1)S(1)}, u32[]{:S(2)}, u32[]{:S(2)}) async-start(bf16[16,8,1280]{2,1,0:T(8,128)(2,1)} %bitcast.6), calls=%async_computation.1 | async-start | bytes 655360 | tf_op jit(solution)/shard_map/all_to_all | solution.py:516
  37.7 0.0 collective-permute-done.other_rows
  37.7 0.0 copy-start.1
  37.7 8.8 %replica_grads.1 = (bf16[640,2560]{1,0:T(8,128)(2,1)}, bf16[1280,1280]{1,0:T(8,128)(2,1)}, bf16[2,256,1280]{2,1,0:T(8,128)(2,1)S(1)}, f32[8,128]{1,0:T(8,128)S(1)}) custom-call(s32[1]{0:T(128)} %bitcast.mine, f32[8,128]{1,0:T(8,128)S(1)} %get-tuple-element.29.after, bf16[128,1280]{1,0:T(8,128)(2,1)S(1)} %bitcast.14, ...), custom_call_target="tpu_custom_call" | custom-call | flops 13421772800 | bytes 104857600 | tf_op jit(solution)/shard_map/replica_grads/pallas_call | solution.py:344
  46.6 2.0 %all-to-all-done.1 = bf16[16,8,1280]{2,1,0:T(8,128)(2,1)S(1)} async-done(((bf16[16,8,1280]{2,1,0:T(8,128)(2,1)}), bf16[16,8,1280]{2,1,0:T(8,128)(2,1)S(1)}, u32[]{:S(2)}, u32[]{:S(2)}) %all-to-all-start.1) | async-done | bytes 327712 | tf_op jit(solution)/shard_map/all_to_all | solution.py:516
  48.6 0.0 copy-done.1
  48.6 3.2 %logits_grads.1 = (bf16[4,32,256]{2,1,0:T(8,128)(2,1)S(1)}, bf16[4,32,1280]{2,1,0:T(8,128)(2,1)S(1)}, bf16[16,1280]{1,0:T(8,128)(2,1)S(1)}, f32[8,128]{1,0:T(8,128)S(1)}) custom-call(f32[8,128]{1,0:T(8,128)S(1)} %get-tuple-element.32.after, bf16[128,1280]{1,0:T(8,128)(2,1)S(1)} %bitcast.11, bf16[4,256,1280]{2,1,0:T(8,128)(2,1)} %tokens.5, ...), custom_call_target="tpu_custom_call" | custom-call | flops 125829120 | bytes 5242880 | tf_op jit(solution)/shard_map/logits_grads/pallas_call | solution.py:434
  51.8 0.1 collective-permute-start.1
  51.9 0.8 %collective-permute-start.2 = (bf16[16,1280]{1,0:T(8,128)(2,1)S(1)}, bf16[16,1280]{1,0:T(8,128)(2,1)S(1)}, u32[]{:S(2)}, u32[]{:S(2)}) collective-permute-start(bf16[16,1280]{1,0:T(8,128)(2,1)S(1)} %get-tuple-element.38.refs_0_), channel_id=1, source_target_pairs={{0,2},{1,3},{2,0},{3,1},{4,6},{5,7},{6,4},{7,5},{8,10},{9,11},{10,... | collective-permute-start | bytes 122888 | tf_op jit(solution)/shard_map/ppermute | solution.py:510
  52.7 1.1 %collective-permute-start.3 = (bf16[16,1280]{1,0:T(8,128)(2,1)S(1)}, bf16[16,1280]{1,0:T(8,128)(2,1)S(1)}, u32[]{:S(2)}, u32[]{:S(2)}) collective-permute-start(bf16[16,1280]{1,0:T(8,128)(2,1)S(1)} %get-tuple-element.38.refs_0_), channel_id=1, source_target_pairs={{0,3},{1,2},{2,1},{3,0},{4,7},{5,6},{6,5},{7,4},{8,11},{9,10},{10,... | collective-permute-start | bytes 122888 | tf_op jit(solution)/shard_map/ppermute | solution.py:510
  53.8 0.5 collective-permute-start.4
  54.3 1.2 %collective-permute-start.5 = (bf16[16,1280]{1,0:T(8,128)(2,1)S(1)}, bf16[16,1280]{1,0:T(8,128)(2,1)S(1)}, u32[]{:S(2)}, u32[]{:S(2)}) collective-permute-start(bf16[16,1280]{1,0:T(8,128)(2,1)S(1)} %get-tuple-element.38.refs_0_), channel_id=1, source_target_pairs={{0,17},{1,16},{2,19},{3,18},{4,21},{5,20},{6,23},{7,22},{8,25},{9,... | collective-permute-start | bytes 122888 | tf_op jit(solution)/shard_map/ppermute | solution.py:510
  55.5 0.0 collective-permute-done.1.refs_1_
  55.5 0.7 collective-permute-start.6
  56.2 0.1 collective-permute-done.2.refs_2_
  56.3 1.9 %collective-permute-start.7 = (bf16[16,1280]{1,0:T(8,128)(2,1)S(1)}, bf16[16,1280]{1,0:T(8,128)(2,1)S(1)}, u32[]{:S(2)}, u32[]{:S(2)}) collective-permute-start(bf16[16,1280]{1,0:T(8,128)(2,1)S(1)} %get-tuple-element.38.refs_0_), channel_id=1, source_target_pairs={{0,19},{1,18},{2,17},{3,16},{4,23},{5,22},{6,21},{7,20},{8,27},{9,... | collective-permute-start | bytes 122888 | tf_op jit(solution)/shard_map/ppermute | solution.py:510
  58.2 0.0 collective-permute-done.3.refs_3_
  58.2 0.0 collective-permute-done.4.refs_4_
  58.2 0.0 collective-permute-done.5.refs_5_
  58.2 2.4 %collective-permute-done.6.refs_6_ = bf16[16,1280]{1,0:T(8,128)(2,1)S(1)} collective-permute-done((bf16[16,1280]{1,0:T(8,128)(2,1)S(1)}, bf16[16,1280]{1,0:T(8,128)(2,1)S(1)}, u32[]{:S(2)}, u32[]{:S(2)}) %collective-permute-start.6) | collective-permute-done | bytes 40992 | tf_op jit(solution)/shard_map/ppermute | solution.py:510
  60.6 0.5 collective-permute-done.7.refs_7_
  61.1 2.0 %collective-permute-start.10 = (bf16[16,1280]{1,0:T(8,128)(2,1)S(1)}, bf16[16,1280]{1,0:T(8,128)(2,1)S(1)}, u32[]{:S(2)}, u32[]{:S(2)}) collective-permute-start(bf16[16,1280]{1,0:T(8,128)(2,1)S(1)} %get-tuple-element.44.refs_0_), channel_id=1, source_target_pairs={{0,12},{1,13},{2,14},{3,15},{4,8},{5,9},{6,10},{7,11},{8,4},{9,5},... | collective-permute-start | bytes 122888 | tf_op jit(solution)/shard_map/ppermute | solution.py:510
  63.1 0.0 collective-permute-start.8
  63.1 2.4 %collective-permute-start.9 = (bf16[16,1280]{1,0:T(8,128)(2,1)S(1)}, bf16[16,1280]{1,0:T(8,128)(2,1)S(1)}, u32[]{:S(2)}, u32[]{:S(2)}) collective-permute-start(bf16[16,1280]{1,0:T(8,128)(2,1)S(1)} %get-tuple-element.44.refs_0_), channel_id=1, source_target_pairs={{0,8},{1,9},{2,10},{3,11},{4,12},{5,13},{6,14},{7,15},{8,0},{9,1},... | collective-permute-start | bytes 122888 | tf_op jit(solution)/shard_map/ppermute | solution.py:510
  65.6 2.7 %tokens_grads.1 = (bf16[4,256,1280]{2,1,0:T(8,128)(2,1)}, f32[8,128]{1,0:T(8,128)S(1)}) custom-call(f32[8,128]{1,0:T(8,128)S(1)} %get-tuple-element.39.after, bf16[4,32,256]{2,1,0:T(8,128)(2,1)S(1)} %get-tuple-element.40.left, bf16[4,32,1280]{2,1,0:T(8,128)(2,1)S(1)} %get-tuple-element.41.right), custom_call_target="tpu_custom_call" | custom-call | flops 83886080 | bytes 2621440 | tf_op jit(solution)/shard_map/tokens_grads/pallas_call | solution.py:465
  68.3 0.0 collective-permute-done.10.refs_3_
  68.3 0.0 collective-permute-done.8.refs_1_
  68.3 0.2 collective-permute-done.9.refs_2_
  68.5 0.7 add_terms.3
  (1 shorter events, 0.0 us)
Async XLA Ops:
  0.6 0.8 %copy-start = (bf16[1280,16]{0,1:T(8,128)(2,1)S(1)}, bf16[1280,16]{0,1:T(8,128)(2,1)}, u32[]{:S(2)}) copy-start(bf16[1280,16]{0,1:T(8,128)(2,1)} %param.6) | copy-start | bytes 122884
  22.9 14.8 %collective-permute-start = (bf16[128,1280]{1,0:T(8,128)(2,1)S(1)}, bf16[128,1280]{1,0:T(8,128)(2,1)S(1)}, u32[]{:S(2)}, u32[]{:S(2)}) collective-permute-start(bf16[128,1280]{1,0:T(8,128)(2,1)S(1)} %bitcast.12), channel_id=1, source_target_pairs={{0,16},{16,0},{1,17},{17,1},{2,18},{18,2},{3,19},{19,3},{4,20},{20... | collective-permute-start | bytes 983048 | tf_op jit(solution)/shard_map/ppermute | solution.py:527
  34.0 14.6 %all-to-all-start.1 = ((bf16[16,8,1280]{2,1,0:T(8,128)(2,1)}), bf16[16,8,1280]{2,1,0:T(8,128)(2,1)S(1)}, u32[]{:S(2)}, u32[]{:S(2)}) async-start(bf16[16,8,1280]{2,1,0:T(8,128)(2,1)} %bitcast.6), calls=%async_computation.1 | async-start | bytes 655360 | tf_op jit(solution)/shard_map/all_to_all | solution.py:516
  37.7 10.9 %copy-start.1 = (bf16[1280,16]{0,1:T(8,128)(2,1)S(1)}, bf16[1280,16]{0,1:T(8,128)(2,1)}, u32[]{:S(2)}) copy-start(bf16[1280,16]{0,1:T(8,128)(2,1)} %param.6) | copy-start | bytes 122884
  51.8 3.6 %collective-permute-start.1 = (bf16[16,1280]{1,0:T(8,128)(2,1)S(1)}, bf16[16,1280]{1,0:T(8,128)(2,1)S(1)}, u32[]{:S(2)}, u32[]{:S(2)}) collective-permute-start(bf16[16,1280]{1,0:T(8,128)(2,1)S(1)} %get-tuple-element.38.refs_0_), channel_id=1, source_target_pairs={{0,1},{1,0},{2,3},{3,2},{4,5},{5,4},{6,7},{7,6},{8,9},{9,8},{10,11... | collective-permute-start | bytes 122888 | tf_op jit(solution)/shard_map/ppermute | solution.py:510
  51.9 4.4 %collective-permute-start.2 = (bf16[16,1280]{1,0:T(8,128)(2,1)S(1)}, bf16[16,1280]{1,0:T(8,128)(2,1)S(1)}, u32[]{:S(2)}, u32[]{:S(2)}) collective-permute-start(bf16[16,1280]{1,0:T(8,128)(2,1)S(1)} %get-tuple-element.38.refs_0_), channel_id=1, source_target_pairs={{0,2},{1,3},{2,0},{3,1},{4,6},{5,7},{6,4},{7,5},{8,10},{9,11},{10,... | collective-permute-start | bytes 122888 | tf_op jit(solution)/shard_map/ppermute | solution.py:510
  52.7 5.5 %collective-permute-start.3 = (bf16[16,1280]{1,0:T(8,128)(2,1)S(1)}, bf16[16,1280]{1,0:T(8,128)(2,1)S(1)}, u32[]{:S(2)}, u32[]{:S(2)}) collective-permute-start(bf16[16,1280]{1,0:T(8,128)(2,1)S(1)} %get-tuple-element.38.refs_0_), channel_id=1, source_target_pairs={{0,3},{1,2},{2,1},{3,0},{4,7},{5,6},{6,5},{7,4},{8,11},{9,10},{10,... | collective-permute-start | bytes 122888 | tf_op jit(solution)/shard_map/ppermute | solution.py:510
  53.8 4.4 %collective-permute-start.4 = (bf16[16,1280]{1,0:T(8,128)(2,1)S(1)}, bf16[16,1280]{1,0:T(8,128)(2,1)S(1)}, u32[]{:S(2)}, u32[]{:S(2)}) collective-permute-start(bf16[16,1280]{1,0:T(8,128)(2,1)S(1)} %get-tuple-element.38.refs_0_), channel_id=1, source_target_pairs={{0,16},{1,17},{2,18},{3,19},{4,20},{5,21},{6,22},{7,23},{8,24},{9,... | collective-permute-start | bytes 122888 | tf_op jit(solution)/shard_map/ppermute | solution.py:510
  54.3 3.9 %collective-permute-start.5 = (bf16[16,1280]{1,0:T(8,128)(2,1)S(1)}, bf16[16,1280]{1,0:T(8,128)(2,1)S(1)}, u32[]{:S(2)}, u32[]{:S(2)}) collective-permute-start(bf16[16,1280]{1,0:T(8,128)(2,1)S(1)} %get-tuple-element.38.refs_0_), channel_id=1, source_target_pairs={{0,17},{1,16},{2,19},{3,18},{4,21},{5,20},{6,23},{7,22},{8,25},{9,... | collective-permute-start | bytes 122888 | tf_op jit(solution)/shard_map/ppermute | solution.py:510
  55.5 5.1 %collective-permute-start.6 = (bf16[16,1280]{1,0:T(8,128)(2,1)S(1)}, bf16[16,1280]{1,0:T(8,128)(2,1)S(1)}, u32[]{:S(2)}, u32[]{:S(2)}) collective-permute-start(bf16[16,1280]{1,0:T(8,128)(2,1)S(1)} %get-tuple-element.38.refs_0_), channel_id=1, source_target_pairs={{0,18},{1,19},{2,16},{3,17},{4,22},{5,23},{6,20},{7,21},{8,26},{9,... | collective-permute-start | bytes 122888 | tf_op jit(solution)/shard_map/ppermute | solution.py:510
  56.3 4.8 %collective-permute-start.7 = (bf16[16,1280]{1,0:T(8,128)(2,1)S(1)}, bf16[16,1280]{1,0:T(8,128)(2,1)S(1)}, u32[]{:S(2)}, u32[]{:S(2)}) collective-permute-start(bf16[16,1280]{1,0:T(8,128)(2,1)S(1)} %get-tuple-element.38.refs_0_), channel_id=1, source_target_pairs={{0,19},{1,18},{2,17},{3,16},{4,23},{5,22},{6,21},{7,20},{8,27},{9,... | collective-permute-start | bytes 122888 | tf_op jit(solution)/shard_map/ppermute | solution.py:510
  61.1 7.2 %collective-permute-start.10 = (bf16[16,1280]{1,0:T(8,128)(2,1)S(1)}, bf16[16,1280]{1,0:T(8,128)(2,1)S(1)}, u32[]{:S(2)}, u32[]{:S(2)}) collective-permute-start(bf16[16,1280]{1,0:T(8,128)(2,1)S(1)} %get-tuple-element.44.refs_0_), channel_id=1, source_target_pairs={{0,12},{1,13},{2,14},{3,15},{4,8},{5,9},{6,10},{7,11},{8,4},{9,5},... | collective-permute-start | bytes 122888 | tf_op jit(solution)/shard_map/ppermute | solution.py:510
  63.1 5.2 %collective-permute-start.8 = (bf16[16,1280]{1,0:T(8,128)(2,1)S(1)}, bf16[16,1280]{1,0:T(8,128)(2,1)S(1)}, u32[]{:S(2)}, u32[]{:S(2)}) collective-permute-start(bf16[16,1280]{1,0:T(8,128)(2,1)S(1)} %get-tuple-element.44.refs_0_), channel_id=1, source_target_pairs={{0,4},{1,5},{2,6},{3,7},{4,0},{5,1},{6,2},{7,3},{8,12},{9,13},{10,... | collective-permute-start | bytes 122888 | tf_op jit(solution)/shard_map/ppermute | solution.py:510
  63.1 5.3 %collective-permute-start.9 = (bf16[16,1280]{1,0:T(8,128)(2,1)S(1)}, bf16[16,1280]{1,0:T(8,128)(2,1)S(1)}, u32[]{:S(2)}, u32[]{:S(2)}) collective-permute-start(bf16[16,1280]{1,0:T(8,128)(2,1)S(1)} %get-tuple-element.44.refs_0_), channel_id=1, source_target_pairs={{0,8},{1,9},{2,10},{3,11},{4,12},{5,13},{6,14},{7,15},{8,0},{9,1},... | collective-permute-start | bytes 122888 | tf_op jit(solution)/shard_map/ppermute | solution.py:510
